TPU v7x, 32 devices: a whole 2x2x4 slice. The times are simulated.
32 devices in a mesh: rows: 4 (over y, x), cols: 8 (over z, core).
Axes of the slice: x: 2, y: 2, z: 4, core: 2. Of those that a mesh axis runs over, the one named last changes fastest.
Arguments:
- file_pixels: bfloat16 [48, 128, 1024], P(None, ('rows', 'cols')), may hold values from -6 to 6
- patchify_weight: bfloat16 [64, 48], replicated, may hold values from -0.875 to 0.875
- patchify_bias: float32 [64], replicated, may hold values from -3 to 3
- norm_gain: float32 [64], replicated, may hold values from 0.5 to 1.5
- norm_offset_vector: float32 [64], replicated, may hold values from -3 to 3
- kernel: float32 [64, 49], replicated, may hold values from -0.875 to 0.875
- kernel_offset: float32 [64], replicated, may hold values from -3 to 3
- cotangent: bfloat16 [64, 128, 1024], P(None, 'rows', 'cols'), may hold values from -10 to 10, as said below
Outputs:
- stem_output: bfloat16 [64, 128, 1024], P(None, 'rows', 'cols')
- weight_grad: float32 [64, 48], replicated
- bias_grad: float32 [64], replicated
- norm_scale_gradient: float32 [64], replicated
- shift_grad: float32 [64], replicated
- kernel_grad: float32 [64, 49], replicated
- offset_grad: float32 [64], replicated
Inputs may be any that keep to these rules, and one draw needn't show every extreme that they name: A cotangent of order one.
All inputs are finite; a program needn't handle non-finite values.
Results may differ from a plain program's by a relative error of at most 0.0055.
Values may be sent and summed in bfloat16 or wider, within the bound.
No kernel may reach another device: no remote copies, remote signals or barrier semaphores. Data moves between devices by JAX's collectives and lax.ppermute only.
A program may use at most 128 MiB of HBM per device.

v0:
```python
import math

import jax
import jax.numpy as jnp
from jax import lax
from jax.sharding import PartitionSpec as P

norm_eps = 1e-06
side = 7


def extended(block, sides, width):
    for axis, dim in sides:
        count = lax.axis_size(axis)
        forward = [(i, i + 1) for i in range(count - 1)]
        backward = [(target, source) for source, target in forward]
        low = lax.ppermute(
            lax.slice_in_dim(block, block.shape[dim] - width, None, axis=dim), axis, forward
        )
        high = lax.ppermute(lax.slice_in_dim(block, 0, width, axis=dim), axis, backward)
        block = jnp.concatenate([low, block, high], axis=dim)
    return block


def embed_patches(pixel_values, weight, bias):
    flat = pixel_values.reshape(pixel_values.shape[0], -1)
    mixed = jnp.dot(weight, flat, preferred_element_type=jnp.float32) + bias[:, None]
    return mixed.astype(jnp.bfloat16).reshape(
        weight.shape[0], pixel_values.shape[1], pixel_values.shape[2]
    )


def apply_layer_norm(patch_embedding):
    values = patch_embedding.astype(jnp.float32)
    center = values - jnp.mean(values, axis=0, keepdims=True)
    spread = jnp.mean(center * center, axis=0, keepdims=True)
    inverse_deviation = lax.rsqrt(spread + norm_eps)
    return (center * inverse_deviation, inverse_deviation)


def depthwise(padded, taps, height, breadth):
    total = jnp.zeros((padded.shape[0], height, breadth), jnp.float32)
    for tap_row in range(side):
        for tap_col in range(side):
            window = padded[:, tap_row : tap_row + height, tap_col : tap_col + breadth].astype(
                jnp.float32
            )
            total = total + taps[:, tap_row * side + tap_col][:, None, None] * window
    return total


def kernel_terms(padded, upstream, height, breadth):
    terms = []
    for tap_row in range(side):
        for tap_col in range(side):
            window = padded[:, tap_row : tap_row + height, tap_col : tap_col + breadth].astype(
                jnp.float32
            )
            terms.append(jnp.sum(window * upstream, axis=(1, 2)))
    return jnp.stack(terms, axis=1)


def per_device(
    file_pixels,
    patchify_weight,
    patchify_bias,
    norm_gain,
    norm_offset_vector,
    kernel,
    kernel_offset,
    cotangent,
):
    height = cotangent.shape[1]
    breadth = cotangent.shape[2]
    factor = 1.0 / math.sqrt(height * lax.axis_size("rows") * breadth * lax.axis_size("cols"))
    patch_embedding = lax.all_to_all(
        embed_patches(file_pixels, patchify_weight, patchify_bias),
        "cols",
        split_axis=2,
        concat_axis=1,
        tiled=True,
    )
    centered_input, inverse_deviation = apply_layer_norm(patch_embedding)
    scale_factor = norm_gain[:, None, None]
    normalized_output = (centered_input * scale_factor + norm_offset_vector[:, None, None]).astype(
        jnp.bfloat16
    )
    tall = extended(normalized_output, (("rows", 1),), 3)
    padded = extended(tall, (("cols", 2),), 3)
    cot_tall = extended(cotangent, (("rows", 1),), 3)
    cot_pad = extended(cot_tall, (("cols", 2),), 3)
    stem_output = (
        depthwise(padded, kernel, height, breadth) + kernel_offset[:, None, None]
    ).astype(jnp.bfloat16)
    upstream = cotangent.astype(jnp.float32) * factor
    kernel_grad = kernel_terms(padded, upstream, height, breadth)
    offset_grad = jnp.sum(upstream, axis=(1, 2))
    normalized_gradient = depthwise(cot_pad, kernel[:, ::-1], height, breadth) * factor
    norm_scale_gradient = jnp.sum(normalized_gradient * centered_input, axis=(1, 2))
    shift_grad = jnp.sum(normalized_gradient, axis=(1, 2))
    input_gradient = normalized_gradient * scale_factor
    patch_gradient = inverse_deviation * (
        input_gradient
        - jnp.mean(input_gradient, axis=0, keepdims=True)
        - centered_input * jnp.mean(input_gradient * centered_input, axis=0, keepdims=True)
    )
    patch_gradient = patch_gradient.astype(jnp.bfloat16)
    local_grad = lax.all_to_all(patch_gradient, "cols", split_axis=1, concat_axis=2, tiled=True)
    partial_weight = lax.dot_general(
        local_grad.reshape(local_grad.shape[0], -1),
        file_pixels.reshape(file_pixels.shape[0], -1),
        (((1,), (1,)), ((), ())),
        preferred_element_type=jnp.float32,
    )
    bias_part = jnp.sum(local_grad.astype(jnp.float32), axis=(1, 2))
    totals = lax.psum(
        (partial_weight, bias_part, norm_scale_gradient, shift_grad, kernel_grad, offset_grad),
        ("rows", "cols"),
    )
    return (stem_output, totals[0], totals[1], totals[2], totals[3], totals[4], totals[5])


def solution(mesh):
    return jax.shard_map(
        per_device,
        mesh=mesh,
        in_specs=(
            P(None, ("rows", "cols"), None),
            P(),
            P(),
            P(),
            P(),
            P(),
            P(),
            P(None, "rows", "cols"),
        ),
        out_specs=(P(None, "rows", "cols"), P(), P(), P(), P(), P(), P()),
        check_vma=False,
    )
```

profile of v0, /device:TPU:0, one launch (start us, length us, event | category | flops | bytes accessed | tf_op | source)
XLA Modules:
  0.0 252.8 jit_solution(2050309835722551886)
XLA Ops:
  6.3 6.5 %all-to-all-start = ((bf16[8,2,16384]{2,1,0:T(2,128)(2,1)}), bf16[8,2,16384]{2,1,0:T(2,128)(2,1)S(1)}, u32[]{:S(2)}, u32[]{:S(2)}) async-start(bf16[8,2,16384]{2,1,0:T(2,128)(2,1)} %reshape.176), calls=%async_computation | async-start | bytes 1048576 | tf_op jit(solution)/shard_map/all_to_all | solution.py:76
  12.8 1.7 copy.133
  16.0 4.6 %collective-permute-start.4 = (bf16[64,3,128]{0,1,2:T(4,128)(2,1)S(1)}, bf16[64,3,128]{0,1,2:T(4,128)(2,1)S(1)}, u32[]{:S(2)}, u32[]{:S(2)}) collective-permute-start(bf16[64,3,128]{0,1,2:T(4,128)(2,1)S(1)} %get-tuple-element.130), channel_id=1, source_target_pairs={{0,8},{8,16},{16,24},{1,9},{9,17},{17,25},{2,10},{10,18},{18,26},{... | collective-permute-start | bytes 147464 | tf_op jit(solution)/shard_map/ppermute | solution.py:17
  26.8 3.2 %collective-permute-done.7 = bf16[64,38,3]{0,1,2:T(8,128)(2,1)S(1)} collective-permute-done((bf16[64,38,3]{0,1,2:T(8,128)(2,1)S(1)}, bf16[64,38,3]{0,1,2:T(8,128)(2,1)S(1)}, u32[]{:S(2)}, u32[]{:S(2)}) %collective-permute-start.7) | collective-permute-done | bytes 14624 | tf_op jit(solution)/shard_map/ppermute | solution.py:20
  30.0 4.0 %maximum_maximum_fusion.1 = (bf16[64,38,131]{0,1,2:T(8,128)(2,1)S(1)}, bf16[64,38,131]{0,1,2:T(8,128)(2,1)S(1)}) fusion(bf16[64,3,128]{0,1,2:T(4,128)(2,1)S(1)} %collective-permute-done.5, bf16[64,32,128]{0,1,2:T(8,128)(2,1)} %copy-done.1, bf16[64,3,128]{0,1,2:T(4,128)(2,1)S(1)} %collective-permute-done.4, ...), kind=kLoop, calls=%fused_computation.244 | loop fusion | flops 5097472 | bytes 1926144 | tf_op jit(solution)/shard_map/concatenate | solution.py:21
  34.0 1.6 reshape.177
  35.6 14.8 %copy.124 = f32[64,4,8,128]{1,0,3,2:T(8,128)} copy(bf16[64,4,8,128]{0,1,3,2:T(4,128)(2,1)} %bitcast.173) | data formatting | bytes 1572864 | tf_op jit(solution)/shard_map/convert_element_type | solution.py:34
  50.4 13.8 %bitcast_reduce_fusion = f32[8,4,128]{1,2,0:T(8,128)S(1)} fusion(f32[64,4,8,128]{1,0,3,2:T(8,128)} %copy.124), kind=kLoop, calls=%fused_computation.330 | loop fusion | flops 258048 | bytes 1064960 | tf_op jit(solution)/shard_map/reduce_sum | solution.py:35
  64.7 19.5 %copy.125 = f32[64,8,4,128]{0,2,1,3:T(4,128)} copy(f32[64,8,4,128]{2,0,3,1:T(8,128)} %bitcast.170) | data formatting | bytes 2097152 | tf_op jit(solution)/shard_map/convert_element_type | solution.py:34
  84.2 15.7 %multiply_reduce_fusion = f32[8,4,128]{1,2,0:T(8,128)} fusion(f32[8,4,128]{1,2,0:T(8,128)S(1)} %copy.129, f32[64,4,8,128]{1,0,3,2:T(8,128)} %copy.124), kind=kLoop, calls=%fused_computation | loop fusion | flops 782336 | bytes 1081344 | tf_op jit(solution)/shard_map/reduce_sum | solution.py:36
  101.4 23.1 %multiply_reduce_fusion.1 = (f32[64]{0:T(128)}, f32[32,128]{0,1:T(8,128)S(1)}, f32[32,128]{0,1:T(8,128)S(1)}, f32[64]{0:T(128)}, f32[64,32,128]{0,1,2:T(8,128)S(1)}) fusion(f32[64,32,128]{0,1,2:T(8,128)} %bitcast.171, f32[32,128]{0,1:T(8,128)S(1)} %copy.132, f32[32,128]{0,1:T(8,128)S(1)} %copy.128, f32[64]{0:T(128)} %broadcast_multiply_fusion.3, ...), kind=kLoop, calls=%fused_computation.226 | loop fusion | flops 45604736 | bytes 24818688 | tf_op jit(solution)/shard_map/reduce_sum | solution.py:99
  124.5 2.5 multiply_convert_fusion
  128.4 5.0 %collective-permute-start = (bf16[64,3,128]{0,1,2:T(4,128)(2,1)S(1)}, bf16[64,3,128]{0,1,2:T(4,128)(2,1)S(1)}, u32[]{:S(2)}, u32[]{:S(2)}) collective-permute-start(bf16[64,3,128]{0,1,2:T(4,128)(2,1)S(1)} %get-tuple-element.132), channel_id=1, source_target_pairs={{0,8},{8,16},{16,24},{1,9},{9,17},{17,25},{2,10},{10,18},{18,26},{... | collective-permute-start | bytes 147464 | tf_op jit(solution)/shard_map/ppermute | solution.py:17
  136.6 3.7 %collective-permute-start.2 = (bf16[64,38,3]{0,1,2:T(8,128)(2,1)S(1)}, bf16[64,38,3]{0,1,2:T(8,128)(2,1)S(1)}, u32[]{:S(2)}, u32[]{:S(2)}) collective-permute-start(bf16[64,38,3]{0,1,2:T(8,128)(2,1)S(1)} %get-tuple-element.128), channel_id=1, source_target_pairs={{0,1},{1,2},{2,3},{3,4},{4,5},{5,6},{6,7},{8,9},{9,10},{10,11},{11... | collective-permute-start | bytes 43784 | tf_op jit(solution)/shard_map/ppermute | solution.py:17
  141.8 1.9 copy.139
  143.7 6.2 %all-to-all-start.1 = ((bf16[64,32,128]{2,0,1:T(8,128)(2,1)}), bf16[64,32,128]{2,0,1:T(8,128)(2,1)}, u32[]{:S(2)}, u32[]{:S(2)}) async-start(bf16[64,32,128]{2,0,1:T(8,128)(2,1)} %copy.139), calls=%async_computation.1 | async-start | bytes 1048576 | tf_op jit(solution)/shard_map/all_to_all | solution.py:108
  149.9 3.6 %maximum_maximum_fusion = (bf16[64,38,131]{0,1,2:T(8,128)(2,1)S(1)}, bf16[64,38,131]{0,1,2:T(8,128)(2,1)S(1)}) fusion(bf16[64,3,128]{0,1,2:T(4,128)(2,1)} %copy-done.4, bf16[64,32,128]{0,1,2:T(8,128)(2,1)S(1)} %get-tuple-element.121, bf16[64,3,128]{0,1,2:T(4,128)(2,1)} %copy-done.6, bf16[64,38,3]{0,1,2:T(8,128)(2,1)S(1)} %collective-permute-done.2, ...), kind=kLoop, calls=%fused_computation.242 | loop fusion | flops 5097472 | bytes 1926144 | tf_op jit(solution)/shard_map/concatenate | solution.py:21
  154.9 7.5 %fusion.143 = (f32[64]{0:T(128)}, f32[64]{0:T(128)}, f32[64]{0:T(128)}, f32[64]{0:T(128)}, f32[64]{0:T(128)}, /*index=5*/f32[64]{0:T(128)}, f32[64]{0:T(128)}, f...) fusion(bf16[64,32,128]{0,1,2:T(8,128)(2,1)S(1)} %copy-done.2, ...), kind=kLoop, calls=%fused_computation.196 | loop fusion | flops 14940992 | bytes 9966336 | tf_op jit(solution)/shard_map/reduce_sum | solution.py:59
  162.7 7.2 %fusion.147 = (f32[64]{0:T(128)}, f32[64]{0:T(128)}, f32[64]{0:T(128)}, f32[64]{0:T(128)}, f32[64]{0:T(128)}, /*index=5*/f32[64]{0:T(128)}, f32[64]{0:T(128)}, f...) fusion(bf16[64,32,128]{0,1,2:T(8,128)(2,1)S(1)} %copy-done.2, ...), kind=kLoop, calls=%fused_computation.200 | loop fusion | flops 14678912 | bytes 9966080 | tf_op jit(solution)/shard_map/reduce_sum | solution.py:59
  170.3 17.8 %add_convert_fusion = bf16[64,32,128]{0,1,2:T(8,128)(2,1)} fusion(bf16[64,32,128]{0,1,2:T(8,128)(2,1)S(1)} %get-tuple-element.121, bf16[64,3,128]{0,1,2:T(4,128)(2,1)S(1)} %copy-done.5, bf16[64,3,128]{0,1,2:T(4,128)(2,1)S(1)} %copy-done.7, f32[64]{0:T(128)} %param.14, f32[64]{0:T(128)} %get-tuple-element.181, f32[64]{0:T(128)} %get-tuple-element.182, ...), kind=kLoop, calls=%fused_computation.229 | loop fusion | flops 43515904 | bytes 23179776 | tf_op jit(solution)/shard_map/convert_element_type | solution.py:94
  188.2 3.6 %copy.141 = bf16[64,32,128]{2,1,0:T(8,128)(2,1)} copy(bf16[64,32,128]{0,1,2:T(8,128)(2,1)} %add_convert_fusion) | data formatting | bytes 1048576
  192.0 6.4 %fusion.146 = (f32[64]{0:T(128)}, f32[64]{0:T(128)}, f32[64]{0:T(128)}, f32[64]{0:T(128)}, f32[64]{0:T(128)}, /*index=5*/f32[64]{0:T(128)}, f32[64]{0:T(128)}, f32[64]{0:T(128)}, f32[64]{0:T(128)}, f32[64]{0:T(128)}) fusion(bf16[64,32,128]{0,1,2:T(8,128)(2,1)S(1)} %copy-done.2, bf16[64,38,131]{0,1,2:T(8,128)(2,1)S(1)} %get-tuple-element.127, ...), kind=kLoop, calls=%fused_computation.199 | loop fusion | flops 13106560 | bytes 2722304 | tf_op jit(solution)/shard_map/reduce_sum | solution.py:59
  198.7 4.2 %stack.199 = f32[64,49]{0,1:T(8,128)S(1)} concatenate(f32[64,1]{0,1:T(1,128)S(1)} %bitcast.200, f32[64,1]{0,1:T(1,128)S(1)} %bitcast.201, f32[64,1]{0,1:T(1,128)S(1)} %bitcast.199, f32[64,1]{0,1:T(1,128)} %bitcast.226, f32[64,1]{0,1:T(1,128)} %bitcast.222, f32[64,1]{0,1:T(1,128)S(1)} %bitcast.182, f32[64,1]{0,1:T(1,128)S(1)} %bitcast.183, f32[64,1]{0,1:T(1,128)S(1)} %bitcast.203, ...), dimensions={1} | concatenate | bytes 25088 | tf_op jit(solution)/shard_map/stack | solution.py:60
  207.2 45.6 %all-reduce = (f32[64,48]{0,1:T(8,128)}, f32[64]{0:T(128)}, f32[64]{0:T(128)}, f32[64]{0:T(128)}, f32[64,49]{0,1:T(8,128)}, /*index=5*/f32[64]{0:T(128)}) all-reduce(f32[64,48]{0,1:T(8,128)S(1)} %fusion.181, f32[64]{0:T(128)S(1)} %convert_reduce_fusion, f32[64]{0:T(128)S(1)} %copy-done.67, ...), channel_id=1, replica_groups=mesh['rows'=4,'cols'=8] {'rows','cols'}, use_global_device_ids=true, to_apply=%region_4.0 | all-reduce | flops 6464 | bytes 51712 | tf_op jit(solution)/shard_map/psum | solution.py:116
  (203 shorter events, 27.3 us)
Async XLA Ops:
  3.9 8.9 %copy-start.9 = (bf16[64,32,128]{2,1,0:T(8,128)(2,1)S(1)}, bf16[64,32,128]{2,1,0:T(8,128)(2,1)}, u32[]{:S(2)}) copy-start(bf16[64,32,128]{2,1,0:T(8,128)(2,1)} %param.15) | copy-start | bytes 1572868
  4.8 15.7 %copy-start.10 = (f32[64,49]{0,1:T(8,128)S(1)}, f32[64,49]{0,1:T(8,128)}, u32[]{:S(2)}) copy-start(f32[64,49]{0,1:T(8,128)} %param.13) | copy-start | bytes 37636
  6.3 20.0 %copy-start.78 = (f32[64]{0:T(128)S(1)}, f32[64]{0:T(128)}, u32[]{:S(2)}) copy-start(f32[64]{0:T(128)} %param.11) | copy-start | bytes 772
  6.3 27.6 %all-to-all-start = ((bf16[8,2,16384]{2,1,0:T(2,128)(2,1)}), bf16[8,2,16384]{2,1,0:T(2,128)(2,1)S(1)}, u32[]{:S(2)}, u32[]{:S(2)}) async-start(bf16[8,2,16384]{2,1,0:T(2,128)(2,1)} %reshape.176), calls=%async_computation | async-start | bytes 1048576 | tf_op jit(solution)/shard_map/all_to_all | solution.py:76
  14.5 12.3 %copy-start.1 = (bf16[64,32,128]{0,1,2:T(8,128)(2,1)}, bf16[64,32,128]{0,1,2:T(8,128)(2,1)S(1)}, u32[]{:S(2)}) copy-start(bf16[64,32,128]{0,1,2:T(8,128)(2,1)S(1)} %copy.133) | copy-start | bytes 1572868
  14.7 7.8 %collective-permute-start.5 = (bf16[64,3,128]{0,1,2:T(4,128)(2,1)S(1)}, bf16[64,3,128]{0,1,2:T(4,128)(2,1)S(1)}, u32[]{:S(2)}, u32[]{:S(2)}) collective-permute-start(bf16[64,3,128]{0,1,2:T(4,128)(2,1)S(1)} %get-tuple-element.131), channel_id=1, source_target_pairs={{8,0},{16,8},{24,16},{9,1},{17,9},{25,17},{10,2},{18,10},{26,18},{... | collective-permute-start | bytes 147464 | tf_op jit(solution)/shard_map/ppermute | solution.py:20
  16.0 7.7 %collective-permute-start.4 = (bf16[64,3,128]{0,1,2:T(4,128)(2,1)S(1)}, bf16[64,3,128]{0,1,2:T(4,128)(2,1)S(1)}, u32[]{:S(2)}, u32[]{:S(2)}) collective-permute-start(bf16[64,3,128]{0,1,2:T(4,128)(2,1)S(1)} %get-tuple-element.130), channel_id=1, source_target_pairs={{0,8},{8,16},{16,24},{1,9},{9,17},{17,25},{2,10},{10,18},{18,26},{... | collective-permute-start | bytes 147464 | tf_op jit(solution)/shard_map/ppermute | solution.py:17
  23.7 3.1 %collective-permute-start.6 = (bf16[64,38,3]{0,1,2:T(8,128)(2,1)S(1)}, bf16[64,38,3]{0,1,2:T(8,128)(2,1)S(1)}, u32[]{:S(2)}, u32[]{:S(2)}) collective-permute-start(bf16[64,38,3]{0,1,2:T(8,128)(2,1)S(1)} %get-tuple-element.124), channel_id=1, source_target_pairs={{0,1},{1,2},{2,3},{3,4},{4,5},{5,6},{6,7},{8,9},{9,10},{10,11},{11... | collective-permute-start | bytes 43784 | tf_op jit(solution)/shard_map/ppermute | solution.py:17
  25.0 5.0 %collective-permute-start.7 = (bf16[64,38,3]{0,1,2:T(8,128)(2,1)S(1)}, bf16[64,38,3]{0,1,2:T(8,128)(2,1)S(1)}, u32[]{:S(2)}, u32[]{:S(2)}) collective-permute-start(bf16[64,38,3]{0,1,2:T(8,128)(2,1)S(1)} %get-tuple-element.125), channel_id=1, source_target_pairs={{1,0},{2,1},{3,2},{4,3},{5,4},{6,5},{7,6},{9,8},{10,9},{11,10},{12... | collective-permute-start | bytes 43784 | tf_op jit(solution)/shard_map/ppermute | solution.py:20
  101.3 23.2 %copy-start.3 = (f32[64,8,4,128]{0,2,1,3:T(4,128)S(1)}, f32[64,8,4,128]{0,2,1,3:T(4,128)}, u32[]{:S(2)}) copy-start(f32[64,8,4,128]{0,2,1,3:T(4,128)} %copy.125) | copy-start | bytes 3145732
  101.4 23.2 %copy-start.77 = (f32[64]{0:T(128)S(1)}, f32[64]{0:T(128)}, u32[]{:S(2)}) copy-start(f32[64]{0:T(128)} %broadcast_multiply_fusion.3) | copy-start | bytes 772
  101.4 23.2 %copy-start.79 = (f32[64]{0:T(128)S(1)}, f32[64]{0:T(128)}, u32[]{:S(2)}) copy-start(f32[64]{0:T(128)} %param.11) | copy-start | bytes 772
  101.4 23.2 %copy-start.80 = (f32[64]{0:T(128)S(1)}, f32[64]{0:T(128)}, u32[]{:S(2)}) copy-start(f32[64]{0:T(128)} %param.12) | copy-start | bytes 772
  127.1 7.3 %collective-permute-start.1 = (bf16[64,3,128]{0,1,2:T(4,128)(2,1)S(1)}, bf16[64,3,128]{0,1,2:T(4,128)(2,1)S(1)}, u32[]{:S(2)}, u32[]{:S(2)}) collective-permute-start(bf16[64,3,128]{0,1,2:T(4,128)(2,1)S(1)} %get-tuple-element.133), channel_id=1, source_target_pairs={{8,0},{16,8},{24,16},{9,1},{17,9},{25,17},{10,2},{18,10},{26,18},{... | collective-permute-start | bytes 147464 | tf_op jit(solution)/shard_map/ppermute | solution.py:20
  128.4 7.5 %collective-permute-start = (bf16[64,3,128]{0,1,2:T(4,128)(2,1)S(1)}, bf16[64,3,128]{0,1,2:T(4,128)(2,1)S(1)}, u32[]{:S(2)}, u32[]{:S(2)}) collective-permute-start(bf16[64,3,128]{0,1,2:T(4,128)(2,1)S(1)} %get-tuple-element.132), channel_id=1, source_target_pairs={{0,8},{8,16},{16,24},{1,9},{9,17},{17,25},{2,10},{10,18},{18,26},{... | collective-permute-start | bytes 147464 | tf_op jit(solution)/shard_map/ppermute | solution.py:17
  136.6 13.2 %collective-permute-start.2 = (bf16[64,38,3]{0,1,2:T(8,128)(2,1)S(1)}, bf16[64,38,3]{0,1,2:T(8,128)(2,1)S(1)}, u32[]{:S(2)}, u32[]{:S(2)}) collective-permute-start(bf16[64,38,3]{0,1,2:T(8,128)(2,1)S(1)} %get-tuple-element.128), channel_id=1, source_target_pairs={{0,1},{1,2},{2,3},{3,4},{4,5},{5,6},{6,7},{8,9},{9,10},{10,11},{11... | collective-permute-start | bytes 43784 | tf_op jit(solution)/shard_map/ppermute | solution.py:17
  140.3 9.6 %collective-permute-start.3 = (bf16[64,38,3]{0,1,2:T(8,128)(2,1)S(1)}, bf16[64,38,3]{0,1,2:T(8,128)(2,1)S(1)}, u32[]{:S(2)}, u32[]{:S(2)}) collective-permute-start(bf16[64,38,3]{0,1,2:T(8,128)(2,1)S(1)} %get-tuple-element.129), channel_id=1, source_target_pairs={{1,0},{2,1},{3,2},{4,3},{5,4},{6,5},{7,6},{9,8},{10,9},{11,10},{12... | collective-permute-start | bytes 43784 | tf_op jit(solution)/shard_map/ppermute | solution.py:20
  143.7 59.2 %all-to-all-start.1 = ((bf16[64,32,128]{2,0,1:T(8,128)(2,1)}), bf16[64,32,128]{2,0,1:T(8,128)(2,1)}, u32[]{:S(2)}, u32[]{:S(2)}) async-start(bf16[64,32,128]{2,0,1:T(8,128)(2,1)} %copy.139), calls=%async_computation.1 | async-start | bytes 1048576 | tf_op jit(solution)/shard_map/all_to_all | solution.py:108
  162.4 7.6 %copy-start.13 = (f32[64]{0:T(128)S(1)}, f32[64]{0:T(128)}, u32[]{:S(2)}) copy-start(f32[64]{0:T(128)} %get-tuple-element.145) | copy-start | bytes 772
  162.4 7.6 %copy-start.14 = (f32[64]{0:T(128)S(1)}, f32[64]{0:T(128)}, u32[]{:S(2)}) copy-start(f32[64]{0:T(128)} %get-tuple-element.146) | copy-start | bytes 772
  162.4 7.6 %copy-start.15 = (f32[64]{0:T(128)S(1)}, f32[64]{0:T(128)}, u32[]{:S(2)}) copy-start(f32[64]{0:T(128)} %get-tuple-element.147) | copy-start | bytes 772
  198.4 8.8 %copy-start.67 = (f32[64]{0:T(128)S(1)}, f32[64]{0:T(128)}, u32[]{:S(2)}) copy-start(f32[64]{0:T(128)} %get-tuple-element.49) | copy-start | bytes 772
  198.4 8.8 %copy-start.68 = (f32[64]{0:T(128)S(1)}, f32[64]{0:T(128)}, u32[]{:S(2)}) copy-start(f32[64]{0:T(128)} %get-tuple-element.104) | copy-start | bytes 772
  198.4 8.8 %copy-start.69 = (f32[64]{0:T(128)S(1)}, f32[64]{0:T(128)}, u32[]{:S(2)}) copy-start(f32[64]{0:T(128)} %get-tuple-element.105) | copy-start | bytes 772
  (67 other events, 455.9 us)
where the time goes:
time: 255 us; the launch traced here: 253 us
  other arithmetic  105 us (41%)
  local copies, waits for them, and re-layouts  58.3 us (23%)
  blocking collectives  45.6 us (18%)
  starting transfers between devices  32.5 us (13%)
  waiting for transfers between devices  6.88 us (3%)
    psum x1, blocking collectives, per_device(): lax.psum((partial_weight, bias_part, norm_scale_gradient, shift_grad, ker...  45.6 us
    convert_element_type x2, local copies, waits for them, and re-layouts, apply_layer_norm(): values = patch_embedding.astype(jnp.float32)  34.3 us
    reduce_sum x1, other arithmetic, per_device(): jnp.sum(normalized_gradient * centered_input, axis=(1, 2))  23.1 us
    reduce_sum x4, other arithmetic, kernel_terms(): terms.append(jnp.sum(window * upstream, axis=(1, 2)))  22.5 us
    convert_element_type x1, other arithmetic, per_device(): stem_output = (depthwise(padded, kernel, height, breadth) + kernel_offset...  17.8 us
    reduce_sum x1, other arithmetic, apply_layer_norm(): spread = jnp.mean(center * center, axis=0, keepdims=True)  15.7 us
    ppermute x4, starting transfers between devices, extended(): lax.ppermute(lax.slice_in_dim(block, block.shape[dim] - width, None, axis...  14.5 us
    reduce_sum x1, other arithmetic, apply_layer_norm(): center = values - jnp.mean(values, axis=0, keepdims=True)  13.8 us
  transfers between devices with their start and end apart: 10, of which 4 were waited for; matrix products, arithmetic and copies ran while one was open for 24% of the time, Pallas kernels for 0%

commit v1 on v0

v1 whole, which is shorter than its diff:
```python
import functools
import math

import jax
import jax.numpy as jnp
from jax import lax
from jax.experimental import pallas as pl
from jax.experimental.pallas import tpu as pltpu
from jax.sharding import PartitionSpec as P

norm_eps = 1e-06
side = 7
LANES = 128
GROUP = 8
PITCH = 48
DEPTH = 8 * PITCH
VMEM = 56 * 1024 * 1024
bf16, f32 = jnp.bfloat16, jnp.float32

NN = (((1,), (0,)), ((), ()))
NT = (((1,), (1,)), ((), ()))
TN = (((0,), (0,)), ((), ()))


def mm(a, b, dims=NN):
    return lax.dot_general(a, b, dims, preferred_element_type=f32)


def iota(shape, axis):
    return lax.broadcasted_iota(jnp.int32, shape, axis)


def split2(x):
    high = x.astype(bf16)
    return high, (x - high.astype(f32)).astype(bf16)


def one_hot(cond):
    return jnp.where(cond, 1.0, 0.0).astype(bf16)


def cdiv(a, b):
    return -(-a // b)


def bucket(x, width, count):
    return sum((x >= width * n).astype(jnp.int32) for n in range(1, count))


def params_kernel(colors, file_rows, wt_ref, taps_ref, bias_ref, gain_ref, off_ref, koff_ref,
                  wk_ref, wh_ref, kb_ref, kf_ref, vec_ref):
    channels = wt_ref.shape[1]
    rows = channels * GROUP
    block = colors * file_rows
    per = GROUP // file_rows

    def weights(width, out_ref):
        lanes = per * width
        src = iota((colors, lanes), 1)
        part = bucket(src, width, per)
        inside = src - part * width
        color = bucket(inside, file_rows, cdiv(width, file_rows))
        spread = one_hot((color == iota((colors, lanes), 0)) & (inside < block))
        wide = mm(wt_ref[...], spread, TN).astype(bf16)
        row = iota((rows, channels), 0)
        tall = one_hot(lax.shift_right_logical(row, 3) == iota((rows, channels), 1))
        full = mm(tall, wide)
        src = iota((rows, lanes), 1)
        part = bucket(src, width, per)
        inside = src - part * width
        own = part * file_rows + lax.bitwise_and(inside, file_rows - 1)
        keep = own == lax.bitwise_and(iota((rows, lanes), 0), GROUP - 1)
        out_ref[...] = jnp.where(keep, full, 0.0).astype(bf16)

    weights(block, wk_ref)
    weights(wh_ref.shape[1] // per, wh_ref)

    taps = taps_ref[...]
    count = taps.shape[0]
    lane = iota((count, DEPTH), 1)
    copy = bucket(lane, PITCH, 8)
    at = lane - copy * PITCH - 5
    tap = at * side + copy
    valid = (at >= 0) & (at < side) & (copy < side)
    forward = jnp.where(valid & (tap == iota((count, DEPTH), 0)), 1.0, 0.0)
    backward = jnp.where(valid & (count - 1 - tap == iota((count, DEPTH), 0)), 1.0, 0.0)
    kf_ref[...] = lax.dot_general(taps, forward, TN, precision=lax.Precision.HIGHEST,
                                  preferred_element_type=f32)
    kb_ref[...] = lax.dot_general(taps, backward, TN, precision=lax.Precision.HIGHEST,
                                  preferred_element_type=f32)

    eye = iota((channels, channels), 0) == iota((channels, channels), 1)
    for n, ref in enumerate((bias_ref, gain_ref, off_ref, koff_ref)):
        row = jnp.broadcast_to(ref[...].reshape(1, channels), (channels, channels))
        column = jnp.sum(jnp.where(eye, row, 0.0), axis=1, keepdims=True)
        vec_ref[n] = jnp.broadcast_to(column, (channels, LANES))


def pack_kernel(x_ref, out_ref):
    colors, file_rows, width = x_ref.shape
    count = width // LANES
    block = colors * file_rows
    row, lane = iota((16, LANES), 0), iota((16, LANES), 1)
    pick = one_hot(((row < 3) & (lane == row + LANES - 3)) | ((row >= 11) & (row < 14) & (lane == row - 11)))
    edges = []
    for d in range(count):
        tile = x_ref[:, :, d * LANES:(d + 1) * LANES].reshape(block, LANES)
        out_ref[d, :block, :] = tile
        edges.append(mm(pick, tile, NT))
    none = jnp.zeros((8, block), f32)
    for d in range(count):
        left = edges[d - 1][:8] if d > 0 else none
        right = edges[d + 1][8:] if d < count - 1 else none
        halo = left + right
        chunks = []
        for start in range(0, 2 * LANES, LANES):
            stop = min(start + LANES, block)
            if stop <= start:
                chunks.append(jnp.zeros((8, LANES), f32))
            elif stop - start < LANES:
                chunks.append(jnp.concatenate(
                    [halo[:, start:stop], jnp.zeros((8, LANES - stop + start), f32)], axis=1))
            else:
                chunks.append(halo[:, start:stop])
        out_ref[d, block:block + 16, :] = jnp.concatenate(chunks, axis=0).astype(bf16)


def edges_kernel(cot_ref, top_ref, bot_ref, all_ref, edge_ref):
    channels, height, width = cot_ref.shape
    zeros = jnp.zeros((channels, 4, width), f32)
    top = jnp.concatenate([zeros, top_ref[...].astype(f32)], axis=1)
    bot = jnp.concatenate([bot_ref[...].astype(f32), zeros], axis=1)
    full = jnp.concatenate([top, cot_ref[...].astype(f32), bot], axis=1).astype(bf16)
    all_ref[...] = full
    row, lane = iota((8, width), 0), iota((8, width), 1)
    pick = one_hot(((row < 3) & (lane == row)) | ((row >= 3) & (row < 6) & (lane == row + width - 6)))
    edge_ref[...] = mm(pick, full.reshape(channels * PITCH, width), NT).astype(bf16)


def shifted(center, halo):
    rows, width = center.shape
    lane = iota((rows, width), 1)
    copies = []
    for move in range(-3, 4):
        if move == 0:
            copies.append(center)
        elif move > 0:
            copies.append(pltpu.roll(jnp.where(lane < move, halo, center), width - move, 1))
        else:
            copies.append(pltpu.roll(jnp.where(lane >= width + move, halo, center), -move, 1))
    copies.append(jnp.zeros((rows, width), center.dtype))
    return jnp.concatenate(copies, axis=0)


def toeplitz(base, height):
    taps = pltpu.roll(jnp.broadcast_to(base, (height, DEPTH)), 0, 1, stride=1, stride_axis=0)
    return jnp.concatenate(split2(taps), axis=0)


def back_kernel(factor, all_ref, left_ref, right_ref, kb_ref, halo_ref, grad_ref, sum_ref):
    channels, _, width = all_ref.shape
    height = grad_ref.shape[1]
    row, lane = iota((8, width), 0), iota((8, width), 1)
    from_left = one_hot((row >= 3) & (row < 6) & (lane == row + width - 6))
    from_right = one_hot((row < 3) & (lane == row))
    halo = mm(left_ref[...], from_left, TN) + mm(right_ref[...], from_right, TN)
    halo_ref[...] = halo.astype(bf16).reshape(channels, PITCH, width)

    def one(k, carry):
        plane = all_ref[k]
        stack = shifted(plane, halo_ref[k])
        both = mm(toeplitz(kb_ref[pl.ds(k, 1), :], height), stack)
        grad = (both[:height] + both[height:]) * factor
        grad_ref[k] = grad
        own = plane.astype(f32)[8:8 + height]
        sum_ref[0, k] = jnp.sum(grad.reshape(height // 8, 8, width), axis=0)
        sum_ref[1, k] = jnp.sum(own.reshape(height // 8, 8, width), axis=0) * factor
        return carry

    lax.fori_loop(0, channels, one, 0, unroll=4)


def layer_norm(patch, channels):
    values = patch.astype(bf16).astype(f32).reshape(channels, GROUP, LANES)
    center = values - jnp.mean(values, axis=0, keepdims=True)
    spread = jnp.mean(center * center, axis=0, keepdims=True)
    inverse = lax.rsqrt(spread + norm_eps)
    return center * inverse, inverse


def per_row(vec_ref, n):
    return vec_ref[n][:, None, :]


def main_kernel(colors, file_rows, factor, x_ref, wk_ref, vec_ref, grad_ref, sum_ref, all_ref, halo_ref,
                norm_ref, out_ref, norm_s, gram_s, diag_s):
    channels, height, width = grad_ref.shape
    block = colors * file_rows
    per = GROUP // file_rows
    inner = per * block
    rows = channels * GROUP
    bias, gain, offset = per_row(vec_ref, 0), per_row(vec_ref, 1), per_row(vec_ref, 2)
    scale_part = jnp.zeros((channels, GROUP, width), f32)
    ones = jnp.where(iota((16, width), 0) == 0, 1.0, 0.0).astype(bf16)
    for g in range(height // GROUP):
        pixels = jnp.concatenate([x_ref[per * g + a, :block, :] for a in range(per)], axis=0)
        patch = mm(wk_ref[...], pixels).reshape(channels, GROUP, width) + bias
        xhat, inverse = layer_norm(patch, channels)
        norm_s[:, g * GROUP:(g + 1) * GROUP, :] = xhat * gain + offset
        grad = grad_ref[:, g * GROUP:(g + 1) * GROUP, :]
        scale_part += grad * xhat
        inside = grad * gain
        mean_a = jnp.mean(inside, axis=0, keepdims=True)
        mean_b = jnp.mean(inside * xhat, axis=0, keepdims=True)
        patch_grad = (inverse * (inside - mean_a - xhat * mean_b)).astype(bf16).reshape(rows, width)
        gram = mm(jnp.concatenate([pixels, ones], axis=0), patch_grad, NT)
        if g == 0:
            gram_s[...] = gram
        else:
            gram_s[...] += gram

    def one(k, carry):
        plane = norm_s[k].astype(bf16)
        norm_ref[k] = plane
        stack = shifted(all_ref[k], halo_ref[k])
        cross = mm(plane, stack, NT)
        total = cross[:8]
        for a in range(1, height // 8):
            total += pltpu.roll(cross[8 * a:8 * a + 8], DEPTH - 8 * a, 1)
        diag_s[k] = total
        return carry

    lax.fori_loop(0, channels, one, 0, unroll=4)

    line = diag_s[:, 0, :]
    for b in range(1, 8):
        line += pltpu.roll(diag_s[:, b, :], DEPTH - b, 1)
    lane = iota((56, DEPTH), 1)
    copy = bucket(lane, PITCH, 8)
    at = lane - copy * PITCH - 5
    valid = (at >= 0) & (at < side) & (copy < side)
    taps = one_hot(valid & (side * side - 1 - at * side - copy == iota((56, DEPTH), 0)))
    line = jnp.concatenate([jnp.zeros((LANES - channels, DEPTH), f32), line], axis=0)
    result = sum(mm(taps, part, NT) for part in split2(line * factor))

    gather = one_hot(lax.shift_right_logical(iota((rows, LANES), 0), 3) == iota((rows, LANES), 1))
    src = iota((inner + 16, rows), 0)
    part = bucket(src, block, per + 1)
    own = part * file_rows + lax.bitwise_and(src - part * block, file_rows - 1)
    keep = (own == lax.bitwise_and(iota((inner + 16, rows), 1), GROUP - 1)) | (src >= inner)
    gram = jnp.where(keep, gram_s[...], 0.0)
    by_channel = sum(mm(part, gather) for part in split2(gram))
    src = iota((56, inner + 16), 1)
    part = bucket(src, block, per + 1)
    color = bucket(src - part * block, file_rows, colors)
    target = iota((56, inner + 16), 0)
    fold = one_hot(((color == target) & (src < inner)) | ((src == inner) & (target == colors)))
    result += sum(mm(fold, part) for part in split2(by_channel))
    for n, part in enumerate((scale_part, sum_ref[0], sum_ref[1])):
        pick = one_hot(iota((56, LANES), 0) == colors + 1 + n)
        line = sum(mm(pick, piece, NT) for piece in split2(part.reshape(rows, width)))
        result += sum(mm(piece, gather) for piece in split2(line))
    out_ref[...] = result


def stem_kernel(colors, file_rows, edge_ref, x_ref, top_ref, bot_ref, wk_ref, wh_ref, vec_ref, kf_ref, norm_ref,
                out_ref, all_s, halo_s):
    channels, height, width = norm_ref.shape
    block = colors * file_rows
    per = GROUP // file_rows
    half = per // 2
    chunks = wh_ref.shape[1] // (per * LANES)
    bias, gain, offset = per_row(vec_ref, 0), per_row(vec_ref, 1), per_row(vec_ref, 2)
    no_top, no_bot = edge_ref[0], edge_ref[1]
    no_left, no_right = edge_ref[2], edge_ref[3]
    shape = (channels, GROUP, width)
    lower = iota(shape, 1) < 4
    row_ok = jnp.where(lower, 1 - no_bot, 1 - no_top) > 0

    outer = [bot_ref[a] for a in range(half)] + [top_ref[a] for a in range(half)]
    pixels = jnp.concatenate([piece[:block] for piece in outer], axis=0)
    xhat, _ = layer_norm(mm(wk_ref[...], pixels).reshape(shape) + bias, channels)
    rows = jnp.where(row_ok, xhat * gain + offset, 0.0).astype(bf16)
    all_s[:, 0:8, :] = rows
    all_s[:, 8 + height:16 + height, :] = rows
    all_s[:, 8:8 + height, :] = norm_ref[...]

    groups = height // GROUP
    lines = []
    for g in range(groups + 1):
        pieces = []
        for a in range(per):
            piece = outer[a][block:block + 16] if g == groups else x_ref[per * g + a, block:block + 16, :]
            piece = piece.astype(f32)
            pieces += [piece[8 * c:8 * c + 8] for c in range(chunks)]
        lines.append(jnp.concatenate(pieces, axis=1))
    lines.append(jnp.zeros((LANES - 8 * len(lines), per * chunks * LANES), f32))
    lines = jnp.concatenate(lines, axis=0).astype(bf16)
    xhat, _ = layer_norm(mm(wh_ref[...], lines, NT).reshape(shape) + bias, channels)
    lane = iota(shape, 2)
    column = lax.bitwise_and(lane, 7)
    ok = jnp.where(column < 3, 1 - no_left, 1 - no_right) > 0
    ok = ok & (row_ok | (lane < 8 * groups))
    halo = jnp.where(ok, xhat * gain + offset, 0.0).astype(bf16).reshape(channels * GROUP, width)
    for g in range(groups + 1):
        moved = pltpu.roll(halo, width - 8 * g - 3, 1).reshape(shape)
        if g < groups:
            halo_s[:, 8 + 8 * g:16 + 8 * g, :] = moved
        else:
            halo_s[:, 0:8, :] = moved
            halo_s[:, 8 + height:16 + height, :] = moved

    def one(k, carry):
        both = mm(toeplitz(kf_ref[pl.ds(k, 1), :], height), shifted(all_s[k], halo_s[k]))
        out_ref[k] = (both[:height] + both[height:] + vec_ref[3, pl.ds(k, 1), :]).astype(bf16)
        return carry

    lax.fori_loop(0, channels, one, 0, unroll=4)


def kernel_call(body, out_shape, us, **kw):
    return pl.pallas_call(
        body,
        out_shape=out_shape,
        compiler_params=pltpu.CompilerParams(vmem_limit_bytes=VMEM),
        cost_estimate=pl.CostEstimate(flops=int(us * 1e9), bytes_accessed=int(us * 3e6), transcendentals=0),
        **kw,
    )


def shaped(shape, dtype):
    return jax.ShapeDtypeStruct(shape, dtype)


def shift(x, axis, step):
    count = lax.axis_size(axis)
    pairs = [(i, i + step) for i in range(count) if 0 <= i + step < count]
    return lax.ppermute(x, axis, pairs)


def total(x):
    for axis in ("cols", "rows"):
        count = lax.axis_size(axis)
        step = 1
        while step < count:
            x = x + lax.ppermute(x, axis, [(i, i ^ step) for i in range(count)])
            step *= 2
    return x


def per_device(
    file_pixels,
    patchify_weight,
    patchify_bias,
    norm_gain,
    norm_offset_vector,
    kernel,
    kernel_offset,
    cotangent,
):
    colors, file_rows, _ = file_pixels.shape
    channels, height, width = cotangent.shape
    n_rows, n_cols = lax.axis_size("rows"), lax.axis_size("cols")
    factor = 1.0 / math.sqrt(height * n_rows * width * n_cols)
    block = colors * file_rows
    per = GROUP // file_rows
    block_rows = block + 16
    padded = cdiv(block, LANES) * LANES
    rows = channels * GROUP
    tile = (channels, height, width)

    packed = kernel_call(pack_kernel, shaped((n_cols, block_rows, LANES), bf16), 2)(file_pixels)
    pixels = lax.all_to_all(packed, "cols", split_axis=0, concat_axis=0, tiled=True)

    top = shift(cotangent[:, height - 4:, :], "rows", 1)
    bot = shift(cotangent[:, :4, :], "rows", -1)
    cot_all, edges = kernel_call(
        edges_kernel,
        (shaped((channels, PITCH, width), bf16), shaped((8, channels * PITCH), bf16)),
        1.5,
    )(cotangent, top, bot)
    from_left = shift(edges, "cols", 1)
    from_right = shift(edges, "cols", -1)
    wk, wh, kb, kf, vec = kernel_call(
        functools.partial(params_kernel, colors, file_rows),
        (
            shaped((rows, per * block), bf16),
            shaped((rows, per * padded), bf16),
            shaped((channels, DEPTH), f32),
            shaped((channels, DEPTH), f32),
            shaped((4, channels, LANES), f32),
        ),
        1.5,
    )(patchify_weight.T, kernel.T, patchify_bias, norm_gain, norm_offset_vector, kernel_offset)
    cot_halo, grad, sums = kernel_call(
        functools.partial(back_kernel, factor),
        (
            shaped((channels, PITCH, width), bf16),
            shaped(tile, f32),
            shaped((2, channels, GROUP, width), f32),
        ),
        5,
    )(cot_all, from_left, from_right, kb)

    norm, part = kernel_call(
        functools.partial(main_kernel, colors, file_rows, factor),
        (shaped(tile, bf16), shaped((56, LANES), f32)),
        6,
        scratch_shapes=[
            pltpu.VMEM(tile, f32),
            pltpu.VMEM((per * block + 16, rows), f32),
            pltpu.VMEM((channels, 8, DEPTH), f32),
        ],
    )(pixels, wk, vec, grad, sums, cot_all, cot_halo)

    half = per // 2
    top = shift(pixels[n_cols - half:], "rows", 1)
    bot = shift(pixels[:half], "rows", -1)
    row_at, col_at = lax.axis_index("rows"), lax.axis_index("cols")
    at_edge = jnp.stack([row_at == 0, row_at == n_rows - 1, col_at == 0, col_at == n_cols - 1])
    vmem = pl.BlockSpec(memory_space=pltpu.VMEM)
    stem_output = kernel_call(
        functools.partial(stem_kernel, colors, file_rows),
        shaped(tile, bf16),
        5,
        in_specs=[pl.BlockSpec(memory_space=pltpu.SMEM)] + [vmem] * 8,
        scratch_shapes=[pltpu.VMEM((channels, PITCH, width), bf16)] * 2,
    )(at_edge.astype(jnp.int32), pixels, top, bot, wk, wh, vec, kf, norm)

    result = total(part)
    taps = side * side
    first, second = result[:, :channels], result[:, channels:2 * channels]
    return (
        stem_output,
        first[:colors].T,
        first[colors],
        first[colors + 1],
        first[colors + 2],
        second[:taps].T,
        first[colors + 3],
    )


def solution(mesh):
    return jax.shard_map(
        per_device,
        mesh=mesh,
        in_specs=(
            P(None, ("rows", "cols"), None),
            P(),
            P(),
            P(),
            P(),
            P(),
            P(),
            P(None, "rows", "cols"),
        ),
        out_specs=(P(None, "rows", "cols"), P(), P(), P(), P(), P(), P()),
        check_vma=False,
    )
```

time: 255 us -> 86.3 us (0.34)
  other arithmetic: 105 us -> 1.36 us
  local copies, waits for them, and re-layouts: 58.3 us -> 6.93 us
  blocking collectives: 45.6 us -> 0 us
  Pallas kernels: 0 us -> 37.4 us
    reduce_sum x8 -> x0, other arithmetic: 76.8 us -> none  [the longest x1 23.1 us: per_device(): jnp.sum(normalized_gradient * centered_input, axis=(1, 2))]
    psum x1 -> x0, blocking collectives: 45.6 us -> none  [per_device(): lax.psum((partial_weight, bias_part, norm_scale_gradient, shift_grad, ker...]
    pallas_call x0 -> x6, Pallas kernels: none -> 37.4 us  [the longest x1 13.6 us: per_device(): kernel_call(functools.partial(main_kernel, colors, file_rows, factor), (s...]
    convert_element_type x3 -> x0, local copies, waits for them, and re-layouts: 36.2 us -> none  [the longest x2 34.3 us: apply_layer_norm(): values = patch_embedding.astype(jnp.float32)]
    convert_element_type x2 -> x1, other arithmetic: 20.3 us -> 0.59 us  [per_device(): at_edge.astype(jnp.int32)]
    unnamed x167 -> x14, local copies, waits for them, and re-layouts: 11.3 us -> 3.24 us
    ppermute x8 -> x11, starting transfers between devices: 19.9 us -> 27.8 us  [the longest x6 15.7 us: shift(): return lax.ppermute(x, axis, pairs)]
    all_to_all x2 -> x1, starting transfers between devices: 12.6 us -> 4.88 us  [per_device(): lax.all_to_all(packed, 'cols', split_axis=0, concat_axis=0, tiled=True)]
  transfers between devices with their start and end apart: 10 -> 12, of which waited for: 4 -> 4; matrix products, arithmetic and copies ran while one was open for 24% -> 2% of each run, Pallas kernels for 0% -> 28%
where the time goes in v1:
time: 86.3 us; the launch traced here: 85.6 us
  Pallas kernels  37.4 us (43%)
  starting transfers between devices  32.7 us (38%)
  local copies, waits for them, and re-layouts  6.93 us (8%)
  waiting for transfers between devices  6.47 us (7%)
  other arithmetic  1.36 us (2%)
    ppermute x6, starting transfers between devices, shift(): return lax.ppermute(x, axis, pairs)  15.7 us
    pallas_call x1, Pallas kernels, per_device(): kernel_call(functools.partial(main_kernel, colors, file_rows, factor), (s...  13.6 us
    ppermute x5, starting transfers between devices, total(): x = x + lax.ppermute(x, axis, [(i, i ^ step) for i in range(count)])  12.2 us
    pallas_call x1, Pallas kernels, per_device(): kernel_call(functools.partial(stem_kernel, colors, file_rows), shaped(til...  8.66 us
    pallas_call x1, Pallas kernels, per_device(): kernel_call(functools.partial(back_kernel, factor), (shaped((channels, PI...  8.49 us
    ppermute x5, waiting for transfers between devices, total(): x = x + lax.ppermute(x, axis, [(i, i ^ step) for i in range(count)])  5.73 us
    all_to_all x1, starting transfers between devices, per_device(): lax.all_to_all(packed, 'cols', split_axis=0, concat_axis=0, tiled=True)  4.88 us
    unnamed x14, local copies, waits for them, and re-layouts  3.24 us
  transfers between devices with their start and end apart: 12, of which 4 were waited for; matrix products, arithmetic and copies ran while one was open for 2% of the time, Pallas kernels for 28%

profile of v1, /device:TPU:0, one launch (start us, length us, event | category | flops | bytes accessed | tf_op | source)
XLA Modules:
  0.0 85.6 jit_solution(11925987859461973866)
XLA Ops:
  0.6 1.0 %fusion = (bf16[64,4,128]{2,1,0:T(4,128)(2,1)S(1)}, bf16[64,4,128]{2,1,0:T(4,128)(2,1)S(1)}) fusion(bf16[64,32,128]{2,1,0:T(8,128)(2,1)} %cot_ref.1), kind=kLoop, calls=%fused_computation.7 | loop fusion | bytes 262144 | tf_op jit(solution)/shard_map/slice | solution.py:376
  1.7 4.8 %collective-permute-start.2 = (bf16[64,4,128]{2,1,0:T(4,128)(2,1)S(1)}, bf16[64,4,128]{2,1,0:T(4,128)(2,1)S(1)}, u32[]{:S(2)}, u32[]{:S(2)}) collective-permute-start(bf16[64,4,128]{2,1,0:T(4,128)(2,1)S(1)} %get-tuple-element.32), channel_id=1, source_target_pairs={{0,8},{8,16},{16,24},{1,9},{9,17},{17,25},{2,10},{10,18},{18,26},{... | collective-permute-start | bytes 196616 | tf_op jit(solution)/shard_map/ppermute | solution.py:338
  6.5 1.3 %collective-permute-start.3 = (bf16[64,4,128]{2,1,0:T(4,128)(2,1)S(1)}, bf16[64,4,128]{2,1,0:T(4,128)(2,1)S(1)}, u32[]{:S(2)}, u32[]{:S(2)}) collective-permute-start(bf16[64,4,128]{2,1,0:T(4,128)(2,1)S(1)} %get-tuple-element.31), channel_id=1, source_target_pairs={{8,0},{16,8},{24,16},{9,1},{17,9},{25,17},{10,2},{18,10},{26,18},{... | collective-permute-start | bytes 196616 | tf_op jit(solution)/shard_map/ppermute | solution.py:338
  7.8 2.1 %shard_map.135 = bf16[8,208,128]{2,1,0:T(8,128)(2,1)} custom-call(bf16[48,4,1024]{2,1,0:T(4,128)(2,1)} %x_ref.1), custom_call_target="tpu_custom_call" | custom-call | flops 2000000000 | bytes 6000000 | tf_op jit(solution)/shard_map/pallas_call | solution.py:372
  9.9 4.9 %all-to-all-start = ((bf16[8,208,128]{2,1,0:T(8,128)(2,1)}), bf16[8,208,128]{2,1,0:T(8,128)(2,1)S(1)}, u32[]{:S(2)}, u32[]{:S(2)}) async-start(bf16[8,208,128]{2,1,0:T(8,128)(2,1)} %shard_map.135), calls=%async_computation | async-start | bytes 851968 | tf_op jit(solution)/shard_map/all_to_all | solution.py:373
  16.0 2.1 %shard_map.137 = (bf16[64,48,128]{2,1,0:T(8,128)(2,1)}, bf16[8,3072]{1,0:T(8,128)(2,1)}) custom-call(bf16[64,32,128]{2,1,0:T(8,128)(2,1)} %cot_ref.1, bf16[64,4,128]{2,1,0:T(4,128)(2,1)} %copy-done.1, bf16[64,4,128]{2,1,0:T(4,128)(2,1)} %copy-done.2), custom_call_target="tpu_custom_call" | custom-call | flops 1500000000 | bytes 4500000 | tf_op jit(solution)/shard_map/pallas_call | solution.py:377
  18.2 2.4 %collective-permute-start.4 = (bf16[8,3072]{1,0:T(8,128)(2,1)}, bf16[8,3072]{1,0:T(8,128)(2,1)S(1)}, u32[]{:S(2)}, u32[]{:S(2)}) collective-permute-start(bf16[8,3072]{1,0:T(8,128)(2,1)} %get-tuple-element.24), channel_id=1, source_target_pairs={{0,1},{1,2},{2,3},{3,4},{4,5},{5,6},{6,7},{8,9},{9,10},{10,11},{11... | collective-permute-start | bytes 147464 | tf_op jit(solution)/shard_map/ppermute | solution.py:338
  20.6 1.3 %collective-permute-start.5 = (bf16[8,3072]{1,0:T(8,128)(2,1)}, bf16[8,3072]{1,0:T(8,128)(2,1)S(1)}, u32[]{:S(2)}, u32[]{:S(2)}) collective-permute-start(bf16[8,3072]{1,0:T(8,128)(2,1)} %get-tuple-element.24), channel_id=1, source_target_pairs={{1,0},{2,1},{3,2},{4,3},{5,4},{6,5},{7,6},{9,8},{10,9},{11,10},{12... | collective-permute-start | bytes 147464 | tf_op jit(solution)/shard_map/ppermute | solution.py:338
  21.9 2.4 %shard_map.136 = (bf16[512,384]{1,0:T(8,128)(2,1)}, bf16[512,512]{1,0:T(8,128)(2,1)}, f32[64,384]{1,0:T(8,128)}, f32[64,384]{1,0:T(8,128)}, f32[4,64,128]{2,1,0:T(8,128)}) custom-call(bf16[48,64]{1,0:T(8,128)(2,1)} %bitcast.19, f32[49,64]{1,0:T(8,128)} %bitcast.18, f32[64]{0:T(128)} %bias_ref.1, f32[64]{0:T(128)} %gain_ref.1, f32[64]{0:T(128)} %off_ref.1, ...), custom_call_target="tpu_custom_call" | custom-call | flops 1500000000 | bytes 4500000 | tf_op jit(solution)/shard_map/pallas_call | solution.py:384
  25.7 8.5 %shard_map.138 = (bf16[64,48,128]{2,1,0:T(8,128)(2,1)}, f32[64,32,128]{2,1,0:T(8,128)}, f32[2,64,8,128]{3,2,1,0:T(8,128)}) custom-call(bf16[64,48,128]{2,1,0:T(8,128)(2,1)} %get-tuple-element.23.all_ref, bf16[8,3072]{1,0:T(8,128)(2,1)} %copy-done.5, bf16[8,3072]{1,0:T(8,128)(2,1)} %copy-done.6, f32[64,384]{1,0:T(8,128)} %get-tuple-element.25.kb_ref), custom_call_target="tpu_custom_call" | custom-call | flops 5000000000 | bytes 15000000 | tf_op jit(solution)/shard_map/pallas_call | solution.py:395
  34.2 0.8 copy-done
  34.9 13.6 %shard_map.139 = (bf16[64,32,128]{2,1,0:T(8,128)(2,1)}, f32[56,128]{1,0:T(8,128)}) custom-call(bf16[8,208,128]{2,1,0:T(8,128)(2,1)} %copy-done, bf16[512,384]{1,0:T(8,128)(2,1)} %get-tuple-element.19.wk_ref, f32[4,64,128]{2,1,0:T(8,128)} %get-tuple-element.21.vec_ref, f32[64,32,128]{2,1,0:T(8,128)} %get-tuple-element.26.grad_ref, ...), custom_call_target="tpu_custom_call" | custom-call | flops 6000000000 | bytes 18000000 | tf_op jit(solution)/shard_map/pallas_call | solution.py:405
  48.5 3.3 %collective-permute-start.6 = (f32[56,128]{1,0:T(8,128)}, f32[56,128]{1,0:T(8,128)S(1)}, u32[]{:S(2)}, u32[]{:S(2)}) collective-permute-start(f32[56,128]{1,0:T(8,128)} %get-tuple-element.30), channel_id=1, source_target_pairs={{0,1},{1,0},{2,3},{3,2},{4,5},{5,4},{6,7},{7,6},{8,9},{9,8},{10,11... | collective-permute-start | bytes 86024 | tf_op jit(solution)/shard_map/ppermute | solution.py:346
  51.8 1.1 %collective-permute-done.6 = f32[56,128]{1,0:T(8,128)S(1)} collective-permute-done((f32[56,128]{1,0:T(8,128)}, f32[56,128]{1,0:T(8,128)S(1)}, u32[]{:S(2)}, u32[]{:S(2)}) %collective-permute-start.6) | collective-permute-done | bytes 28704 | tf_op jit(solution)/shard_map/ppermute | solution.py:346
  53.7 0.9 %collective-permute-start.7 = (f32[56,128]{1,0:T(8,128)S(1)}, f32[56,128]{1,0:T(8,128)S(1)}, u32[]{:S(2)}, u32[]{:S(2)}) collective-permute-start(f32[56,128]{1,0:T(8,128)S(1)} %add.15), channel_id=1, source_target_pairs={{0,2},{1,3},{2,0},{3,1},{4,6},{5,7},{6,4},{7,5},{8,10},{9,11},{10,... | collective-permute-start | bytes 86024 | tf_op jit(solution)/shard_map/ppermute | solution.py:346
  54.6 2.9 %collective-permute-done.7 = f32[56,128]{1,0:T(8,128)S(1)} collective-permute-done((f32[56,128]{1,0:T(8,128)S(1)}, f32[56,128]{1,0:T(8,128)S(1)}, u32[]{:S(2)}, u32[]{:S(2)}) %collective-permute-start.7) | collective-permute-done | bytes 28704 | tf_op jit(solution)/shard_map/ppermute | solution.py:346
  57.5 1.8 %collective-permute-start.8 = (f32[56,128]{1,0:T(8,128)S(1)}, f32[56,128]{1,0:T(8,128)S(1)}, u32[]{:S(2)}, u32[]{:S(2)}) collective-permute-start(f32[56,128]{1,0:T(8,128)S(1)} %add.16), channel_id=1, source_target_pairs={{0,4},{1,5},{2,6},{3,7},{4,0},{5,1},{6,2},{7,3},{8,12},{9,13},{10,... | collective-permute-start | bytes 86024 | tf_op jit(solution)/shard_map/ppermute | solution.py:346
  59.4 0.8 fusion.1
  60.2 4.5 %collective-permute-start = (bf16[1,208,128]{2,1,0:T(8,128)(2,1)S(1)}, bf16[1,208,128]{2,1,0:T(8,128)(2,1)S(1)}, u32[]{:S(2)}, u32[]{:S(2)}) collective-permute-start(bf16[1,208,128]{2,1,0:T(8,128)(2,1)S(1)} %get-tuple-element.34), channel_id=1, source_target_pairs={{0,8},{8,16},{16,24},{1,9},{9,17},{17,25},{2,10},{10,18},{18,26},{... | collective-permute-start | bytes 159752 | tf_op jit(solution)/shard_map/ppermute | solution.py:338
  64.7 1.3 %collective-permute-start.1 = (bf16[1,208,128]{2,1,0:T(8,128)(2,1)S(1)}, bf16[1,208,128]{2,1,0:T(8,128)(2,1)S(1)}, u32[]{:S(2)}, u32[]{:S(2)}) collective-permute-start(bf16[1,208,128]{2,1,0:T(8,128)(2,1)S(1)} %get-tuple-element.33), channel_id=1, source_target_pairs={{8,0},{16,8},{24,16},{9,1},{17,9},{25,17},{10,2},{18,10},{26,18},{... | collective-permute-start | bytes 159752 | tf_op jit(solution)/shard_map/ppermute | solution.py:338
  66.1 3.1 %collective-permute-start.9 = (f32[56,128]{1,0:T(8,128)S(1)}, f32[56,128]{1,0:T(8,128)S(1)}, u32[]{:S(2)}, u32[]{:S(2)}) collective-permute-start(f32[56,128]{1,0:T(8,128)S(1)} %add.17), channel_id=1, source_target_pairs={{0,8},{8,0},{16,24},{24,16},{1,9},{9,1},{17,25},{25,17},{2,10},{10... | collective-permute-start | bytes 86024 | tf_op jit(solution)/shard_map/ppermute | solution.py:346
  69.7 1.7 %collective-permute-done.9 = f32[56,128]{1,0:T(8,128)S(1)} collective-permute-done((f32[56,128]{1,0:T(8,128)S(1)}, f32[56,128]{1,0:T(8,128)S(1)}, u32[]{:S(2)}, u32[]{:S(2)}) %collective-permute-start.9) | collective-permute-done | bytes 28704 | tf_op jit(solution)/shard_map/ppermute | solution.py:346
  71.5 3.0 %collective-permute-start.10 = (f32[56,128]{1,0:T(8,128)S(1)}, f32[56,128]{1,0:T(8,128)S(1)}, u32[]{:S(2)}, u32[]{:S(2)}) collective-permute-start(f32[56,128]{1,0:T(8,128)S(1)} %add.18), channel_id=1, source_target_pairs={{0,16},{8,24},{16,0},{24,8},{1,17},{9,25},{17,1},{25,9},{2,18},{10... | collective-permute-start | bytes 86024 | tf_op jit(solution)/shard_map/ppermute | solution.py:346
  75.1 8.7 %shard_map.140 = bf16[64,32,128]{2,1,0:T(8,128)(2,1)} custom-call(s32[4]{0:T(128)} %add_convert_fusion.edge_ref, bf16[8,208,128]{2,1,0:T(8,128)(2,1)} %copy-done, bf16[1,208,128]{2,1,0:T(8,128)(2,1)} %copy-done.3, bf16[1,208,128]{2,1,0:T(8,128)(2,1)} %copy-done.4, bf16[512,384]{1,0:T(8,128)(2,1)} %get-tuple-element.19.wk_ref, ...), custom_call_target="tpu_custom_call" | custom-call | flops 5000000000 | bytes 15000000 | tf_op jit(solution)/shard_map/pallas_call | solution.py:422
  (31 shorter events, 6.4 us)
Async XLA Ops:
  1.7 13.1 %collective-permute-start.2 = (bf16[64,4,128]{2,1,0:T(4,128)(2,1)S(1)}, bf16[64,4,128]{2,1,0:T(4,128)(2,1)S(1)}, u32[]{:S(2)}, u32[]{:S(2)}) collective-permute-start(bf16[64,4,128]{2,1,0:T(4,128)(2,1)S(1)} %get-tuple-element.32), channel_id=1, source_target_pairs={{0,8},{8,16},{16,24},{1,9},{9,17},{17,25},{2,10},{10,18},{18,26},{... | collective-permute-start | bytes 196616 | tf_op jit(solution)/shard_map/ppermute | solution.py:338
  6.5 8.3 %collective-permute-start.3 = (bf16[64,4,128]{2,1,0:T(4,128)(2,1)S(1)}, bf16[64,4,128]{2,1,0:T(4,128)(2,1)S(1)}, u32[]{:S(2)}, u32[]{:S(2)}) collective-permute-start(bf16[64,4,128]{2,1,0:T(4,128)(2,1)S(1)} %get-tuple-element.31), channel_id=1, source_target_pairs={{8,0},{16,8},{24,16},{9,1},{17,9},{25,17},{10,2},{18,10},{26,18},{... | collective-permute-start | bytes 196616 | tf_op jit(solution)/shard_map/ppermute | solution.py:338
  9.9 24.3 %all-to-all-start = ((bf16[8,208,128]{2,1,0:T(8,128)(2,1)}), bf16[8,208,128]{2,1,0:T(8,128)(2,1)S(1)}, u32[]{:S(2)}, u32[]{:S(2)}) async-start(bf16[8,208,128]{2,1,0:T(8,128)(2,1)} %shard_map.135), calls=%async_computation | async-start | bytes 851968 | tf_op jit(solution)/shard_map/all_to_all | solution.py:373
  14.8 0.6 copy-start.1
  15.4 0.6 copy-start.2
  18.2 6.1 %collective-permute-start.4 = (bf16[8,3072]{1,0:T(8,128)(2,1)}, bf16[8,3072]{1,0:T(8,128)(2,1)S(1)}, u32[]{:S(2)}, u32[]{:S(2)}) collective-permute-start(bf16[8,3072]{1,0:T(8,128)(2,1)} %get-tuple-element.24), channel_id=1, source_target_pairs={{0,1},{1,2},{2,3},{3,4},{4,5},{5,6},{6,7},{8,9},{9,10},{10,11},{11... | collective-permute-start | bytes 147464 | tf_op jit(solution)/shard_map/ppermute | solution.py:338
  20.6 4.5 %collective-permute-start.5 = (bf16[8,3072]{1,0:T(8,128)(2,1)}, bf16[8,3072]{1,0:T(8,128)(2,1)S(1)}, u32[]{:S(2)}, u32[]{:S(2)}) collective-permute-start(bf16[8,3072]{1,0:T(8,128)(2,1)} %get-tuple-element.24), channel_id=1, source_target_pairs={{1,0},{2,1},{3,2},{4,3},{5,4},{6,5},{7,6},{9,8},{10,9},{11,10},{12... | collective-permute-start | bytes 147464 | tf_op jit(solution)/shard_map/ppermute | solution.py:338
  24.3 0.7 copy-start.5
  25.1 0.6 copy-start.6
  34.2 0.8 copy-start
  48.5 4.4 %collective-permute-start.6 = (f32[56,128]{1,0:T(8,128)}, f32[56,128]{1,0:T(8,128)S(1)}, u32[]{:S(2)}, u32[]{:S(2)}) collective-permute-start(f32[56,128]{1,0:T(8,128)} %get-tuple-element.30), channel_id=1, source_target_pairs={{0,1},{1,0},{2,3},{3,2},{4,5},{5,4},{6,7},{7,6},{8,9},{9,8},{10,11... | collective-permute-start | bytes 86024 | tf_op jit(solution)/shard_map/ppermute | solution.py:346
  53.7 3.9 %collective-permute-start.7 = (f32[56,128]{1,0:T(8,128)S(1)}, f32[56,128]{1,0:T(8,128)S(1)}, u32[]{:S(2)}, u32[]{:S(2)}) collective-permute-start(f32[56,128]{1,0:T(8,128)S(1)} %add.15), channel_id=1, source_target_pairs={{0,2},{1,3},{2,0},{3,1},{4,6},{5,7},{6,4},{7,5},{8,10},{9,11},{10,... | collective-permute-start | bytes 86024 | tf_op jit(solution)/shard_map/ppermute | solution.py:346
  57.5 8.5 %collective-permute-start.8 = (f32[56,128]{1,0:T(8,128)S(1)}, f32[56,128]{1,0:T(8,128)S(1)}, u32[]{:S(2)}, u32[]{:S(2)}) collective-permute-start(f32[56,128]{1,0:T(8,128)S(1)} %add.16), channel_id=1, source_target_pairs={{0,4},{1,5},{2,6},{3,7},{4,0},{5,1},{6,2},{7,3},{8,12},{9,13},{10,... | collective-permute-start | bytes 86024 | tf_op jit(solution)/shard_map/ppermute | solution.py:346
  60.2 14.3 %collective-permute-start = (bf16[1,208,128]{2,1,0:T(8,128)(2,1)S(1)}, bf16[1,208,128]{2,1,0:T(8,128)(2,1)S(1)}, u32[]{:S(2)}, u32[]{:S(2)}) collective-permute-start(bf16[1,208,128]{2,1,0:T(8,128)(2,1)S(1)} %get-tuple-element.34), channel_id=1, source_target_pairs={{0,8},{8,16},{16,24},{1,9},{9,17},{17,25},{2,10},{10,18},{18,26},{... | collective-permute-start | bytes 159752 | tf_op jit(solution)/shard_map/ppermute | solution.py:338
  64.7 9.7 %collective-permute-start.1 = (bf16[1,208,128]{2,1,0:T(8,128)(2,1)S(1)}, bf16[1,208,128]{2,1,0:T(8,128)(2,1)S(1)}, u32[]{:S(2)}, u32[]{:S(2)}) collective-permute-start(bf16[1,208,128]{2,1,0:T(8,128)(2,1)S(1)} %get-tuple-element.33), channel_id=1, source_target_pairs={{8,0},{16,8},{24,16},{9,1},{17,9},{25,17},{10,2},{18,10},{26,18},{... | collective-permute-start | bytes 159752 | tf_op jit(solution)/shard_map/ppermute | solution.py:338
  66.1 5.4 %collective-permute-start.9 = (f32[56,128]{1,0:T(8,128)S(1)}, f32[56,128]{1,0:T(8,128)S(1)}, u32[]{:S(2)}, u32[]{:S(2)}) collective-permute-start(f32[56,128]{1,0:T(8,128)S(1)} %add.17), channel_id=1, source_target_pairs={{0,8},{8,0},{16,24},{24,16},{1,9},{9,1},{17,25},{25,17},{2,10},{10... | collective-permute-start | bytes 86024 | tf_op jit(solution)/shard_map/ppermute | solution.py:346
  71.5 12.3 %collective-permute-start.10 = (f32[56,128]{1,0:T(8,128)S(1)}, f32[56,128]{1,0:T(8,128)S(1)}, u32[]{:S(2)}, u32[]{:S(2)}) collective-permute-start(f32[56,128]{1,0:T(8,128)S(1)} %add.18), channel_id=1, source_target_pairs={{0,16},{8,24},{16,0},{24,8},{1,17},{9,25},{17,1},{25,9},{2,18},{10... | collective-permute-start | bytes 86024 | tf_op jit(solution)/shard_map/ppermute | solution.py:346
  74.5 0.6 copy-start.3
  74.5 0.6 copy-start.4

commit v2 on v1

v2 whole, which is shorter than its diff:
```python
import functools
import math

import jax
import jax.numpy as jnp
import numpy as np
from jax import lax
from jax.experimental import pallas as pl
from jax.experimental.pallas import tpu as pltpu
from jax.sharding import PartitionSpec as P

norm_eps = 1e-06
side = 7
LANES = 128
GROUP = 8
PITCH = 48
DEPTH = 8 * PITCH
VMEM = 20 * 1024 * 1024
UNROLL = 16
bf16, f32 = jnp.bfloat16, jnp.float32

NN = (((1,), (0,)), ((), ()))
NT = (((1,), (1,)), ((), ()))
TN = (((0,), (0,)), ((), ()))


def mm(a, b, dims=NN):
    return lax.dot_general(a, b, dims, preferred_element_type=f32)


def iota(shape, axis):
    return lax.broadcasted_iota(jnp.int32, shape, axis)


def split2(x):
    high = x.astype(bf16)
    return high, (x - high.astype(f32)).astype(bf16)


def one_hot(cond):
    return jnp.where(cond, 1.0, 0.0).astype(bf16)


def cdiv(a, b):
    return -(-a // b)


def constants(colors, file_rows, channels):
    block = colors * file_rows
    per = GROUP // file_rows
    rows = channels * GROUP
    inner = per * block
    out = {}

    def source(width):
        at = np.arange(per * width)
        part, inside = at // width, at % width
        ok = inside < block
        return np.where(ok, inside // file_rows, -1), np.where(ok, part * file_rows + inside % file_rows, -1)

    for name, width in (("", block), ("_halo", cdiv(block, LANES) * LANES)):
        color, row = source(width)
        out["spread" + name] = color[None, :] == np.arange(colors)[:, None]
        out["keep" + name] = row[None, :] == (np.arange(rows) % GROUP)[:, None]
    out["tall"] = (np.arange(rows) // GROUP)[:, None] == np.arange(channels)[None, :]
    out["gather"] = (np.arange(rows) // GROUP)[:, None] == np.arange(LANES)[None, :]
    color, row = source(block)
    out["diagonal"] = np.concatenate([out["keep"].T, np.ones((16, rows), bool)])
    fold = np.zeros((56, inner + 16), bool)
    fold[color, np.arange(inner)] = True
    fold[colors, inner] = True
    out["fold"] = fold
    lane = np.arange(DEPTH)
    copy, at = lane // PITCH, lane % PITCH - 5
    tap = np.where((at >= 0) & (at < side) & (copy < side), at * side + copy, -1)
    count = side * side
    out["forward"] = tap[None, :] == np.arange(count)[:, None]
    out["backward"] = (tap >= 0)[None, :] & (count - 1 - tap[None, :] == np.arange(count)[:, None])
    out["taps"] = np.concatenate([out["backward"], np.zeros((56 - count, DEPTH), bool)])
    pick = np.zeros((3, 56, LANES), bool)
    for n in range(3):
        pick[n, colors + 1 + n] = True
    out["pick"] = np.concatenate(list(pick), axis=1)
    return {k: jnp.asarray(v, f32 if k in ("forward", "backward") else bf16) for k, v in out.items()}


def params_kernel(wt_ref, taps_ref, bias_ref, gain_ref, off_ref, koff_ref, spread_ref, keep_ref, spread_h_ref,
                  keep_h_ref, tall_ref, forward_ref, backward_ref, wk_ref, wh_ref, kb_ref, kf_ref, vec_ref):
    channels = wt_ref.shape[1]
    for spread, keep, out_ref in ((spread_ref, keep_ref, wk_ref), (spread_h_ref, keep_h_ref, wh_ref)):
        wide = mm(wt_ref[...], spread[...], TN).astype(bf16)
        out_ref[...] = mm(tall_ref[...], wide).astype(bf16) * keep[...]
    for place, out_ref in ((forward_ref, kf_ref), (backward_ref, kb_ref)):
        out_ref[...] = lax.dot_general(taps_ref[...], place[...], TN, precision=lax.Precision.HIGHEST,
                                       preferred_element_type=f32)
    eye = iota((channels, channels), 0) == iota((channels, channels), 1)
    for n, ref in enumerate((bias_ref, gain_ref, off_ref, koff_ref)):
        row = jnp.broadcast_to(ref[...].reshape(1, channels), (channels, channels))
        column = jnp.sum(jnp.where(eye, row, 0.0), axis=1, keepdims=True)
        vec_ref[n] = jnp.broadcast_to(column, (channels, LANES))


def pack_kernel(at_ref, x_hbm, cot_hbm, cot_ref, keep_ref, give_ref, edge_ref, edge_s, x_ref, sems):
    colors, file_rows, width = x_ref.shape
    channels, height, _ = cot_ref.shape
    chips, block_rows, _ = keep_ref.shape
    count = width // LANES
    block = colors * file_rows
    core, chip = at_ref[0], at_ref[1]
    load_x = pltpu.make_async_copy(x_hbm, x_ref, sems.at[0])
    load_cot = pltpu.make_async_copy(cot_hbm, cot_ref, sems.at[1])
    load_x.start()
    load_cot.start()
    load_cot.wait()

    row, lane = iota((8, LANES), 0), iota((8, LANES), 1)
    pick = one_hot(((row < 3) & (lane == row)) | ((row >= 3) & (row < 6) & (lane == row + LANES - 6)))
    edges = mm(pick, cot_ref[...].reshape(channels * height, LANES), NT)
    edges = jnp.concatenate(
        [edges[:, n:n + LANES] for n in range(0, channels * height, LANES)], axis=0).astype(bf16)
    edge_ref[...] = edges
    give_ref[chips * block_rows:, :] = edges
    load_x.wait()

    row, lane = iota((16, LANES), 0), iota((16, LANES), 1)
    pick = one_hot(((row < 3) & (lane == row + LANES - 3)) | ((row >= 11) & (row < 14) & (lane == row - 11)))
    zeros = jnp.zeros((16, block), f32)
    edge_s[0] = zeros
    edge_s[count + 1] = zeros
    for d in range(count):
        tile = x_ref[:, :, d * LANES:(d + 1) * LANES].reshape(block, LANES)
        edge_s[d + 1] = mm(pick, tile, NT)

    def halo(d):
        both = edge_s[d][:8] + edge_s[d + 2][8:]
        chunks = []
        for start in range(0, 2 * LANES, LANES):
            stop = min(start + LANES, block)
            if stop <= start:
                chunks.append(jnp.zeros((8, LANES), f32))
            elif stop - start < LANES:
                chunks.append(jnp.concatenate(
                    [both[:, start:stop], jnp.zeros((8, LANES - stop + start), f32)], axis=1))
            else:
                chunks.append(both[:, start:stop])
        return jnp.concatenate(chunks, axis=0).astype(bf16)

    for away in range(chips):
        there = lax.rem(chip + away, chips)
        for other in range(2):
            d = 2 * there + (core if other == 0 else 1 - core)
            tile = x_ref[:, :, pl.ds(pl.multiple_of(d * LANES, LANES), LANES)].reshape(block, LANES)
            if other == 0:
                keep_ref[away, :block, :] = tile
                keep_ref[away, block:, :] = halo(d)
            else:
                start = away * block_rows
                give_ref[start:start + block, :] = tile
                give_ref[start + block:start + block_rows, :] = halo(d)


def pair_kernel(keep_ref, got_ref, *pair_refs):
    _, block_rows, _ = keep_ref.shape
    for away, ref in enumerate(pair_refs):
        ref[0] = keep_ref[away]
        ref[1] = got_ref[away * block_rows:(away + 1) * block_rows, :]


def strips_kernel(at_ref, cot_ref, near_ref, far_ref, halo_ref, one_ref, two_ref):
    channels, height, width = cot_ref.shape
    size = far_ref.shape[0]
    core = at_ref[0]
    near = near_ref[near_ref.shape[0] - size:, :].astype(f32)
    far = far_ref[...].astype(f32)
    left = jnp.where(core == 0, far, near)
    right = jnp.where(core == 0, near, far)
    left = jnp.concatenate([left[n:n + 8] for n in range(0, size, 8)], axis=1).astype(bf16)
    right = jnp.concatenate([right[n:n + 8] for n in range(0, size, 8)], axis=1).astype(bf16)
    row, lane = iota((8, width), 0), iota((8, width), 1)
    from_left = one_hot((row >= 3) & (row < 6) & (lane == row + width - 6) & (at_ref[4] == 0))
    from_right = one_hot((row < 3) & (lane == row) & (at_ref[5] == 0))
    halo = (mm(left, from_left, TN) + mm(right, from_right, TN)).reshape(channels, height, width)
    halo_ref[...] = halo.astype(bf16)
    own = cot_ref[...].astype(f32)
    up = jnp.concatenate([own[:, :4], halo[:, :4]], axis=1)
    down = jnp.concatenate([own[:, height - 4:], halo[:, height - 4:]], axis=1)
    even = at_ref[6] == 0
    one_ref[...] = jnp.where(even, down, up).astype(bf16)
    two_ref[...] = jnp.where(even, up, down).astype(bf16)


def shifted(center, halo):
    rows, width = center.shape
    lane = iota((rows, width), 1)
    copies = []
    for move in range(-3, 4):
        if move == 0:
            copies.append(center)
        elif move > 0:
            copies.append(pltpu.roll(jnp.where(lane < move, halo, center), width - move, 1))
        else:
            copies.append(pltpu.roll(jnp.where(lane >= width + move, halo, center), -move, 1))
    copies.append(jnp.zeros((rows, width), center.dtype))
    return jnp.concatenate(copies, axis=0)


def toeplitz(base, height):
    taps = pltpu.roll(jnp.broadcast_to(base, (height, DEPTH)), 0, 1, stride=1, stride_axis=0)
    return jnp.concatenate(split2(taps), axis=0)


def back_kernel(factor, at_ref, cot_ref, beside_ref, one_ref, two_ref, kb_ref, all_ref, halo_ref, grad_ref, sum_ref):
    channels, height, width = cot_ref.shape
    even = at_ref[6] == 0
    one, two = one_ref[...].astype(f32), two_ref[...].astype(f32)
    top = jnp.where(at_ref[2] == 0, jnp.where(even, two, one), 0.0)
    bot = jnp.where(at_ref[3] == 0, jnp.where(even, one, two), 0.0)
    none = jnp.zeros((channels, 4, width), f32)
    for part, middle, ref in ((slice(0, 4), cot_ref, all_ref), (slice(4, 8), beside_ref, halo_ref)):
        ref[:, 0:8, :] = jnp.concatenate([none, top[:, part]], axis=1).astype(bf16)
        ref[:, 8:8 + height, :] = middle[...]
        ref[:, 8 + height:, :] = jnp.concatenate([bot[:, part], none], axis=1).astype(bf16)

    def one(k, carry):
        plane = all_ref[k]
        stack = shifted(plane, halo_ref[k])
        both = mm(toeplitz(kb_ref[pl.ds(k, 1), :], height), stack)
        grad = (both[:height] + both[height:]) * factor
        grad_ref[k] = grad
        own = plane.astype(f32)[8:8 + height]
        sum_ref[0, k] = jnp.sum(grad.reshape(height // 8, 8, width), axis=0)
        sum_ref[1, k] = jnp.sum(own.reshape(height // 8, 8, width), axis=0) * factor
        return carry

    lax.fori_loop(0, channels, one, 0, unroll=UNROLL)


def layer_norm(patch, channels):
    values = patch.astype(bf16).astype(f32).reshape(channels, GROUP, LANES)
    center = values - jnp.mean(values, axis=0, keepdims=True)
    spread = jnp.mean(center * center, axis=0, keepdims=True)
    inverse = lax.rsqrt(spread + norm_eps)
    return center * inverse, inverse


def per_row(vec_ref, n):
    return vec_ref[n][:, None, :]


def order_kernel(at_ref, *refs):
    pair_refs, (x_ref, one_ref, two_ref) = refs[:-3], refs[-3:]
    chips = len(pair_refs)
    core, chip = at_ref[0], at_ref[1]
    for away, ref in enumerate(pair_refs):
        there = lax.rem(chip - away + chips, chips)
        x_ref[2 * there + core] = ref[0]
        x_ref[2 * there + 1 - core] = ref[1]
    half = one_ref.shape[0]
    up = x_ref[:half]
    down = x_ref[2 * chips - half:]
    even = at_ref[6] == 0
    one_ref[...] = jnp.where(even, down, up)
    two_ref[...] = jnp.where(even, up, down)


def main_kernel(colors, file_rows, factor, x_ref, wk_ref, vec_ref, grad_ref, sum_ref, all_ref, halo_ref,
                taps_ref, gather_ref, diagonal_ref, fold_ref, pick_ref,
                norm_ref, out_ref, norm_s, gram_s, diag_s):
    channels, height, width = grad_ref.shape
    block = colors * file_rows
    per = GROUP // file_rows
    rows = channels * GROUP
    bias, gain, offset = per_row(vec_ref, 0), per_row(vec_ref, 1), per_row(vec_ref, 2)
    scale_part = jnp.zeros((channels, GROUP, width), f32)
    ones = jnp.where(iota((16, width), 0) == 0, 1.0, 0.0).astype(bf16)
    for g in range(height // GROUP):
        pixels = jnp.concatenate([x_ref[per * g + a, :block, :] for a in range(per)], axis=0)
        patch = mm(wk_ref[...], pixels).reshape(channels, GROUP, width) + bias
        xhat, inverse = layer_norm(patch, channels)
        norm_s[:, g * GROUP:(g + 1) * GROUP, :] = xhat * gain + offset
        grad = grad_ref[:, g * GROUP:(g + 1) * GROUP, :]
        scale_part += grad * xhat
        inside = grad * gain
        mean_a = jnp.mean(inside, axis=0, keepdims=True)
        mean_b = jnp.mean(inside * xhat, axis=0, keepdims=True)
        patch_grad = (inverse * (inside - mean_a - xhat * mean_b)).astype(bf16).reshape(rows, width)
        gram = mm(jnp.concatenate([pixels, ones], axis=0), patch_grad, NT)
        if g == 0:
            gram_s[...] = gram
        else:
            gram_s[...] += gram

    def one(k, carry):
        plane = norm_s[k].astype(bf16)
        norm_ref[k] = plane
        stack = shifted(all_ref[k], halo_ref[k])
        cross = mm(plane, stack, NT)
        total = cross[:8]
        for a in range(1, height // 8):
            total += pltpu.roll(cross[8 * a:8 * a + 8], DEPTH - 8 * a, 1)
        diag_s[k] = total
        return carry

    lax.fori_loop(0, channels, one, 0, unroll=UNROLL)

    line = diag_s[:, 0, :]
    for b in range(1, 8):
        line += pltpu.roll(diag_s[:, b, :], DEPTH - b, 1)
    line = jnp.concatenate([jnp.zeros((LANES - channels, DEPTH), f32), line * factor], axis=0)
    result = sum(mm(taps_ref[...], part, NT) for part in split2(line))

    gather = gather_ref[...]
    gram = gram_s[...] * diagonal_ref[...].astype(f32)
    by_channel = sum(mm(part, gather) for part in split2(gram))
    result += sum(mm(fold_ref[...], part) for part in split2(by_channel))
    parts = [part.reshape(rows, width) for part in (scale_part, sum_ref[0], sum_ref[1])]
    line = sum(mm(pick_ref[...], piece, NT) for piece in split2(jnp.concatenate(parts, axis=1)))
    result += sum(mm(piece, gather) for piece in split2(line))
    out_ref[...] = result


def stem_halo_kernel(colors, file_rows, at_ref, x_ref, one_ref, two_ref, wk_ref, wh_ref, vec_ref, norm_ref,
                     all_s, halo_s):
    channels, height, width = norm_ref.shape
    block = colors * file_rows
    per = GROUP // file_rows
    half = per // 2
    chunks = wh_ref.shape[1] // (per * LANES)
    bias, gain, offset = per_row(vec_ref, 0), per_row(vec_ref, 1), per_row(vec_ref, 2)
    no_top, no_bot = at_ref[2], at_ref[3]
    no_left, no_right = at_ref[4], at_ref[5]
    shape = (channels, GROUP, width)
    lower = iota(shape, 1) < 4
    row_ok = jnp.where(lower, 1 - no_bot, 1 - no_top) > 0

    even = at_ref[6] == 0
    one, two = one_ref[...], two_ref[...]
    top, bot = jnp.where(even, two, one), jnp.where(even, one, two)
    outer = [bot[a] for a in range(half)] + [top[a] for a in range(half)]
    pixels = jnp.concatenate([piece[:block] for piece in outer], axis=0)
    xhat, _ = layer_norm(mm(wk_ref[...], pixels).reshape(shape) + bias, channels)
    rows = jnp.where(row_ok, xhat * gain + offset, 0.0).astype(bf16)
    all_s[:, 0:8, :] = rows
    all_s[:, 8 + height:16 + height, :] = rows
    all_s[:, 8:8 + height, :] = norm_ref[...]

    groups = height // GROUP
    lines = []
    for g in range(groups + 1):
        pieces = []
        for a in range(per):
            piece = outer[a][block:block + 16] if g == groups else x_ref[per * g + a, block:block + 16, :]
            piece = piece.astype(f32)
            pieces += [piece[8 * c:8 * c + 8] for c in range(chunks)]
        lines.append(jnp.concatenate(pieces, axis=1))
    lines.append(jnp.zeros((LANES - 8 * len(lines), per * chunks * LANES), f32))
    lines = jnp.concatenate(lines, axis=0).astype(bf16)
    xhat, _ = layer_norm(mm(wh_ref[...], lines, NT).reshape(shape) + bias, channels)
    lane = iota(shape, 2)
    column = lax.bitwise_and(lane, 7)
    ok = jnp.where(column < 3, 1 - no_left, 1 - no_right) > 0
    ok = ok & (row_ok | (lane < 8 * groups))
    halo = jnp.where(ok, xhat * gain + offset, 0.0).astype(bf16).reshape(channels * GROUP, width)
    for g in range(groups + 1):
        moved = pltpu.roll(halo, width - 8 * g - 3, 1).reshape(shape)
        if g < groups:
            halo_s[:, 8 + 8 * g:16 + 8 * g, :] = moved
        else:
            halo_s[:, 0:8, :] = moved
            halo_s[:, 8 + height:16 + height, :] = moved


def stem_kernel(start, *refs):
    all_ref, halo_ref, kf_ref, vec_ref = refs[:4]
    out_ref, out_s, sem = refs[-3:]
    count, height, _ = out_s.shape

    def one(n, carry):
        k = start + n
        both = mm(toeplitz(kf_ref[pl.ds(k, 1), :], height), shifted(all_ref[k], halo_ref[k]))
        out_s[n] = (both[:height] + both[height:] + vec_ref[3, pl.ds(k, 1), :]).astype(bf16)
        return carry

    lax.fori_loop(0, count, one, 0, unroll=UNROLL)
    copy = pltpu.make_async_copy(out_s, out_ref.at[pl.ds(start, count)], sem)
    copy.start()
    copy.wait()


def last_kernel(colors, x_ref, y_ref, *outs):
    total = x_ref[...] + y_ref[...]
    channels = outs[1].shape[0]
    first = total[:, :channels]
    second = total[:, channels:2 * channels]
    outs[0][...] = first[:colors]
    for n in range(4):
        outs[1 + n][...] = first[colors + n]
    outs[5][...] = second[:outs[5].shape[0]]


def in_vmem(shape, dtype):
    return pltpu.VMEM(shape, dtype)


def kernel_call(body, out_shape, us, *args, loose=(), **kw):
    loose = tuple(loose) + tuple(kw.get("input_output_aliases", {}))
    args = [
        arg if n in loose or arg.dtype == jnp.int32 else pltpu.with_memory_space_constraint(arg, pltpu.VMEM)
        for n, arg in enumerate(args)
    ]
    return pl.pallas_call(
        body,
        out_shape=out_shape,
        compiler_params=pltpu.CompilerParams(vmem_limit_bytes=VMEM),
        cost_estimate=pl.CostEstimate(flops=int(us * 1e9), bytes_accessed=int(us * 3e6), transcendentals=0),
        **kw,
    )(*args)


def shaped(shape, dtype):
    return jax.ShapeDtypeStruct(shape, dtype)


def pairing(count, odd):
    return [(i, (i + 1 if (i + odd) % 2 == 0 else i - 1) % count) for i in range(count)]


def swap(parts, axis):
    return [lax.ppermute(part, axis, pairing(lax.axis_size(axis), n)) for n, part in enumerate(parts)]


def per_device(
    file_pixels,
    patchify_weight,
    patchify_bias,
    norm_gain,
    norm_offset_vector,
    kernel,
    kernel_offset,
    cotangent,
):
    colors, file_rows, _ = file_pixels.shape
    channels, height, width = cotangent.shape
    n_rows, n_cols = lax.axis_size("rows"), lax.axis_size("cols")
    factor = 1.0 / math.sqrt(height * n_rows * width * n_cols)
    block = colors * file_rows
    per = GROUP // file_rows
    block_rows = block + 16
    padded = cdiv(block, LANES) * LANES
    rows = channels * GROUP
    tile = (channels, height, width)
    tall = (channels, PITCH, width)
    const = constants(colors, file_rows, channels)

    row_at, col_at = lax.axis_index("rows"), lax.axis_index("cols")
    chips = n_cols // 2
    at = jnp.stack([
        col_at % 2, col_at // 2, row_at == 0, row_at == n_rows - 1, col_at == 0, col_at == n_cols - 1, row_at % 2,
    ]).astype(jnp.int32)
    smem = pl.BlockSpec(memory_space=pltpu.SMEM)
    vmem = pl.BlockSpec(memory_space=pltpu.VMEM)
    edge_rows = channels * height // 16

    beyond = pl.BlockSpec(memory_space=pl.ANY)
    cot, keep, give, edges = kernel_call(
        pack_kernel,
        (
            in_vmem(tile, bf16),
            in_vmem((chips, block_rows, LANES), bf16),
            in_vmem((chips * block_rows + edge_rows, LANES), bf16),
            in_vmem((edge_rows, LANES), bf16),
        ),
        2,
        at, *(pltpu.with_memory_space_constraint(arg, pltpu.HBM) for arg in (file_pixels, cotangent)),
        loose=(1, 2),
        in_specs=[smem] + [beyond] * 2,
        scratch_shapes=[
            pltpu.VMEM((n_cols + 2, 16, block), f32),
            pltpu.VMEM(file_pixels.shape, bf16),
            pltpu.SemaphoreType.DMA((2,)),
        ],
    )
    got = lax.ppermute(give, "cols", [(i, i ^ 1) for i in range(n_cols)])
    far = lax.ppermute(edges, "cols", pairing(n_cols, 1))
    pairs = kernel_call(pair_kernel, (in_vmem((2, block_rows, LANES), bf16),) * chips, 0.5, keep, got)
    pairs = [pairs[0]] + [
        lax.ppermute(pairs[n], "cols", [(i, (i + 2 * n) % n_cols) for i in range(n_cols)])
        for n in range(1, chips)
    ]

    kept, far = lax.optimization_barrier((pairs[0], far))
    pairs[0] = kept
    beside, *strips = kernel_call(
        strips_kernel,
        (in_vmem(tile, bf16), in_vmem((channels, 8, width), bf16), in_vmem((channels, 8, width), bf16)),
        1,
        at, cot, got, far,
        in_specs=[smem] + [vmem] * 3,
    )
    beside, taps = lax.optimization_barrier((beside, kernel))
    strips = swap(strips, "rows")
    wk, wh, kb, kf, vec = kernel_call(
        params_kernel,
        (
            in_vmem((rows, per * block), bf16),
            in_vmem((rows, per * padded), bf16),
            in_vmem((channels, DEPTH), f32),
            in_vmem((channels, DEPTH), f32),
            in_vmem((4, channels, LANES), f32),
        ),
        1.5,
        patchify_weight.T, taps.T, patchify_bias, norm_gain, norm_offset_vector, kernel_offset,
        const["spread"], const["keep"], const["spread_halo"], const["keep_halo"], const["tall"],
        const["forward"], const["backward"],
    )
    cot_all, cot_halo, grad, sums = kernel_call(
        functools.partial(back_kernel, factor),
        (in_vmem(tall, bf16), in_vmem(tall, bf16), in_vmem(tile, f32), in_vmem((2, channels, GROUP, width), f32)),
        5,
        at, cot, beside, *strips, kb,
        in_specs=[smem] + [vmem] * 5,
    )

    half = per // 2
    pixels, *ends = kernel_call(
        order_kernel,
        (in_vmem((n_cols, block_rows, LANES), bf16),) + (in_vmem((half, block_rows, LANES), bf16),) * 2,
        0.5,
        at, *pairs,
        in_specs=[smem] + [vmem] * chips,
    )
    ends = swap(ends, "rows")
    norm, result = kernel_call(
        functools.partial(main_kernel, colors, file_rows, factor),
        (in_vmem(tile, bf16), in_vmem((56, LANES), f32)),
        6,
        pixels, wk, vec, grad, sums, cot_all, cot_halo,
        const["taps"], const["gather"], const["diagonal"], const["fold"], const["pick"],
        scratch_shapes=[
            pltpu.VMEM(tile, f32),
            pltpu.VMEM((per * block + 16, rows), f32),
            pltpu.VMEM((channels, 8, DEPTH), f32),
        ],
    )

    size = n_rows * n_cols
    chunk = channels // 4
    jobs = ["halo"] + list(range(0, channels, chunk))
    stem_output = None
    rounds = (size - 1).bit_length()
    for n in range(rounds):
        step = 1 if n == 0 else (1 << n) + 1
        other = lax.ppermute(result, ("rows", "cols"), [(i, i ^ step) for i in range(size)])
        final = n == rounds - 1
        if n > 0:
            for job in jobs if final else jobs[:1]:
                if job == "halo":
                    result, norm = lax.optimization_barrier((result, norm))
                    norm_all, norm_halo = kernel_call(
                        functools.partial(stem_halo_kernel, colors, file_rows),
                        (in_vmem(tall, bf16), in_vmem(tall, bf16)),
                        2,
                        at, pixels, *ends, wk, wh, vec, norm,
                        in_specs=[smem] + [vmem] * 7,
                    )
                    result, norm_all = lax.optimization_barrier((result, norm_all))
                else:
                    result, norm_all = lax.optimization_barrier((result, norm_all))
                    before = () if stem_output is None else (stem_output,)
                    stem_output = kernel_call(
                        functools.partial(stem_kernel, job),
                        shaped(tile, bf16),
                        1.5,
                        norm_all, norm_halo, kf, vec, *before,
                        in_specs=[vmem] * 4 + [beyond] * len(before),
                        out_specs=beyond,
                        input_output_aliases={4: 0} if before else {},
                        scratch_shapes=[pltpu.VMEM((chunk, height, width), bf16), pltpu.SemaphoreType.DMA],
                    )
                    result, stem_output = lax.optimization_barrier((result, stem_output))
            jobs = [] if final else jobs[1:]
        if not final:
            result = result + other

    taps = side * side
    outs = kernel_call(
        functools.partial(last_kernel, colors),
        (shaped((colors, channels), f32),) + (shaped((channels,), f32),) * 4 + (shaped((taps, channels), f32),),
        1,
        result, other,
    )
    return (stem_output, outs[0].T, outs[1], outs[2], outs[3], outs[5].T, outs[4])


def solution(mesh):
    return jax.shard_map(
        per_device,
        mesh=mesh,
        in_specs=(
            P(None, ("rows", "cols"), None),
            P(),
            P(),
            P(),
            P(),
            P(),
            P(),
            P(None, "rows", "cols"),
        ),
        out_specs=(P(None, "rows", "cols"), P(), P(), P(), P(), P(), P()),
        check_vma=False,
    )
```

time: 86.3 us -> 57.7 us (0.67)
  Pallas kernels: 37.4 us -> 24.2 us
  starting transfers between devices: 32.7 us -> 20.1 us
  local copies, waits for them, and re-layouts: 6.93 us -> 0.76 us
  waiting for transfers between devices: 6.47 us -> 11.4 us
  other arithmetic: 1.36 us -> 0.02 us
    pallas_call x6 -> x13, Pallas kernels: 37.4 us -> 24.2 us  [kernel_call(): pl.pallas_call(body, out_shape=out_shape, compiler_params=pltpu.CompilerP...]
    ppermute x11 -> x14, starting transfers between devices: 27.8 us -> 20.1 us  [the longest x5 5.99 us: per_device(): lax.ppermute(result, ('rows', 'cols'), [(i, i ^ step) for i in range(size)])]
    ppermute x11 -> x14, waiting for transfers between devices: 6.47 us -> 11.4 us  [the longest x3 5.91 us: per_device(): lax.ppermute(pairs[n], 'cols', [(i, (i + 2 * n) % n_cols) for i in range(...]
    all_to_all x1 -> x0, starting transfers between devices: 4.88 us -> none  [per_device(): lax.all_to_all(packed, 'cols', split_axis=0, concat_axis=0, tiled=True)]
    unnamed x14 -> x36, local copies, waits for them, and re-layouts: 3.24 us -> 0.68 us
    slice x2 -> x0, local copies, waits for them, and re-layouts: 1.87 us -> none  [the longest x1 1.03 us: per_device(): bot = shift(cotangent[:, :4, :], 'rows', -1)]
    transpose x2 -> x0, local copies, waits for them, and re-layouts: 1.3 us -> none  [the longest x1 0.69 us: per_device(): second[:taps]]
  transfers between devices with their start and end apart: 12 -> 14, of which waited for: 4 -> 8; matrix products, arithmetic and copies ran while one was open for 2% -> 0% of each run, Pallas kernels for 28% -> 35%
where the time goes in v2:
time: 57.7 us; the launch traced here: 57.5 us
  Pallas kernels  24.2 us (42%)
  starting transfers between devices  20.1 us (35%)
  waiting for transfers between devices  11.4 us (20%)
  between operations  0.99 us (2%)
  local copies, waits for them, and re-layouts  0.76 us (1%)
    pallas_call x13, Pallas kernels, kernel_call(): pl.pallas_call(body, out_shape=out_shape, compiler_params=pltpu.CompilerP...  24.2 us
    ppermute x5, starting transfers between devices, per_device(): lax.ppermute(result, ('rows', 'cols'), [(i, i ^ step) for i in range(size)])  5.99 us
    ppermute x3, waiting for transfers between devices, per_device(): lax.ppermute(pairs[n], 'cols', [(i, (i + 2 * n) % n_cols) for i in range(...  5.91 us
    ppermute x4, starting transfers between devices, swap(): lax.ppermute(part, axis, pairing(lax.axis_size(axis), n))  5.08 us
    ppermute x1, starting transfers between devices, per_device(): far = lax.ppermute(edges, 'cols', pairing(n_cols, 1))  4.71 us
    ppermute x5, waiting for transfers between devices, per_device(): lax.ppermute(result, ('rows', 'cols'), [(i, i ^ step) for i in range(size)])  3.84 us
    ppermute x3, starting transfers between devices, per_device(): lax.ppermute(pairs[n], 'cols', [(i, (i + 2 * n) % n_cols) for i in range(...  3.83 us
    ppermute x1, waiting for transfers between devices, per_device(): far = lax.ppermute(edges, 'cols', pairing(n_cols, 1))  1.64 us
  transfers between devices with their start and end apart: 14, of which 8 were waited for; matrix products, arithmetic and copies ran while one was open for 0% of the time, Pallas kernels for 35%

profile of v2, /device:TPU:0, one launch (start us, length us, event | category | flops | bytes accessed | tf_op | source)
XLA Modules:
  0.0 57.5 jit_solution(1496466190660191942)
XLA Ops:
  0.8 2.5 %shard_map.243 = (bf16[64,32,128]{2,1,0:T(8,128)(2,1)S(1)}, bf16[4,208,128]{2,1,0:T(8,128)(2,1)S(1)}, bf16[960,128]{1,0:T(8,128)(2,1)S(1)}, bf16[128,128]{1,0:T(8,128)(2,1)S(1)}) custom-call(s32[7]{0:T(128)S(1)} %stack.47.at_ref, bf16[48,4,1024]{2,1,0:T(4,128)(2,1)} %x_hbm.1, bf16[64,32,128]{2,1,0:T(8,128)(2,1)} %cot_hbm.1), custom_call_target="tpu_custom_call" | custom-call | flops 2000000000 | bytes 6000000 | tf_op jit(solution)/shard_map/pallas_call | solution.py:411
  3.8 4.7 %collective-permute-start.1 = (bf16[128,128]{1,0:T(8,128)(2,1)S(1)}, bf16[128,128]{1,0:T(8,128)(2,1)S(1)}, u32[]{:S(2)}, u32[]{:S(2)}) collective-permute-start(bf16[128,128]{1,0:T(8,128)(2,1)S(1)} %get-tuple-element.67), channel_id=1, source_target_pairs={{0,7},{1,2},{2,1},{3,4},{4,3},{5,6},{6,5},{7,0},{8,15},{9,10},{10,... | collective-permute-start | bytes 98312 | tf_op jit(solution)/shard_map/ppermute | solution.py:484
  8.5 1.6 %collective-permute-done.1.far_ref = bf16[128,128]{1,0:T(8,128)(2,1)S(1)} collective-permute-done((bf16[128,128]{1,0:T(8,128)(2,1)S(1)}, bf16[128,128]{1,0:T(8,128)(2,1)S(1)}, u32[]{:S(2)}, u32[]{:S(2)}) %collective-permute-start.1) | collective-permute-done | bytes 32800 | tf_op jit(solution)/shard_map/ppermute | solution.py:484
  10.2 1.0 %shard_map.246 = (bf16[64,32,128]{2,1,0:T(8,128)(2,1)S(1)}, bf16[64,8,128]{2,1,0:T(8,128)(2,1)S(1)}, bf16[64,8,128]{2,1,0:T(8,128)(2,1)S(1)}) custom-call(s32[7]{0:T(128)S(1)} %stack.47.at_ref, bf16[64,32,128]{2,1,0:T(8,128)(2,1)S(1)} %get-tuple-element.73.cot_ref, bf16[960,128]{1,0:T(8,128)(2,1)S(1)} %collective-permute-done.got_ref.near_ref, ...), custom_call_target="tpu_custom_call" | custom-call | flops 1000000000 | bytes 3000000 | tf_op jit(solution)/shard_map/pallas_call | solution.py:411
  11.3 1.6 %collective-permute-start.5 = (bf16[64,8,128]{2,1,0:T(8,128)(2,1)S(1)}, bf16[64,8,128]{2,1,0:T(8,128)(2,1)S(1)}, u32[]{:S(2)}, u32[]{:S(2)}) collective-permute-start(bf16[64,8,128]{2,1,0:T(8,128)(2,1)S(1)} %get-tuple-element.80), channel_id=1, source_target_pairs={{0,8},{8,0},{16,24},{24,16},{1,9},{9,1},{17,25},{25,17},{2,10},{10... | collective-permute-start | bytes 393224 | tf_op jit(solution)/shard_map/ppermute | solution.py:429
  12.8 1.5 %collective-permute-start.6 = (bf16[64,8,128]{2,1,0:T(8,128)(2,1)S(1)}, bf16[64,8,128]{2,1,0:T(8,128)(2,1)S(1)}, u32[]{:S(2)}, u32[]{:S(2)}) collective-permute-start(bf16[64,8,128]{2,1,0:T(8,128)(2,1)S(1)} %get-tuple-element.81), channel_id=1, source_target_pairs={{0,24},{8,16},{16,8},{24,0},{1,25},{9,17},{17,9},{25,1},{2,26},{10... | collective-permute-start | bytes 393224 | tf_op jit(solution)/shard_map/ppermute | solution.py:429
  14.3 2.2 %collective-permute-start.3 = (bf16[2,208,128]{2,1,0:T(8,128)(2,1)S(1)}, bf16[2,208,128]{2,1,0:T(8,128)(2,1)S(1)}, u32[]{:S(2)}, u32[]{:S(2)}) collective-permute-start(bf16[2,208,128]{2,1,0:T(8,128)(2,1)S(1)} %get-tuple-element.70), channel_id=1, source_target_pairs={{0,4},{1,5},{2,6},{3,7},{4,0},{5,1},{6,2},{7,3},{8,12},{9,13},{10,... | collective-permute-start | bytes 319496 | tf_op jit(solution)/shard_map/ppermute | solution.py:487
  16.5 1.6 %collective-permute-start.4 = (bf16[2,208,128]{2,1,0:T(8,128)(2,1)S(1)}, bf16[2,208,128]{2,1,0:T(8,128)(2,1)S(1)}, u32[]{:S(2)}, u32[]{:S(2)}) collective-permute-start(bf16[2,208,128]{2,1,0:T(8,128)(2,1)S(1)} %get-tuple-element.71), channel_id=1, source_target_pairs={{0,6},{1,7},{2,0},{3,1},{4,2},{5,3},{6,4},{7,5},{8,14},{9,15},{10,... | collective-permute-start | bytes 319496 | tf_op jit(solution)/shard_map/ppermute | solution.py:487
  18.8 0.9 %shard_map.247 = (bf16[512,384]{1,0:T(8,128)(2,1)S(1)}, bf16[512,512]{1,0:T(8,128)(2,1)S(1)}, f32[64,384]{1,0:T(8,128)S(1)}, f32[64,384]{1,0:T(8,128)S(1)}, f32[4,64,128]{2,1,0:T(8,128)S(1)}) custom-call(bf16[48,64]{1,0:T(8,128)(2,1)S(1)} %bitcast.12, f32[49,64]{1,0:T(8,128)S(1)} %bitcast.11, f32[64]{0:T(128)S(1)} %copy-done.2, f32[64]{0:T(128)S(1)} %copy-done.3, ...), custom_call_target="tpu_custom_call" | custom-call | flops 1500000000 | bytes 4500000 | tf_op jit(solution)/shard_map/pallas_call | solution.py:411
  19.7 2.4 %collective-permute-done.2.refs_1_ = bf16[2,208,128]{2,1,0:T(8,128)(2,1)S(1)} collective-permute-done((bf16[2,208,128]{2,1,0:T(8,128)(2,1)S(1)}, bf16[2,208,128]{2,1,0:T(8,128)(2,1)S(1)}, u32[]{:S(2)}, u32[]{:S(2)}) %collective-permute-start.2) | collective-permute-done | bytes 106528 | tf_op jit(solution)/shard_map/ppermute | solution.py:487
  22.1 3.2 %collective-permute-done.3.refs_2_ = bf16[2,208,128]{2,1,0:T(8,128)(2,1)S(1)} collective-permute-done((bf16[2,208,128]{2,1,0:T(8,128)(2,1)S(1)}, bf16[2,208,128]{2,1,0:T(8,128)(2,1)S(1)}, u32[]{:S(2)}, u32[]{:S(2)}) %collective-permute-start.3) | collective-permute-done | bytes 106528 | tf_op jit(solution)/shard_map/ppermute | solution.py:487
  26.2 1.6 %collective-permute-start.8 = (bf16[1,208,128]{2,1,0:T(8,128)(2,1)S(1)}, bf16[1,208,128]{2,1,0:T(8,128)(2,1)S(1)}, u32[]{:S(2)}, u32[]{:S(2)}) collective-permute-start(bf16[1,208,128]{2,1,0:T(8,128)(2,1)S(1)} %get-tuple-element.90), channel_id=1, source_target_pairs={{0,8},{8,0},{16,24},{24,16},{1,9},{9,1},{17,25},{25,17},{2,10},{10... | collective-permute-start | bytes 159752 | tf_op jit(solution)/shard_map/ppermute | solution.py:429
  28.3 3.9 %shard_map.248 = (bf16[64,48,128]{2,1,0:T(8,128)(2,1)S(1)}, bf16[64,48,128]{2,1,0:T(8,128)(2,1)S(1)}, f32[64,32,128]{2,1,0:T(8,128)S(1)}, f32[2,64,8,128]{3,2,1,0:T(8,128)S(1)}) custom-call(s32[7]{0:T(128)S(1)} %stack.47.at_ref, bf16[64,32,128]{2,1,0:T(8,128)(2,1)S(1)} %get-tuple-element.73.cot_ref, bf16[64,32,128]{2,1,0:T(8,128)(2,1)S(1)} %get-tuple-element.79.beside_ref, ...), custom_call_target="tpu_custom_call" | custom-call | flops 5000000000 | bytes 15000000 | tf_op jit(solution)/shard_map/pallas_call | solution.py:411
  32.3 7.5 %shard_map.249 = (bf16[64,32,128]{2,1,0:T(8,128)(2,1)S(1)}, f32[56,128]{1,0:T(8,128)S(1)}) custom-call(bf16[8,208,128]{2,1,0:T(8,128)(2,1)S(1)} %get-tuple-element.72.x_ref, bf16[512,384]{1,0:T(8,128)(2,1)S(1)} %get-tuple-element.77.wk_ref, f32[4,64,128]{2,1,0:T(8,128)S(1)} %get-tuple-element.78.vec_ref.refs_3_, ...), custom_call_target="tpu_custom_call" | custom-call | flops 6000000000 | bytes 18000000 | tf_op jit(solution)/shard_map/pallas_call | solution.py:411
  39.9 1.2 %collective-permute-done.7 = f32[56,128]{1,0:T(8,128)S(1)} collective-permute-done((f32[56,128]{1,0:T(8,128)S(1)}, f32[56,128]{1,0:T(8,128)S(1)}, u32[]{:S(2)}, u32[]{:S(2)}) %collective-permute-start.7) | collective-permute-done | bytes 28704 | tf_op jit(solution)/shard_map/ppermute | solution.py:553
  41.1 2.3 %collective-permute-start.10 = (f32[56,128]{1,0:T(8,128)S(1)}, f32[56,128]{1,0:T(8,128)S(1)}, u32[]{:S(2)}, u32[]{:S(2)}) collective-permute-start(f32[56,128]{1,0:T(8,128)S(1)} %add.22), channel_id=1, source_target_pairs={{0,3},{1,2},{2,1},{3,0},{4,7},{5,6},{6,5},{7,4},{8,11},{9,10},{10,... | collective-permute-start | bytes 86024 | tf_op jit(solution)/shard_map/ppermute | solution.py:553
  43.4 1.4 %shard_map.250 = (bf16[64,48,128]{2,1,0:T(8,128)(2,1)S(1)}, bf16[64,48,128]{2,1,0:T(8,128)(2,1)S(1)}) custom-call(s32[7]{0:T(128)S(1)} %stack.47.at_ref, bf16[8,208,128]{2,1,0:T(8,128)(2,1)S(1)} %get-tuple-element.72.x_ref, bf16[1,208,128]{2,1,0:T(8,128)(2,1)S(1)} %collective-permute-done.8.one_ref, bf16[1,208,128]{2,1,0:T(8,128)(2,1)S(1)} %collective-permute-done.9.two_ref, ...), custom_call_target="tpu_custom_call" | custom-call | flops 2000000000 | bytes 6000000 | tf_op jit(solution)/shard_map/pallas_call | solution.py:411
  45.7 1.4 %shard_map.251.refs_4_ = bf16[64,32,128]{2,1,0:T(8,128)(2,1)} custom-call(bf16[64,48,128]{2,1,0:T(8,128)(2,1)S(1)} %get-tuple-element.111.refs_0_, bf16[64,48,128]{2,1,0:T(8,128)(2,1)S(1)} %get-tuple-element.99.refs_1_, f32[64,384]{1,0:T(8,128)S(1)} %get-tuple-element.100.refs_2_, f32[4,64,128]{2,1,0:T(8,128)S(1)} %get-tuple-element.78.vec_ref.refs_3_), custom_call_target="tpu_custom_call" | custom-call | flops 1500000000 | bytes 4500000 | tf_op jit(solution)/shard_map/pallas_call | solution.py:411
  47.1 2.1 %collective-permute-done.11 = f32[56,128]{1,0:T(8,128)S(1)} collective-permute-done((f32[56,128]{1,0:T(8,128)S(1)}, f32[56,128]{1,0:T(8,128)S(1)}, u32[]{:S(2)}, u32[]{:S(2)}) %collective-permute-start.11) | collective-permute-done | bytes 28704 | tf_op jit(solution)/shard_map/ppermute | solution.py:553
  49.2 1.4 %collective-permute-start.12 = (f32[56,128]{1,0:T(8,128)S(1)}, f32[56,128]{1,0:T(8,128)S(1)}, u32[]{:S(2)}, u32[]{:S(2)}) collective-permute-start(f32[56,128]{1,0:T(8,128)S(1)} %add.24), channel_id=1, source_target_pairs={{0,9},{1,8},{2,11},{3,10},{4,13},{5,12},{6,15},{7,14},{8,1},{9,0},... | collective-permute-start | bytes 86024 | tf_op jit(solution)/shard_map/ppermute | solution.py:553
  50.6 1.4 %shard_map.252.refs_4_ = bf16[64,32,128]{2,1,0:T(8,128)(2,1)} custom-call(bf16[64,48,128]{2,1,0:T(8,128)(2,1)S(1)} %get-tuple-element.111.refs_0_, bf16[64,48,128]{2,1,0:T(8,128)(2,1)S(1)} %get-tuple-element.99.refs_1_, f32[64,384]{1,0:T(8,128)S(1)} %get-tuple-element.100.refs_2_, ...), custom_call_target="tpu_custom_call", output_to_operand_aliasing={{}: (4, {})} | custom-call | flops 1500000000 | bytes 4500000 | tf_op jit(solution)/shard_map/pallas_call | solution.py:411
  52.5 1.5 %collective-permute-start.13 = (f32[56,128]{1,0:T(8,128)S(1)}, f32[56,128]{1,0:T(8,128)S(1)}, u32[]{:S(2)}, u32[]{:S(2)}) collective-permute-start(f32[56,128]{1,0:T(8,128)S(1)} %add.25.x_ref), channel_id=1, source_target_pairs={{0,17},{1,16},{2,19},{3,18},{4,21},{5,20},{6,23},{7,22},{8,25},{9,... | collective-permute-start | bytes 86024 | tf_op jit(solution)/shard_map/ppermute | solution.py:553
  53.9 1.4 %shard_map.253.refs_4_ = bf16[64,32,128]{2,1,0:T(8,128)(2,1)} custom-call(bf16[64,48,128]{2,1,0:T(8,128)(2,1)S(1)} %get-tuple-element.111.refs_0_, bf16[64,48,128]{2,1,0:T(8,128)(2,1)S(1)} %get-tuple-element.99.refs_1_, f32[64,384]{1,0:T(8,128)S(1)} %get-tuple-element.100.refs_2_, ...), custom_call_target="tpu_custom_call", output_to_operand_aliasing={{}: (4, {})} | custom-call | flops 1500000000 | bytes 4500000 | tf_op jit(solution)/shard_map/pallas_call | solution.py:411
  55.4 1.4 %shard_map.254 = bf16[64,32,128]{2,1,0:T(8,128)(2,1)} custom-call(bf16[64,48,128]{2,1,0:T(8,128)(2,1)S(1)} %get-tuple-element.111.refs_0_, bf16[64,48,128]{2,1,0:T(8,128)(2,1)S(1)} %get-tuple-element.99.refs_1_, f32[64,384]{1,0:T(8,128)S(1)} %get-tuple-element.100.refs_2_, ...), custom_call_target="tpu_custom_call", output_to_operand_aliasing={{}: (4, {})} | custom-call | flops 1500000000 | bytes 4500000 | tf_op jit(solution)/shard_map/pallas_call | solution.py:411
  (58 shorter events, 4.8 us)
Async XLA Ops:
  3.2 5.2 %collective-permute-start = (bf16[960,128]{1,0:T(8,128)(2,1)S(1)}, bf16[960,128]{1,0:T(8,128)(2,1)S(1)}, u32[]{:S(2)}, u32[]{:S(2)}) collective-permute-start(bf16[960,128]{1,0:T(8,128)(2,1)S(1)} %get-tuple-element.65), channel_id=1, source_target_pairs={{0,1},{1,0},{2,3},{3,2},{4,5},{5,4},{6,7},{7,6},{8,9},{9,8},{10,11... | collective-permute-start | bytes 737288 | tf_op jit(solution)/shard_map/ppermute | solution.py:483
  3.8 6.4 %collective-permute-start.1 = (bf16[128,128]{1,0:T(8,128)(2,1)S(1)}, bf16[128,128]{1,0:T(8,128)(2,1)S(1)}, u32[]{:S(2)}, u32[]{:S(2)}) collective-permute-start(bf16[128,128]{1,0:T(8,128)(2,1)S(1)} %get-tuple-element.67), channel_id=1, source_target_pairs={{0,7},{1,2},{2,1},{3,4},{4,3},{5,6},{6,5},{7,0},{8,15},{9,10},{10,... | collective-permute-start | bytes 98312 | tf_op jit(solution)/shard_map/ppermute | solution.py:484
  10.2 8.0 %copy-start = (f32[64,49]{0,1:T(8,128)S(1)}, f32[64,49]{0,1:T(8,128)}, u32[]{:S(2)}) copy-start(f32[64,49]{0,1:T(8,128)} %param.25) | copy-start | bytes 37636
  10.2 8.0 %copy-start.5 = (f32[64]{0:T(128)S(1)}, f32[64]{0:T(128)}, u32[]{:S(2)}) copy-start(f32[64]{0:T(128)} %koff_ref.1) | copy-start | bytes 772
  10.2 8.0 %copy-start.6 = (bf16[512,512]{1,0:T(8,128)(2,1)S(1)}, bf16[512,512]{1,0:T(8,128)(2,1)}, u32[]{:S(2)}) copy-start(bf16[512,512]{1,0:T(8,128)(2,1)} %constant.68.clone.keep_h_ref) | copy-start | bytes 1572868
  10.2 8.0 %copy-start.8 = (bf16[512,384]{1,0:T(8,128)(2,1)S(1)}, bf16[512,384]{1,0:T(8,128)(2,1)}, u32[]{:S(2)}) copy-start(bf16[512,384]{1,0:T(8,128)(2,1)} %constant.66.clone.keep_ref) | copy-start | bytes 1179652
  10.2 8.0 %copy-start.10 = (bf16[512,64]{1,0:T(8,128)(2,1)S(1)}, bf16[512,64]{1,0:T(8,128)(2,1)}, u32[]{:S(2)}) copy-start(bf16[512,64]{1,0:T(8,128)(2,1)} %constant.69.clone.tall_ref) | copy-start | bytes 196612
  10.2 8.0 %copy-start.11 = (f32[49,384]{1,0:T(8,128)S(1)}, f32[49,384]{1,0:T(8,128)}, u32[]{:S(2)}) copy-start(f32[49,384]{1,0:T(8,128)} %constant.73.clone.forward_ref) | copy-start | bytes 225796
  10.2 8.0 %copy-start.12 = (f32[49,384]{1,0:T(8,128)S(1)}, f32[49,384]{1,0:T(8,128)}, u32[]{:S(2)}) copy-start(f32[49,384]{1,0:T(8,128)} %constant.74.clone.backward_ref) | copy-start | bytes 225796
  10.2 8.0 %copy-start.14 = (bf16[48,512]{1,0:T(8,128)(2,1)S(1)}, bf16[48,512]{1,0:T(8,128)(2,1)}, u32[]{:S(2)}) copy-start(bf16[48,512]{1,0:T(8,128)(2,1)} %constant.67.clone.spread_h_ref) | copy-start | bytes 147460
  10.2 8.0 %copy-start.17 = (bf16[48,384]{1,0:T(8,128)(2,1)S(1)}, bf16[48,384]{1,0:T(8,128)(2,1)}, u32[]{:S(2)}) copy-start(bf16[48,384]{1,0:T(8,128)(2,1)} %constant.65.clone.spread_ref) | copy-start | bytes 110596
  11.3 7.0 %copy-start.1 = (bf16[64,48]{0,1:T(8,128)(2,1)S(1)}, bf16[64,48]{0,1:T(8,128)(2,1)}, u32[]{:S(2)}) copy-start(bf16[64,48]{0,1:T(8,128)(2,1)} %param.21) | copy-start | bytes 18436
  11.3 17.0 %collective-permute-start.5 = (bf16[64,8,128]{2,1,0:T(8,128)(2,1)S(1)}, bf16[64,8,128]{2,1,0:T(8,128)(2,1)S(1)}, u32[]{:S(2)}, u32[]{:S(2)}) collective-permute-start(bf16[64,8,128]{2,1,0:T(8,128)(2,1)S(1)} %get-tuple-element.80), channel_id=1, source_target_pairs={{0,8},{8,0},{16,24},{24,16},{1,9},{9,1},{17,25},{25,17},{2,10},{10... | collective-permute-start | bytes 393224 | tf_op jit(solution)/shard_map/ppermute | solution.py:429
  12.8 15.4 %collective-permute-start.6 = (bf16[64,8,128]{2,1,0:T(8,128)(2,1)S(1)}, bf16[64,8,128]{2,1,0:T(8,128)(2,1)S(1)}, u32[]{:S(2)}, u32[]{:S(2)}) collective-permute-start(bf16[64,8,128]{2,1,0:T(8,128)(2,1)S(1)} %get-tuple-element.81), channel_id=1, source_target_pairs={{0,24},{8,16},{16,8},{24,0},{1,25},{9,17},{17,9},{25,1},{2,26},{10... | collective-permute-start | bytes 393224 | tf_op jit(solution)/shard_map/ppermute | solution.py:429
  14.3 7.8 %collective-permute-start.2 = (bf16[2,208,128]{2,1,0:T(8,128)(2,1)S(1)}, bf16[2,208,128]{2,1,0:T(8,128)(2,1)S(1)}, u32[]{:S(2)}, u32[]{:S(2)}) collective-permute-start(bf16[2,208,128]{2,1,0:T(8,128)(2,1)S(1)} %get-tuple-element.69), channel_id=1, source_target_pairs={{0,2},{1,3},{2,4},{3,5},{4,6},{5,7},{6,0},{7,1},{8,10},{9,11},{10,... | collective-permute-start | bytes 319496 | tf_op jit(solution)/shard_map/ppermute | solution.py:487
  14.3 11.0 %collective-permute-start.3 = (bf16[2,208,128]{2,1,0:T(8,128)(2,1)S(1)}, bf16[2,208,128]{2,1,0:T(8,128)(2,1)S(1)}, u32[]{:S(2)}, u32[]{:S(2)}) collective-permute-start(bf16[2,208,128]{2,1,0:T(8,128)(2,1)S(1)} %get-tuple-element.70), channel_id=1, source_target_pairs={{0,4},{1,5},{2,6},{3,7},{4,0},{5,1},{6,2},{7,3},{8,12},{9,13},{10,... | collective-permute-start | bytes 319496 | tf_op jit(solution)/shard_map/ppermute | solution.py:487
  16.5 9.1 %collective-permute-start.4 = (bf16[2,208,128]{2,1,0:T(8,128)(2,1)S(1)}, bf16[2,208,128]{2,1,0:T(8,128)(2,1)S(1)}, u32[]{:S(2)}, u32[]{:S(2)}) collective-permute-start(bf16[2,208,128]{2,1,0:T(8,128)(2,1)S(1)} %get-tuple-element.71), channel_id=1, source_target_pairs={{0,6},{1,7},{2,0},{3,1},{4,2},{5,3},{6,4},{7,5},{8,14},{9,15},{10,... | collective-permute-start | bytes 319496 | tf_op jit(solution)/shard_map/ppermute | solution.py:487
  26.2 17.2 %collective-permute-start.8 = (bf16[1,208,128]{2,1,0:T(8,128)(2,1)S(1)}, bf16[1,208,128]{2,1,0:T(8,128)(2,1)S(1)}, u32[]{:S(2)}, u32[]{:S(2)}) collective-permute-start(bf16[1,208,128]{2,1,0:T(8,128)(2,1)S(1)} %get-tuple-element.90), channel_id=1, source_target_pairs={{0,8},{8,0},{16,24},{24,16},{1,9},{9,1},{17,25},{25,17},{2,10},{10... | collective-permute-start | bytes 159752 | tf_op jit(solution)/shard_map/ppermute | solution.py:429
  27.8 15.6 %collective-permute-start.9 = (bf16[1,208,128]{2,1,0:T(8,128)(2,1)S(1)}, bf16[1,208,128]{2,1,0:T(8,128)(2,1)S(1)}, u32[]{:S(2)}, u32[]{:S(2)}) collective-permute-start(bf16[1,208,128]{2,1,0:T(8,128)(2,1)S(1)} %get-tuple-element.91), channel_id=1, source_target_pairs={{0,24},{8,16},{16,8},{24,0},{1,25},{9,17},{17,9},{25,1},{2,26},{10... | collective-permute-start | bytes 159752 | tf_op jit(solution)/shard_map/ppermute | solution.py:429
  39.8 1.3 %collective-permute-start.7 = (f32[56,128]{1,0:T(8,128)S(1)}, f32[56,128]{1,0:T(8,128)S(1)}, u32[]{:S(2)}, u32[]{:S(2)}) collective-permute-start(f32[56,128]{1,0:T(8,128)S(1)} %get-tuple-element.87), channel_id=1, source_target_pairs={{0,1},{1,0},{2,3},{3,2},{4,5},{5,4},{6,7},{7,6},{8,9},{9,8},{10,11... | collective-permute-start | bytes 86024 | tf_op jit(solution)/shard_map/ppermute | solution.py:553
  41.1 3.9 %collective-permute-start.10 = (f32[56,128]{1,0:T(8,128)S(1)}, f32[56,128]{1,0:T(8,128)S(1)}, u32[]{:S(2)}, u32[]{:S(2)}) collective-permute-start(f32[56,128]{1,0:T(8,128)S(1)} %add.22), channel_id=1, source_target_pairs={{0,3},{1,2},{2,1},{3,0},{4,7},{5,6},{6,5},{7,4},{8,11},{9,10},{10,... | collective-permute-start | bytes 86024 | tf_op jit(solution)/shard_map/ppermute | solution.py:553
  45.0 4.2 %collective-permute-start.11 = (f32[56,128]{1,0:T(8,128)S(1)}, f32[56,128]{1,0:T(8,128)S(1)}, u32[]{:S(2)}, u32[]{:S(2)}) collective-permute-start(f32[56,128]{1,0:T(8,128)S(1)} %add.23), channel_id=1, source_target_pairs={{0,5},{1,4},{2,7},{3,6},{4,1},{5,0},{6,3},{7,2},{8,13},{9,12},{10,... | collective-permute-start | bytes 86024 | tf_op jit(solution)/shard_map/ppermute | solution.py:553
  49.2 3.3 %collective-permute-start.12 = (f32[56,128]{1,0:T(8,128)S(1)}, f32[56,128]{1,0:T(8,128)S(1)}, u32[]{:S(2)}, u32[]{:S(2)}) collective-permute-start(f32[56,128]{1,0:T(8,128)S(1)} %add.24), channel_id=1, source_target_pairs={{0,9},{1,8},{2,11},{3,10},{4,13},{5,12},{6,15},{7,14},{8,1},{9,0},... | collective-permute-start | bytes 86024 | tf_op jit(solution)/shard_map/ppermute | solution.py:553
  52.5 4.3 %collective-permute-start.13 = (f32[56,128]{1,0:T(8,128)S(1)}, f32[56,128]{1,0:T(8,128)S(1)}, u32[]{:S(2)}, u32[]{:S(2)}) collective-permute-start(f32[56,128]{1,0:T(8,128)S(1)} %add.25.x_ref), channel_id=1, source_target_pairs={{0,17},{1,16},{2,19},{3,18},{4,21},{5,20},{6,23},{7,22},{8,25},{9,... | collective-permute-start | bytes 86024 | tf_op jit(solution)/shard_map/ppermute | solution.py:553
  (8 other events, 21.9 us)

commit v3 on v2

--- a/solution.py
+++ b/solution.py
@@ -16,7 +16,7 @@
 PITCH = 48
 DEPTH = 8 * PITCH
 VMEM = 20 * 1024 * 1024
-UNROLL = 16
+UNROLL = 32
 bf16, f32 = jnp.bfloat16, jnp.float32
 
 NN = (((1,), (0,)), ((), ()))
@@ -49,27 +49,16 @@
     block = colors * file_rows
     per = GROUP // file_rows
     rows = channels * GROUP
-    inner = per * block
     out = {}
-
-    def source(width):
+    for name, width in (("", block), ("_halo", cdiv(block, LANES) * LANES)):
         at = np.arange(per * width)
         part, inside = at // width, at % width
         ok = inside < block
-        return np.where(ok, inside // file_rows, -1), np.where(ok, part * file_rows + inside % file_rows, -1)
-
-    for name, width in (("", block), ("_halo", cdiv(block, LANES) * LANES)):
-        color, row = source(width)
+        color = np.where(ok, inside % colors, -1)
+        row = np.where(ok, part * file_rows + inside // colors, -1)
         out["spread" + name] = color[None, :] == np.arange(colors)[:, None]
         out["keep" + name] = row[None, :] == (np.arange(rows) % GROUP)[:, None]
     out["tall"] = (np.arange(rows) // GROUP)[:, None] == np.arange(channels)[None, :]
-    out["gather"] = (np.arange(rows) // GROUP)[:, None] == np.arange(LANES)[None, :]
-    color, row = source(block)
-    out["diagonal"] = np.concatenate([out["keep"].T, np.ones((16, rows), bool)])
-    fold = np.zeros((56, inner + 16), bool)
-    fold[color, np.arange(inner)] = True
-    fold[colors, inner] = True
-    out["fold"] = fold
     lane = np.arange(DEPTH)
     copy, at = lane // PITCH, lane % PITCH - 5
     tap = np.where((at >= 0) & (at < side) & (copy < side), at * side + copy, -1)
@@ -100,13 +89,13 @@
         vec_ref[n] = jnp.broadcast_to(column, (channels, LANES))
 
 
-def pack_kernel(at_ref, x_hbm, cot_hbm, cot_ref, keep_ref, give_ref, edge_ref, edge_s, x_ref, sems):
+def pack_kernel(at_ref, x_hbm, cot_hbm, cot_ref, keep_ref, give_ref, edge_ref, edge_s, x_ref, y_ref, sems):
     colors, file_rows, width = x_ref.shape
     channels, height, _ = cot_ref.shape
     chips, block_rows, _ = keep_ref.shape
     count = width // LANES
     block = colors * file_rows
-    core, chip = at_ref[0], at_ref[1]
+    core, chip = at_ref[0, 0], at_ref[1, 0]
     load_x = pltpu.make_async_copy(x_hbm, x_ref, sems.at[0])
     load_cot = pltpu.make_async_copy(cot_hbm, cot_ref, sems.at[1])
     load_x.start()
@@ -118,9 +107,15 @@
     edges = mm(pick, cot_ref[...].reshape(channels * height, LANES), NT)
     edges = jnp.concatenate(
         [edges[:, n:n + LANES] for n in range(0, channels * height, LANES)], axis=0).astype(bf16)
-    edge_ref[...] = edges
+    edge_ref[:edges.shape[0]] = edges
+    edge_ref[edges.shape[0]:] = edges[:edge_ref.shape[0] - edges.shape[0]]
     give_ref[chips * block_rows:, :] = edges
+
+    row, src = iota((block, block), 0), iota((block, block), 1)
+    part = sum((row >= colors * n).astype(jnp.int32) for n in range(1, file_rows)) if file_rows > 1 else 0
+    move = one_hot(src == (row - colors * part) * file_rows + part)
     load_x.wait()
+    y_ref[...] = mm(move, x_ref[...].reshape(block, width)).astype(bf16)
 
     row, lane = iota((16, LANES), 0), iota((16, LANES), 1)
     pick = one_hot(((row < 3) & (lane == row + LANES - 3)) | ((row >= 11) & (row < 14) & (lane == row - 11)))
@@ -128,7 +123,7 @@
     edge_s[0] = zeros
     edge_s[count + 1] = zeros
     for d in range(count):
-        tile = x_ref[:, :, d * LANES:(d + 1) * LANES].reshape(block, LANES)
+        tile = y_ref[:, d * LANES:(d + 1) * LANES]
         edge_s[d + 1] = mm(pick, tile, NT)
 
     def halo(d):
@@ -149,7 +144,7 @@
         there = lax.rem(chip + away, chips)
         for other in range(2):
             d = 2 * there + (core if other == 0 else 1 - core)
-            tile = x_ref[:, :, pl.ds(pl.multiple_of(d * LANES, LANES), LANES)].reshape(block, LANES)
+            tile = y_ref[:, pl.ds(pl.multiple_of(d * LANES, LANES), LANES)]
             if other == 0:
                 keep_ref[away, :block, :] = tile
                 keep_ref[away, block:, :] = halo(d)
@@ -168,25 +163,33 @@
 
 def strips_kernel(at_ref, cot_ref, near_ref, far_ref, halo_ref, one_ref, two_ref):
     channels, height, width = cot_ref.shape
-    size = far_ref.shape[0]
-    core = at_ref[0]
+    size = channels * height // 16
+    core = at_ref[0, 0]
     near = near_ref[near_ref.shape[0] - size:, :].astype(f32)
-    far = far_ref[...].astype(f32)
+    far = far_ref[:size, :].astype(f32)
     left = jnp.where(core == 0, far, near)
     right = jnp.where(core == 0, near, far)
     left = jnp.concatenate([left[n:n + 8] for n in range(0, size, 8)], axis=1).astype(bf16)
     right = jnp.concatenate([right[n:n + 8] for n in range(0, size, 8)], axis=1).astype(bf16)
     row, lane = iota((8, width), 0), iota((8, width), 1)
-    from_left = one_hot((row >= 3) & (row < 6) & (lane == row + width - 6) & (at_ref[4] == 0))
-    from_right = one_hot((row < 3) & (lane == row) & (at_ref[5] == 0))
+    from_left = one_hot((row >= 3) & (row < 6) & (lane == row + width - 6) & (at_ref[4, 0] == 0))
+    from_right = one_hot((row < 3) & (lane == row) & (at_ref[5, 0] == 0))
     halo = (mm(left, from_left, TN) + mm(right, from_right, TN)).reshape(channels, height, width)
     halo_ref[...] = halo.astype(bf16)
     own = cot_ref[...].astype(f32)
-    up = jnp.concatenate([own[:, :4], halo[:, :4]], axis=1)
-    down = jnp.concatenate([own[:, height - 4:], halo[:, height - 4:]], axis=1)
-    even = at_ref[6] == 0
-    one_ref[...] = jnp.where(even, down, up).astype(bf16)
-    two_ref[...] = jnp.where(even, up, down).astype(bf16)
+    pick = one_hot((lane == row + width - 3) & (row < 3) | (lane == row - 3) & (row >= 3) & (row < 6))
+    up, down = own[:, :4], own[:, height - 4:]
+    up_halo, down_halo = halo[:, :4], halo[:, height - 4:]
+    even = at_ref[6, 0] == 0
+    for ref, rows, beside in (
+        (one_ref, jnp.where(even, down, up), jnp.where(even, down_halo, up_halo)),
+        (two_ref, jnp.where(even, up, down), jnp.where(even, up_halo, down_halo)),
+    ):
+        ref[:channels] = rows.astype(bf16)
+        dense = mm(pick, beside.reshape(channels * 4, width).astype(bf16), NT)
+        for n in range(0, channels * 4, LANES):
+            for q in range(2):
+                ref[channels + n // 64 + q] = dense[4 * q:4 * q + 4, n:n + LANES].astype(bf16)
 
 
 def shifted(center, halo):
@@ -209,21 +212,41 @@
     return jnp.concatenate(split2(taps), axis=0)
 
 
-def back_kernel(factor, at_ref, cot_ref, beside_ref, one_ref, two_ref, kb_ref, all_ref, halo_ref, grad_ref, sum_ref):
+def back_kernel(factor, at_ref, cot_ref, beside_ref, one_ref, two_ref, kb_ref,
+                flip_ref, grad_ref, total_ref, all_ref, halo_ref, sum_ref):
     channels, height, width = cot_ref.shape
-    even = at_ref[6] == 0
+    even = at_ref[6, 0] == 0
     one, two = one_ref[...].astype(f32), two_ref[...].astype(f32)
-    top = jnp.where(at_ref[2] == 0, jnp.where(even, two, one), 0.0)
-    bot = jnp.where(at_ref[3] == 0, jnp.where(even, one, two), 0.0)
+    top = jnp.where(at_ref[2, 0] == 0, jnp.where(even, two, one), 0.0)
+    bot = jnp.where(at_ref[3, 0] == 0, jnp.where(even, one, two), 0.0)
+    row, lane = iota((8, width), 0), iota((8, width), 1)
+    place = one_hot((lane == row + width - 3) & (row < 3) | (lane == row - 3) & (row >= 3) & (row < 6))
+
+    def beside(part):
+        dense = jnp.concatenate(
+            [
+                jnp.concatenate([part[channels + n // 64 + q] for q in range(2)], axis=0)
+                for n in range(0, channels * 4, LANES)
+            ],
+            axis=1,
+        )
+        return mm(dense.astype(bf16), place, TN).reshape(channels, 4, width)
+
     none = jnp.zeros((channels, 4, width), f32)
-    for part, middle, ref in ((slice(0, 4), cot_ref, all_ref), (slice(4, 8), beside_ref, halo_ref)):
-        ref[:, 0:8, :] = jnp.concatenate([none, top[:, part]], axis=1).astype(bf16)
+    for above, middle, below, ref in (
+        (top[:channels], cot_ref, bot[:channels], all_ref),
+        (beside(top), beside_ref, beside(bot), halo_ref),
+    ):
+        ref[:, 0:8, :] = jnp.concatenate([none, above], axis=1).astype(bf16)
         ref[:, 8:8 + height, :] = middle[...]
-        ref[:, 8 + height:, :] = jnp.concatenate([bot[:, part], none], axis=1).astype(bf16)
+        ref[:, 8 + height:, :] = jnp.concatenate([below, none], axis=1).astype(bf16)
+
+    eye = one_hot(iota((width, width), 0) == iota((width, width), 1))
 
     def one(k, carry):
         plane = all_ref[k]
         stack = shifted(plane, halo_ref[k])
+        flip_ref[k] = mm(eye, stack, NT).astype(bf16)
         both = mm(toeplitz(kb_ref[pl.ds(k, 1), :], height), stack)
         grad = (both[:height] + both[height:]) * factor
         grad_ref[k] = grad
@@ -233,6 +256,8 @@
         return carry
 
     lax.fori_loop(0, channels, one, 0, unroll=UNROLL)
+    for n in range(2):
+        total_ref[n] = sum(sum_ref[n, :, b, :] for b in range(8))
 
 
 def layer_norm(patch, channels):
@@ -250,7 +275,7 @@
 def order_kernel(at_ref, *refs):
     pair_refs, (x_ref, one_ref, two_ref) = refs[:-3], refs[-3:]
     chips = len(pair_refs)
-    core, chip = at_ref[0], at_ref[1]
+    core, chip = at_ref[0, 0], at_ref[1, 0]
     for away, ref in enumerate(pair_refs):
         there = lax.rem(chip - away + chips, chips)
         x_ref[2 * there + core] = ref[0]
@@ -258,14 +283,13 @@
     half = one_ref.shape[0]
     up = x_ref[:half]
     down = x_ref[2 * chips - half:]
-    even = at_ref[6] == 0
+    even = at_ref[6, 0] == 0
     one_ref[...] = jnp.where(even, down, up)
     two_ref[...] = jnp.where(even, up, down)
 
 
-def main_kernel(colors, file_rows, factor, x_ref, wk_ref, vec_ref, grad_ref, sum_ref, all_ref, halo_ref,
-                taps_ref, gather_ref, diagonal_ref, fold_ref, pick_ref,
-                norm_ref, out_ref, norm_s, gram_s, diag_s):
+def main_kernel(colors, file_rows, factor, x_ref, wk_ref, vec_ref, grad_ref, total_ref, flip_ref, taps_ref, pick_ref,
+                norm_ref, out_ref, norm_s, grad_s, diag_s):
     channels, height, width = grad_ref.shape
     block = colors * file_rows
     per = GROUP // file_rows
@@ -273,9 +297,10 @@
     bias, gain, offset = per_row(vec_ref, 0), per_row(vec_ref, 1), per_row(vec_ref, 2)
     scale_part = jnp.zeros((channels, GROUP, width), f32)
     ones = jnp.where(iota((16, width), 0) == 0, 1.0, 0.0).astype(bf16)
+    by_color = jnp.zeros((colors + 16, channels), f32)
     for g in range(height // GROUP):
-        pixels = jnp.concatenate([x_ref[per * g + a, :block, :] for a in range(per)], axis=0)
-        patch = mm(wk_ref[...], pixels).reshape(channels, GROUP, width) + bias
+        blocks = [x_ref[per * g + a, :block, :] for a in range(per)]
+        patch = mm(wk_ref[...], jnp.concatenate(blocks, axis=0)).reshape(channels, GROUP, width) + bias
         xhat, inverse = layer_norm(patch, channels)
         norm_s[:, g * GROUP:(g + 1) * GROUP, :] = xhat * gain + offset
         grad = grad_ref[:, g * GROUP:(g + 1) * GROUP, :]
@@ -283,18 +308,18 @@
         inside = grad * gain
         mean_a = jnp.mean(inside, axis=0, keepdims=True)
         mean_b = jnp.mean(inside * xhat, axis=0, keepdims=True)
-        patch_grad = (inverse * (inside - mean_a - xhat * mean_b)).astype(bf16).reshape(rows, width)
-        gram = mm(jnp.concatenate([pixels, ones], axis=0), patch_grad, NT)
-        if g == 0:
-            gram_s[...] = gram
-        else:
-            gram_s[...] += gram
+        grad_s[g] = (inverse * (inside - mean_a - xhat * mean_b)).reshape(rows, width)
+        left, right = [], []
+        for h in range(GROUP):
+            start = h % file_rows * colors
+            left.append(jnp.concatenate([blocks[h // file_rows][start:start + colors], ones], axis=0))
+            right.append(grad_s[g, pl.ds(h, channels, stride=GROUP), :].astype(bf16))
+        by_color += mm(jnp.concatenate(left, axis=1), jnp.concatenate(right, axis=1), NT)
 
     def one(k, carry):
         plane = norm_s[k].astype(bf16)
         norm_ref[k] = plane
-        stack = shifted(all_ref[k], halo_ref[k])
-        cross = mm(plane, stack, NT)
+        cross = mm(plane, flip_ref[k])
         total = cross[:8]
         for a in range(1, height // 8):
             total += pltpu.roll(cross[8 * a:8 * a + 8], DEPTH - 8 * a, 1)
@@ -307,16 +332,10 @@
     for b in range(1, 8):
         line += pltpu.roll(diag_s[:, b, :], DEPTH - b, 1)
     line = jnp.concatenate([jnp.zeros((LANES - channels, DEPTH), f32), line * factor], axis=0)
-    result = sum(mm(taps_ref[...], part, NT) for part in split2(line))
-
-    gather = gather_ref[...]
-    gram = gram_s[...] * diagonal_ref[...].astype(f32)
-    by_channel = sum(mm(part, gather) for part in split2(gram))
-    result += sum(mm(fold_ref[...], part) for part in split2(by_channel))
-    parts = [part.reshape(rows, width) for part in (scale_part, sum_ref[0], sum_ref[1])]
-    line = sum(mm(pick_ref[...], piece, NT) for piece in split2(jnp.concatenate(parts, axis=1)))
-    result += sum(mm(piece, gather) for piece in split2(line))
-    out_ref[...] = result
+    out_ref[...] = sum(mm(taps_ref[...], part, NT) for part in split2(line))
+    parts = jnp.concatenate([jnp.sum(scale_part, axis=1), total_ref[0], total_ref[1]], axis=1)
+    first = sum(mm(pick_ref[...], part, NT) for part in split2(parts))
+    out_ref[:, :channels] = first + by_color[:56]
 
 
 def stem_halo_kernel(colors, file_rows, at_ref, x_ref, one_ref, two_ref, wk_ref, wh_ref, vec_ref, norm_ref,
@@ -327,13 +346,13 @@
     half = per // 2
     chunks = wh_ref.shape[1] // (per * LANES)
     bias, gain, offset = per_row(vec_ref, 0), per_row(vec_ref, 1), per_row(vec_ref, 2)
-    no_top, no_bot = at_ref[2], at_ref[3]
-    no_left, no_right = at_ref[4], at_ref[5]
+    no_top, no_bot = at_ref[2, 0], at_ref[3, 0]
+    no_left, no_right = at_ref[4, 0], at_ref[5, 0]
     shape = (channels, GROUP, width)
     lower = iota(shape, 1) < 4
     row_ok = jnp.where(lower, 1 - no_bot, 1 - no_top) > 0
 
-    even = at_ref[6] == 0
+    even = at_ref[6, 0] == 0
     one, two = one_ref[...], two_ref[...]
     top, bot = jnp.where(even, two, one), jnp.where(even, one, two)
     outer = [bot[a] for a in range(half)] + [top[a] for a in range(half)]
@@ -405,7 +424,7 @@
 def kernel_call(body, out_shape, us, *args, loose=(), **kw):
     loose = tuple(loose) + tuple(kw.get("input_output_aliases", {}))
     args = [
-        arg if n in loose or arg.dtype == jnp.int32 else pltpu.with_memory_space_constraint(arg, pltpu.VMEM)
+        arg if n in loose else pltpu.with_memory_space_constraint(arg, pltpu.VMEM)
         for n, arg in enumerate(args)
     ]
     return pl.pallas_call(
@@ -455,9 +474,9 @@
     row_at, col_at = lax.axis_index("rows"), lax.axis_index("cols")
     chips = n_cols // 2
     at = jnp.stack([
-        col_at % 2, col_at // 2, row_at == 0, row_at == n_rows - 1, col_at == 0, col_at == n_cols - 1, row_at % 2,
+        col_at % 2, col_at // 2, row_at == 0, row_at == n_rows - 1, col_at == 0, col_at == n_cols - 1, row_at % 2, 0,
     ]).astype(jnp.int32)
-    smem = pl.BlockSpec(memory_space=pltpu.SMEM)
+    at = jnp.broadcast_to(at[:, None], (8, LANES))
     vmem = pl.BlockSpec(memory_space=pltpu.VMEM)
     edge_rows = channels * height // 16
 
@@ -468,15 +487,16 @@
             in_vmem(tile, bf16),
             in_vmem((chips, block_rows, LANES), bf16),
             in_vmem((chips * block_rows + edge_rows, LANES), bf16),
-            in_vmem((edge_rows, LANES), bf16),
+            in_vmem((edge_rows + 48, LANES), bf16),
         ),
         2,
         at, *(pltpu.with_memory_space_constraint(arg, pltpu.HBM) for arg in (file_pixels, cotangent)),
         loose=(1, 2),
-        in_specs=[smem] + [beyond] * 2,
+        in_specs=[vmem] + [beyond] * 2,
         scratch_shapes=[
             pltpu.VMEM((n_cols + 2, 16, block), f32),
             pltpu.VMEM(file_pixels.shape, bf16),
+            pltpu.VMEM((block, n_cols * LANES), bf16),
             pltpu.SemaphoreType.DMA((2,)),
         ],
     )
@@ -492,10 +512,10 @@
     pairs[0] = kept
     beside, *strips = kernel_call(
         strips_kernel,
-        (in_vmem(tile, bf16), in_vmem((channels, 8, width), bf16), in_vmem((channels, 8, width), bf16)),
-        1,
+        (in_vmem(tile, bf16), in_vmem((channels + channels // 16, 4, width), bf16), in_vmem((channels + channels // 16, 4, width), bf16)),
+        0.01,
         at, cot, got, far,
-        in_specs=[smem] + [vmem] * 3,
+        in_specs=[vmem] + [vmem] * 3,
     )
     beside, taps = lax.optimization_barrier((beside, kernel))
     strips = swap(strips, "rows")
@@ -508,78 +528,80 @@
             in_vmem((channels, DEPTH), f32),
             in_vmem((4, channels, LANES), f32),
         ),
-        1.5,
+        0.01,
         patchify_weight.T, taps.T, patchify_bias, norm_gain, norm_offset_vector, kernel_offset,
         const["spread"], const["keep"], const["spread_halo"], const["keep_halo"], const["tall"],
         const["forward"], const["backward"],
     )
-    cot_all, cot_halo, grad, sums = kernel_call(
+    flipped, grad, totals = kernel_call(
         functools.partial(back_kernel, factor),
-        (in_vmem(tall, bf16), in_vmem(tall, bf16), in_vmem(tile, f32), in_vmem((2, channels, GROUP, width), f32)),
-        5,
+        (in_vmem((channels, width, DEPTH), bf16), in_vmem(tile, f32), in_vmem((2, channels, width), f32)),
+        0.01,
         at, cot, beside, *strips, kb,
-        in_specs=[smem] + [vmem] * 5,
+        scratch_shapes=[
+            pltpu.VMEM(tall, bf16),
+            pltpu.VMEM(tall, bf16),
+            pltpu.VMEM((2, channels, GROUP, width), f32),
+        ],
     )
 
     half = per // 2
+    grad, *pairs = lax.optimization_barrier((grad, *pairs))
     pixels, *ends = kernel_call(
         order_kernel,
         (in_vmem((n_cols, block_rows, LANES), bf16),) + (in_vmem((half, block_rows, LANES), bf16),) * 2,
-        0.5,
+        0.01,
         at, *pairs,
-        in_specs=[smem] + [vmem] * chips,
-    )
-    ends = swap(ends, "rows")
+        in_specs=[vmem] + [vmem] * chips,
+    )
     norm, result = kernel_call(
         functools.partial(main_kernel, colors, file_rows, factor),
         (in_vmem(tile, bf16), in_vmem((56, LANES), f32)),
         6,
-        pixels, wk, vec, grad, sums, cot_all, cot_halo,
-        const["taps"], const["gather"], const["diagonal"], const["fold"], const["pick"],
+        pixels, wk, vec, grad, totals, flipped, const["taps"], const["pick"],
         scratch_shapes=[
             pltpu.VMEM(tile, f32),
-            pltpu.VMEM((per * block + 16, rows), f32),
+            pltpu.VMEM((height // GROUP, rows, width), f32),
             pltpu.VMEM((channels, 8, DEPTH), f32),
         ],
     )
 
     size = n_rows * n_cols
-    chunk = channels // 4
-    jobs = ["halo"] + list(range(0, channels, chunk))
+    chunk = channels // 2
+    rounds = (size - 1).bit_length()
+    jobs = {0: ["one"], 1: ["two"], 2: ["halo"], 3: [0], rounds - 1: [chunk]}
     stem_output = None
-    rounds = (size - 1).bit_length()
     for n in range(rounds):
         step = 1 if n == 0 else (1 << n) + 1
         other = lax.ppermute(result, ("rows", "cols"), [(i, i ^ step) for i in range(size)])
-        final = n == rounds - 1
-        if n > 0:
-            for job in jobs if final else jobs[:1]:
-                if job == "halo":
-                    result, norm = lax.optimization_barrier((result, norm))
-                    norm_all, norm_halo = kernel_call(
-                        functools.partial(stem_halo_kernel, colors, file_rows),
-                        (in_vmem(tall, bf16), in_vmem(tall, bf16)),
-                        2,
-                        at, pixels, *ends, wk, wh, vec, norm,
-                        in_specs=[smem] + [vmem] * 7,
-                    )
-                    result, norm_all = lax.optimization_barrier((result, norm_all))
-                else:
-                    result, norm_all = lax.optimization_barrier((result, norm_all))
-                    before = () if stem_output is None else (stem_output,)
-                    stem_output = kernel_call(
-                        functools.partial(stem_kernel, job),
-                        shaped(tile, bf16),
-                        1.5,
-                        norm_all, norm_halo, kf, vec, *before,
-                        in_specs=[vmem] * 4 + [beyond] * len(before),
-                        out_specs=beyond,
-                        input_output_aliases={4: 0} if before else {},
-                        scratch_shapes=[pltpu.VMEM((chunk, height, width), bf16), pltpu.SemaphoreType.DMA],
-                    )
-                    result, stem_output = lax.optimization_barrier((result, stem_output))
-            jobs = [] if final else jobs[1:]
-        if not final:
+        for job in jobs.get(n, []):
+            if job in ("one", "two"):
+                which = ("one", "two").index(job)
+                result, end = lax.optimization_barrier((result, ends[which]))
+                ends[which] = lax.ppermute(end, "rows", pairing(n_rows, which))
+            elif job == "halo":
+                result, norm = lax.optimization_barrier((result, norm))
+                norm_all, norm_halo = kernel_call(
+                    functools.partial(stem_halo_kernel, colors, file_rows),
+                    (in_vmem(tall, bf16), in_vmem(tall, bf16)),
+                    2,
+                    at, pixels, *ends, wk, wh, vec, norm,
+                )
+            else:
+                result, norm_all = lax.optimization_barrier((result, norm_all))
+                before = () if stem_output is None else (stem_output,)
+                stem_output = kernel_call(
+                    functools.partial(stem_kernel, job),
+                    shaped(tile, bf16),
+                    1.5,
+                    norm_all, norm_halo, kf, vec, *before,
+                    in_specs=[vmem] * 4 + [beyond] * len(before),
+                    out_specs=beyond,
+                    input_output_aliases={4: 0} if before else {},
+                    scratch_shapes=[pltpu.VMEM((chunk, height, width), bf16), pltpu.SemaphoreType.DMA],
+                )
+                result, stem_output = lax.optimization_barrier((result, stem_output))
+        if n < rounds - 1:
             result = result + other
 
     taps = side * side

time: 57.7 us -> 48.2 us (0.84)
  Pallas kernels: 24.2 us -> 18.7 us
  starting transfers between devices: 20.1 us -> 17.7 us
  waiting for transfers between devices: 11.4 us -> 10.4 us
    ppermute x3, waiting for transfers between devices: 5.91 us -> 0.01 us  [per_device(): lax.ppermute(pairs[n], 'cols', [(i, (i + 2 * n) % n_cols) for i in range(...]
    pallas_call x13 -> x11, Pallas kernels: 24.2 us -> 18.7 us  [kernel_call(): pl.pallas_call(body, out_shape=out_shape, compiler_params=pltpu.CompilerP...]
    ppermute x5, waiting for transfers between devices: 3.84 us -> 7.63 us  [per_device(): lax.ppermute(result, ('rows', 'cols'), [(i, i ^ step) for i in range(size)])]
    ppermute x5, starting transfers between devices: 5.99 us -> 2.79 us  [per_device(): lax.ppermute(result, ('rows', 'cols'), [(i, i ^ step) for i in range(size)])]
    ppermute x0 -> x2, starting transfers between devices: none -> 2.81 us  [per_device(): ends[which] = lax.ppermute(end, 'rows', pairing(n_rows, which))]
    ppermute x4 -> x2, waiting for transfers between devices: 0.01 us -> 2.76 us  [swap(): lax.ppermute(part, axis, pairing(lax.axis_size(axis), n))]
    ppermute x4 -> x2, starting transfers between devices: 5.08 us -> 3 us  [swap(): lax.ppermute(part, axis, pairing(lax.axis_size(axis), n))]
    ppermute x1, waiting for transfers between devices: 1.64 us -> 0.01 us  [per_device(): far = lax.ppermute(edges, 'cols', pairing(n_cols, 1))]
  transfers between devices with their start and end apart: 14 -> 14, of which waited for: 8 -> 7; matrix products, arithmetic and copies ran while one was open for 0% -> 0% of each run, Pallas kernels for 35% -> 24%
where the time goes in v3:
time: 48.2 us; the launch traced here: 48.1 us
  Pallas kernels  18.7 us (39%)
  starting transfers between devices  17.7 us (37%)
  waiting for transfers between devices  10.4 us (22%)
  between operations  0.98 us (2%)
    pallas_call x11, Pallas kernels, kernel_call(): pl.pallas_call(body, out_shape=out_shape, compiler_params=pltpu.CompilerP...  18.7 us
    ppermute x5, waiting for transfers between devices, per_device(): lax.ppermute(result, ('rows', 'cols'), [(i, i ^ step) for i in range(size)])  7.63 us
    ppermute x1, starting transfers between devices, per_device(): far = lax.ppermute(edges, 'cols', pairing(n_cols, 1))  4.71 us
    ppermute x3, starting transfers between devices, per_device(): lax.ppermute(pairs[n], 'cols', [(i, (i + 2 * n) % n_cols) for i in range(...  3.87 us
    ppermute x2, starting transfers between devices, swap(): lax.ppermute(part, axis, pairing(lax.axis_size(axis), n))  3 us
    ppermute x2, starting transfers between devices, per_device(): ends[which] = lax.ppermute(end, 'rows', pairing(n_rows, which))  2.81 us
    ppermute x5, starting transfers between devices, per_device(): lax.ppermute(result, ('rows', 'cols'), [(i, i ^ step) for i in range(size)])  2.79 us
    ppermute x2, waiting for transfers between devices, swap(): lax.ppermute(part, axis, pairing(lax.axis_size(axis), n))  2.76 us
  transfers between devices with their start and end apart: 14, of which 7 were waited for; matrix products, arithmetic and copies ran while one was open for 0% of the time, Pallas kernels for 24%

profile of v3, /device:TPU:0, one launch (start us, length us, event | category | flops | bytes accessed | tf_op | source)
XLA Modules:
  0.0 48.1 jit_solution(9422687556080788668)
XLA Ops:
  1.0 2.2 %shard_map.216 = (bf16[64,32,128]{2,1,0:T(8,128)(2,1)S(1)}, bf16[4,208,128]{2,1,0:T(8,128)(2,1)S(1)}, bf16[960,128]{1,0:T(8,128)(2,1)S(1)}, bf16[176,128]{1,0:T(8,128)(2,1)S(1)}) custom-call(s32[8,128]{1,0:T(8,128)S(1)} %broadcast_in_dim.2.at_ref, bf16[48,4,1024]{2,1,0:T(4,128)(2,1)} %x_hbm.1, bf16[64,32,128]{2,1,0:T(8,128)(2,1)} %cot_hbm.1), custom_call_target="tpu_custom_call" | custom-call | flops 2000000000 | bytes 6000000 | tf_op jit(solution)/shard_map/pallas_call | solution.py:430
  3.1 0.5 %collective-permute-start = (bf16[960,128]{1,0:T(8,128)(2,1)S(1)}, bf16[960,128]{1,0:T(8,128)(2,1)S(1)}, u32[]{:S(2)}, u32[]{:S(2)}) collective-permute-start(bf16[960,128]{1,0:T(8,128)(2,1)S(1)} %get-tuple-element.63), channel_id=1, source_target_pairs={{0,1},{1,0},{2,3},{3,2},{4,5},{5,4},{6,7},{7,6},{8,9},{9,8},{10,11... | collective-permute-start | bytes 737288 | tf_op jit(solution)/shard_map/ppermute | solution.py:503
  3.7 4.7 %collective-permute-start.1 = (bf16[176,128]{1,0:T(8,128)(2,1)S(1)}, bf16[176,128]{1,0:T(8,128)(2,1)S(1)}, u32[]{:S(2)}, u32[]{:S(2)}) collective-permute-start(bf16[176,128]{1,0:T(8,128)(2,1)S(1)} %get-tuple-element.66), channel_id=1, source_target_pairs={{0,7},{1,2},{2,1},{3,4},{4,3},{5,6},{6,5},{7,0},{8,15},{9,10},{10,... | collective-permute-start | bytes 135176 | tf_op jit(solution)/shard_map/ppermute | solution.py:504
  8.5 1.9 %collective-permute-start.5 = (bf16[2,208,128]{2,1,0:T(8,128)(2,1)S(1)}, bf16[2,208,128]{2,1,0:T(8,128)(2,1)S(1)}, u32[]{:S(2)}, u32[]{:S(2)}) collective-permute-start(bf16[2,208,128]{2,1,0:T(8,128)(2,1)S(1)} %get-tuple-element.77), channel_id=1, source_target_pairs={{0,4},{1,5},{2,6},{3,7},{4,0},{5,1},{6,2},{7,3},{8,12},{9,13},{10,... | collective-permute-start | bytes 319496 | tf_op jit(solution)/shard_map/ppermute | solution.py:507
  10.4 1.9 %collective-permute-start.6 = (bf16[2,208,128]{2,1,0:T(8,128)(2,1)S(1)}, bf16[2,208,128]{2,1,0:T(8,128)(2,1)S(1)}, u32[]{:S(2)}, u32[]{:S(2)}) collective-permute-start(bf16[2,208,128]{2,1,0:T(8,128)(2,1)S(1)} %get-tuple-element.78), channel_id=1, source_target_pairs={{0,6},{1,7},{2,0},{3,1},{4,2},{5,3},{6,4},{7,5},{8,14},{9,15},{10,... | collective-permute-start | bytes 319496 | tf_op jit(solution)/shard_map/ppermute | solution.py:507
  12.3 0.7 %shard_map.218 = (bf16[64,32,128]{2,1,0:T(8,128)(2,1)S(1)}, bf16[68,4,128]{2,1,0:T(4,128)(2,1)S(1)}, bf16[68,4,128]{2,1,0:T(4,128)(2,1)S(1)}) custom-call(s32[8,128]{1,0:T(8,128)S(1)} %broadcast_in_dim.2.at_ref, bf16[64,32,128]{2,1,0:T(8,128)(2,1)S(1)} %get-tuple-element.62.cot_ref, bf16[960,128]{1,0:T(8,128)(2,1)S(1)} %collective-permute-done.got_ref.near_ref, ...), custom_call_target="tpu_custom_call" | custom-call | flops 10000000 | bytes 30000 | tf_op jit(solution)/shard_map/pallas_call | solution.py:430
  13.0 1.5 %collective-permute-start.2 = (bf16[68,4,128]{2,1,0:T(4,128)(2,1)S(1)}, bf16[68,4,128]{2,1,0:T(4,128)(2,1)S(1)}, u32[]{:S(2)}, u32[]{:S(2)}) collective-permute-start(bf16[68,4,128]{2,1,0:T(4,128)(2,1)S(1)} %get-tuple-element.70), channel_id=1, source_target_pairs={{0,8},{8,0},{16,24},{24,16},{1,9},{9,1},{17,25},{25,17},{2,10},{10... | collective-permute-start | bytes 208904 | tf_op jit(solution)/shard_map/ppermute | solution.py:448
  14.5 1.5 %collective-permute-start.3 = (bf16[68,4,128]{2,1,0:T(4,128)(2,1)S(1)}, bf16[68,4,128]{2,1,0:T(4,128)(2,1)S(1)}, u32[]{:S(2)}, u32[]{:S(2)}) collective-permute-start(bf16[68,4,128]{2,1,0:T(4,128)(2,1)S(1)} %get-tuple-element.71), channel_id=1, source_target_pairs={{0,24},{8,16},{16,8},{24,0},{1,25},{9,17},{17,9},{25,1},{2,26},{10... | collective-permute-start | bytes 208904 | tf_op jit(solution)/shard_map/ppermute | solution.py:448
  16.1 0.9 %shard_map.219 = (bf16[512,384]{1,0:T(8,128)(2,1)S(1)}, bf16[512,512]{1,0:T(8,128)(2,1)S(1)}, f32[64,384]{1,0:T(8,128)S(1)}, f32[64,384]{1,0:T(8,128)S(1)}, f32[4,64,128]{2,1,0:T(8,128)S(1)}) custom-call(bf16[48,64]{1,0:T(8,128)(2,1)S(1)} %bitcast.12, f32[49,64]{1,0:T(8,128)S(1)} %bitcast.11, f32[64]{0:T(128)S(1)} %copy-done.9, f32[64]{0:T(128)S(1)} %copy-done.10, ...), custom_call_target="tpu_custom_call" | custom-call | flops 10000000 | bytes 30000 | tf_op jit(solution)/shard_map/pallas_call | solution.py:430
  17.0 1.0 %collective-permute-done.2.one_ref = bf16[68,4,128]{2,1,0:T(4,128)(2,1)S(1)} collective-permute-done((bf16[68,4,128]{2,1,0:T(4,128)(2,1)S(1)}, bf16[68,4,128]{2,1,0:T(4,128)(2,1)S(1)}, u32[]{:S(2)}, u32[]{:S(2)}) %collective-permute-start.2) | collective-permute-done | bytes 69664 | tf_op jit(solution)/shard_map/ppermute | solution.py:448
  18.0 1.7 %collective-permute-done.3.two_ref = bf16[68,4,128]{2,1,0:T(4,128)(2,1)S(1)} collective-permute-done((bf16[68,4,128]{2,1,0:T(4,128)(2,1)S(1)}, bf16[68,4,128]{2,1,0:T(4,128)(2,1)S(1)}, u32[]{:S(2)}, u32[]{:S(2)}) %collective-permute-start.3) | collective-permute-done | bytes 69664 | tf_op jit(solution)/shard_map/ppermute | solution.py:448
  19.7 4.7 %shard_map.220 = (bf16[64,128,384]{2,1,0:T(8,128)(2,1)S(1)}, f32[64,32,128]{2,1,0:T(8,128)S(1)}, f32[2,64,128]{2,1,0:T(8,128)S(1)}) custom-call(s32[8,128]{1,0:T(8,128)S(1)} %broadcast_in_dim.2.at_ref, bf16[64,32,128]{2,1,0:T(8,128)(2,1)S(1)} %get-tuple-element.62.cot_ref, bf16[64,32,128]{2,1,0:T(8,128)(2,1)S(1)} %get-tuple-element.69.beside_ref, ...), custom_call_target="tpu_custom_call" | custom-call | flops 10000000 | bytes 30000 | tf_op jit(solution)/shard_map/pallas_call | solution.py:430
  24.6 4.4 %shard_map.222 = (bf16[64,32,128]{2,1,0:T(8,128)(2,1)S(1)}, f32[56,128]{1,0:T(8,128)S(1)}) custom-call(bf16[8,208,128]{2,1,0:T(8,128)(2,1)S(1)} %get-tuple-element.83.x_ref, bf16[512,384]{1,0:T(8,128)(2,1)S(1)} %get-tuple-element.84.wk_ref, f32[4,64,128]{2,1,0:T(8,128)S(1)} %get-tuple-element.85.vec_ref.refs_3_, ...), custom_call_target="tpu_custom_call" | custom-call | flops 6000000000 | bytes 18000000 | tf_op jit(solution)/shard_map/pallas_call | solution.py:430
  29.0 0.9 %collective-permute-start.10 = (bf16[1,208,128]{2,1,0:T(8,128)(2,1)S(1)}, bf16[1,208,128]{2,1,0:T(8,128)(2,1)S(1)}, u32[]{:S(2)}, u32[]{:S(2)}) collective-permute-start(bf16[1,208,128]{2,1,0:T(8,128)(2,1)S(1)} %get-tuple-element.96), channel_id=1, source_target_pairs={{0,8},{8,0},{16,24},{24,16},{1,9},{9,1},{17,25},{25,17},{2,10},{10... | collective-permute-start | bytes 159752 | tf_op jit(solution)/shard_map/ppermute | solution.py:581
  30.2 1.9 %collective-permute-start.11 = (bf16[1,208,128]{2,1,0:T(8,128)(2,1)S(1)}, bf16[1,208,128]{2,1,0:T(8,128)(2,1)S(1)}, u32[]{:S(2)}, u32[]{:S(2)}) collective-permute-start(bf16[1,208,128]{2,1,0:T(8,128)(2,1)S(1)} %get-tuple-element.97), channel_id=1, source_target_pairs={{0,24},{8,16},{16,8},{24,0},{1,25},{9,17},{17,9},{25,1},{2,26},{10... | collective-permute-start | bytes 159752 | tf_op jit(solution)/shard_map/ppermute | solution.py:581
  32.2 3.5 %collective-permute-done.8 = f32[56,128]{1,0:T(8,128)S(1)} collective-permute-done((f32[56,128]{1,0:T(8,128)S(1)}, f32[56,128]{1,0:T(8,128)S(1)}, u32[]{:S(2)}, u32[]{:S(2)}) %collective-permute-start.8) | collective-permute-done | bytes 28704 | tf_op jit(solution)/shard_map/ppermute | solution.py:576
  35.7 1.7 %collective-permute-start.9 = (f32[56,128]{1,0:T(8,128)S(1)}, f32[56,128]{1,0:T(8,128)S(1)}, u32[]{:S(2)}, u32[]{:S(2)}) collective-permute-start(f32[56,128]{1,0:T(8,128)S(1)} %add.23), channel_id=1, source_target_pairs={{0,5},{1,4},{2,7},{3,6},{4,1},{5,0},{6,3},{7,2},{8,13},{9,12},{10,... | collective-permute-start | bytes 86024 | tf_op jit(solution)/shard_map/ppermute | solution.py:576
  37.4 0.9 %shard_map.223 = (bf16[64,48,128]{2,1,0:T(8,128)(2,1)S(1)}, bf16[64,48,128]{2,1,0:T(8,128)(2,1)S(1)}) custom-call(s32[8,128]{1,0:T(8,128)S(1)} %broadcast_in_dim.2.at_ref, bf16[8,208,128]{2,1,0:T(8,128)(2,1)S(1)} %get-tuple-element.83.x_ref, bf16[1,208,128]{2,1,0:T(8,128)(2,1)S(1)} %collective-permute-done.10.one_ref, ...), custom_call_target="tpu_custom_call" | custom-call | flops 2000000000 | bytes 6000000 | tf_op jit(solution)/shard_map/pallas_call | solution.py:430
  38.4 2.4 %collective-permute-done.9 = f32[56,128]{1,0:T(8,128)S(1)} collective-permute-done((f32[56,128]{1,0:T(8,128)S(1)}, f32[56,128]{1,0:T(8,128)S(1)}, u32[]{:S(2)}, u32[]{:S(2)}) %collective-permute-start.9) | collective-permute-done | bytes 28704 | tf_op jit(solution)/shard_map/ppermute | solution.py:576
  40.8 0.8 %collective-permute-start.12 = (f32[56,128]{1,0:T(8,128)S(1)}, f32[56,128]{1,0:T(8,128)S(1)}, u32[]{:S(2)}, u32[]{:S(2)}) collective-permute-start(f32[56,128]{1,0:T(8,128)S(1)} %add.24), channel_id=1, source_target_pairs={{0,9},{1,8},{2,11},{3,10},{4,13},{5,12},{6,15},{7,14},{8,1},{9,0},... | collective-permute-start | bytes 86024 | tf_op jit(solution)/shard_map/ppermute | solution.py:576
  41.6 2.1 %shard_map.224.refs_4_ = bf16[64,32,128]{2,1,0:T(8,128)(2,1)} custom-call(bf16[64,48,128]{2,1,0:T(8,128)(2,1)S(1)} %get-tuple-element.107.refs_0_, bf16[64,48,128]{2,1,0:T(8,128)(2,1)S(1)} %get-tuple-element.103.refs_1_, f32[64,384]{1,0:T(8,128)S(1)} %get-tuple-element.104.refs_2_, f32[4,64,128]{2,1,0:T(8,128)S(1)} %get-tuple-element.85.vec_ref.refs_3_), custom_call_target="tpu_custom_call" | custom-call | flops 1500000000 | bytes 4500000 | tf_op jit(solution)/shard_map/pallas_call | solution.py:430
  44.2 2.1 %shard_map.225 = bf16[64,32,128]{2,1,0:T(8,128)(2,1)} custom-call(bf16[64,48,128]{2,1,0:T(8,128)(2,1)S(1)} %get-tuple-element.107.refs_0_, bf16[64,48,128]{2,1,0:T(8,128)(2,1)S(1)} %get-tuple-element.103.refs_1_, f32[64,384]{1,0:T(8,128)S(1)} %get-tuple-element.104.refs_2_, ...), custom_call_target="tpu_custom_call", output_to_operand_aliasing={{}: (4, {})} | custom-call | flops 1500000000 | bytes 4500000 | tf_op jit(solution)/shard_map/pallas_call | solution.py:430
  46.4 1.0 %collective-permute-done.13.y_ref = f32[56,128]{1,0:T(8,128)S(1)} collective-permute-done((f32[56,128]{1,0:T(8,128)S(1)}, f32[56,128]{1,0:T(8,128)S(1)}, u32[]{:S(2)}, u32[]{:S(2)}) %collective-permute-start.13) | collective-permute-done | bytes 28704 | tf_op jit(solution)/shard_map/ppermute | solution.py:576
  47.4 0.7 %shard_map.226 = (f32[48,64]{1,0:T(8,128)}, f32[64]{0:T(128)}, f32[64]{0:T(128)}, f32[64]{0:T(128)}, f32[64]{0:T(128)}, /*index=5*/f32[49,64]{1,0:T(8,128)}) custom-call(f32[56,128]{1,0:T(8,128)S(1)} %add.25.x_ref, f32[56,128]{1,0:T(8,128)S(1)} %collective-permute-done.13.y_ref), custom_call_target="tpu_custom_call" | custom-call | flops 1000000000 | bytes 3000000 | tf_op jit(solution)/shard_map/pallas_call | solution.py:430
  (51 shorter events, 1.5 us)
Async XLA Ops:
  0.6 15.4 %copy-start.3 = (f32[49,384]{1,0:T(8,128)S(1)}, f32[49,384]{1,0:T(8,128)}, u32[]{:S(2)}) copy-start(f32[49,384]{1,0:T(8,128)} %constant.67.clone.backward_ref) | copy-start | bytes 225796
  0.6 15.4 %copy-start.4 = (f32[49,384]{1,0:T(8,128)S(1)}, f32[49,384]{1,0:T(8,128)}, u32[]{:S(2)}) copy-start(f32[49,384]{1,0:T(8,128)} %constant.66.clone.forward_ref) | copy-start | bytes 225796
  0.7 15.4 %copy-start.2 = (bf16[512,64]{1,0:T(8,128)(2,1)S(1)}, bf16[512,64]{1,0:T(8,128)(2,1)}, u32[]{:S(2)}) copy-start(bf16[512,64]{1,0:T(8,128)(2,1)} %constant.65.clone.tall_ref) | copy-start | bytes 196612
  0.7 15.4 %copy-start = (bf16[512,512]{1,0:T(8,128)(2,1)S(1)}, bf16[512,512]{1,0:T(8,128)(2,1)}, u32[]{:S(2)}) copy-start(bf16[512,512]{1,0:T(8,128)(2,1)} %constant.64.clone.keep_h_ref) | copy-start | bytes 1572868
  0.7 15.4 %copy-start.5 = (bf16[48,512]{1,0:T(8,128)(2,1)S(1)}, bf16[48,512]{1,0:T(8,128)(2,1)}, u32[]{:S(2)}) copy-start(bf16[48,512]{1,0:T(8,128)(2,1)} %constant.63.clone.spread_h_ref) | copy-start | bytes 147460
  0.7 15.4 %copy-start.1 = (bf16[512,384]{1,0:T(8,128)(2,1)S(1)}, bf16[512,384]{1,0:T(8,128)(2,1)}, u32[]{:S(2)}) copy-start(bf16[512,384]{1,0:T(8,128)(2,1)} %constant.62.clone.keep_ref) | copy-start | bytes 1179652
  0.7 15.4 %copy-start.6 = (bf16[48,384]{1,0:T(8,128)(2,1)S(1)}, bf16[48,384]{1,0:T(8,128)(2,1)}, u32[]{:S(2)}) copy-start(bf16[48,384]{1,0:T(8,128)(2,1)} %constant.61.clone.spread_ref) | copy-start | bytes 110596
  0.7 15.4 %copy-start.7 = (f32[64,49]{0,1:T(8,128)S(1)}, f32[64,49]{0,1:T(8,128)}, u32[]{:S(2)}) copy-start(f32[64,49]{0,1:T(8,128)} %param.22) | copy-start | bytes 37636
  1.0 23.6 %copy-start.13 = (bf16[56,384]{1,0:T(8,128)(2,1)S(1)}, bf16[56,384]{1,0:T(8,128)(2,1)}, u32[]{:S(2)}) copy-start(bf16[56,384]{1,0:T(8,128)(2,1)} %constant.69.clone.pick_ref) | copy-start | bytes 129028
  1.0 23.6 %copy-start.14 = (bf16[56,384]{1,0:T(8,128)(2,1)S(1)}, bf16[56,384]{1,0:T(8,128)(2,1)}, u32[]{:S(2)}) copy-start(bf16[56,384]{1,0:T(8,128)(2,1)} %constant.68.clone.taps_ref) | copy-start | bytes 129028
  3.1 5.2 %collective-permute-start = (bf16[960,128]{1,0:T(8,128)(2,1)S(1)}, bf16[960,128]{1,0:T(8,128)(2,1)S(1)}, u32[]{:S(2)}, u32[]{:S(2)}) collective-permute-start(bf16[960,128]{1,0:T(8,128)(2,1)S(1)} %get-tuple-element.63), channel_id=1, source_target_pairs={{0,1},{1,0},{2,3},{3,2},{4,5},{5,4},{6,7},{7,6},{8,9},{9,8},{10,11... | collective-permute-start | bytes 737288 | tf_op jit(solution)/shard_map/ppermute | solution.py:503
  3.7 8.6 %collective-permute-start.1 = (bf16[176,128]{1,0:T(8,128)(2,1)S(1)}, bf16[176,128]{1,0:T(8,128)(2,1)S(1)}, u32[]{:S(2)}, u32[]{:S(2)}) collective-permute-start(bf16[176,128]{1,0:T(8,128)(2,1)S(1)} %get-tuple-element.66), channel_id=1, source_target_pairs={{0,7},{1,2},{2,1},{3,4},{4,3},{5,6},{6,5},{7,0},{8,15},{9,10},{10,... | collective-permute-start | bytes 135176 | tf_op jit(solution)/shard_map/ppermute | solution.py:504
  8.4 16.0 %collective-permute-start.4 = (bf16[2,208,128]{2,1,0:T(8,128)(2,1)S(1)}, bf16[2,208,128]{2,1,0:T(8,128)(2,1)S(1)}, u32[]{:S(2)}, u32[]{:S(2)}) collective-permute-start(bf16[2,208,128]{2,1,0:T(8,128)(2,1)S(1)} %get-tuple-element.76), channel_id=1, source_target_pairs={{0,2},{1,3},{2,4},{3,5},{4,6},{5,7},{6,0},{7,1},{8,10},{9,11},{10,... | collective-permute-start | bytes 319496 | tf_op jit(solution)/shard_map/ppermute | solution.py:507
  8.5 16.0 %collective-permute-start.5 = (bf16[2,208,128]{2,1,0:T(8,128)(2,1)S(1)}, bf16[2,208,128]{2,1,0:T(8,128)(2,1)S(1)}, u32[]{:S(2)}, u32[]{:S(2)}) collective-permute-start(bf16[2,208,128]{2,1,0:T(8,128)(2,1)S(1)} %get-tuple-element.77), channel_id=1, source_target_pairs={{0,4},{1,5},{2,6},{3,7},{4,0},{5,1},{6,2},{7,3},{8,12},{9,13},{10,... | collective-permute-start | bytes 319496 | tf_op jit(solution)/shard_map/ppermute | solution.py:507
  10.4 14.0 %collective-permute-start.6 = (bf16[2,208,128]{2,1,0:T(8,128)(2,1)S(1)}, bf16[2,208,128]{2,1,0:T(8,128)(2,1)S(1)}, u32[]{:S(2)}, u32[]{:S(2)}) collective-permute-start(bf16[2,208,128]{2,1,0:T(8,128)(2,1)S(1)} %get-tuple-element.78), channel_id=1, source_target_pairs={{0,6},{1,7},{2,0},{3,1},{4,2},{5,3},{6,4},{7,5},{8,14},{9,15},{10,... | collective-permute-start | bytes 319496 | tf_op jit(solution)/shard_map/ppermute | solution.py:507
  13.0 5.0 %collective-permute-start.2 = (bf16[68,4,128]{2,1,0:T(4,128)(2,1)S(1)}, bf16[68,4,128]{2,1,0:T(4,128)(2,1)S(1)}, u32[]{:S(2)}, u32[]{:S(2)}) collective-permute-start(bf16[68,4,128]{2,1,0:T(4,128)(2,1)S(1)} %get-tuple-element.70), channel_id=1, source_target_pairs={{0,8},{8,0},{16,24},{24,16},{1,9},{9,1},{17,25},{25,17},{2,10},{10... | collective-permute-start | bytes 208904 | tf_op jit(solution)/shard_map/ppermute | solution.py:448
  14.5 5.2 %collective-permute-start.3 = (bf16[68,4,128]{2,1,0:T(4,128)(2,1)S(1)}, bf16[68,4,128]{2,1,0:T(4,128)(2,1)S(1)}, u32[]{:S(2)}, u32[]{:S(2)}) collective-permute-start(bf16[68,4,128]{2,1,0:T(4,128)(2,1)S(1)} %get-tuple-element.71), channel_id=1, source_target_pairs={{0,24},{8,16},{16,8},{24,0},{1,25},{9,17},{17,9},{25,1},{2,26},{10... | collective-permute-start | bytes 208904 | tf_op jit(solution)/shard_map/ppermute | solution.py:448
  28.9 1.3 %collective-permute-start.7 = (f32[56,128]{1,0:T(8,128)S(1)}, f32[56,128]{1,0:T(8,128)S(1)}, u32[]{:S(2)}, u32[]{:S(2)}) collective-permute-start(f32[56,128]{1,0:T(8,128)S(1)} %get-tuple-element.91), channel_id=1, source_target_pairs={{0,1},{1,0},{2,3},{3,2},{4,5},{5,4},{6,7},{7,6},{8,9},{9,8},{10,11... | collective-permute-start | bytes 86024 | tf_op jit(solution)/shard_map/ppermute | solution.py:576
  29.0 8.4 %collective-permute-start.10 = (bf16[1,208,128]{2,1,0:T(8,128)(2,1)S(1)}, bf16[1,208,128]{2,1,0:T(8,128)(2,1)S(1)}, u32[]{:S(2)}, u32[]{:S(2)}) collective-permute-start(bf16[1,208,128]{2,1,0:T(8,128)(2,1)S(1)} %get-tuple-element.96), channel_id=1, source_target_pairs={{0,8},{8,0},{16,24},{24,16},{1,9},{9,1},{17,25},{25,17},{2,10},{10... | collective-permute-start | bytes 159752 | tf_op jit(solution)/shard_map/ppermute | solution.py:581
  30.2 7.2 %collective-permute-start.11 = (bf16[1,208,128]{2,1,0:T(8,128)(2,1)S(1)}, bf16[1,208,128]{2,1,0:T(8,128)(2,1)S(1)}, u32[]{:S(2)}, u32[]{:S(2)}) collective-permute-start(bf16[1,208,128]{2,1,0:T(8,128)(2,1)S(1)} %get-tuple-element.97), channel_id=1, source_target_pairs={{0,24},{8,16},{16,8},{24,0},{1,25},{9,17},{17,9},{25,1},{2,26},{10... | collective-permute-start | bytes 159752 | tf_op jit(solution)/shard_map/ppermute | solution.py:581
  32.1 3.5 %collective-permute-start.8 = (f32[56,128]{1,0:T(8,128)S(1)}, f32[56,128]{1,0:T(8,128)S(1)}, u32[]{:S(2)}, u32[]{:S(2)}) collective-permute-start(f32[56,128]{1,0:T(8,128)S(1)} %add.22), channel_id=1, source_target_pairs={{0,3},{1,2},{2,1},{3,0},{4,7},{5,6},{6,5},{7,4},{8,11},{9,10},{10,... | collective-permute-start | bytes 86024 | tf_op jit(solution)/shard_map/ppermute | solution.py:576
  35.7 5.1 %collective-permute-start.9 = (f32[56,128]{1,0:T(8,128)S(1)}, f32[56,128]{1,0:T(8,128)S(1)}, u32[]{:S(2)}, u32[]{:S(2)}) collective-permute-start(f32[56,128]{1,0:T(8,128)S(1)} %add.23), channel_id=1, source_target_pairs={{0,5},{1,4},{2,7},{3,6},{4,1},{5,0},{6,3},{7,2},{8,13},{9,12},{10,... | collective-permute-start | bytes 86024 | tf_op jit(solution)/shard_map/ppermute | solution.py:576
  40.8 3.3 %collective-permute-start.12 = (f32[56,128]{1,0:T(8,128)S(1)}, f32[56,128]{1,0:T(8,128)S(1)}, u32[]{:S(2)}, u32[]{:S(2)}) collective-permute-start(f32[56,128]{1,0:T(8,128)S(1)} %add.24), channel_id=1, source_target_pairs={{0,9},{1,8},{2,11},{3,10},{4,13},{5,12},{6,15},{7,14},{8,1},{9,0},... | collective-permute-start | bytes 86024 | tf_op jit(solution)/shard_map/ppermute | solution.py:576
  44.1 3.3 %collective-permute-start.13 = (f32[56,128]{1,0:T(8,128)S(1)}, f32[56,128]{1,0:T(8,128)S(1)}, u32[]{:S(2)}, u32[]{:S(2)}) collective-permute-start(f32[56,128]{1,0:T(8,128)S(1)} %add.25.x_ref), channel_id=1, source_target_pairs={{0,17},{1,16},{2,19},{3,18},{4,21},{5,20},{6,23},{7,22},{8,25},{9,... | collective-permute-start | bytes 86024 | tf_op jit(solution)/shard_map/ppermute | solution.py:576
  (5 other events, 76.8 us)

commit v4 on v3

--- a/solution.py
+++ b/solution.py
@@ -13,10 +13,9 @@
 side = 7
 LANES = 128
 GROUP = 8
-PITCH = 48
-DEPTH = 8 * PITCH
+OUTER = 8 * 16
 VMEM = 20 * 1024 * 1024
-UNROLL = 32
+UNROLL = 64
 bf16, f32 = jnp.bfloat16, jnp.float32
 
 NN = (((1,), (0,)), ((), ()))
@@ -45,7 +44,7 @@
     return -(-a // b)
 
 
-def constants(colors, file_rows, channels):
+def constants(colors, file_rows, channels, height):
     block = colors * file_rows
     per = GROUP // file_rows
     rows = channels * GROUP
@@ -59,18 +58,29 @@
         out["spread" + name] = color[None, :] == np.arange(colors)[:, None]
         out["keep" + name] = row[None, :] == (np.arange(rows) % GROUP)[:, None]
     out["tall"] = (np.arange(rows) // GROUP)[:, None] == np.arange(channels)[None, :]
-    lane = np.arange(DEPTH)
-    copy, at = lane // PITCH, lane % PITCH - 5
-    tap = np.where((at >= 0) & (at < side) & (copy < side), at * side + copy, -1)
+    inner = 8 * height
     count = side * side
-    out["forward"] = tap[None, :] == np.arange(count)[:, None]
-    out["backward"] = (tap >= 0)[None, :] & (count - 1 - tap[None, :] == np.arange(count)[:, None])
-    out["taps"] = np.concatenate([out["backward"], np.zeros((56 - count, DEPTH), bool)])
+    forward = np.zeros((count, inner + 2 * OUTER), bool)
+    taps = np.zeros((56, inner + OUTER), bool)
+    for tap in range(count):
+        down, copy = divmod(tap, side)
+        own, above, below = height * copy + down - 3, 16 * copy + down + 5, 16 * copy + down - 3
+        forward[tap, own % inner] = True
+        forward[tap, inner + above] = True
+        forward[tap, inner + OUTER + below % OUTER] = True
+        taps[count - 1 - tap, own % inner] = True
+        taps[count - 1 - tap, inner + above] = True
+    out["forward"], out["backward"], out["taps"] = forward, forward[::-1], taps
+    lane, row = np.arange(inner)[None, :], np.arange(height)[:, None]
+    out["band"] = (abs(lane % height - row) <= 3) & (lane < height * side)
+    lane, row = np.arange(OUTER)[None, :], np.arange(8)[:, None]
+    at = lane % 16
+    out["fringe"] = np.concatenate([(at < 8) & (at >= row + 5), (at >= 8) & (at <= row + 3)]) & (lane < 16 * side)
     pick = np.zeros((3, 56, LANES), bool)
     for n in range(3):
         pick[n, colors + 1 + n] = True
     out["pick"] = np.concatenate(list(pick), axis=1)
-    return {k: jnp.asarray(v, f32 if k in ("forward", "backward") else bf16) for k, v in out.items()}
+    return {k: jnp.asarray(v, f32 if k in ("forward", "backward", "band", "fringe") else bf16) for k, v in out.items()}
 
 
 def params_kernel(wt_ref, taps_ref, bias_ref, gain_ref, off_ref, koff_ref, spread_ref, keep_ref, spread_h_ref,
@@ -141,9 +151,9 @@
         return jnp.concatenate(chunks, axis=0).astype(bf16)
 
     for away in range(chips):
-        there = lax.rem(chip + away, chips)
+        there = lax.bitwise_xor(chip, away)
         for other in range(2):
-            d = 2 * there + (core if other == 0 else 1 - core)
+            d = 2 * there + (core if (other == 0) == (away == 0) else 1 - core)
             tile = y_ref[:, pl.ds(pl.multiple_of(d * LANES, LANES), LANES)]
             if other == 0:
                 keep_ref[away, :block, :] = tile
@@ -207,14 +217,42 @@
     return jnp.concatenate(copies, axis=0)
 
 
-def toeplitz(base, height):
-    taps = pltpu.roll(jnp.broadcast_to(base, (height, DEPTH)), 0, 1, stride=1, stride_axis=0)
-    return jnp.concatenate(split2(taps), axis=0)
-
-
-def back_kernel(factor, at_ref, cot_ref, beside_ref, one_ref, two_ref, kb_ref,
-                flip_ref, grad_ref, total_ref, all_ref, halo_ref, sum_ref):
+def toeplitz(base, mask):
+    return pltpu.roll(jnp.broadcast_to(base, mask.shape), 0, 1, stride=1, stride_axis=0) * mask
+
+
+def inner_taps(base_ref, k, band_ref):
+    inner = band_ref.shape[1]
+    base = base_ref[pl.ds(k, 1), :]
+    return jnp.concatenate(split2(toeplitz(base[:, :inner], band_ref[...])), axis=0)
+
+
+def outer_taps(base_ref, k, inner, fringe_ref):
+    base = base_ref[pl.ds(k, 1), :]
+    above = toeplitz(base[:, inner:inner + OUTER], fringe_ref[:8])
+    below = toeplitz(base[:, inner + OUTER:], fringe_ref[8:])
+    return jnp.concatenate(split2(jnp.concatenate([above, below], axis=0)), axis=0)
+
+
+def back_inner_kernel(factor, cot_ref, beside_ref, kb_ref, band_ref, stack_ref, grad_ref, total_ref, sum_ref):
     channels, height, width = cot_ref.shape
+
+    def one(k, carry):
+        plane = cot_ref[k]
+        stack = shifted(plane, beside_ref[k])
+        stack_ref[k] = stack
+        both = mm(inner_taps(kb_ref, k, band_ref), stack)
+        grad_ref[k] = (both[:height] + both[height:]) * factor
+        sum_ref[k] = jnp.sum(plane.astype(f32).reshape(height // 8, 8, width), axis=0)
+        return carry
+
+    lax.fori_loop(0, channels, one, 0, unroll=UNROLL)
+    total_ref[...] = sum(sum_ref[:, b, :] for b in range(8)) * factor
+
+
+def back_outer_kernel(factor, at_ref, one_ref, two_ref, grad_ref, kb_ref, fringe_ref,
+                      stack_ref, edge_ref, plane_ref, halo_ref):
+    channels, height, width = grad_ref.shape
     even = at_ref[6, 0] == 0
     one, two = one_ref[...].astype(f32), two_ref[...].astype(f32)
     top = jnp.where(at_ref[2, 0] == 0, jnp.where(even, two, one), 0.0)
@@ -233,31 +271,18 @@
         return mm(dense.astype(bf16), place, TN).reshape(channels, 4, width)
 
     none = jnp.zeros((channels, 4, width), f32)
-    for above, middle, below, ref in (
-        (top[:channels], cot_ref, bot[:channels], all_ref),
-        (beside(top), beside_ref, beside(bot), halo_ref),
-    ):
-        ref[:, 0:8, :] = jnp.concatenate([none, above], axis=1).astype(bf16)
-        ref[:, 8:8 + height, :] = middle[...]
-        ref[:, 8 + height:, :] = jnp.concatenate([below, none], axis=1).astype(bf16)
-
-    eye = one_hot(iota((width, width), 0) == iota((width, width), 1))
+    plane_ref[...] = jnp.concatenate([none, top[:channels], bot[:channels], none], axis=1).astype(bf16)
+    halo_ref[...] = jnp.concatenate([none, beside(top), beside(bot), none], axis=1).astype(bf16)
 
     def one(k, carry):
-        plane = all_ref[k]
-        stack = shifted(plane, halo_ref[k])
-        flip_ref[k] = mm(eye, stack, NT).astype(bf16)
-        both = mm(toeplitz(kb_ref[pl.ds(k, 1), :], height), stack)
-        grad = (both[:height] + both[height:]) * factor
-        grad_ref[k] = grad
-        own = plane.astype(f32)[8:8 + height]
-        sum_ref[0, k] = jnp.sum(grad.reshape(height // 8, 8, width), axis=0)
-        sum_ref[1, k] = jnp.sum(own.reshape(height // 8, 8, width), axis=0) * factor
+        stack = shifted(plane_ref[k], halo_ref[k])
+        stack_ref[k] = stack
+        both = mm(outer_taps(kb_ref, k, 8 * height, fringe_ref), stack)
+        edge = (both[:16] + both[16:]) * factor
+        edge_ref[k] = edge + jnp.concatenate([grad_ref[k, :8, :], grad_ref[k, height - 8:, :]], axis=0)
         return carry
 
     lax.fori_loop(0, channels, one, 0, unroll=UNROLL)
-    for n in range(2):
-        total_ref[n] = sum(sum_ref[n, :, b, :] for b in range(8))
 
 
 def layer_norm(patch, channels):
@@ -277,9 +302,9 @@
     chips = len(pair_refs)
     core, chip = at_ref[0, 0], at_ref[1, 0]
     for away, ref in enumerate(pair_refs):
-        there = lax.rem(chip - away + chips, chips)
-        x_ref[2 * there + core] = ref[0]
-        x_ref[2 * there + 1 - core] = ref[1]
+        there = lax.bitwise_xor(chip, away)
+        x_ref[2 * there + core] = ref[0 if away == 0 else 1]
+        x_ref[2 * there + 1 - core] = ref[1 if away == 0 else 0]
     half = one_ref.shape[0]
     up = x_ref[:half]
     down = x_ref[2 * chips - half:]
@@ -288,14 +313,16 @@
     two_ref[...] = jnp.where(even, up, down)
 
 
-def main_kernel(colors, file_rows, factor, x_ref, wk_ref, vec_ref, grad_ref, total_ref, flip_ref, taps_ref, pick_ref,
-                norm_ref, out_ref, norm_s, grad_s, diag_s):
+def main_kernel(colors, file_rows, factor, x_ref, wk_ref, vec_ref, grad_ref, edge_ref, total_ref, stack_ref, rim_ref,
+                taps_ref, pick_ref, band_ref, fringe_ref, norm_ref, out_ref, norm_s, grad_s, diag_s):
     channels, height, width = grad_ref.shape
     block = colors * file_rows
     per = GROUP // file_rows
     rows = channels * GROUP
     bias, gain, offset = per_row(vec_ref, 0), per_row(vec_ref, 1), per_row(vec_ref, 2)
     scale_part = jnp.zeros((channels, GROUP, width), f32)
+    shift_part = jnp.zeros((channels, GROUP, width), f32)
+    inner = 8 * height
     ones = jnp.where(iota((16, width), 0) == 0, 1.0, 0.0).astype(bf16)
     by_color = jnp.zeros((colors + 16, channels), f32)
     for g in range(height // GROUP):
@@ -303,8 +330,14 @@
         patch = mm(wk_ref[...], jnp.concatenate(blocks, axis=0)).reshape(channels, GROUP, width) + bias
         xhat, inverse = layer_norm(patch, channels)
         norm_s[:, g * GROUP:(g + 1) * GROUP, :] = xhat * gain + offset
-        grad = grad_ref[:, g * GROUP:(g + 1) * GROUP, :]
+        if g == 0:
+            grad = edge_ref[:, :8, :]
+        elif g == height // GROUP - 1:
+            grad = edge_ref[:, 8:, :]
+        else:
+            grad = grad_ref[:, g * GROUP:(g + 1) * GROUP, :]
         scale_part += grad * xhat
+        shift_part += grad
         inside = grad * gain
         mean_a = jnp.mean(inside, axis=0, keepdims=True)
         mean_b = jnp.mean(inside * xhat, axis=0, keepdims=True)
@@ -319,91 +352,123 @@
     def one(k, carry):
         plane = norm_s[k].astype(bf16)
         norm_ref[k] = plane
-        cross = mm(plane, flip_ref[k])
-        total = cross[:8]
+        both = mm(plane, jnp.concatenate([stack_ref[k], rim_ref[k]], axis=0), NT)
+        cross = both[:, :inner]
+        total = cross[:8] * band_ref[:8]
         for a in range(1, height // 8):
-            total += pltpu.roll(cross[8 * a:8 * a + 8], DEPTH - 8 * a, 1)
-        diag_s[k] = total
+            rows = cross[8 * a:8 * a + 8]
+            if a == height // 8 - 1:
+                rows = rows * band_ref[8 * a:]
+            total += pltpu.roll(rows, inner - 8 * a, 1)
+        cross = both[:, inner:]
+        rim = cross[:8] * fringe_ref[:8] + pltpu.roll(cross[height - 8:] * fringe_ref[8:], 8, 1)
+        diag_s[k] = jnp.concatenate([total, rim], axis=1)
         return carry
 
     lax.fori_loop(0, channels, one, 0, unroll=UNROLL)
 
-    line = diag_s[:, 0, :]
+    line, rim = diag_s[:, 0, :inner], diag_s[:, 0, inner:]
     for b in range(1, 8):
-        line += pltpu.roll(diag_s[:, b, :], DEPTH - b, 1)
-    line = jnp.concatenate([jnp.zeros((LANES - channels, DEPTH), f32), line * factor], axis=0)
+        line += pltpu.roll(diag_s[:, b, :inner], inner - b, 1)
+        rim += pltpu.roll(diag_s[:, b, inner:], OUTER - b, 1)
+    line = jnp.concatenate([line, rim], axis=1) * factor
+    line = jnp.concatenate([jnp.zeros((LANES - channels, line.shape[1]), f32), line], axis=0)
     out_ref[...] = sum(mm(taps_ref[...], part, NT) for part in split2(line))
-    parts = jnp.concatenate([jnp.sum(scale_part, axis=1), total_ref[0], total_ref[1]], axis=1)
+    parts = jnp.concatenate([jnp.sum(scale_part, axis=1), jnp.sum(shift_part, axis=1), total_ref[...]], axis=1)
     first = sum(mm(pick_ref[...], part, NT) for part in split2(parts))
     out_ref[:, :channels] = first + by_color[:56]
 
 
-def stem_halo_kernel(colors, file_rows, at_ref, x_ref, one_ref, two_ref, wk_ref, wh_ref, vec_ref, norm_ref,
-                     all_s, halo_s):
-    channels, height, width = norm_ref.shape
+def side_columns(at_ref, wh_ref, vec_ref, lines, row_ok):
+    channels = vec_ref.shape[1]
+    shape = (channels, GROUP, LANES)
+    bias, gain, offset = per_row(vec_ref, 0), per_row(vec_ref, 1), per_row(vec_ref, 2)
+    lines.append(jnp.zeros((LANES - 8 * len(lines), wh_ref.shape[1]), f32))
+    lines = jnp.concatenate(lines, axis=0).astype(bf16)
+    xhat, _ = layer_norm(mm(wh_ref[...], lines, NT).reshape(shape) + bias, channels)
+    column = lax.bitwise_and(iota(shape, 2), 7)
+    ok = jnp.where(column < 3, 1 - at_ref[4, 0], 1 - at_ref[5, 0]) > 0
+    if row_ok is not None:
+        ok = ok & row_ok
+    return jnp.where(ok, xhat * gain + offset, 0.0).astype(bf16).reshape(channels * GROUP, LANES)
+
+
+def side_line(pieces, chunks):
+    pieces = [piece.astype(f32) for piece in pieces]
+    return jnp.concatenate([piece[8 * c:8 * c + 8] for piece in pieces for c in range(chunks)], axis=1)
+
+
+def stem_side_kernel(colors, file_rows, at_ref, x_ref, wh_ref, vec_ref, halo_ref):
+    channels, height, width = halo_ref.shape
+    block = colors * file_rows
+    per = GROUP // file_rows
+    chunks = wh_ref.shape[1] // (per * LANES)
+    groups = height // GROUP
+    lines = [
+        side_line([x_ref[per * g + a, block:block + 16, :] for a in range(per)], chunks) for g in range(groups)
+    ]
+    halo = side_columns(at_ref, wh_ref, vec_ref, lines, None)
+    for g in range(groups):
+        moved = pltpu.roll(halo, width - 8 * g - 3, 1).reshape(channels, GROUP, width)
+        halo_ref[:, 8 * g:8 * g + 8, :] = moved
+
+
+def stem_inner_kernel(start, norm_ref, side_ref, kf_ref, vec_ref, band_ref, out_ref):
+    count, height, _ = out_ref.shape
+
+    def one(n, carry):
+        k = start + n
+        both = mm(inner_taps(kf_ref, k, band_ref), shifted(norm_ref[k], side_ref[k]))
+        out_ref[n] = both[:height] + both[height:] + vec_ref[3, pl.ds(k, 1), :]
+        return carry
+
+    lax.fori_loop(0, count, one, 0, unroll=UNROLL)
+
+
+def stem_outer_kernel(colors, file_rows, parts, at_ref, one_ref, two_ref, wk_ref, wh_ref, vec_ref, kf_ref, fringe_ref,
+                      *refs):
+    inner_refs, (out_ref, plane_s, halo_s, out_s, sems) = refs[:parts], refs[parts:]
+    channels, height, width = out_s.shape
     block = colors * file_rows
     per = GROUP // file_rows
     half = per // 2
     chunks = wh_ref.shape[1] // (per * LANES)
+    shape = (channels, GROUP, width)
     bias, gain, offset = per_row(vec_ref, 0), per_row(vec_ref, 1), per_row(vec_ref, 2)
-    no_top, no_bot = at_ref[2, 0], at_ref[3, 0]
-    no_left, no_right = at_ref[4, 0], at_ref[5, 0]
-    shape = (channels, GROUP, width)
-    lower = iota(shape, 1) < 4
-    row_ok = jnp.where(lower, 1 - no_bot, 1 - no_top) > 0
+    row_ok = jnp.where(iota(shape, 1) < 4, 1 - at_ref[3, 0], 1 - at_ref[2, 0]) > 0
 
     even = at_ref[6, 0] == 0
     one, two = one_ref[...], two_ref[...]
     top, bot = jnp.where(even, two, one), jnp.where(even, one, two)
-    outer = [bot[a] for a in range(half)] + [top[a] for a in range(half)]
-    pixels = jnp.concatenate([piece[:block] for piece in outer], axis=0)
+    blocks = [bot[a] for a in range(half)] + [top[a] for a in range(half)]
+    pixels = jnp.concatenate([piece[:block] for piece in blocks], axis=0)
     xhat, _ = layer_norm(mm(wk_ref[...], pixels).reshape(shape) + bias, channels)
     rows = jnp.where(row_ok, xhat * gain + offset, 0.0).astype(bf16)
-    all_s[:, 0:8, :] = rows
-    all_s[:, 8 + height:16 + height, :] = rows
-    all_s[:, 8:8 + height, :] = norm_ref[...]
-
-    groups = height // GROUP
-    lines = []
-    for g in range(groups + 1):
-        pieces = []
-        for a in range(per):
-            piece = outer[a][block:block + 16] if g == groups else x_ref[per * g + a, block:block + 16, :]
-            piece = piece.astype(f32)
-            pieces += [piece[8 * c:8 * c + 8] for c in range(chunks)]
-        lines.append(jnp.concatenate(pieces, axis=1))
-    lines.append(jnp.zeros((LANES - 8 * len(lines), per * chunks * LANES), f32))
-    lines = jnp.concatenate(lines, axis=0).astype(bf16)
-    xhat, _ = layer_norm(mm(wh_ref[...], lines, NT).reshape(shape) + bias, channels)
-    lane = iota(shape, 2)
-    column = lax.bitwise_and(lane, 7)
-    ok = jnp.where(column < 3, 1 - no_left, 1 - no_right) > 0
-    ok = ok & (row_ok | (lane < 8 * groups))
-    halo = jnp.where(ok, xhat * gain + offset, 0.0).astype(bf16).reshape(channels * GROUP, width)
-    for g in range(groups + 1):
-        moved = pltpu.roll(halo, width - 8 * g - 3, 1).reshape(shape)
-        if g < groups:
-            halo_s[:, 8 + 8 * g:16 + 8 * g, :] = moved
-        else:
-            halo_s[:, 0:8, :] = moved
-            halo_s[:, 8 + height:16 + height, :] = moved
-
-
-def stem_kernel(start, *refs):
-    all_ref, halo_ref, kf_ref, vec_ref = refs[:4]
-    out_ref, out_s, sem = refs[-3:]
-    count, height, _ = out_s.shape
-
-    def one(n, carry):
-        k = start + n
-        both = mm(toeplitz(kf_ref[pl.ds(k, 1), :], height), shifted(all_ref[k], halo_ref[k]))
-        out_s[n] = (both[:height] + both[height:] + vec_ref[3, pl.ds(k, 1), :]).astype(bf16)
-        return carry
-
-    lax.fori_loop(0, count, one, 0, unroll=UNROLL)
-    copy = pltpu.make_async_copy(out_s, out_ref.at[pl.ds(start, count)], sem)
-    copy.start()
-    copy.wait()
+    line = side_line([piece[block:block + 16] for piece in blocks], chunks)
+    side = side_columns(at_ref, wh_ref, vec_ref, [line], row_ok)
+    side = pltpu.roll(side, width - 3, 1).reshape(shape)
+    for start in (0, 8):
+        plane_s[:, start:start + 8, :] = rows
+        halo_s[:, start:start + 8, :] = side
+
+    count = channels // parts
+    copies = []
+    for part, inner_ref in enumerate(inner_refs):
+        def one(n, carry, part=part, inner_ref=inner_ref):
+            k = part * count + n
+            both = mm(outer_taps(kf_ref, k, 8 * height, fringe_ref), shifted(plane_s[k], halo_s[k]))
+            edge = both[:16] + both[16:]
+            own = inner_ref[n]
+            out_s[k] = jnp.concatenate(
+                [own[:8] + edge[:8], own[8:height - 8], own[height - 8:] + edge[8:]], axis=0).astype(bf16)
+            return carry
+
+        lax.fori_loop(0, count, one, 0, unroll=UNROLL)
+        here = pl.ds(part * count, count)
+        copies.append(pltpu.make_async_copy(out_s.at[here], out_ref.at[here], sems.at[part]))
+        copies[-1].start()
+    for copy in copies:
+        copy.wait()
 
 
 def last_kernel(colors, x_ref, y_ref, *outs):
@@ -468,8 +533,8 @@
     padded = cdiv(block, LANES) * LANES
     rows = channels * GROUP
     tile = (channels, height, width)
-    tall = (channels, PITCH, width)
-    const = constants(colors, file_rows, channels)
+    inner = 8 * height
+    const = constants(colors, file_rows, channels, height)
 
     row_at, col_at = lax.axis_index("rows"), lax.axis_index("cols")
     chips = n_cols // 2
@@ -504,7 +569,7 @@
     far = lax.ppermute(edges, "cols", pairing(n_cols, 1))
     pairs = kernel_call(pair_kernel, (in_vmem((2, block_rows, LANES), bf16),) * chips, 0.5, keep, got)
     pairs = [pairs[0]] + [
-        lax.ppermute(pairs[n], "cols", [(i, (i + 2 * n) % n_cols) for i in range(n_cols)])
+        lax.ppermute(pairs[n], "cols", [(i, i ^ (2 * n + 1)) for i in range(n_cols)])
         for n in range(1, chips)
     ]
 
@@ -524,8 +589,8 @@
         (
             in_vmem((rows, per * block), bf16),
             in_vmem((rows, per * padded), bf16),
-            in_vmem((channels, DEPTH), f32),
-            in_vmem((channels, DEPTH), f32),
+            in_vmem((channels, inner + 2 * OUTER), f32),
+            in_vmem((channels, inner + 2 * OUTER), f32),
             in_vmem((4, channels, LANES), f32),
         ),
         0.01,
@@ -533,20 +598,23 @@
         const["spread"], const["keep"], const["spread_halo"], const["keep_halo"], const["tall"],
         const["forward"], const["backward"],
     )
-    flipped, grad, totals = kernel_call(
-        functools.partial(back_kernel, factor),
-        (in_vmem((channels, width, DEPTH), bf16), in_vmem(tile, f32), in_vmem((2, channels, width), f32)),
+    stack, grad, total = kernel_call(
+        functools.partial(back_inner_kernel, factor),
+        (in_vmem((channels, inner, width), bf16), in_vmem(tile, f32), in_vmem((channels, width), f32)),
         0.01,
-        at, cot, beside, *strips, kb,
-        scratch_shapes=[
-            pltpu.VMEM(tall, bf16),
-            pltpu.VMEM(tall, bf16),
-            pltpu.VMEM((2, channels, GROUP, width), f32),
-        ],
+        cot, beside, kb, const["band"],
+        scratch_shapes=[pltpu.VMEM((channels, 8, width), f32)],
+    )
+    rim, edge = kernel_call(
+        functools.partial(back_outer_kernel, factor),
+        (in_vmem((channels, OUTER, width), bf16), in_vmem((channels, 16, width), f32)),
+        0.01,
+        at, *strips, grad, kb, const["fringe"],
+        scratch_shapes=[pltpu.VMEM((channels, 16, width), bf16)] * 2,
     )
 
     half = per // 2
-    grad, *pairs = lax.optimization_barrier((grad, *pairs))
+    edge, *pairs = lax.optimization_barrier((edge, *pairs))
     pixels, *ends = kernel_call(
         order_kernel,
         (in_vmem((n_cols, block_rows, LANES), bf16),) + (in_vmem((half, block_rows, LANES), bf16),) * 2,
@@ -558,19 +626,19 @@
         functools.partial(main_kernel, colors, file_rows, factor),
         (in_vmem(tile, bf16), in_vmem((56, LANES), f32)),
         6,
-        pixels, wk, vec, grad, totals, flipped, const["taps"], const["pick"],
+        pixels, wk, vec, grad, edge, total, stack, rim, const["taps"], const["pick"], const["band"], const["fringe"],
         scratch_shapes=[
             pltpu.VMEM(tile, f32),
             pltpu.VMEM((height // GROUP, rows, width), f32),
-            pltpu.VMEM((channels, 8, DEPTH), f32),
+            pltpu.VMEM((channels, 8, inner + OUTER), f32),
         ],
     )
 
     size = n_rows * n_cols
-    chunk = channels // 2
+    chunk = channels
     rounds = (size - 1).bit_length()
-    jobs = {0: ["one"], 1: ["two"], 2: ["halo"], 3: [0], rounds - 1: [chunk]}
-    stem_output = None
+    jobs = {0: ["side"], 1: ["one"], 2: ["two"], 3: [0], rounds - 1: ["outer"]}
+    parts = []
     for n in range(rounds):
         step = 1 if n == 0 else (1 << n) + 1
         other = lax.ppermute(result, ("rows", "cols"), [(i, i ^ step) for i in range(size)])
@@ -579,28 +647,42 @@
                 which = ("one", "two").index(job)
                 result, end = lax.optimization_barrier((result, ends[which]))
                 ends[which] = lax.ppermute(end, "rows", pairing(n_rows, which))
-            elif job == "halo":
-                result, norm = lax.optimization_barrier((result, norm))
-                norm_all, norm_halo = kernel_call(
-                    functools.partial(stem_halo_kernel, colors, file_rows),
-                    (in_vmem(tall, bf16), in_vmem(tall, bf16)),
-                    2,
-                    at, pixels, *ends, wk, wh, vec, norm,
+            elif job == "side":
+                result, pixels = lax.optimization_barrier((result, pixels))
+                beside = kernel_call(
+                    functools.partial(stem_side_kernel, colors, file_rows),
+                    in_vmem(tile, bf16),
+                    1,
+                    at, pixels, wh, vec,
                 )
-            else:
-                result, norm_all = lax.optimization_barrier((result, norm_all))
-                before = () if stem_output is None else (stem_output,)
+                result, beside = lax.optimization_barrier((result, beside))
+            elif job == "outer":
+                result, *parts = lax.optimization_barrier((result, *parts))
                 stem_output = kernel_call(
-                    functools.partial(stem_kernel, job),
+                    functools.partial(stem_outer_kernel, colors, file_rows, len(parts)),
                     shaped(tile, bf16),
-                    1.5,
-                    norm_all, norm_halo, kf, vec, *before,
-                    in_specs=[vmem] * 4 + [beyond] * len(before),
+                    3,
+                    at, *ends, wk, wh, vec, kf, const["fringe"], *parts,
+                    in_specs=[vmem] * (8 + len(parts)),
                     out_specs=beyond,
-                    input_output_aliases={4: 0} if before else {},
-                    scratch_shapes=[pltpu.VMEM((chunk, height, width), bf16), pltpu.SemaphoreType.DMA],
+                    scratch_shapes=[
+                        pltpu.VMEM((channels, 16, width), bf16),
+                        pltpu.VMEM((channels, 16, width), bf16),
+                        pltpu.VMEM(tile, bf16),
+                        pltpu.SemaphoreType.DMA((len(parts),)),
+                    ],
                 )
                 result, stem_output = lax.optimization_barrier((result, stem_output))
+            else:
+                result, norm = lax.optimization_barrier((result, norm))
+                part = kernel_call(
+                    functools.partial(stem_inner_kernel, job * chunk),
+                    in_vmem((chunk, height, width), f32),
+                    2,
+                    norm, beside, kf, vec, const["band"],
+                )
+                result, part = lax.optimization_barrier((result, part))
+                parts.append(part)
         if n < rounds - 1:
             result = result + other
 

time: 48.2 us -> 42.2 us (0.88)
  waiting for transfers between devices: 10.4 us -> 5.25 us
  Pallas kernels: 18.7 us -> 16.5 us
  starting transfers between devices: 17.7 us -> 19.1 us
    ppermute x5, waiting for transfers between devices: 7.63 us -> 3.48 us  [per_device(): lax.ppermute(result, ('rows', 'cols'), [(i, i ^ step) for i in range(size)])]
    ppermute x5, starting transfers between devices: 2.79 us -> 6.05 us  [per_device(): lax.ppermute(result, ('rows', 'cols'), [(i, i ^ step) for i in range(size)])]
    pallas_call x11 -> x12, Pallas kernels: 18.7 us -> 16.5 us  [kernel_call(): pl.pallas_call(body, out_shape=out_shape, compiler_params=pltpu.CompilerP...]
    ppermute x3, starting transfers between devices: 3.87 us -> 1.82 us  [per_device(): lax.ppermute(pairs[n], 'cols', [(i, i ^ 2 * n + 1) for i in range(n_cols)])]
    ppermute x2, waiting for transfers between devices: 2.76 us -> 1.68 us  [swap(): lax.ppermute(part, axis, pairing(lax.axis_size(axis), n))]
  transfers between devices with their start and end apart: 14 -> 14, of which waited for: 7 -> 6; matrix products, arithmetic and copies ran while one was open for 0% -> 0% of each run, Pallas kernels for 24% -> 21%
where the time goes in v4:
time: 42.2 us; the launch traced here: 42.1 us
  starting transfers between devices  19.1 us (45%)
  Pallas kernels  16.5 us (39%)
  waiting for transfers between devices  5.25 us (12%)
  between operations  0.99 us (2%)
    pallas_call x12, Pallas kernels, kernel_call(): pl.pallas_call(body, out_shape=out_shape, compiler_params=pltpu.CompilerP...  16.5 us
    ppermute x5, starting transfers between devices, per_device(): lax.ppermute(result, ('rows', 'cols'), [(i, i ^ step) for i in range(size)])  6.05 us
    ppermute x1, starting transfers between devices, per_device(): far = lax.ppermute(edges, 'cols', pairing(n_cols, 1))  4.71 us
    ppermute x5, waiting for transfers between devices, per_device(): lax.ppermute(result, ('rows', 'cols'), [(i, i ^ step) for i in range(size)])  3.48 us
    ppermute x2, starting transfers between devices, swap(): lax.ppermute(part, axis, pairing(lax.axis_size(axis), n))  3 us
    ppermute x2, starting transfers between devices, per_device(): ends[which] = lax.ppermute(end, 'rows', pairing(n_rows, which))  2.98 us
    ppermute x3, starting transfers between devices, per_device(): lax.ppermute(pairs[n], 'cols', [(i, i ^ 2 * n + 1) for i in range(n_cols)])  1.82 us
    ppermute x2, waiting for transfers between devices, swap(): lax.ppermute(part, axis, pairing(lax.axis_size(axis), n))  1.68 us
  transfers between devices with their start and end apart: 14, of which 6 were waited for; matrix products, arithmetic and copies ran while one was open for 0% of the time, Pallas kernels for 21%

profile of v4, /device:TPU:0, one launch (start us, length us, event | category | flops | bytes accessed | tf_op | source)
XLA Modules:
  0.0 42.1 jit_solution(10319491976038266353)
XLA Ops:
  1.0 2.1 %shard_map.234 = (bf16[64,32,128]{2,1,0:T(8,128)(2,1)S(1)}, bf16[4,208,128]{2,1,0:T(8,128)(2,1)S(1)}, bf16[960,128]{1,0:T(8,128)(2,1)S(1)}, bf16[176,128]{1,0:T(8,128)(2,1)S(1)}) custom-call(s32[8,128]{1,0:T(8,128)S(1)} %broadcast_in_dim.2.at_ref, bf16[48,4,1024]{2,1,0:T(4,128)(2,1)} %x_hbm.1, bf16[64,32,128]{2,1,0:T(8,128)(2,1)} %cot_hbm.1), custom_call_target="tpu_custom_call" | custom-call | flops 2000000000 | bytes 6000000 | tf_op jit(solution)/shard_map/pallas_call | solution.py:495
  3.6 4.7 %collective-permute-start.1 = (bf16[176,128]{1,0:T(8,128)(2,1)S(1)}, bf16[176,128]{1,0:T(8,128)(2,1)S(1)}, u32[]{:S(2)}, u32[]{:S(2)}) collective-permute-start(bf16[176,128]{1,0:T(8,128)(2,1)S(1)} %get-tuple-element.68), channel_id=1, source_target_pairs={{0,7},{1,2},{2,1},{3,4},{4,3},{5,6},{6,5},{7,0},{8,15},{9,10},{10,... | collective-permute-start | bytes 135176 | tf_op jit(solution)/shard_map/ppermute | solution.py:569
  8.4 1.7 %collective-permute-start.5 = (bf16[2,208,128]{2,1,0:T(8,128)(2,1)S(1)}, bf16[2,208,128]{2,1,0:T(8,128)(2,1)S(1)}, u32[]{:S(2)}, u32[]{:S(2)}) collective-permute-start(bf16[2,208,128]{2,1,0:T(8,128)(2,1)S(1)} %get-tuple-element.80), channel_id=1, source_target_pairs={{0,5},{1,4},{2,7},{3,6},{4,1},{5,0},{6,3},{7,2},{8,13},{9,12},{10,... | collective-permute-start | bytes 319496 | tf_op jit(solution)/shard_map/ppermute | solution.py:572
  10.2 0.7 %shard_map.236 = (bf16[64,32,128]{2,1,0:T(8,128)(2,1)S(1)}, bf16[68,4,128]{2,1,0:T(4,128)(2,1)S(1)}, bf16[68,4,128]{2,1,0:T(4,128)(2,1)S(1)}) custom-call(s32[8,128]{1,0:T(8,128)S(1)} %broadcast_in_dim.2.at_ref, bf16[64,32,128]{2,1,0:T(8,128)(2,1)S(1)} %get-tuple-element.64.cot_ref, bf16[960,128]{1,0:T(8,128)(2,1)S(1)} %collective-permute-done.got_ref.near_ref, ...), custom_call_target="tpu_custom_call" | custom-call | flops 10000000 | bytes 30000 | tf_op jit(solution)/shard_map/pallas_call | solution.py:495
  11.0 1.5 %collective-permute-start.2 = (bf16[68,4,128]{2,1,0:T(4,128)(2,1)S(1)}, bf16[68,4,128]{2,1,0:T(4,128)(2,1)S(1)}, u32[]{:S(2)}, u32[]{:S(2)}) collective-permute-start(bf16[68,4,128]{2,1,0:T(4,128)(2,1)S(1)} %get-tuple-element.70), channel_id=1, source_target_pairs={{0,8},{8,0},{16,24},{24,16},{1,9},{9,1},{17,25},{25,17},{2,10},{10... | collective-permute-start | bytes 208904 | tf_op jit(solution)/shard_map/ppermute | solution.py:513
  12.5 1.5 %collective-permute-start.3 = (bf16[68,4,128]{2,1,0:T(4,128)(2,1)S(1)}, bf16[68,4,128]{2,1,0:T(4,128)(2,1)S(1)}, u32[]{:S(2)}, u32[]{:S(2)}) collective-permute-start(bf16[68,4,128]{2,1,0:T(4,128)(2,1)S(1)} %get-tuple-element.71), channel_id=1, source_target_pairs={{0,24},{8,16},{16,8},{24,0},{1,25},{9,17},{17,9},{25,1},{2,26},{10... | collective-permute-start | bytes 208904 | tf_op jit(solution)/shard_map/ppermute | solution.py:513
  14.1 0.9 %shard_map.237 = (bf16[512,384]{1,0:T(8,128)(2,1)S(1)}, bf16[512,512]{1,0:T(8,128)(2,1)S(1)}, f32[64,512]{1,0:T(8,128)S(1)}, f32[64,512]{1,0:T(8,128)S(1)}, f32[4,64,128]{2,1,0:T(8,128)S(1)}) custom-call(bf16[48,64]{1,0:T(8,128)(2,1)S(1)} %bitcast.12, f32[49,64]{1,0:T(8,128)S(1)} %bitcast.11, f32[64]{0:T(128)S(1)} %copy-done.11, f32[64]{0:T(128)S(1)} %copy-done.12, ...), custom_call_target="tpu_custom_call" | custom-call | flops 10000000 | bytes 30000 | tf_op jit(solution)/shard_map/pallas_call | solution.py:495
  15.0 1.7 %shard_map.238 = (bf16[64,256,128]{2,1,0:T(8,128)(2,1)S(1)}, f32[64,32,128]{2,1,0:T(8,128)S(1)}, f32[64,128]{1,0:T(8,128)S(1)}) custom-call(bf16[64,32,128]{2,1,0:T(8,128)(2,1)S(1)} %get-tuple-element.64.cot_ref, bf16[64,32,128]{2,1,0:T(8,128)(2,1)S(1)} %get-tuple-element.73.beside_ref, f32[64,512]{1,0:T(8,128)S(1)} %get-tuple-element.75.kb_ref, ...), custom_call_target="tpu_custom_call" | custom-call | flops 10000000 | bytes 30000 | tf_op jit(solution)/shard_map/pallas_call | solution.py:495
  16.8 1.7 %collective-permute-done.3.two_ref = bf16[68,4,128]{2,1,0:T(4,128)(2,1)S(1)} collective-permute-done((bf16[68,4,128]{2,1,0:T(4,128)(2,1)S(1)}, bf16[68,4,128]{2,1,0:T(4,128)(2,1)S(1)}, u32[]{:S(2)}, u32[]{:S(2)}) %collective-permute-start.3) | collective-permute-done | bytes 69664 | tf_op jit(solution)/shard_map/ppermute | solution.py:513
  18.4 1.0 %shard_map.239 = (bf16[64,128,128]{2,1,0:T(8,128)(2,1)S(1)}, f32[64,16,128]{2,1,0:T(8,128)S(1)}) custom-call(s32[8,128]{1,0:T(8,128)S(1)} %broadcast_in_dim.2.at_ref, bf16[68,4,128]{2,1,0:T(4,128)(2,1)S(1)} %collective-permute-done.2.one_ref, bf16[68,4,128]{2,1,0:T(4,128)(2,1)S(1)} %collective-permute-done.3.two_ref, ...), custom_call_target="tpu_custom_call" | custom-call | flops 10000000 | bytes 30000 | tf_op jit(solution)/shard_map/pallas_call | solution.py:495
  19.6 4.7 %shard_map.241 = (bf16[64,32,128]{2,1,0:T(8,128)(2,1)S(1)}, f32[56,128]{1,0:T(8,128)S(1)}) custom-call(bf16[8,208,128]{2,1,0:T(8,128)(2,1)S(1)} %get-tuple-element.95.x_ref, bf16[512,384]{1,0:T(8,128)(2,1)S(1)} %get-tuple-element.87.wk_ref, f32[4,64,128]{2,1,0:T(8,128)S(1)} %get-tuple-element.88.vec_ref, f32[64,32,128]{2,1,0:T(8,128)S(1)} %get-tuple-element.76.grad_ref, ...), custom_call_target="tpu_custom_call" | custom-call | flops 6000000000 | bytes 18000000 | tf_op jit(solution)/shard_map/pallas_call | solution.py:495
  24.3 0.9 %collective-permute-start.7 = (f32[56,128]{1,0:T(8,128)S(1)}, f32[56,128]{1,0:T(8,128)S(1)}, u32[]{:S(2)}, u32[]{:S(2)}) collective-permute-start(f32[56,128]{1,0:T(8,128)S(1)} %get-tuple-element.97), channel_id=1, source_target_pairs={{0,1},{1,0},{2,3},{3,2},{4,5},{5,4},{6,7},{7,6},{8,9},{9,8},{10,11... | collective-permute-start | bytes 86024 | tf_op jit(solution)/shard_map/ppermute | solution.py:644
  25.3 0.6 %shard_map.242.side_ref = bf16[64,32,128]{2,1,0:T(8,128)(2,1)S(1)} custom-call(s32[8,128]{1,0:T(8,128)S(1)} %broadcast_in_dim.2.at_ref, bf16[8,208,128]{2,1,0:T(8,128)(2,1)S(1)} %get-tuple-element.95.x_ref, bf16[512,512]{1,0:T(8,128)(2,1)S(1)} %get-tuple-element.96.wh_ref, f32[4,64,128]{2,1,0:T(8,128)S(1)} %get-tuple-element.88.vec_ref), custom_call_target="tpu_custom_call" | custom-call | flops 1000000000 | bytes 3000000 | tf_op jit(solution)/shard_map/pallas_call | solution.py:495
  26.1 1.5 %collective-permute-start.8 = (f32[56,128]{1,0:T(8,128)S(1)}, f32[56,128]{1,0:T(8,128)S(1)}, u32[]{:S(2)}, u32[]{:S(2)}) collective-permute-start(f32[56,128]{1,0:T(8,128)S(1)} %add.22), channel_id=1, source_target_pairs={{0,3},{1,2},{2,1},{3,0},{4,7},{5,6},{6,5},{7,4},{8,11},{9,10},{10,... | collective-permute-start | bytes 86024 | tf_op jit(solution)/shard_map/ppermute | solution.py:644
  27.6 1.8 %collective-permute-done.8 = f32[56,128]{1,0:T(8,128)S(1)} collective-permute-done((f32[56,128]{1,0:T(8,128)S(1)}, f32[56,128]{1,0:T(8,128)S(1)}, u32[]{:S(2)}, u32[]{:S(2)}) %collective-permute-start.8) | collective-permute-done | bytes 28704 | tf_op jit(solution)/shard_map/ppermute | solution.py:644
  29.4 2.0 %collective-permute-start.9 = (f32[56,128]{1,0:T(8,128)S(1)}, f32[56,128]{1,0:T(8,128)S(1)}, u32[]{:S(2)}, u32[]{:S(2)}) collective-permute-start(f32[56,128]{1,0:T(8,128)S(1)} %add.23), channel_id=1, source_target_pairs={{0,5},{1,4},{2,7},{3,6},{4,1},{5,0},{6,3},{7,2},{8,13},{9,12},{10,... | collective-permute-start | bytes 86024 | tf_op jit(solution)/shard_map/ppermute | solution.py:644
  31.4 1.5 %collective-permute-start.11 = (bf16[1,208,128]{2,1,0:T(8,128)(2,1)S(1)}, bf16[1,208,128]{2,1,0:T(8,128)(2,1)S(1)}, u32[]{:S(2)}, u32[]{:S(2)}) collective-permute-start(bf16[1,208,128]{2,1,0:T(8,128)(2,1)S(1)} %get-tuple-element.110), channel_id=1, source_target_pairs={{0,8},{8,0},{16,24},{24,16},{1,9},{9,1},{17,25},{25,17},{2,10},{10... | collective-permute-start | bytes 159752 | tf_op jit(solution)/shard_map/ppermute | solution.py:649
  32.9 1.5 %collective-permute-start.12 = (bf16[1,208,128]{2,1,0:T(8,128)(2,1)S(1)}, bf16[1,208,128]{2,1,0:T(8,128)(2,1)S(1)}, u32[]{:S(2)}, u32[]{:S(2)}) collective-permute-start(bf16[1,208,128]{2,1,0:T(8,128)(2,1)S(1)} %get-tuple-element.111), channel_id=1, source_target_pairs={{0,24},{8,16},{16,8},{24,0},{1,25},{9,17},{17,9},{25,1},{2,26},{10... | collective-permute-start | bytes 159752 | tf_op jit(solution)/shard_map/ppermute | solution.py:649
  34.4 0.9 %collective-permute-start.10 = (f32[56,128]{1,0:T(8,128)S(1)}, f32[56,128]{1,0:T(8,128)S(1)}, u32[]{:S(2)}, u32[]{:S(2)}) collective-permute-start(f32[56,128]{1,0:T(8,128)S(1)} %add.24), channel_id=1, source_target_pairs={{0,9},{1,8},{2,11},{3,10},{4,13},{5,12},{6,15},{7,14},{8,1},{9,0},... | collective-permute-start | bytes 86024 | tf_op jit(solution)/shard_map/ppermute | solution.py:644
  35.3 1.7 %shard_map.243.refs_0_ = f32[64,32,128]{2,1,0:T(8,128)S(1)} custom-call(bf16[64,32,128]{2,1,0:T(8,128)(2,1)S(1)} %get-tuple-element.104.norm_ref, bf16[64,32,128]{2,1,0:T(8,128)(2,1)S(1)} %shard_map.242.side_ref, f32[64,512]{1,0:T(8,128)S(1)} %get-tuple-element.106.kf_ref, f32[4,64,128]{2,1,0:T(8,128)S(1)} %get-tuple-element.88.vec_ref, f32[32,256]{1,0:T(8,128)S(1)} %copy-done.7), custom_call_target="tpu_custom_call" | custom-call | flops 2000000000 | bytes 6000000 | tf_op jit(solution)/shard_map/pallas_call | solution.py:495
  37.0 1.1 %collective-permute-done.10 = f32[56,128]{1,0:T(8,128)S(1)} collective-permute-done((f32[56,128]{1,0:T(8,128)S(1)}, f32[56,128]{1,0:T(8,128)S(1)}, u32[]{:S(2)}, u32[]{:S(2)}) %collective-permute-start.10) | collective-permute-done | bytes 28704 | tf_op jit(solution)/shard_map/ppermute | solution.py:644
  38.1 0.8 %collective-permute-start.13 = (f32[56,128]{1,0:T(8,128)S(1)}, f32[56,128]{1,0:T(8,128)S(1)}, u32[]{:S(2)}, u32[]{:S(2)}) collective-permute-start(f32[56,128]{1,0:T(8,128)S(1)} %add.25.x_ref), channel_id=1, source_target_pairs={{0,17},{1,16},{2,19},{3,18},{4,21},{5,20},{6,23},{7,22},{8,25},{9,... | collective-permute-start | bytes 86024 | tf_op jit(solution)/shard_map/ppermute | solution.py:644
  38.8 2.2 %shard_map.244 = bf16[64,32,128]{2,1,0:T(8,128)(2,1)} custom-call(s32[8,128]{1,0:T(8,128)S(1)} %broadcast_in_dim.2.at_ref, bf16[1,208,128]{2,1,0:T(8,128)(2,1)S(1)} %collective-permute-done.11.one_ref, bf16[1,208,128]{2,1,0:T(8,128)(2,1)S(1)} %collective-permute-done.12.two_ref, bf16[512,384]{1,0:T(8,128)(2,1)S(1)} %get-tuple-element.87.wk_ref, ...), custom_call_target="tpu_custom_call" | custom-call | flops 3000000000 | bytes 9000000 | tf_op jit(solution)/shard_map/pallas_call | solution.py:495
  41.4 0.7 %shard_map.245 = (f32[48,64]{1,0:T(8,128)}, f32[64]{0:T(128)}, f32[64]{0:T(128)}, f32[64]{0:T(128)}, f32[64]{0:T(128)}, /*index=5*/f32[49,64]{1,0:T(8,128)}) custom-call(f32[56,128]{1,0:T(8,128)S(1)} %add.25.x_ref, f32[56,128]{1,0:T(8,128)S(1)} %collective-permute-done.13.y_ref), custom_call_target="tpu_custom_call" | custom-call | flops 1000000000 | bytes 3000000 | tf_op jit(solution)/shard_map/pallas_call | solution.py:495
  (56 shorter events, 1.7 us)
Async XLA Ops:
  0.8 13.1 %copy-start.1 = (bf16[512,384]{1,0:T(8,128)(2,1)S(1)}, bf16[512,384]{1,0:T(8,128)(2,1)}, u32[]{:S(2)}) copy-start(bf16[512,384]{1,0:T(8,128)(2,1)} %constant.66.clone.keep_ref) | copy-start | bytes 1179652
  0.8 13.1 %copy-start.2 = (bf16[512,64]{1,0:T(8,128)(2,1)S(1)}, bf16[512,64]{1,0:T(8,128)(2,1)}, u32[]{:S(2)}) copy-start(bf16[512,64]{1,0:T(8,128)(2,1)} %constant.69.clone.tall_ref) | copy-start | bytes 196612
  0.8 13.2 %copy-start.3 = (f32[49,512]{1,0:T(8,128)S(1)}, f32[49,512]{1,0:T(8,128)}, u32[]{:S(2)}) copy-start(f32[49,512]{1,0:T(8,128)} %constant.71.clone.backward_ref) | copy-start | bytes 301060
  0.8 13.2 %copy-start.4 = (f32[49,512]{1,0:T(8,128)S(1)}, f32[49,512]{1,0:T(8,128)}, u32[]{:S(2)}) copy-start(f32[49,512]{1,0:T(8,128)} %constant.70.clone.forward_ref) | copy-start | bytes 301060
  0.8 13.2 %copy-start.5 = (bf16[48,512]{1,0:T(8,128)(2,1)S(1)}, bf16[48,512]{1,0:T(8,128)(2,1)}, u32[]{:S(2)}) copy-start(bf16[48,512]{1,0:T(8,128)(2,1)} %constant.67.clone.spread_h_ref) | copy-start | bytes 147460
  0.9 13.1 %copy-start.6 = (bf16[48,384]{1,0:T(8,128)(2,1)S(1)}, bf16[48,384]{1,0:T(8,128)(2,1)}, u32[]{:S(2)}) copy-start(bf16[48,384]{1,0:T(8,128)(2,1)} %constant.65.clone.spread_ref) | copy-start | bytes 110596
  0.9 14.0 %copy-start.7 = (f32[32,256]{1,0:T(8,128)S(1)}, f32[32,256]{1,0:T(8,128)}, u32[]{:S(2)}) copy-start(f32[32,256]{1,0:T(8,128)} %constant.73.clone.band_ref) | copy-start | bytes 98308
  3.0 15.4 %copy-start.10 = (f32[16,128]{1,0:T(8,128)S(1)}, f32[16,128]{1,0:T(8,128)}, u32[]{:S(2)}) copy-start(f32[16,128]{1,0:T(8,128)} %constant.74.clone.fringe_ref) | copy-start | bytes 24580
  3.0 16.5 %copy-start.15 = (bf16[56,384]{1,0:T(8,128)(2,1)S(1)}, bf16[56,384]{1,0:T(8,128)(2,1)}, u32[]{:S(2)}) copy-start(bf16[56,384]{1,0:T(8,128)(2,1)} %constant.75.clone.pick_ref) | copy-start | bytes 129028
  3.1 16.5 %copy-start.16 = (bf16[56,384]{1,0:T(8,128)(2,1)S(1)}, bf16[56,384]{1,0:T(8,128)(2,1)}, u32[]{:S(2)}) copy-start(bf16[56,384]{1,0:T(8,128)(2,1)} %constant.72.clone.taps_ref) | copy-start | bytes 129028
  3.1 5.2 %collective-permute-start = (bf16[960,128]{1,0:T(8,128)(2,1)S(1)}, bf16[960,128]{1,0:T(8,128)(2,1)S(1)}, u32[]{:S(2)}, u32[]{:S(2)}) collective-permute-start(bf16[960,128]{1,0:T(8,128)(2,1)S(1)} %get-tuple-element.65), channel_id=1, source_target_pairs={{0,1},{1,0},{2,3},{3,2},{4,5},{5,4},{6,7},{7,6},{8,9},{9,8},{10,11... | collective-permute-start | bytes 737288 | tf_op jit(solution)/shard_map/ppermute | solution.py:568
  3.6 6.6 %collective-permute-start.1 = (bf16[176,128]{1,0:T(8,128)(2,1)S(1)}, bf16[176,128]{1,0:T(8,128)(2,1)S(1)}, u32[]{:S(2)}, u32[]{:S(2)}) collective-permute-start(bf16[176,128]{1,0:T(8,128)(2,1)S(1)} %get-tuple-element.68), channel_id=1, source_target_pairs={{0,7},{1,2},{2,1},{3,4},{4,3},{5,6},{6,5},{7,0},{8,15},{9,10},{10,... | collective-permute-start | bytes 135176 | tf_op jit(solution)/shard_map/ppermute | solution.py:569
  8.3 11.1 %collective-permute-start.4 = (bf16[2,208,128]{2,1,0:T(8,128)(2,1)S(1)}, bf16[2,208,128]{2,1,0:T(8,128)(2,1)S(1)}, u32[]{:S(2)}, u32[]{:S(2)}) collective-permute-start(bf16[2,208,128]{2,1,0:T(8,128)(2,1)S(1)} %get-tuple-element.79), channel_id=1, source_target_pairs={{0,3},{1,2},{2,1},{3,0},{4,7},{5,6},{6,5},{7,4},{8,11},{9,10},{10,... | collective-permute-start | bytes 319496 | tf_op jit(solution)/shard_map/ppermute | solution.py:572
  8.4 11.1 %collective-permute-start.5 = (bf16[2,208,128]{2,1,0:T(8,128)(2,1)S(1)}, bf16[2,208,128]{2,1,0:T(8,128)(2,1)S(1)}, u32[]{:S(2)}, u32[]{:S(2)}) collective-permute-start(bf16[2,208,128]{2,1,0:T(8,128)(2,1)S(1)} %get-tuple-element.80), channel_id=1, source_target_pairs={{0,5},{1,4},{2,7},{3,6},{4,1},{5,0},{6,3},{7,2},{8,13},{9,12},{10,... | collective-permute-start | bytes 319496 | tf_op jit(solution)/shard_map/ppermute | solution.py:572
  10.1 9.4 %collective-permute-start.6 = (bf16[2,208,128]{2,1,0:T(8,128)(2,1)S(1)}, bf16[2,208,128]{2,1,0:T(8,128)(2,1)S(1)}, u32[]{:S(2)}, u32[]{:S(2)}) collective-permute-start(bf16[2,208,128]{2,1,0:T(8,128)(2,1)S(1)} %get-tuple-element.81), channel_id=1, source_target_pairs={{0,7},{1,6},{2,5},{3,4},{4,3},{5,2},{6,1},{7,0},{8,15},{9,14},{10,... | collective-permute-start | bytes 319496 | tf_op jit(solution)/shard_map/ppermute | solution.py:572
  11.0 5.8 %collective-permute-start.2 = (bf16[68,4,128]{2,1,0:T(4,128)(2,1)S(1)}, bf16[68,4,128]{2,1,0:T(4,128)(2,1)S(1)}, u32[]{:S(2)}, u32[]{:S(2)}) collective-permute-start(bf16[68,4,128]{2,1,0:T(4,128)(2,1)S(1)} %get-tuple-element.70), channel_id=1, source_target_pairs={{0,8},{8,0},{16,24},{24,16},{1,9},{9,1},{17,25},{25,17},{2,10},{10... | collective-permute-start | bytes 208904 | tf_op jit(solution)/shard_map/ppermute | solution.py:513
  12.5 6.0 %collective-permute-start.3 = (bf16[68,4,128]{2,1,0:T(4,128)(2,1)S(1)}, bf16[68,4,128]{2,1,0:T(4,128)(2,1)S(1)}, u32[]{:S(2)}, u32[]{:S(2)}) collective-permute-start(bf16[68,4,128]{2,1,0:T(4,128)(2,1)S(1)} %get-tuple-element.71), channel_id=1, source_target_pairs={{0,24},{8,16},{16,8},{24,0},{1,25},{9,17},{17,9},{25,1},{2,26},{10... | collective-permute-start | bytes 208904 | tf_op jit(solution)/shard_map/ppermute | solution.py:513
  24.3 1.8 %collective-permute-start.7 = (f32[56,128]{1,0:T(8,128)S(1)}, f32[56,128]{1,0:T(8,128)S(1)}, u32[]{:S(2)}, u32[]{:S(2)}) collective-permute-start(f32[56,128]{1,0:T(8,128)S(1)} %get-tuple-element.97), channel_id=1, source_target_pairs={{0,1},{1,0},{2,3},{3,2},{4,5},{5,4},{6,7},{7,6},{8,9},{9,8},{10,11... | collective-permute-start | bytes 86024 | tf_op jit(solution)/shard_map/ppermute | solution.py:644
  26.1 3.3 %collective-permute-start.8 = (f32[56,128]{1,0:T(8,128)S(1)}, f32[56,128]{1,0:T(8,128)S(1)}, u32[]{:S(2)}, u32[]{:S(2)}) collective-permute-start(f32[56,128]{1,0:T(8,128)S(1)} %add.22), channel_id=1, source_target_pairs={{0,3},{1,2},{2,1},{3,0},{4,7},{5,6},{6,5},{7,4},{8,11},{9,10},{10,... | collective-permute-start | bytes 86024 | tf_op jit(solution)/shard_map/ppermute | solution.py:644
  29.4 5.0 %collective-permute-start.9 = (f32[56,128]{1,0:T(8,128)S(1)}, f32[56,128]{1,0:T(8,128)S(1)}, u32[]{:S(2)}, u32[]{:S(2)}) collective-permute-start(f32[56,128]{1,0:T(8,128)S(1)} %add.23), channel_id=1, source_target_pairs={{0,5},{1,4},{2,7},{3,6},{4,1},{5,0},{6,3},{7,2},{8,13},{9,12},{10,... | collective-permute-start | bytes 86024 | tf_op jit(solution)/shard_map/ppermute | solution.py:644
  31.4 7.4 %collective-permute-start.11 = (bf16[1,208,128]{2,1,0:T(8,128)(2,1)S(1)}, bf16[1,208,128]{2,1,0:T(8,128)(2,1)S(1)}, u32[]{:S(2)}, u32[]{:S(2)}) collective-permute-start(bf16[1,208,128]{2,1,0:T(8,128)(2,1)S(1)} %get-tuple-element.110), channel_id=1, source_target_pairs={{0,8},{8,0},{16,24},{24,16},{1,9},{9,1},{17,25},{25,17},{2,10},{10... | collective-permute-start | bytes 159752 | tf_op jit(solution)/shard_map/ppermute | solution.py:649
  32.9 5.9 %collective-permute-start.12 = (bf16[1,208,128]{2,1,0:T(8,128)(2,1)S(1)}, bf16[1,208,128]{2,1,0:T(8,128)(2,1)S(1)}, u32[]{:S(2)}, u32[]{:S(2)}) collective-permute-start(bf16[1,208,128]{2,1,0:T(8,128)(2,1)S(1)} %get-tuple-element.111), channel_id=1, source_target_pairs={{0,24},{8,16},{16,8},{24,0},{1,25},{9,17},{17,9},{25,1},{2,26},{10... | collective-permute-start | bytes 159752 | tf_op jit(solution)/shard_map/ppermute | solution.py:649
  34.4 3.7 %collective-permute-start.10 = (f32[56,128]{1,0:T(8,128)S(1)}, f32[56,128]{1,0:T(8,128)S(1)}, u32[]{:S(2)}, u32[]{:S(2)}) collective-permute-start(f32[56,128]{1,0:T(8,128)S(1)} %add.24), channel_id=1, source_target_pairs={{0,9},{1,8},{2,11},{3,10},{4,13},{5,12},{6,15},{7,14},{8,1},{9,0},... | collective-permute-start | bytes 86024 | tf_op jit(solution)/shard_map/ppermute | solution.py:644
  38.1 3.3 %collective-permute-start.13 = (f32[56,128]{1,0:T(8,128)S(1)}, f32[56,128]{1,0:T(8,128)S(1)}, u32[]{:S(2)}, u32[]{:S(2)}) collective-permute-start(f32[56,128]{1,0:T(8,128)S(1)} %add.25.x_ref), channel_id=1, source_target_pairs={{0,17},{1,16},{2,19},{3,18},{4,21},{5,20},{6,23},{7,22},{8,25},{9,... | collective-permute-start | bytes 86024 | tf_op jit(solution)/shard_map/ppermute | solution.py:644
  (7 other events, 92.0 us)

commit v5 on v4

--- a/solution.py
+++ b/solution.py
@@ -49,14 +49,9 @@
     per = GROUP // file_rows
     rows = channels * GROUP
     out = {}
-    for name, width in (("", block), ("_halo", cdiv(block, LANES) * LANES)):
-        at = np.arange(per * width)
-        part, inside = at // width, at % width
-        ok = inside < block
-        color = np.where(ok, inside % colors, -1)
-        row = np.where(ok, part * file_rows + inside // colors, -1)
-        out["spread" + name] = color[None, :] == np.arange(colors)[:, None]
-        out["keep" + name] = row[None, :] == (np.arange(rows) % GROUP)[:, None]
+    at = np.arange(per * block)
+    out["spread"] = (at % colors)[None, :] == np.arange(colors)[:, None]
+    out["keep"] = (at // colors)[None, :] == (np.arange(rows) % GROUP)[:, None]
     out["tall"] = (np.arange(rows) // GROUP)[:, None] == np.arange(channels)[None, :]
     inner = 8 * height
     count = side * side
@@ -80,18 +75,17 @@
     for n in range(3):
         pick[n, colors + 1 + n] = True
     out["pick"] = np.concatenate(list(pick), axis=1)
-    return {k: jnp.asarray(v, f32 if k in ("forward", "backward", "band", "fringe") else bf16) for k, v in out.items()}
-
-
-def params_kernel(wt_ref, taps_ref, bias_ref, gain_ref, off_ref, koff_ref, spread_ref, keep_ref, spread_h_ref,
-                  keep_h_ref, tall_ref, forward_ref, backward_ref, wk_ref, wh_ref, kb_ref, kf_ref, vec_ref):
+    return {k: jnp.asarray(v, f32 if k in ("band", "fringe") else bf16) for k, v in out.items()}
+
+
+def params_kernel(wt_ref, taps_ref, bias_ref, gain_ref, off_ref, koff_ref, spread_ref, keep_ref, tall_ref, forward_ref,
+                  backward_ref, wk_ref, kb_ref, kf_ref, vec_ref):
     channels = wt_ref.shape[1]
-    for spread, keep, out_ref in ((spread_ref, keep_ref, wk_ref), (spread_h_ref, keep_h_ref, wh_ref)):
-        wide = mm(wt_ref[...], spread[...], TN).astype(bf16)
-        out_ref[...] = mm(tall_ref[...], wide).astype(bf16) * keep[...]
+    wide = mm(wt_ref[...], spread_ref[...], TN).astype(bf16)
+    wk_ref[...] = mm(tall_ref[...], wide).astype(bf16) * keep_ref[...]
+    parts = split2(taps_ref[...])
     for place, out_ref in ((forward_ref, kf_ref), (backward_ref, kb_ref)):
-        out_ref[...] = lax.dot_general(taps_ref[...], place[...], TN, precision=lax.Precision.HIGHEST,
-                                       preferred_element_type=f32)
+        out_ref[...] = sum(mm(part, place[...], TN) for part in parts)
     eye = iota((channels, channels), 0) == iota((channels, channels), 1)
     for n, ref in enumerate((bias_ref, gain_ref, off_ref, koff_ref)):
         row = jnp.broadcast_to(ref[...].reshape(1, channels), (channels, channels))
@@ -110,17 +104,6 @@
     load_cot = pltpu.make_async_copy(cot_hbm, cot_ref, sems.at[1])
     load_x.start()
     load_cot.start()
-    load_cot.wait()
-
-    row, lane = iota((8, LANES), 0), iota((8, LANES), 1)
-    pick = one_hot(((row < 3) & (lane == row)) | ((row >= 3) & (row < 6) & (lane == row + LANES - 6)))
-    edges = mm(pick, cot_ref[...].reshape(channels * height, LANES), NT)
-    edges = jnp.concatenate(
-        [edges[:, n:n + LANES] for n in range(0, channels * height, LANES)], axis=0).astype(bf16)
-    edge_ref[:edges.shape[0]] = edges
-    edge_ref[edges.shape[0]:] = edges[:edge_ref.shape[0] - edges.shape[0]]
-    give_ref[chips * block_rows:, :] = edges
-
     row, src = iota((block, block), 0), iota((block, block), 1)
     part = sum((row >= colors * n).astype(jnp.int32) for n in range(1, file_rows)) if file_rows > 1 else 0
     move = one_hot(src == (row - colors * part) * file_rows + part)
@@ -163,6 +146,17 @@
                 give_ref[start:start + block, :] = tile
                 give_ref[start + block:start + block_rows, :] = halo(d)
 
+    load_cot.wait()
+
+    row, lane = iota((8, LANES), 0), iota((8, LANES), 1)
+    pick = one_hot(((row < 3) & (lane == row)) | ((row >= 3) & (row < 6) & (lane == row + LANES - 6)))
+    edges = mm(pick, cot_ref[...].reshape(channels * height, LANES), NT)
+    edges = jnp.concatenate(
+        [edges[:, n:n + LANES] for n in range(0, channels * height, LANES)], axis=0).astype(bf16)
+    edge_ref[:edges.shape[0]] = edges
+    edge_ref[edges.shape[0]:] = edges[:edge_ref.shape[0] - edges.shape[0]]
+    give_ref[chips * block_rows:, :] = edges
+
 
 def pair_kernel(keep_ref, got_ref, *pair_refs):
     _, block_rows, _ = keep_ref.shape
@@ -179,14 +173,19 @@
     far = far_ref[:size, :].astype(f32)
     left = jnp.where(core == 0, far, near)
     right = jnp.where(core == 0, near, far)
-    left = jnp.concatenate([left[n:n + 8] for n in range(0, size, 8)], axis=1).astype(bf16)
-    right = jnp.concatenate([right[n:n + 8] for n in range(0, size, 8)], axis=1).astype(bf16)
+    sides = jnp.concatenate(
+        [jnp.concatenate([side[n:n + 8] for n in range(0, size, 8)], axis=1) for side in (left, right)], axis=0)
+    row, lane = iota((16, width), 0), iota((16, width), 1)
+    from_left = (row >= 3) & (row < 6) & (lane == row + width - 6) & (at_ref[4, 0] == 0)
+    from_right = (row >= 8) & (row < 11) & (lane == row - 8) & (at_ref[5, 0] == 0)
+    halo = mm(sides.astype(bf16), one_hot(from_left | from_right), TN).reshape(channels, height, width)
+    halo_ref[...] = halo.astype(bf16)
+    write_strips(at_ref, cot_ref[...].astype(f32), halo, one_ref, two_ref)
+
+
+def write_strips(at_ref, own, halo, one_ref, two_ref):
+    channels, height, width = own.shape
     row, lane = iota((8, width), 0), iota((8, width), 1)
-    from_left = one_hot((row >= 3) & (row < 6) & (lane == row + width - 6) & (at_ref[4, 0] == 0))
-    from_right = one_hot((row < 3) & (lane == row) & (at_ref[5, 0] == 0))
-    halo = (mm(left, from_left, TN) + mm(right, from_right, TN)).reshape(channels, height, width)
-    halo_ref[...] = halo.astype(bf16)
-    own = cot_ref[...].astype(f32)
     pick = one_hot((lane == row + width - 3) & (row < 3) | (lane == row - 3) & (row >= 3) & (row < 6))
     up, down = own[:, :4], own[:, height - 4:]
     up_halo, down_halo = halo[:, :4], halo[:, height - 4:]
@@ -202,6 +201,30 @@
                 ref[channels + n // 64 + q] = dense[4 * q:4 * q + 4, n:n + LANES].astype(bf16)
 
 
+def read_strips(at_ref, one_ref, two_ref, plane_ref, halo_ref):
+    channels, _, width = plane_ref.shape
+    even = at_ref[6, 0] == 0
+    one, two = one_ref[...].astype(f32), two_ref[...].astype(f32)
+    top = jnp.where(at_ref[2, 0] == 0, jnp.where(even, two, one), 0.0)
+    bot = jnp.where(at_ref[3, 0] == 0, jnp.where(even, one, two), 0.0)
+    row, lane = iota((8, width), 0), iota((8, width), 1)
+    place = one_hot((lane == row + width - 3) & (row < 3) | (lane == row - 3) & (row >= 3) & (row < 6))
+
+    def beside(part):
+        dense = jnp.concatenate(
+            [
+                jnp.concatenate([part[channels + n // 64 + q] for q in range(2)], axis=0)
+                for n in range(0, channels * 4, LANES)
+            ],
+            axis=1,
+        )
+        return mm(dense.astype(bf16), place, TN).reshape(channels, 4, width)
+
+    none = jnp.zeros((channels, 4, width), f32)
+    plane_ref[...] = jnp.concatenate([none, top[:channels], bot[:channels], none], axis=1).astype(bf16)
+    halo_ref[...] = jnp.concatenate([none, beside(top), beside(bot), none], axis=1).astype(bf16)
+
+
 def shifted(center, halo):
     rows, width = center.shape
     lane = iota((rows, width), 1)
@@ -253,26 +276,7 @@
 def back_outer_kernel(factor, at_ref, one_ref, two_ref, grad_ref, kb_ref, fringe_ref,
                       stack_ref, edge_ref, plane_ref, halo_ref):
     channels, height, width = grad_ref.shape
-    even = at_ref[6, 0] == 0
-    one, two = one_ref[...].astype(f32), two_ref[...].astype(f32)
-    top = jnp.where(at_ref[2, 0] == 0, jnp.where(even, two, one), 0.0)
-    bot = jnp.where(at_ref[3, 0] == 0, jnp.where(even, one, two), 0.0)
-    row, lane = iota((8, width), 0), iota((8, width), 1)
-    place = one_hot((lane == row + width - 3) & (row < 3) | (lane == row - 3) & (row >= 3) & (row < 6))
-
-    def beside(part):
-        dense = jnp.concatenate(
-            [
-                jnp.concatenate([part[channels + n // 64 + q] for q in range(2)], axis=0)
-                for n in range(0, channels * 4, LANES)
-            ],
-            axis=1,
-        )
-        return mm(dense.astype(bf16), place, TN).reshape(channels, 4, width)
-
-    none = jnp.zeros((channels, 4, width), f32)
-    plane_ref[...] = jnp.concatenate([none, top[:channels], bot[:channels], none], axis=1).astype(bf16)
-    halo_ref[...] = jnp.concatenate([none, beside(top), beside(bot), none], axis=1).astype(bf16)
+    read_strips(at_ref, one_ref, two_ref, plane_ref, halo_ref)
 
     def one(k, carry):
         stack = shifted(plane_ref[k], halo_ref[k])
@@ -298,19 +302,13 @@
 
 
 def order_kernel(at_ref, *refs):
-    pair_refs, (x_ref, one_ref, two_ref) = refs[:-3], refs[-3:]
+    pair_refs, x_ref = refs[:-1], refs[-1]
     chips = len(pair_refs)
     core, chip = at_ref[0, 0], at_ref[1, 0]
     for away, ref in enumerate(pair_refs):
         there = lax.bitwise_xor(chip, away)
         x_ref[2 * there + core] = ref[0 if away == 0 else 1]
         x_ref[2 * there + 1 - core] = ref[1 if away == 0 else 0]
-    half = one_ref.shape[0]
-    up = x_ref[:half]
-    down = x_ref[2 * chips - half:]
-    even = at_ref[6, 0] == 0
-    one_ref[...] = jnp.where(even, down, up)
-    two_ref[...] = jnp.where(even, up, down)
 
 
 def main_kernel(colors, file_rows, factor, x_ref, wk_ref, vec_ref, grad_ref, edge_ref, total_ref, stack_ref, rim_ref,
@@ -324,7 +322,7 @@
     shift_part = jnp.zeros((channels, GROUP, width), f32)
     inner = 8 * height
     ones = jnp.where(iota((16, width), 0) == 0, 1.0, 0.0).astype(bf16)
-    by_color = jnp.zeros((colors + 16, channels), f32)
+    by_color = jnp.zeros((channels, colors + 16), f32)
     for g in range(height // GROUP):
         blocks = [x_ref[per * g + a, :block, :] for a in range(per)]
         patch = mm(wk_ref[...], jnp.concatenate(blocks, axis=0)).reshape(channels, GROUP, width) + bias
@@ -347,25 +345,34 @@
             start = h % file_rows * colors
             left.append(jnp.concatenate([blocks[h // file_rows][start:start + colors], ones], axis=0))
             right.append(grad_s[g, pl.ds(h, channels, stride=GROUP), :].astype(bf16))
-        by_color += mm(jnp.concatenate(left, axis=1), jnp.concatenate(right, axis=1), NT)
-
-    def one(k, carry):
-        plane = norm_s[k].astype(bf16)
-        norm_ref[k] = plane
-        both = mm(plane, jnp.concatenate([stack_ref[k], rim_ref[k]], axis=0), NT)
-        cross = both[:, :inner]
-        total = cross[:8] * band_ref[:8]
-        for a in range(1, height // 8):
-            rows = cross[8 * a:8 * a + 8]
-            if a == height // 8 - 1:
-                rows = rows * band_ref[8 * a:]
-            total += pltpu.roll(rows, inner - 8 * a, 1)
-        cross = both[:, inner:]
-        rim = cross[:8] * fringe_ref[:8] + pltpu.roll(cross[height - 8:] * fringe_ref[8:], 8, 1)
-        diag_s[k] = jnp.concatenate([total, rim], axis=1)
+        by_color += mm(jnp.concatenate(right, axis=1), jnp.concatenate(left, axis=1), NT)
+
+    band, fringe = band_ref[...], fringe_ref[...]
+    none = jnp.zeros((height, width), bf16)
+
+    def one(n, carry):
+        planes, stacks = [], []
+        for m in range(2):
+            k = 2 * n + m
+            plane = norm_s[k].astype(bf16)
+            norm_ref[k] = plane
+            planes.append(jnp.concatenate([plane, none] if m == 0 else [none, plane], axis=1))
+            stacks.append(jnp.concatenate([stack_ref[k], rim_ref[k]], axis=0))
+        both = mm(jnp.concatenate(planes, axis=0), jnp.concatenate(stacks, axis=1), NT)
+        for m in range(2):
+            cross = both[m * height:(m + 1) * height, :inner]
+            total = cross[:8] * band[:8]
+            for a in range(1, height // 8):
+                rows = cross[8 * a:8 * a + 8]
+                if a == height // 8 - 1:
+                    rows = rows * band[8 * a:]
+                total += pltpu.roll(rows, inner - 8 * a, 1)
+            cross = both[m * height:(m + 1) * height, inner:]
+            rim = cross[:8] * fringe[:8] + pltpu.roll(cross[height - 8:] * fringe[8:], 8, 1)
+            diag_s[2 * n + m] = jnp.concatenate([total, rim], axis=1)
         return carry
 
-    lax.fori_loop(0, channels, one, 0, unroll=UNROLL)
+    lax.fori_loop(0, channels // 2, one, 0, unroll=UNROLL // 2)
 
     line, rim = diag_s[:, 0, :inner], diag_s[:, 0, inner:]
     for b in range(1, 8):
@@ -376,41 +383,37 @@
     out_ref[...] = sum(mm(taps_ref[...], part, NT) for part in split2(line))
     parts = jnp.concatenate([jnp.sum(scale_part, axis=1), jnp.sum(shift_part, axis=1), total_ref[...]], axis=1)
     first = sum(mm(pick_ref[...], part, NT) for part in split2(parts))
-    out_ref[:, :channels] = first + by_color[:56]
-
-
-def side_columns(at_ref, wh_ref, vec_ref, lines, row_ok):
-    channels = vec_ref.shape[1]
-    shape = (channels, GROUP, LANES)
-    bias, gain, offset = per_row(vec_ref, 0), per_row(vec_ref, 1), per_row(vec_ref, 2)
-    lines.append(jnp.zeros((LANES - 8 * len(lines), wh_ref.shape[1]), f32))
-    lines = jnp.concatenate(lines, axis=0).astype(bf16)
-    xhat, _ = layer_norm(mm(wh_ref[...], lines, NT).reshape(shape) + bias, channels)
-    column = lax.bitwise_and(iota(shape, 2), 7)
-    ok = jnp.where(column < 3, 1 - at_ref[4, 0], 1 - at_ref[5, 0]) > 0
-    if row_ok is not None:
-        ok = ok & row_ok
-    return jnp.where(ok, xhat * gain + offset, 0.0).astype(bf16).reshape(channels * GROUP, LANES)
-
-
-def side_line(pieces, chunks):
-    pieces = [piece.astype(f32) for piece in pieces]
-    return jnp.concatenate([piece[8 * c:8 * c + 8] for piece in pieces for c in range(chunks)], axis=1)
-
-
-def stem_side_kernel(colors, file_rows, at_ref, x_ref, wh_ref, vec_ref, halo_ref):
+    out_ref[:, :channels] = first + by_color.T[:56]
+
+
+def side_line(pieces, block):
+    parts = []
+    for piece in pieces:
+        piece = piece.astype(f32)
+        for start in range(0, block, LANES):
+            at = start // LANES * 8
+            parts.append(piece[at:at + 8, :min(LANES, block - start)])
+    return jnp.concatenate(parts, axis=1)
+
+
+def stem_side_kernel(colors, file_rows, at_ref, x_ref, norm_ref, wk_ref, vec_ref, halo_ref, one_ref, two_ref):
     channels, height, width = halo_ref.shape
     block = colors * file_rows
     per = GROUP // file_rows
-    chunks = wh_ref.shape[1] // (per * LANES)
     groups = height // GROUP
-    lines = [
-        side_line([x_ref[per * g + a, block:block + 16, :] for a in range(per)], chunks) for g in range(groups)
-    ]
-    halo = side_columns(at_ref, wh_ref, vec_ref, lines, None)
+    shape = (channels, GROUP, LANES)
+    bias, gain, offset = per_row(vec_ref, 0), per_row(vec_ref, 1), per_row(vec_ref, 2)
+    lines = [side_line([x_ref[per * g + a, block:block + 16, :] for a in range(per)], block) for g in range(groups)]
+    lines.append(jnp.zeros((LANES - 8 * groups, wk_ref.shape[1]), f32))
+    lines = jnp.concatenate(lines, axis=0).astype(bf16)
+    xhat, _ = layer_norm(mm(wk_ref[...], lines, NT).reshape(shape) + bias, channels)
+    column = lax.bitwise_and(iota(shape, 2), 7)
+    ok = jnp.where(column < 3, 1 - at_ref[4, 0], 1 - at_ref[5, 0]) > 0
+    halo = jnp.where(ok, xhat * gain + offset, 0.0).astype(bf16).reshape(channels * GROUP, LANES)
     for g in range(groups):
         moved = pltpu.roll(halo, width - 8 * g - 3, 1).reshape(channels, GROUP, width)
         halo_ref[:, 8 * g:8 * g + 8, :] = moved
+    write_strips(at_ref, norm_ref[...].astype(f32), halo_ref[...].astype(f32), one_ref, two_ref)
 
 
 def stem_inner_kernel(start, norm_ref, side_ref, kf_ref, vec_ref, band_ref, out_ref):
@@ -422,35 +425,13 @@
         out_ref[n] = both[:height] + both[height:] + vec_ref[3, pl.ds(k, 1), :]
         return carry
 
-    lax.fori_loop(0, count, one, 0, unroll=UNROLL)
-
-
-def stem_outer_kernel(colors, file_rows, parts, at_ref, one_ref, two_ref, wk_ref, wh_ref, vec_ref, kf_ref, fringe_ref,
-                      *refs):
+    lax.fori_loop(0, count, one, 0, unroll=min(UNROLL, count))
+
+
+def stem_outer_kernel(parts, at_ref, one_ref, two_ref, kf_ref, fringe_ref, *refs):
     inner_refs, (out_ref, plane_s, halo_s, out_s, sems) = refs[:parts], refs[parts:]
-    channels, height, width = out_s.shape
-    block = colors * file_rows
-    per = GROUP // file_rows
-    half = per // 2
-    chunks = wh_ref.shape[1] // (per * LANES)
-    shape = (channels, GROUP, width)
-    bias, gain, offset = per_row(vec_ref, 0), per_row(vec_ref, 1), per_row(vec_ref, 2)
-    row_ok = jnp.where(iota(shape, 1) < 4, 1 - at_ref[3, 0], 1 - at_ref[2, 0]) > 0
-
-    even = at_ref[6, 0] == 0
-    one, two = one_ref[...], two_ref[...]
-    top, bot = jnp.where(even, two, one), jnp.where(even, one, two)
-    blocks = [bot[a] for a in range(half)] + [top[a] for a in range(half)]
-    pixels = jnp.concatenate([piece[:block] for piece in blocks], axis=0)
-    xhat, _ = layer_norm(mm(wk_ref[...], pixels).reshape(shape) + bias, channels)
-    rows = jnp.where(row_ok, xhat * gain + offset, 0.0).astype(bf16)
-    line = side_line([piece[block:block + 16] for piece in blocks], chunks)
-    side = side_columns(at_ref, wh_ref, vec_ref, [line], row_ok)
-    side = pltpu.roll(side, width - 3, 1).reshape(shape)
-    for start in (0, 8):
-        plane_s[:, start:start + 8, :] = rows
-        halo_s[:, start:start + 8, :] = side
-
+    channels, height, _ = out_s.shape
+    read_strips(at_ref, one_ref, two_ref, plane_s, halo_s)
     count = channels // parts
     copies = []
     for part, inner_ref in enumerate(inner_refs):
@@ -463,7 +444,7 @@
                 [own[:8] + edge[:8], own[8:height - 8], own[height - 8:] + edge[8:]], axis=0).astype(bf16)
             return carry
 
-        lax.fori_loop(0, count, one, 0, unroll=UNROLL)
+        lax.fori_loop(0, count, one, 0, unroll=min(UNROLL, count))
         here = pl.ds(part * count, count)
         copies.append(pltpu.make_async_copy(out_s.at[here], out_ref.at[here], sems.at[part]))
         copies[-1].start()
@@ -471,8 +452,9 @@
         copy.wait()
 
 
-def last_kernel(colors, x_ref, y_ref, *outs):
-    total = x_ref[...] + y_ref[...]
+def last_kernel(colors, *refs):
+    parts, outs = refs[:-6], refs[-6:]
+    total = sum(part[...] for part in parts)
     channels = outs[1].shape[0]
     first = total[:, :channels]
     second = total[:, channels:2 * channels]
@@ -530,7 +512,6 @@
     block = colors * file_rows
     per = GROUP // file_rows
     block_rows = block + 16
-    padded = cdiv(block, LANES) * LANES
     rows = channels * GROUP
     tile = (channels, height, width)
     inner = 8 * height
@@ -538,10 +519,8 @@
 
     row_at, col_at = lax.axis_index("rows"), lax.axis_index("cols")
     chips = n_cols // 2
-    at = jnp.stack([
-        col_at % 2, col_at // 2, row_at == 0, row_at == n_rows - 1, col_at == 0, col_at == n_cols - 1, row_at % 2, 0,
-    ]).astype(jnp.int32)
-    at = jnp.broadcast_to(at[:, None], (8, LANES))
+    at = (col_at % 2, col_at // 2, row_at == 0, row_at == n_rows - 1, col_at == 0, col_at == n_cols - 1, row_at % 2)
+    at = sum(jnp.where(iota((8, LANES), 0) == n, x.astype(jnp.int32), 0) for n, x in enumerate(at))
     vmem = pl.BlockSpec(memory_space=pltpu.VMEM)
     edge_rows = channels * height // 16
 
@@ -584,19 +563,17 @@
     )
     beside, taps = lax.optimization_barrier((beside, kernel))
     strips = swap(strips, "rows")
-    wk, wh, kb, kf, vec = kernel_call(
+    wk, kb, kf, vec = kernel_call(
         params_kernel,
         (
             in_vmem((rows, per * block), bf16),
-            in_vmem((rows, per * padded), bf16),
             in_vmem((channels, inner + 2 * OUTER), f32),
             in_vmem((channels, inner + 2 * OUTER), f32),
             in_vmem((4, channels, LANES), f32),
         ),
         0.01,
         patchify_weight.T, taps.T, patchify_bias, norm_gain, norm_offset_vector, kernel_offset,
-        const["spread"], const["keep"], const["spread_halo"], const["keep_halo"], const["tall"],
-        const["forward"], const["backward"],
+        const["spread"], const["keep"], const["tall"], const["forward"], const["backward"],
     )
     stack, grad, total = kernel_call(
         functools.partial(back_inner_kernel, factor),
@@ -613,15 +590,8 @@
         scratch_shapes=[pltpu.VMEM((channels, 16, width), bf16)] * 2,
     )
 
-    half = per // 2
     edge, *pairs = lax.optimization_barrier((edge, *pairs))
-    pixels, *ends = kernel_call(
-        order_kernel,
-        (in_vmem((n_cols, block_rows, LANES), bf16),) + (in_vmem((half, block_rows, LANES), bf16),) * 2,
-        0.01,
-        at, *pairs,
-        in_specs=[vmem] + [vmem] * chips,
-    )
+    pixels = kernel_call(order_kernel, in_vmem((n_cols, block_rows, LANES), bf16), 0.01, at, *pairs)
     norm, result = kernel_call(
         functools.partial(main_kernel, colors, file_rows, factor),
         (in_vmem(tile, bf16), in_vmem((56, LANES), f32)),
@@ -635,35 +605,34 @@
     )
 
     size = n_rows * n_cols
-    chunk = channels
-    rounds = (size - 1).bit_length()
-    jobs = {0: ["side"], 1: ["one"], 2: ["two"], 3: [0], rounds - 1: ["outer"]}
+    chunk = channels // 2
+    stages = [[1], [3, 5, 7], [9, 17, 25]]
+    jobs = {0: ["side"], 1: ["one", "two", 0], 2: [1, "outer"]}
     parts = []
-    for n in range(rounds):
-        step = 1 if n == 0 else (1 << n) + 1
-        other = lax.ppermute(result, ("rows", "cols"), [(i, i ^ step) for i in range(size)])
+    for n, steps in enumerate(stages):
+        others = [lax.ppermute(result, ("rows", "cols"), [(i, i ^ step) for i in range(size)]) for step in steps]
         for job in jobs.get(n, []):
             if job in ("one", "two"):
                 which = ("one", "two").index(job)
                 result, end = lax.optimization_barrier((result, ends[which]))
                 ends[which] = lax.ppermute(end, "rows", pairing(n_rows, which))
             elif job == "side":
-                result, pixels = lax.optimization_barrier((result, pixels))
-                beside = kernel_call(
+                result, norm = lax.optimization_barrier((result, norm))
+                beside, *ends = kernel_call(
                     functools.partial(stem_side_kernel, colors, file_rows),
-                    in_vmem(tile, bf16),
+                    (in_vmem(tile, bf16),) + (in_vmem((channels + channels // 16, 4, width), bf16),) * 2,
                     1,
-                    at, pixels, wh, vec,
+                    at, pixels, norm, wk, vec,
                 )
                 result, beside = lax.optimization_barrier((result, beside))
             elif job == "outer":
                 result, *parts = lax.optimization_barrier((result, *parts))
                 stem_output = kernel_call(
-                    functools.partial(stem_outer_kernel, colors, file_rows, len(parts)),
+                    functools.partial(stem_outer_kernel, len(parts)),
                     shaped(tile, bf16),
                     3,
-                    at, *ends, wk, wh, vec, kf, const["fringe"], *parts,
-                    in_specs=[vmem] * (8 + len(parts)),
+                    at, *ends, kf, const["fringe"], *parts,
+                    in_specs=[vmem] * (5 + len(parts)),
                     out_specs=beyond,
                     scratch_shapes=[
                         pltpu.VMEM((channels, 16, width), bf16),
@@ -683,15 +652,15 @@
                 )
                 result, part = lax.optimization_barrier((result, part))
                 parts.append(part)
-        if n < rounds - 1:
-            result = result + other
+        if n < len(stages) - 1:
+            result = sum(others, result)
 
     taps = side * side
     outs = kernel_call(
         functools.partial(last_kernel, colors),
         (shaped((colors, channels), f32),) + (shaped((channels,), f32),) * 4 + (shaped((taps, channels), f32),),
         1,
-        result, other,
+        result, *others,
     )
     return (stem_output, outs[0].T, outs[1], outs[2], outs[3], outs[5].T, outs[4])
 

time: 42.2 us -> 39.5 us (0.936)
  waiting for transfers between devices: 5.25 us -> 2.66 us
  Pallas kernels: 16.5 us -> 15.3 us
  starting transfers between devices: 19.1 us -> 20.2 us
    ppermute x5 -> x7, waiting for transfers between devices: 3.48 us -> 0.44 us  [per_device(): lax.ppermute(result, ('rows', 'cols'), [(i, i ^ step) for i in range(size)])]
    ppermute x5 -> x7, starting transfers between devices: 6.05 us -> 7.51 us  [per_device(): lax.ppermute(result, ('rows', 'cols'), [(i, i ^ step) for i in range(size)])]
    pallas_call x12 -> x13, Pallas kernels: 16.5 us -> 15.3 us  [kernel_call(): pl.pallas_call(body, out_shape=out_shape, compiler_params=pltpu.CompilerP...]
    ppermute x2, waiting for transfers between devices: 1.68 us -> 2.14 us  [swap(): lax.ppermute(part, axis, pairing(lax.axis_size(axis), n))]
  transfers between devices with their start and end apart: 14 -> 16, of which waited for: 6 -> 3; matrix products, arithmetic and copies ran while one was open for 0% -> 0% of each run, Pallas kernels for 21% -> 21%
where the time goes in v5:
time: 39.5 us; the launch traced here: 39.4 us
  starting transfers between devices  20.2 us (51%)
  Pallas kernels  15.3 us (39%)
  waiting for transfers between devices  2.66 us (7%)
  between operations  1.02 us (3%)
    pallas_call x13, Pallas kernels, kernel_call(): pl.pallas_call(body, out_shape=out_shape, compiler_params=pltpu.CompilerP...  15.3 us
    ppermute x7, starting transfers between devices, per_device(): lax.ppermute(result, ('rows', 'cols'), [(i, i ^ step) for i in range(size)])  7.51 us
    ppermute x1, starting transfers between devices, per_device(): far = lax.ppermute(edges, 'cols', pairing(n_cols, 1))  4.71 us
    ppermute x2, starting transfers between devices, swap(): lax.ppermute(part, axis, pairing(lax.axis_size(axis), n))  3.01 us
    ppermute x2, starting transfers between devices, per_device(): ends[which] = lax.ppermute(end, 'rows', pairing(n_rows, which))  2.64 us
    ppermute x2, waiting for transfers between devices, swap(): lax.ppermute(part, axis, pairing(lax.axis_size(axis), n))  2.14 us
    ppermute x3, starting transfers between devices, per_device(): lax.ppermute(pairs[n], 'cols', [(i, i ^ 2 * n + 1) for i in range(n_cols)])  1.82 us
  transfers between devices with their start and end apart: 16, of which 3 were waited for; matrix products, arithmetic and copies ran while one was open for 0% of the time, Pallas kernels for 21%

profile of v5, /device:TPU:0, one launch (start us, length us, event | category | flops | bytes accessed | tf_op | source)
XLA Modules:
  0.0 39.4 jit_solution(16551005425365833169)
XLA Ops:
  0.9 1.9 %shard_map.216 = (bf16[64,32,128]{2,1,0:T(8,128)(2,1)S(1)}, bf16[4,208,128]{2,1,0:T(8,128)(2,1)S(1)}, bf16[960,128]{1,0:T(8,128)(2,1)S(1)}, bf16[176,128]{1,0:T(8,128)(2,1)S(1)}) custom-call(s32[8,128]{1,0:T(8,128)S(1)} %iota.37.at_ref, bf16[48,4,1024]{2,1,0:T(4,128)(2,1)} %x_hbm.1, bf16[64,32,128]{2,1,0:T(8,128)(2,1)} %cot_hbm.1), custom_call_target="tpu_custom_call" | custom-call | flops 2000000000 | bytes 6000000 | tf_op jit(solution)/shard_map/pallas_call | solution.py:477
  2.8 0.5 %collective-permute-start = (bf16[960,128]{1,0:T(8,128)(2,1)S(1)}, bf16[960,128]{1,0:T(8,128)(2,1)S(1)}, u32[]{:S(2)}, u32[]{:S(2)}) collective-permute-start(bf16[960,128]{1,0:T(8,128)(2,1)S(1)} %get-tuple-element.69), channel_id=1, source_target_pairs={{0,1},{1,0},{2,3},{3,2},{4,5},{5,4},{6,7},{7,6},{8,9},{9,8},{10,11... | collective-permute-start | bytes 737288 | tf_op jit(solution)/shard_map/ppermute | solution.py:547
  3.3 4.7 %collective-permute-start.1 = (bf16[176,128]{1,0:T(8,128)(2,1)S(1)}, bf16[176,128]{1,0:T(8,128)(2,1)S(1)}, u32[]{:S(2)}, u32[]{:S(2)}) collective-permute-start(bf16[176,128]{1,0:T(8,128)(2,1)S(1)} %get-tuple-element.72), channel_id=1, source_target_pairs={{0,7},{1,2},{2,1},{3,4},{4,3},{5,6},{6,5},{7,0},{8,15},{9,10},{10,... | collective-permute-start | bytes 135176 | tf_op jit(solution)/shard_map/ppermute | solution.py:548
  8.1 1.7 %collective-permute-start.5 = (bf16[2,208,128]{2,1,0:T(8,128)(2,1)S(1)}, bf16[2,208,128]{2,1,0:T(8,128)(2,1)S(1)}, u32[]{:S(2)}, u32[]{:S(2)}) collective-permute-start(bf16[2,208,128]{2,1,0:T(8,128)(2,1)S(1)} %get-tuple-element.84), channel_id=1, source_target_pairs={{0,5},{1,4},{2,7},{3,6},{4,1},{5,0},{6,3},{7,2},{8,13},{9,12},{10,... | collective-permute-start | bytes 319496 | tf_op jit(solution)/shard_map/ppermute | solution.py:551
  10.0 0.6 %shard_map.218 = (bf16[64,32,128]{2,1,0:T(8,128)(2,1)S(1)}, bf16[68,4,128]{2,1,0:T(4,128)(2,1)S(1)}, bf16[68,4,128]{2,1,0:T(4,128)(2,1)S(1)}) custom-call(s32[8,128]{1,0:T(8,128)S(1)} %iota.37.at_ref, bf16[64,32,128]{2,1,0:T(8,128)(2,1)S(1)} %get-tuple-element.68.cot_ref, bf16[960,128]{1,0:T(8,128)(2,1)S(1)} %collective-permute-done.got_ref.near_ref, ...), custom_call_target="tpu_custom_call" | custom-call | flops 10000000 | bytes 30000 | tf_op jit(solution)/shard_map/pallas_call | solution.py:477
  10.6 1.5 %collective-permute-start.2 = (bf16[68,4,128]{2,1,0:T(4,128)(2,1)S(1)}, bf16[68,4,128]{2,1,0:T(4,128)(2,1)S(1)}, u32[]{:S(2)}, u32[]{:S(2)}) collective-permute-start(bf16[68,4,128]{2,1,0:T(4,128)(2,1)S(1)} %get-tuple-element.74), channel_id=1, source_target_pairs={{0,8},{8,0},{16,24},{24,16},{1,9},{9,1},{17,25},{25,17},{2,10},{10... | collective-permute-start | bytes 208904 | tf_op jit(solution)/shard_map/ppermute | solution.py:495
  12.1 1.5 %collective-permute-start.3 = (bf16[68,4,128]{2,1,0:T(4,128)(2,1)S(1)}, bf16[68,4,128]{2,1,0:T(4,128)(2,1)S(1)}, u32[]{:S(2)}, u32[]{:S(2)}) collective-permute-start(bf16[68,4,128]{2,1,0:T(4,128)(2,1)S(1)} %get-tuple-element.75), channel_id=1, source_target_pairs={{0,24},{8,16},{16,8},{24,0},{1,25},{9,17},{17,9},{25,1},{2,26},{10... | collective-permute-start | bytes 208904 | tf_op jit(solution)/shard_map/ppermute | solution.py:495
  14.2 1.7 %shard_map.220 = (bf16[64,256,128]{2,1,0:T(8,128)(2,1)S(1)}, f32[64,32,128]{2,1,0:T(8,128)S(1)}, f32[64,128]{1,0:T(8,128)S(1)}) custom-call(bf16[64,32,128]{2,1,0:T(8,128)(2,1)S(1)} %get-tuple-element.68.cot_ref, bf16[64,32,128]{2,1,0:T(8,128)(2,1)S(1)} %get-tuple-element.77.beside_ref, f32[64,512]{1,0:T(8,128)S(1)} %get-tuple-element.79.kb_ref, ...), custom_call_target="tpu_custom_call" | custom-call | flops 10000000 | bytes 30000 | tf_op jit(solution)/shard_map/pallas_call | solution.py:477
  15.9 2.1 %collective-permute-done.3.two_ref = bf16[68,4,128]{2,1,0:T(4,128)(2,1)S(1)} collective-permute-done((bf16[68,4,128]{2,1,0:T(4,128)(2,1)S(1)}, bf16[68,4,128]{2,1,0:T(4,128)(2,1)S(1)}, u32[]{:S(2)}, u32[]{:S(2)}) %collective-permute-start.3) | collective-permute-done | bytes 69664 | tf_op jit(solution)/shard_map/ppermute | solution.py:495
  18.1 1.0 %shard_map.221 = (bf16[64,128,128]{2,1,0:T(8,128)(2,1)S(1)}, f32[64,16,128]{2,1,0:T(8,128)S(1)}) custom-call(s32[8,128]{1,0:T(8,128)S(1)} %iota.37.at_ref, bf16[68,4,128]{2,1,0:T(4,128)(2,1)S(1)} %collective-permute-done.2.one_ref, bf16[68,4,128]{2,1,0:T(4,128)(2,1)S(1)} %collective-permute-done.3.two_ref, f32[64,32,128]{2,1,0:T(8,128)S(1)} %get-tuple-element.80.grad_ref, ...), custom_call_target="tpu_custom_call" | custom-call | flops 10000000 | bytes 30000 | tf_op jit(solution)/shard_map/pallas_call | solution.py:477
  19.2 4.3 %shard_map.223 = (bf16[64,32,128]{2,1,0:T(8,128)(2,1)S(1)}, f32[56,128]{1,0:T(8,128)S(1)}) custom-call(bf16[8,208,128]{2,1,0:T(8,128)(2,1)S(1)} %shard_map.222.x_ref, bf16[512,384]{1,0:T(8,128)(2,1)S(1)} %get-tuple-element.90.wk_ref, f32[4,64,128]{2,1,0:T(8,128)S(1)} %get-tuple-element.91.vec_ref, f32[64,32,128]{2,1,0:T(8,128)S(1)} %get-tuple-element.80.grad_ref, ...), custom_call_target="tpu_custom_call" | custom-call | flops 6000000000 | bytes 18000000 | tf_op jit(solution)/shard_map/pallas_call | solution.py:477
  23.5 0.9 %collective-permute-start.7 = (f32[56,128]{1,0:T(8,128)S(1)}, f32[56,128]{1,0:T(8,128)S(1)}, u32[]{:S(2)}, u32[]{:S(2)}) collective-permute-start(f32[56,128]{1,0:T(8,128)S(1)} %get-tuple-element.101), channel_id=1, source_target_pairs={{0,1},{1,0},{2,3},{3,2},{4,5},{5,4},{6,7},{7,6},{8,9},{9,8},{10,11... | collective-permute-start | bytes 86024 | tf_op jit(solution)/shard_map/ppermute | solution.py:613
  24.4 0.8 %shard_map.224 = (bf16[64,32,128]{2,1,0:T(8,128)(2,1)S(1)}, bf16[68,4,128]{2,1,0:T(4,128)(2,1)S(1)}, bf16[68,4,128]{2,1,0:T(4,128)(2,1)S(1)}) custom-call(s32[8,128]{1,0:T(8,128)S(1)} %iota.37.at_ref, bf16[8,208,128]{2,1,0:T(8,128)(2,1)S(1)} %shard_map.222.x_ref, bf16[64,32,128]{2,1,0:T(8,128)(2,1)S(1)} %get-tuple-element.112.norm_ref, ...), custom_call_target="tpu_custom_call" | custom-call | flops 1000000000 | bytes 3000000 | tf_op jit(solution)/shard_map/pallas_call | solution.py:477
  25.3 2.3 %collective-permute-start.10 = (f32[56,128]{1,0:T(8,128)S(1)}, f32[56,128]{1,0:T(8,128)S(1)}, u32[]{:S(2)}, u32[]{:S(2)}) collective-permute-start(f32[56,128]{1,0:T(8,128)S(1)} %add.51), channel_id=1, source_target_pairs={{0,7},{1,6},{2,5},{3,4},{4,3},{5,2},{6,1},{7,0},{8,15},{9,14},{10,... | collective-permute-start | bytes 86024 | tf_op jit(solution)/shard_map/ppermute | solution.py:613
  27.6 0.7 %collective-permute-start.9 = (f32[56,128]{1,0:T(8,128)S(1)}, f32[56,128]{1,0:T(8,128)S(1)}, u32[]{:S(2)}, u32[]{:S(2)}) collective-permute-start(f32[56,128]{1,0:T(8,128)S(1)} %add.51), channel_id=1, source_target_pairs={{0,5},{1,4},{2,7},{3,6},{4,1},{5,0},{6,3},{7,2},{8,13},{9,12},{10,... | collective-permute-start | bytes 86024 | tf_op jit(solution)/shard_map/ppermute | solution.py:613
  28.3 1.1 %collective-permute-start.8 = (f32[56,128]{1,0:T(8,128)S(1)}, f32[56,128]{1,0:T(8,128)S(1)}, u32[]{:S(2)}, u32[]{:S(2)}) collective-permute-start(f32[56,128]{1,0:T(8,128)S(1)} %add.51), channel_id=1, source_target_pairs={{0,3},{1,2},{2,1},{3,0},{4,7},{5,6},{6,5},{7,4},{8,11},{9,10},{10,... | collective-permute-start | bytes 86024 | tf_op jit(solution)/shard_map/ppermute | solution.py:613
  29.3 1.6 %collective-permute-start.12 = (bf16[68,4,128]{2,1,0:T(4,128)(2,1)S(1)}, bf16[68,4,128]{2,1,0:T(4,128)(2,1)S(1)}, u32[]{:S(2)}, u32[]{:S(2)}) collective-permute-start(bf16[68,4,128]{2,1,0:T(4,128)(2,1)S(1)} %get-tuple-element.118), channel_id=1, source_target_pairs={{0,24},{8,16},{16,8},{24,0},{1,25},{9,17},{17,9},{25,1},{2,26},{10... | collective-permute-start | bytes 208904 | tf_op jit(solution)/shard_map/ppermute | solution.py:618
  31.0 1.0 %collective-permute-start.11 = (bf16[68,4,128]{2,1,0:T(4,128)(2,1)S(1)}, bf16[68,4,128]{2,1,0:T(4,128)(2,1)S(1)}, u32[]{:S(2)}, u32[]{:S(2)}) collective-permute-start(bf16[68,4,128]{2,1,0:T(4,128)(2,1)S(1)} %get-tuple-element.117), channel_id=1, source_target_pairs={{0,8},{8,0},{16,24},{24,16},{1,9},{9,1},{17,25},{25,17},{2,10},{10... | collective-permute-start | bytes 208904 | tf_op jit(solution)/shard_map/ppermute | solution.py:618
  32.0 1.0 %shard_map.225.refs_0_ = f32[32,32,128]{2,1,0:T(8,128)S(1)} custom-call(bf16[64,32,128]{2,1,0:T(8,128)(2,1)S(1)} %get-tuple-element.112.norm_ref, bf16[64,32,128]{2,1,0:T(8,128)(2,1)S(1)} %get-tuple-element.108.side_ref, f32[64,512]{1,0:T(8,128)S(1)} %get-tuple-element.109.kf_ref, f32[4,64,128]{2,1,0:T(8,128)S(1)} %get-tuple-element.91.vec_ref, ...), custom_call_target="tpu_custom_call" | custom-call | flops 2000000000 | bytes 6000000 | tf_op jit(solution)/shard_map/pallas_call | solution.py:477
  33.0 0.9 %collective-permute-start.15 = (f32[56,128]{1,0:T(8,128)S(1)}, f32[56,128]{1,0:T(8,128)S(1)}, u32[]{:S(2)}, u32[]{:S(2)}) collective-permute-start(f32[56,128]{1,0:T(8,128)S(1)} %add_add_fusion.refs_0_), channel_id=1, source_target_pairs={{0,25},{1,24},{2,27},{3,26},{4,29},{5,28},{6,31},{7,30},{8,17},{9,... | collective-permute-start | bytes 86024 | tf_op jit(solution)/shard_map/ppermute | solution.py:613
  33.9 1.3 %collective-permute-start.14 = (f32[56,128]{1,0:T(8,128)S(1)}, f32[56,128]{1,0:T(8,128)S(1)}, u32[]{:S(2)}, u32[]{:S(2)}) collective-permute-start(f32[56,128]{1,0:T(8,128)S(1)} %add_add_fusion.refs_0_), channel_id=1, source_target_pairs={{0,17},{1,16},{2,19},{3,18},{4,21},{5,20},{6,23},{7,22},{8,25},{9,... | collective-permute-start | bytes 86024 | tf_op jit(solution)/shard_map/ppermute | solution.py:613
  35.5 1.0 %shard_map.226.refs_1_ = f32[32,32,128]{2,1,0:T(8,128)S(1)} custom-call(bf16[64,32,128]{2,1,0:T(8,128)(2,1)S(1)} %get-tuple-element.112.norm_ref, bf16[64,32,128]{2,1,0:T(8,128)(2,1)S(1)} %get-tuple-element.108.side_ref, f32[64,512]{1,0:T(8,128)S(1)} %get-tuple-element.109.kf_ref, f32[4,64,128]{2,1,0:T(8,128)S(1)} %get-tuple-element.91.vec_ref, ...), custom_call_target="tpu_custom_call" | custom-call | flops 2000000000 | bytes 6000000 | tf_op jit(solution)/shard_map/pallas_call | solution.py:477
  36.5 1.7 %shard_map.227 = bf16[64,32,128]{2,1,0:T(8,128)(2,1)} custom-call(s32[8,128]{1,0:T(8,128)S(1)} %iota.37.at_ref, bf16[68,4,128]{2,1,0:T(4,128)(2,1)S(1)} %collective-permute-done.11.one_ref, bf16[68,4,128]{2,1,0:T(4,128)(2,1)S(1)} %collective-permute-done.12.two_ref, f32[64,512]{1,0:T(8,128)S(1)} %get-tuple-element.109.kf_ref, f32[16,128]{1,0:T(8,128)S(1)} %copy-done.8, ...), custom_call_target="tpu_custom_call" | custom-call | flops 3000000000 | bytes 9000000 | tf_op jit(solution)/shard_map/pallas_call | solution.py:477
  38.7 0.7 %shard_map.228 = (f32[48,64]{1,0:T(8,128)}, f32[64]{0:T(128)}, f32[64]{0:T(128)}, f32[64]{0:T(128)}, f32[64]{0:T(128)}, /*index=5*/f32[49,64]{1,0:T(8,128)}) custom-call(f32[56,128]{1,0:T(8,128)S(1)} %add_add_fusion.refs_0_, f32[56,128]{1,0:T(8,128)S(1)} %collective-permute-done.13.refs_1_, f32[56,128]{1,0:T(8,128)S(1)} %collective-permute-done.14.refs_2_, ...), custom_call_target="tpu_custom_call" | custom-call | flops 1000000000 | bytes 3000000 | tf_op jit(solution)/shard_map/pallas_call | solution.py:477
  (55 shorter events, 1.7 us)
Async XLA Ops:
  0.8 12.9 %copy-start.4 = (bf16[48,384]{1,0:T(8,128)(2,1)S(1)}, bf16[48,384]{1,0:T(8,128)(2,1)}, u32[]{:S(2)}) copy-start(bf16[48,384]{1,0:T(8,128)(2,1)} %constant.69.clone.spread_ref) | copy-start | bytes 110596
  0.8 12.9 %copy-start.6 = (f32[64,49]{0,1:T(8,128)S(1)}, f32[64,49]{0,1:T(8,128)}, u32[]{:S(2)}) copy-start(f32[64,49]{0,1:T(8,128)} %param.22) | copy-start | bytes 37636
  0.8 12.9 %copy-start.7 = (bf16[64,48]{0,1:T(8,128)(2,1)S(1)}, bf16[64,48]{0,1:T(8,128)(2,1)}, u32[]{:S(2)}) copy-start(bf16[64,48]{0,1:T(8,128)(2,1)} %param.18) | copy-start | bytes 18436
  0.8 12.9 %copy-start.9 = (f32[64]{0:T(128)S(1)}, f32[64]{0:T(128)}, u32[]{:S(2)}) copy-start(f32[64]{0:T(128)} %bias_ref.1) | copy-start | bytes 772
  0.8 13.3 %copy-start.5 = (f32[32,256]{1,0:T(8,128)S(1)}, f32[32,256]{1,0:T(8,128)}, u32[]{:S(2)}) copy-start(f32[32,256]{1,0:T(8,128)} %constant.75.clone.band_ref) | copy-start | bytes 98308
  0.9 17.2 %copy-start.8 = (f32[16,128]{1,0:T(8,128)S(1)}, f32[16,128]{1,0:T(8,128)}, u32[]{:S(2)}) copy-start(f32[16,128]{1,0:T(8,128)} %constant.76.clone.fringe_ref) | copy-start | bytes 24580
  2.8 16.4 %copy-start.13 = (bf16[56,384]{1,0:T(8,128)(2,1)S(1)}, bf16[56,384]{1,0:T(8,128)(2,1)}, u32[]{:S(2)}) copy-start(bf16[56,384]{1,0:T(8,128)(2,1)} %constant.77.clone.pick_ref) | copy-start | bytes 129028
  2.8 16.4 %copy-start.14 = (bf16[56,384]{1,0:T(8,128)(2,1)S(1)}, bf16[56,384]{1,0:T(8,128)(2,1)}, u32[]{:S(2)}) copy-start(bf16[56,384]{1,0:T(8,128)(2,1)} %constant.74.clone.taps_ref) | copy-start | bytes 129028
  2.8 5.2 %collective-permute-start = (bf16[960,128]{1,0:T(8,128)(2,1)S(1)}, bf16[960,128]{1,0:T(8,128)(2,1)S(1)}, u32[]{:S(2)}, u32[]{:S(2)}) collective-permute-start(bf16[960,128]{1,0:T(8,128)(2,1)S(1)} %get-tuple-element.69), channel_id=1, source_target_pairs={{0,1},{1,0},{2,3},{3,2},{4,5},{5,4},{6,7},{7,6},{8,9},{9,8},{10,11... | collective-permute-start | bytes 737288 | tf_op jit(solution)/shard_map/ppermute | solution.py:547
  3.3 6.6 %collective-permute-start.1 = (bf16[176,128]{1,0:T(8,128)(2,1)S(1)}, bf16[176,128]{1,0:T(8,128)(2,1)S(1)}, u32[]{:S(2)}, u32[]{:S(2)}) collective-permute-start(bf16[176,128]{1,0:T(8,128)(2,1)S(1)} %get-tuple-element.72), channel_id=1, source_target_pairs={{0,7},{1,2},{2,1},{3,4},{4,3},{5,6},{6,5},{7,0},{8,15},{9,10},{10,... | collective-permute-start | bytes 135176 | tf_op jit(solution)/shard_map/ppermute | solution.py:548
  8.1 11.0 %collective-permute-start.4 = (bf16[2,208,128]{2,1,0:T(8,128)(2,1)S(1)}, bf16[2,208,128]{2,1,0:T(8,128)(2,1)S(1)}, u32[]{:S(2)}, u32[]{:S(2)}) collective-permute-start(bf16[2,208,128]{2,1,0:T(8,128)(2,1)S(1)} %get-tuple-element.83), channel_id=1, source_target_pairs={{0,3},{1,2},{2,1},{3,0},{4,7},{5,6},{6,5},{7,4},{8,11},{9,10},{10,... | collective-permute-start | bytes 319496 | tf_op jit(solution)/shard_map/ppermute | solution.py:551
  8.1 11.0 %collective-permute-start.5 = (bf16[2,208,128]{2,1,0:T(8,128)(2,1)S(1)}, bf16[2,208,128]{2,1,0:T(8,128)(2,1)S(1)}, u32[]{:S(2)}, u32[]{:S(2)}) collective-permute-start(bf16[2,208,128]{2,1,0:T(8,128)(2,1)S(1)} %get-tuple-element.84), channel_id=1, source_target_pairs={{0,5},{1,4},{2,7},{3,6},{4,1},{5,0},{6,3},{7,2},{8,13},{9,12},{10,... | collective-permute-start | bytes 319496 | tf_op jit(solution)/shard_map/ppermute | solution.py:551
  9.8 9.3 %collective-permute-start.6 = (bf16[2,208,128]{2,1,0:T(8,128)(2,1)S(1)}, bf16[2,208,128]{2,1,0:T(8,128)(2,1)S(1)}, u32[]{:S(2)}, u32[]{:S(2)}) collective-permute-start(bf16[2,208,128]{2,1,0:T(8,128)(2,1)S(1)} %get-tuple-element.85), channel_id=1, source_target_pairs={{0,7},{1,6},{2,5},{3,4},{4,3},{5,2},{6,1},{7,0},{8,15},{9,14},{10,... | collective-permute-start | bytes 319496 | tf_op jit(solution)/shard_map/ppermute | solution.py:551
  10.6 5.3 %collective-permute-start.2 = (bf16[68,4,128]{2,1,0:T(4,128)(2,1)S(1)}, bf16[68,4,128]{2,1,0:T(4,128)(2,1)S(1)}, u32[]{:S(2)}, u32[]{:S(2)}) collective-permute-start(bf16[68,4,128]{2,1,0:T(4,128)(2,1)S(1)} %get-tuple-element.74), channel_id=1, source_target_pairs={{0,8},{8,0},{16,24},{24,16},{1,9},{9,1},{17,25},{25,17},{2,10},{10... | collective-permute-start | bytes 208904 | tf_op jit(solution)/shard_map/ppermute | solution.py:495
  12.1 6.0 %collective-permute-start.3 = (bf16[68,4,128]{2,1,0:T(4,128)(2,1)S(1)}, bf16[68,4,128]{2,1,0:T(4,128)(2,1)S(1)}, u32[]{:S(2)}, u32[]{:S(2)}) collective-permute-start(bf16[68,4,128]{2,1,0:T(4,128)(2,1)S(1)} %get-tuple-element.75), channel_id=1, source_target_pairs={{0,24},{8,16},{16,8},{24,0},{1,25},{9,17},{17,9},{25,1},{2,26},{10... | collective-permute-start | bytes 208904 | tf_op jit(solution)/shard_map/ppermute | solution.py:495
  23.5 1.8 %collective-permute-start.7 = (f32[56,128]{1,0:T(8,128)S(1)}, f32[56,128]{1,0:T(8,128)S(1)}, u32[]{:S(2)}, u32[]{:S(2)}) collective-permute-start(f32[56,128]{1,0:T(8,128)S(1)} %get-tuple-element.101), channel_id=1, source_target_pairs={{0,1},{1,0},{2,3},{3,2},{4,5},{5,4},{6,7},{7,6},{8,9},{9,8},{10,11... | collective-permute-start | bytes 86024 | tf_op jit(solution)/shard_map/ppermute | solution.py:613
  25.3 7.7 %collective-permute-start.10 = (f32[56,128]{1,0:T(8,128)S(1)}, f32[56,128]{1,0:T(8,128)S(1)}, u32[]{:S(2)}, u32[]{:S(2)}) collective-permute-start(f32[56,128]{1,0:T(8,128)S(1)} %add.51), channel_id=1, source_target_pairs={{0,7},{1,6},{2,5},{3,4},{4,3},{5,2},{6,1},{7,0},{8,15},{9,14},{10,... | collective-permute-start | bytes 86024 | tf_op jit(solution)/shard_map/ppermute | solution.py:613
  27.6 5.4 %collective-permute-start.9 = (f32[56,128]{1,0:T(8,128)S(1)}, f32[56,128]{1,0:T(8,128)S(1)}, u32[]{:S(2)}, u32[]{:S(2)}) collective-permute-start(f32[56,128]{1,0:T(8,128)S(1)} %add.51), channel_id=1, source_target_pairs={{0,5},{1,4},{2,7},{3,6},{4,1},{5,0},{6,3},{7,2},{8,13},{9,12},{10,... | collective-permute-start | bytes 86024 | tf_op jit(solution)/shard_map/ppermute | solution.py:613
  28.3 4.7 %collective-permute-start.8 = (f32[56,128]{1,0:T(8,128)S(1)}, f32[56,128]{1,0:T(8,128)S(1)}, u32[]{:S(2)}, u32[]{:S(2)}) collective-permute-start(f32[56,128]{1,0:T(8,128)S(1)} %add.51), channel_id=1, source_target_pairs={{0,3},{1,2},{2,1},{3,0},{4,7},{5,6},{6,5},{7,4},{8,11},{9,10},{10,... | collective-permute-start | bytes 86024 | tf_op jit(solution)/shard_map/ppermute | solution.py:613
  29.3 7.2 %collective-permute-start.12 = (bf16[68,4,128]{2,1,0:T(4,128)(2,1)S(1)}, bf16[68,4,128]{2,1,0:T(4,128)(2,1)S(1)}, u32[]{:S(2)}, u32[]{:S(2)}) collective-permute-start(bf16[68,4,128]{2,1,0:T(4,128)(2,1)S(1)} %get-tuple-element.118), channel_id=1, source_target_pairs={{0,24},{8,16},{16,8},{24,0},{1,25},{9,17},{17,9},{25,1},{2,26},{10... | collective-permute-start | bytes 208904 | tf_op jit(solution)/shard_map/ppermute | solution.py:618
  31.0 5.6 %collective-permute-start.11 = (bf16[68,4,128]{2,1,0:T(4,128)(2,1)S(1)}, bf16[68,4,128]{2,1,0:T(4,128)(2,1)S(1)}, u32[]{:S(2)}, u32[]{:S(2)}) collective-permute-start(bf16[68,4,128]{2,1,0:T(4,128)(2,1)S(1)} %get-tuple-element.117), channel_id=1, source_target_pairs={{0,8},{8,0},{16,24},{24,16},{1,9},{9,1},{17,25},{25,17},{2,10},{10... | collective-permute-start | bytes 208904 | tf_op jit(solution)/shard_map/ppermute | solution.py:618
  33.0 5.3 %collective-permute-start.15 = (f32[56,128]{1,0:T(8,128)S(1)}, f32[56,128]{1,0:T(8,128)S(1)}, u32[]{:S(2)}, u32[]{:S(2)}) collective-permute-start(f32[56,128]{1,0:T(8,128)S(1)} %add_add_fusion.refs_0_), channel_id=1, source_target_pairs={{0,25},{1,24},{2,27},{3,26},{4,29},{5,28},{6,31},{7,30},{8,17},{9,... | collective-permute-start | bytes 86024 | tf_op jit(solution)/shard_map/ppermute | solution.py:613
  33.9 4.4 %collective-permute-start.14 = (f32[56,128]{1,0:T(8,128)S(1)}, f32[56,128]{1,0:T(8,128)S(1)}, u32[]{:S(2)}, u32[]{:S(2)}) collective-permute-start(f32[56,128]{1,0:T(8,128)S(1)} %add_add_fusion.refs_0_), channel_id=1, source_target_pairs={{0,17},{1,16},{2,19},{3,18},{4,21},{5,20},{6,23},{7,22},{8,25},{9,... | collective-permute-start | bytes 86024 | tf_op jit(solution)/shard_map/ppermute | solution.py:613
  35.3 3.4 %collective-permute-start.13 = (f32[56,128]{1,0:T(8,128)S(1)}, f32[56,128]{1,0:T(8,128)S(1)}, u32[]{:S(2)}, u32[]{:S(2)}) collective-permute-start(f32[56,128]{1,0:T(8,128)S(1)} %add_add_fusion.refs_0_), channel_id=1, source_target_pairs={{0,9},{1,8},{2,11},{3,10},{4,13},{5,12},{6,15},{7,14},{8,1},{9,0},... | collective-permute-start | bytes 86024 | tf_op jit(solution)/shard_map/ppermute | solution.py:613
  (7 other events, 90.0 us)

commit v6 on v5

--- a/solution.py
+++ b/solution.py
@@ -322,10 +322,13 @@
     shift_part = jnp.zeros((channels, GROUP, width), f32)
     inner = 8 * height
     ones = jnp.where(iota((16, width), 0) == 0, 1.0, 0.0).astype(bf16)
-    by_color = jnp.zeros((channels, colors + 16), f32)
+    by_color = jnp.zeros((colors + 16, channels), f32)
     for g in range(height // GROUP):
-        blocks = [x_ref[per * g + a, :block, :] for a in range(per)]
-        patch = mm(wk_ref[...], jnp.concatenate(blocks, axis=0)).reshape(channels, GROUP, width) + bias
+        if g == 0:
+            pixels = [[x_ref[per * n + a, :block, :] for a in range(per)] for n in range(height // GROUP)]
+            patches = mm(wk_ref[...], jnp.concatenate([jnp.concatenate(x, axis=0) for x in pixels], axis=1))
+        blocks = pixels[g]
+        patch = patches[:, g * width:(g + 1) * width].reshape(channels, GROUP, width) + bias
         xhat, inverse = layer_norm(patch, channels)
         norm_s[:, g * GROUP:(g + 1) * GROUP, :] = xhat * gain + offset
         if g == 0:
@@ -345,7 +348,7 @@
             start = h % file_rows * colors
             left.append(jnp.concatenate([blocks[h // file_rows][start:start + colors], ones], axis=0))
             right.append(grad_s[g, pl.ds(h, channels, stride=GROUP), :].astype(bf16))
-        by_color += mm(jnp.concatenate(right, axis=1), jnp.concatenate(left, axis=1), NT)
+        by_color += mm(jnp.concatenate(left, axis=1), jnp.concatenate(right, axis=1), NT)
 
     band, fringe = band_ref[...], fringe_ref[...]
     none = jnp.zeros((height, width), bf16)
@@ -383,7 +386,7 @@
     out_ref[...] = sum(mm(taps_ref[...], part, NT) for part in split2(line))
     parts = jnp.concatenate([jnp.sum(scale_part, axis=1), jnp.sum(shift_part, axis=1), total_ref[...]], axis=1)
     first = sum(mm(pick_ref[...], part, NT) for part in split2(parts))
-    out_ref[:, :channels] = first + by_color.T[:56]
+    out_ref[:, :channels] = first + by_color[:56]
 
 
 def side_line(pieces, block):

time: 39.5 us -> 39.1 us (0.990)
  Pallas kernels: 15.3 us -> 14.9 us
    pallas_call x13, Pallas kernels: 15.3 us -> 14.9 us  [kernel_call(): pl.pallas_call(body, out_shape=out_shape, compiler_params=pltpu.CompilerP...]
where the time goes in v6:
time: 39.1 us; the launch traced here: 39 us
  starting transfers between devices  20.2 us (52%)
  Pallas kernels  14.9 us (38%)
  waiting for transfers between devices  2.65 us (7%)
  between operations  1.02 us (3%)
    pallas_call x13, Pallas kernels, kernel_call(): pl.pallas_call(body, out_shape=out_shape, compiler_params=pltpu.CompilerP...  14.9 us
    ppermute x7, starting transfers between devices, per_device(): lax.ppermute(result, ('rows', 'cols'), [(i, i ^ step) for i in range(size)])  7.52 us
    ppermute x1, starting transfers between devices, per_device(): far = lax.ppermute(edges, 'cols', pairing(n_cols, 1))  4.71 us
    ppermute x2, starting transfers between devices, swap(): lax.ppermute(part, axis, pairing(lax.axis_size(axis), n))  3.01 us
    ppermute x2, starting transfers between devices, per_device(): ends[which] = lax.ppermute(end, 'rows', pairing(n_rows, which))  2.64 us
    ppermute x2, waiting for transfers between devices, swap(): lax.ppermute(part, axis, pairing(lax.axis_size(axis), n))  2.14 us
    ppermute x3, starting transfers between devices, per_device(): lax.ppermute(pairs[n], 'cols', [(i, i ^ 2 * n + 1) for i in range(n_cols)])  1.82 us
  transfers between devices with their start and end apart: 16, of which 3 were waited for; matrix products, arithmetic and copies ran while one was open for 0% of the time, Pallas kernels for 21%

profile of v6, /device:TPU:0, one launch (start us, length us, event | category | flops | bytes accessed | tf_op | source)
XLA Modules:
  0.0 39.0 jit_solution(9376647958135681763)
XLA Ops:
  0.9 1.9 %shard_map.216 = (bf16[64,32,128]{2,1,0:T(8,128)(2,1)S(1)}, bf16[4,208,128]{2,1,0:T(8,128)(2,1)S(1)}, bf16[960,128]{1,0:T(8,128)(2,1)S(1)}, bf16[176,128]{1,0:T(8,128)(2,1)S(1)}) custom-call(s32[8,128]{1,0:T(8,128)S(1)} %iota.37.at_ref, bf16[48,4,1024]{2,1,0:T(4,128)(2,1)} %x_hbm.1, bf16[64,32,128]{2,1,0:T(8,128)(2,1)} %cot_hbm.1), custom_call_target="tpu_custom_call" | custom-call | flops 2000000000 | bytes 6000000 | tf_op jit(solution)/shard_map/pallas_call | solution.py:480
  2.8 0.5 %collective-permute-start = (bf16[960,128]{1,0:T(8,128)(2,1)S(1)}, bf16[960,128]{1,0:T(8,128)(2,1)S(1)}, u32[]{:S(2)}, u32[]{:S(2)}) collective-permute-start(bf16[960,128]{1,0:T(8,128)(2,1)S(1)} %get-tuple-element.69), channel_id=1, source_target_pairs={{0,1},{1,0},{2,3},{3,2},{4,5},{5,4},{6,7},{7,6},{8,9},{9,8},{10,11... | collective-permute-start | bytes 737288 | tf_op jit(solution)/shard_map/ppermute | solution.py:550
  3.3 4.7 %collective-permute-start.1 = (bf16[176,128]{1,0:T(8,128)(2,1)S(1)}, bf16[176,128]{1,0:T(8,128)(2,1)S(1)}, u32[]{:S(2)}, u32[]{:S(2)}) collective-permute-start(bf16[176,128]{1,0:T(8,128)(2,1)S(1)} %get-tuple-element.72), channel_id=1, source_target_pairs={{0,7},{1,2},{2,1},{3,4},{4,3},{5,6},{6,5},{7,0},{8,15},{9,10},{10,... | collective-permute-start | bytes 135176 | tf_op jit(solution)/shard_map/ppermute | solution.py:551
  8.1 1.7 %collective-permute-start.5 = (bf16[2,208,128]{2,1,0:T(8,128)(2,1)S(1)}, bf16[2,208,128]{2,1,0:T(8,128)(2,1)S(1)}, u32[]{:S(2)}, u32[]{:S(2)}) collective-permute-start(bf16[2,208,128]{2,1,0:T(8,128)(2,1)S(1)} %get-tuple-element.84), channel_id=1, source_target_pairs={{0,5},{1,4},{2,7},{3,6},{4,1},{5,0},{6,3},{7,2},{8,13},{9,12},{10,... | collective-permute-start | bytes 319496 | tf_op jit(solution)/shard_map/ppermute | solution.py:554
  10.0 0.6 %shard_map.218 = (bf16[64,32,128]{2,1,0:T(8,128)(2,1)S(1)}, bf16[68,4,128]{2,1,0:T(4,128)(2,1)S(1)}, bf16[68,4,128]{2,1,0:T(4,128)(2,1)S(1)}) custom-call(s32[8,128]{1,0:T(8,128)S(1)} %iota.37.at_ref, bf16[64,32,128]{2,1,0:T(8,128)(2,1)S(1)} %get-tuple-element.68.cot_ref, bf16[960,128]{1,0:T(8,128)(2,1)S(1)} %collective-permute-done.got_ref.near_ref, ...), custom_call_target="tpu_custom_call" | custom-call | flops 10000000 | bytes 30000 | tf_op jit(solution)/shard_map/pallas_call | solution.py:480
  10.6 1.5 %collective-permute-start.2 = (bf16[68,4,128]{2,1,0:T(4,128)(2,1)S(1)}, bf16[68,4,128]{2,1,0:T(4,128)(2,1)S(1)}, u32[]{:S(2)}, u32[]{:S(2)}) collective-permute-start(bf16[68,4,128]{2,1,0:T(4,128)(2,1)S(1)} %get-tuple-element.74), channel_id=1, source_target_pairs={{0,8},{8,0},{16,24},{24,16},{1,9},{9,1},{17,25},{25,17},{2,10},{10... | collective-permute-start | bytes 208904 | tf_op jit(solution)/shard_map/ppermute | solution.py:498
  12.1 1.5 %collective-permute-start.3 = (bf16[68,4,128]{2,1,0:T(4,128)(2,1)S(1)}, bf16[68,4,128]{2,1,0:T(4,128)(2,1)S(1)}, u32[]{:S(2)}, u32[]{:S(2)}) collective-permute-start(bf16[68,4,128]{2,1,0:T(4,128)(2,1)S(1)} %get-tuple-element.75), channel_id=1, source_target_pairs={{0,24},{8,16},{16,8},{24,0},{1,25},{9,17},{17,9},{25,1},{2,26},{10... | collective-permute-start | bytes 208904 | tf_op jit(solution)/shard_map/ppermute | solution.py:498
  14.2 1.7 %shard_map.220 = (bf16[64,256,128]{2,1,0:T(8,128)(2,1)S(1)}, f32[64,32,128]{2,1,0:T(8,128)S(1)}, f32[64,128]{1,0:T(8,128)S(1)}) custom-call(bf16[64,32,128]{2,1,0:T(8,128)(2,1)S(1)} %get-tuple-element.68.cot_ref, bf16[64,32,128]{2,1,0:T(8,128)(2,1)S(1)} %get-tuple-element.77.beside_ref, f32[64,512]{1,0:T(8,128)S(1)} %get-tuple-element.79.kb_ref, ...), custom_call_target="tpu_custom_call" | custom-call | flops 10000000 | bytes 30000 | tf_op jit(solution)/shard_map/pallas_call | solution.py:480
  15.9 2.1 %collective-permute-done.3.two_ref = bf16[68,4,128]{2,1,0:T(4,128)(2,1)S(1)} collective-permute-done((bf16[68,4,128]{2,1,0:T(4,128)(2,1)S(1)}, bf16[68,4,128]{2,1,0:T(4,128)(2,1)S(1)}, u32[]{:S(2)}, u32[]{:S(2)}) %collective-permute-start.3) | collective-permute-done | bytes 69664 | tf_op jit(solution)/shard_map/ppermute | solution.py:498
  18.1 1.0 %shard_map.221 = (bf16[64,128,128]{2,1,0:T(8,128)(2,1)S(1)}, f32[64,16,128]{2,1,0:T(8,128)S(1)}) custom-call(s32[8,128]{1,0:T(8,128)S(1)} %iota.37.at_ref, bf16[68,4,128]{2,1,0:T(4,128)(2,1)S(1)} %collective-permute-done.2.one_ref, bf16[68,4,128]{2,1,0:T(4,128)(2,1)S(1)} %collective-permute-done.3.two_ref, f32[64,32,128]{2,1,0:T(8,128)S(1)} %get-tuple-element.80.grad_ref, ...), custom_call_target="tpu_custom_call" | custom-call | flops 10000000 | bytes 30000 | tf_op jit(solution)/shard_map/pallas_call | solution.py:480
  19.2 3.9 %shard_map.223 = (bf16[64,32,128]{2,1,0:T(8,128)(2,1)S(1)}, f32[56,128]{1,0:T(8,128)S(1)}) custom-call(bf16[8,208,128]{2,1,0:T(8,128)(2,1)S(1)} %shard_map.222.x_ref, bf16[512,384]{1,0:T(8,128)(2,1)S(1)} %get-tuple-element.90.wk_ref, f32[4,64,128]{2,1,0:T(8,128)S(1)} %get-tuple-element.91.vec_ref, f32[64,32,128]{2,1,0:T(8,128)S(1)} %get-tuple-element.80.grad_ref, ...), custom_call_target="tpu_custom_call" | custom-call | flops 6000000000 | bytes 18000000 | tf_op jit(solution)/shard_map/pallas_call | solution.py:480
  23.1 0.9 %collective-permute-start.7 = (f32[56,128]{1,0:T(8,128)S(1)}, f32[56,128]{1,0:T(8,128)S(1)}, u32[]{:S(2)}, u32[]{:S(2)}) collective-permute-start(f32[56,128]{1,0:T(8,128)S(1)} %get-tuple-element.101), channel_id=1, source_target_pairs={{0,1},{1,0},{2,3},{3,2},{4,5},{5,4},{6,7},{7,6},{8,9},{9,8},{10,11... | collective-permute-start | bytes 86024 | tf_op jit(solution)/shard_map/ppermute | solution.py:616
  24.0 0.8 %shard_map.224 = (bf16[64,32,128]{2,1,0:T(8,128)(2,1)S(1)}, bf16[68,4,128]{2,1,0:T(4,128)(2,1)S(1)}, bf16[68,4,128]{2,1,0:T(4,128)(2,1)S(1)}) custom-call(s32[8,128]{1,0:T(8,128)S(1)} %iota.37.at_ref, bf16[8,208,128]{2,1,0:T(8,128)(2,1)S(1)} %shard_map.222.x_ref, bf16[64,32,128]{2,1,0:T(8,128)(2,1)S(1)} %get-tuple-element.112.norm_ref, ...), custom_call_target="tpu_custom_call" | custom-call | flops 1000000000 | bytes 3000000 | tf_op jit(solution)/shard_map/pallas_call | solution.py:480
  24.9 2.3 %collective-permute-start.10 = (f32[56,128]{1,0:T(8,128)S(1)}, f32[56,128]{1,0:T(8,128)S(1)}, u32[]{:S(2)}, u32[]{:S(2)}) collective-permute-start(f32[56,128]{1,0:T(8,128)S(1)} %add.51), channel_id=1, source_target_pairs={{0,7},{1,6},{2,5},{3,4},{4,3},{5,2},{6,1},{7,0},{8,15},{9,14},{10,... | collective-permute-start | bytes 86024 | tf_op jit(solution)/shard_map/ppermute | solution.py:616
  27.2 0.7 %collective-permute-start.9 = (f32[56,128]{1,0:T(8,128)S(1)}, f32[56,128]{1,0:T(8,128)S(1)}, u32[]{:S(2)}, u32[]{:S(2)}) collective-permute-start(f32[56,128]{1,0:T(8,128)S(1)} %add.51), channel_id=1, source_target_pairs={{0,5},{1,4},{2,7},{3,6},{4,1},{5,0},{6,3},{7,2},{8,13},{9,12},{10,... | collective-permute-start | bytes 86024 | tf_op jit(solution)/shard_map/ppermute | solution.py:616
  27.9 1.1 %collective-permute-start.8 = (f32[56,128]{1,0:T(8,128)S(1)}, f32[56,128]{1,0:T(8,128)S(1)}, u32[]{:S(2)}, u32[]{:S(2)}) collective-permute-start(f32[56,128]{1,0:T(8,128)S(1)} %add.51), channel_id=1, source_target_pairs={{0,3},{1,2},{2,1},{3,0},{4,7},{5,6},{6,5},{7,4},{8,11},{9,10},{10,... | collective-permute-start | bytes 86024 | tf_op jit(solution)/shard_map/ppermute | solution.py:616
  29.0 1.6 %collective-permute-start.12 = (bf16[68,4,128]{2,1,0:T(4,128)(2,1)S(1)}, bf16[68,4,128]{2,1,0:T(4,128)(2,1)S(1)}, u32[]{:S(2)}, u32[]{:S(2)}) collective-permute-start(bf16[68,4,128]{2,1,0:T(4,128)(2,1)S(1)} %get-tuple-element.118), channel_id=1, source_target_pairs={{0,24},{8,16},{16,8},{24,0},{1,25},{9,17},{17,9},{25,1},{2,26},{10... | collective-permute-start | bytes 208904 | tf_op jit(solution)/shard_map/ppermute | solution.py:621
  30.6 1.0 %collective-permute-start.11 = (bf16[68,4,128]{2,1,0:T(4,128)(2,1)S(1)}, bf16[68,4,128]{2,1,0:T(4,128)(2,1)S(1)}, u32[]{:S(2)}, u32[]{:S(2)}) collective-permute-start(bf16[68,4,128]{2,1,0:T(4,128)(2,1)S(1)} %get-tuple-element.117), channel_id=1, source_target_pairs={{0,8},{8,0},{16,24},{24,16},{1,9},{9,1},{17,25},{25,17},{2,10},{10... | collective-permute-start | bytes 208904 | tf_op jit(solution)/shard_map/ppermute | solution.py:621
  31.6 1.0 %shard_map.225.refs_0_ = f32[32,32,128]{2,1,0:T(8,128)S(1)} custom-call(bf16[64,32,128]{2,1,0:T(8,128)(2,1)S(1)} %get-tuple-element.112.norm_ref, bf16[64,32,128]{2,1,0:T(8,128)(2,1)S(1)} %get-tuple-element.108.side_ref, f32[64,512]{1,0:T(8,128)S(1)} %get-tuple-element.109.kf_ref, f32[4,64,128]{2,1,0:T(8,128)S(1)} %get-tuple-element.91.vec_ref, ...), custom_call_target="tpu_custom_call" | custom-call | flops 2000000000 | bytes 6000000 | tf_op jit(solution)/shard_map/pallas_call | solution.py:480
  32.6 0.9 %collective-permute-start.15 = (f32[56,128]{1,0:T(8,128)S(1)}, f32[56,128]{1,0:T(8,128)S(1)}, u32[]{:S(2)}, u32[]{:S(2)}) collective-permute-start(f32[56,128]{1,0:T(8,128)S(1)} %add_add_fusion.refs_0_), channel_id=1, source_target_pairs={{0,25},{1,24},{2,27},{3,26},{4,29},{5,28},{6,31},{7,30},{8,17},{9,... | collective-permute-start | bytes 86024 | tf_op jit(solution)/shard_map/ppermute | solution.py:616
  33.5 1.3 %collective-permute-start.14 = (f32[56,128]{1,0:T(8,128)S(1)}, f32[56,128]{1,0:T(8,128)S(1)}, u32[]{:S(2)}, u32[]{:S(2)}) collective-permute-start(f32[56,128]{1,0:T(8,128)S(1)} %add_add_fusion.refs_0_), channel_id=1, source_target_pairs={{0,17},{1,16},{2,19},{3,18},{4,21},{5,20},{6,23},{7,22},{8,25},{9,... | collective-permute-start | bytes 86024 | tf_op jit(solution)/shard_map/ppermute | solution.py:616
  35.2 1.0 %shard_map.226.refs_1_ = f32[32,32,128]{2,1,0:T(8,128)S(1)} custom-call(bf16[64,32,128]{2,1,0:T(8,128)(2,1)S(1)} %get-tuple-element.112.norm_ref, bf16[64,32,128]{2,1,0:T(8,128)(2,1)S(1)} %get-tuple-element.108.side_ref, f32[64,512]{1,0:T(8,128)S(1)} %get-tuple-element.109.kf_ref, f32[4,64,128]{2,1,0:T(8,128)S(1)} %get-tuple-element.91.vec_ref, ...), custom_call_target="tpu_custom_call" | custom-call | flops 2000000000 | bytes 6000000 | tf_op jit(solution)/shard_map/pallas_call | solution.py:480
  36.2 1.7 %shard_map.227 = bf16[64,32,128]{2,1,0:T(8,128)(2,1)} custom-call(s32[8,128]{1,0:T(8,128)S(1)} %iota.37.at_ref, bf16[68,4,128]{2,1,0:T(4,128)(2,1)S(1)} %collective-permute-done.11.one_ref, bf16[68,4,128]{2,1,0:T(4,128)(2,1)S(1)} %collective-permute-done.12.two_ref, f32[64,512]{1,0:T(8,128)S(1)} %get-tuple-element.109.kf_ref, f32[16,128]{1,0:T(8,128)S(1)} %copy-done.8, ...), custom_call_target="tpu_custom_call" | custom-call | flops 3000000000 | bytes 9000000 | tf_op jit(solution)/shard_map/pallas_call | solution.py:480
  38.3 0.7 %shard_map.228 = (f32[48,64]{1,0:T(8,128)}, f32[64]{0:T(128)}, f32[64]{0:T(128)}, f32[64]{0:T(128)}, f32[64]{0:T(128)}, /*index=5*/f32[49,64]{1,0:T(8,128)}) custom-call(f32[56,128]{1,0:T(8,128)S(1)} %add_add_fusion.refs_0_, f32[56,128]{1,0:T(8,128)S(1)} %collective-permute-done.13.refs_1_, f32[56,128]{1,0:T(8,128)S(1)} %collective-permute-done.14.refs_2_, ...), custom_call_target="tpu_custom_call" | custom-call | flops 1000000000 | bytes 3000000 | tf_op jit(solution)/shard_map/pallas_call | solution.py:480
  (55 shorter events, 1.7 us)
Async XLA Ops:
  0.8 12.9 %copy-start.4 = (bf16[48,384]{1,0:T(8,128)(2,1)S(1)}, bf16[48,384]{1,0:T(8,128)(2,1)}, u32[]{:S(2)}) copy-start(bf16[48,384]{1,0:T(8,128)(2,1)} %constant.69.clone.spread_ref) | copy-start | bytes 110596
  0.8 12.9 %copy-start.6 = (f32[64,49]{0,1:T(8,128)S(1)}, f32[64,49]{0,1:T(8,128)}, u32[]{:S(2)}) copy-start(f32[64,49]{0,1:T(8,128)} %param.22) | copy-start | bytes 37636
  0.8 12.9 %copy-start.7 = (bf16[64,48]{0,1:T(8,128)(2,1)S(1)}, bf16[64,48]{0,1:T(8,128)(2,1)}, u32[]{:S(2)}) copy-start(bf16[64,48]{0,1:T(8,128)(2,1)} %param.18) | copy-start | bytes 18436
  0.8 12.9 %copy-start.9 = (f32[64]{0:T(128)S(1)}, f32[64]{0:T(128)}, u32[]{:S(2)}) copy-start(f32[64]{0:T(128)} %bias_ref.1) | copy-start | bytes 772
  0.8 13.3 %copy-start.5 = (f32[32,256]{1,0:T(8,128)S(1)}, f32[32,256]{1,0:T(8,128)}, u32[]{:S(2)}) copy-start(f32[32,256]{1,0:T(8,128)} %constant.75.clone.band_ref) | copy-start | bytes 98308
  0.9 17.2 %copy-start.8 = (f32[16,128]{1,0:T(8,128)S(1)}, f32[16,128]{1,0:T(8,128)}, u32[]{:S(2)}) copy-start(f32[16,128]{1,0:T(8,128)} %constant.76.clone.fringe_ref) | copy-start | bytes 24580
  2.8 16.4 %copy-start.13 = (bf16[56,384]{1,0:T(8,128)(2,1)S(1)}, bf16[56,384]{1,0:T(8,128)(2,1)}, u32[]{:S(2)}) copy-start(bf16[56,384]{1,0:T(8,128)(2,1)} %constant.77.clone.pick_ref) | copy-start | bytes 129028
  2.8 16.4 %copy-start.14 = (bf16[56,384]{1,0:T(8,128)(2,1)S(1)}, bf16[56,384]{1,0:T(8,128)(2,1)}, u32[]{:S(2)}) copy-start(bf16[56,384]{1,0:T(8,128)(2,1)} %constant.74.clone.taps_ref) | copy-start | bytes 129028
  2.8 5.2 %collective-permute-start = (bf16[960,128]{1,0:T(8,128)(2,1)S(1)}, bf16[960,128]{1,0:T(8,128)(2,1)S(1)}, u32[]{:S(2)}, u32[]{:S(2)}) collective-permute-start(bf16[960,128]{1,0:T(8,128)(2,1)S(1)} %get-tuple-element.69), channel_id=1, source_target_pairs={{0,1},{1,0},{2,3},{3,2},{4,5},{5,4},{6,7},{7,6},{8,9},{9,8},{10,11... | collective-permute-start | bytes 737288 | tf_op jit(solution)/shard_map/ppermute | solution.py:550
  3.3 6.6 %collective-permute-start.1 = (bf16[176,128]{1,0:T(8,128)(2,1)S(1)}, bf16[176,128]{1,0:T(8,128)(2,1)S(1)}, u32[]{:S(2)}, u32[]{:S(2)}) collective-permute-start(bf16[176,128]{1,0:T(8,128)(2,1)S(1)} %get-tuple-element.72), channel_id=1, source_target_pairs={{0,7},{1,2},{2,1},{3,4},{4,3},{5,6},{6,5},{7,0},{8,15},{9,10},{10,... | collective-permute-start | bytes 135176 | tf_op jit(solution)/shard_map/ppermute | solution.py:551
  8.1 11.0 %collective-permute-start.4 = (bf16[2,208,128]{2,1,0:T(8,128)(2,1)S(1)}, bf16[2,208,128]{2,1,0:T(8,128)(2,1)S(1)}, u32[]{:S(2)}, u32[]{:S(2)}) collective-permute-start(bf16[2,208,128]{2,1,0:T(8,128)(2,1)S(1)} %get-tuple-element.83), channel_id=1, source_target_pairs={{0,3},{1,2},{2,1},{3,0},{4,7},{5,6},{6,5},{7,4},{8,11},{9,10},{10,... | collective-permute-start | bytes 319496 | tf_op jit(solution)/shard_map/ppermute | solution.py:554
  8.1 11.0 %collective-permute-start.5 = (bf16[2,208,128]{2,1,0:T(8,128)(2,1)S(1)}, bf16[2,208,128]{2,1,0:T(8,128)(2,1)S(1)}, u32[]{:S(2)}, u32[]{:S(2)}) collective-permute-start(bf16[2,208,128]{2,1,0:T(8,128)(2,1)S(1)} %get-tuple-element.84), channel_id=1, source_target_pairs={{0,5},{1,4},{2,7},{3,6},{4,1},{5,0},{6,3},{7,2},{8,13},{9,12},{10,... | collective-permute-start | bytes 319496 | tf_op jit(solution)/shard_map/ppermute | solution.py:554
  9.8 9.3 %collective-permute-start.6 = (bf16[2,208,128]{2,1,0:T(8,128)(2,1)S(1)}, bf16[2,208,128]{2,1,0:T(8,128)(2,1)S(1)}, u32[]{:S(2)}, u32[]{:S(2)}) collective-permute-start(bf16[2,208,128]{2,1,0:T(8,128)(2,1)S(1)} %get-tuple-element.85), channel_id=1, source_target_pairs={{0,7},{1,6},{2,5},{3,4},{4,3},{5,2},{6,1},{7,0},{8,15},{9,14},{10,... | collective-permute-start | bytes 319496 | tf_op jit(solution)/shard_map/ppermute | solution.py:554
  10.6 5.3 %collective-permute-start.2 = (bf16[68,4,128]{2,1,0:T(4,128)(2,1)S(1)}, bf16[68,4,128]{2,1,0:T(4,128)(2,1)S(1)}, u32[]{:S(2)}, u32[]{:S(2)}) collective-permute-start(bf16[68,4,128]{2,1,0:T(4,128)(2,1)S(1)} %get-tuple-element.74), channel_id=1, source_target_pairs={{0,8},{8,0},{16,24},{24,16},{1,9},{9,1},{17,25},{25,17},{2,10},{10... | collective-permute-start | bytes 208904 | tf_op jit(solution)/shard_map/ppermute | solution.py:498
  12.1 6.0 %collective-permute-start.3 = (bf16[68,4,128]{2,1,0:T(4,128)(2,1)S(1)}, bf16[68,4,128]{2,1,0:T(4,128)(2,1)S(1)}, u32[]{:S(2)}, u32[]{:S(2)}) collective-permute-start(bf16[68,4,128]{2,1,0:T(4,128)(2,1)S(1)} %get-tuple-element.75), channel_id=1, source_target_pairs={{0,24},{8,16},{16,8},{24,0},{1,25},{9,17},{17,9},{25,1},{2,26},{10... | collective-permute-start | bytes 208904 | tf_op jit(solution)/shard_map/ppermute | solution.py:498
  23.1 1.8 %collective-permute-start.7 = (f32[56,128]{1,0:T(8,128)S(1)}, f32[56,128]{1,0:T(8,128)S(1)}, u32[]{:S(2)}, u32[]{:S(2)}) collective-permute-start(f32[56,128]{1,0:T(8,128)S(1)} %get-tuple-element.101), channel_id=1, source_target_pairs={{0,1},{1,0},{2,3},{3,2},{4,5},{5,4},{6,7},{7,6},{8,9},{9,8},{10,11... | collective-permute-start | bytes 86024 | tf_op jit(solution)/shard_map/ppermute | solution.py:616
  24.9 7.7 %collective-permute-start.10 = (f32[56,128]{1,0:T(8,128)S(1)}, f32[56,128]{1,0:T(8,128)S(1)}, u32[]{:S(2)}, u32[]{:S(2)}) collective-permute-start(f32[56,128]{1,0:T(8,128)S(1)} %add.51), channel_id=1, source_target_pairs={{0,7},{1,6},{2,5},{3,4},{4,3},{5,2},{6,1},{7,0},{8,15},{9,14},{10,... | collective-permute-start | bytes 86024 | tf_op jit(solution)/shard_map/ppermute | solution.py:616
  27.2 5.4 %collective-permute-start.9 = (f32[56,128]{1,0:T(8,128)S(1)}, f32[56,128]{1,0:T(8,128)S(1)}, u32[]{:S(2)}, u32[]{:S(2)}) collective-permute-start(f32[56,128]{1,0:T(8,128)S(1)} %add.51), channel_id=1, source_target_pairs={{0,5},{1,4},{2,7},{3,6},{4,1},{5,0},{6,3},{7,2},{8,13},{9,12},{10,... | collective-permute-start | bytes 86024 | tf_op jit(solution)/shard_map/ppermute | solution.py:616
  27.9 4.7 %collective-permute-start.8 = (f32[56,128]{1,0:T(8,128)S(1)}, f32[56,128]{1,0:T(8,128)S(1)}, u32[]{:S(2)}, u32[]{:S(2)}) collective-permute-start(f32[56,128]{1,0:T(8,128)S(1)} %add.51), channel_id=1, source_target_pairs={{0,3},{1,2},{2,1},{3,0},{4,7},{5,6},{6,5},{7,4},{8,11},{9,10},{10,... | collective-permute-start | bytes 86024 | tf_op jit(solution)/shard_map/ppermute | solution.py:616
  29.0 7.2 %collective-permute-start.12 = (bf16[68,4,128]{2,1,0:T(4,128)(2,1)S(1)}, bf16[68,4,128]{2,1,0:T(4,128)(2,1)S(1)}, u32[]{:S(2)}, u32[]{:S(2)}) collective-permute-start(bf16[68,4,128]{2,1,0:T(4,128)(2,1)S(1)} %get-tuple-element.118), channel_id=1, source_target_pairs={{0,24},{8,16},{16,8},{24,0},{1,25},{9,17},{17,9},{25,1},{2,26},{10... | collective-permute-start | bytes 208904 | tf_op jit(solution)/shard_map/ppermute | solution.py:621
  30.6 5.6 %collective-permute-start.11 = (bf16[68,4,128]{2,1,0:T(4,128)(2,1)S(1)}, bf16[68,4,128]{2,1,0:T(4,128)(2,1)S(1)}, u32[]{:S(2)}, u32[]{:S(2)}) collective-permute-start(bf16[68,4,128]{2,1,0:T(4,128)(2,1)S(1)} %get-tuple-element.117), channel_id=1, source_target_pairs={{0,8},{8,0},{16,24},{24,16},{1,9},{9,1},{17,25},{25,17},{2,10},{10... | collective-permute-start | bytes 208904 | tf_op jit(solution)/shard_map/ppermute | solution.py:621
  32.6 5.3 %collective-permute-start.15 = (f32[56,128]{1,0:T(8,128)S(1)}, f32[56,128]{1,0:T(8,128)S(1)}, u32[]{:S(2)}, u32[]{:S(2)}) collective-permute-start(f32[56,128]{1,0:T(8,128)S(1)} %add_add_fusion.refs_0_), channel_id=1, source_target_pairs={{0,25},{1,24},{2,27},{3,26},{4,29},{5,28},{6,31},{7,30},{8,17},{9,... | collective-permute-start | bytes 86024 | tf_op jit(solution)/shard_map/ppermute | solution.py:616
  33.5 4.4 %collective-permute-start.14 = (f32[56,128]{1,0:T(8,128)S(1)}, f32[56,128]{1,0:T(8,128)S(1)}, u32[]{:S(2)}, u32[]{:S(2)}) collective-permute-start(f32[56,128]{1,0:T(8,128)S(1)} %add_add_fusion.refs_0_), channel_id=1, source_target_pairs={{0,17},{1,16},{2,19},{3,18},{4,21},{5,20},{6,23},{7,22},{8,25},{9,... | collective-permute-start | bytes 86024 | tf_op jit(solution)/shard_map/ppermute | solution.py:616
  34.9 3.4 %collective-permute-start.13 = (f32[56,128]{1,0:T(8,128)S(1)}, f32[56,128]{1,0:T(8,128)S(1)}, u32[]{:S(2)}, u32[]{:S(2)}) collective-permute-start(f32[56,128]{1,0:T(8,128)S(1)} %add_add_fusion.refs_0_), channel_id=1, source_target_pairs={{0,9},{1,8},{2,11},{3,10},{4,13},{5,12},{6,15},{7,14},{8,1},{9,0},... | collective-permute-start | bytes 86024 | tf_op jit(solution)/shard_map/ppermute | solution.py:616
  (7 other events, 90.0 us)

commit v7 on v6

--- a/solution.py
+++ b/solution.py
@@ -431,25 +431,33 @@
     lax.fori_loop(0, count, one, 0, unroll=min(UNROLL, count))
 
 
-def stem_outer_kernel(parts, at_ref, one_ref, two_ref, kf_ref, fringe_ref, *refs):
-    inner_refs, (out_ref, plane_s, halo_s, out_s, sems) = refs[:parts], refs[parts:]
+def stem_outer_kernel(at_ref, one_ref, two_ref, norm_ref, side_ref, kf_ref, vec_ref, band_ref, fringe_ref, inner_ref,
+                      out_ref, plane_s, halo_s, out_s, sems):
     channels, height, _ = out_s.shape
+    done = inner_ref.shape[0]
     read_strips(at_ref, one_ref, two_ref, plane_s, halo_s)
-    count = channels // parts
+
+    def one(k, own):
+        both = mm(outer_taps(kf_ref, k, 8 * height, fringe_ref), shifted(plane_s[k], halo_s[k]))
+        edge = both[:16] + both[16:]
+        out_s[k] = jnp.concatenate(
+            [own[:8] + edge[:8], own[8:height - 8], own[height - 8:] + edge[8:]], axis=0).astype(bf16)
+
+    def first(k, carry):
+        one(k, inner_ref[k])
+        return carry
+
+    def second(n, carry):
+        k = done + n
+        both = mm(inner_taps(kf_ref, k, band_ref), shifted(norm_ref[k], side_ref[k]))
+        one(k, both[:height] + both[height:] + vec_ref[3, pl.ds(k, 1), :])
+        return carry
+
     copies = []
-    for part, inner_ref in enumerate(inner_refs):
-        def one(n, carry, part=part, inner_ref=inner_ref):
-            k = part * count + n
-            both = mm(outer_taps(kf_ref, k, 8 * height, fringe_ref), shifted(plane_s[k], halo_s[k]))
-            edge = both[:16] + both[16:]
-            own = inner_ref[n]
-            out_s[k] = jnp.concatenate(
-                [own[:8] + edge[:8], own[8:height - 8], own[height - 8:] + edge[8:]], axis=0).astype(bf16)
-            return carry
-
-        lax.fori_loop(0, count, one, 0, unroll=min(UNROLL, count))
-        here = pl.ds(part * count, count)
-        copies.append(pltpu.make_async_copy(out_s.at[here], out_ref.at[here], sems.at[part]))
+    for start, count, body in ((0, done, first), (done, channels - done, second)):
+        lax.fori_loop(0, count, body, 0, unroll=min(UNROLL, count))
+        here = pl.ds(start, count)
+        copies.append(pltpu.make_async_copy(out_s.at[here], out_ref.at[here], sems.at[len(copies)]))
         copies[-1].start()
     for copy in copies:
         copy.wait()
@@ -608,9 +616,9 @@
     )
 
     size = n_rows * n_cols
-    chunk = channels // 2
+    chunk = channels // 4
     stages = [[1], [3, 5, 7], [9, 17, 25]]
-    jobs = {0: ["side"], 1: ["one", "two", 0], 2: [1, "outer"]}
+    jobs = {0: ["side"], 1: ["one", "two", 0], 2: ["outer"]}
     parts = []
     for n, steps in enumerate(stages):
         others = [lax.ppermute(result, ("rows", "cols"), [(i, i ^ step) for i in range(size)]) for step in steps]
@@ -631,17 +639,17 @@
             elif job == "outer":
                 result, *parts = lax.optimization_barrier((result, *parts))
                 stem_output = kernel_call(
-                    functools.partial(stem_outer_kernel, len(parts)),
+                    stem_outer_kernel,
                     shaped(tile, bf16),
                     3,
-                    at, *ends, kf, const["fringe"], *parts,
-                    in_specs=[vmem] * (5 + len(parts)),
+                    at, *ends, norm, beside, kf, vec, const["band"], const["fringe"], *parts,
+                    in_specs=[vmem] * 10,
                     out_specs=beyond,
                     scratch_shapes=[
                         pltpu.VMEM((channels, 16, width), bf16),
                         pltpu.VMEM((channels, 16, width), bf16),
                         pltpu.VMEM(tile, bf16),
-                        pltpu.SemaphoreType.DMA((len(parts),)),
+                        pltpu.SemaphoreType.DMA((2,)),
                     ],
                 )
                 result, stem_output = lax.optimization_barrier((result, stem_output))

time: 39.1 us -> 39.1 us (level)
    pallas_call x13 -> x12, Pallas kernels: 14.9 us -> 14.7 us  [kernel_call(): pl.pallas_call(body, out_shape=out_shape, compiler_params=pltpu.CompilerP...]
where the time goes in v7:
time: 39.1 us; the launch traced here: 38.9 us
  starting transfers between devices  20.4 us (52%)
  Pallas kernels  14.7 us (38%)
  waiting for transfers between devices  2.63 us (7%)
  between operations  1.01 us (3%)
    pallas_call x12, Pallas kernels, kernel_call(): pl.pallas_call(body, out_shape=out_shape, compiler_params=pltpu.CompilerP...  14.7 us
    ppermute x7, starting transfers between devices, per_device(): lax.ppermute(result, ('rows', 'cols'), [(i, i ^ step) for i in range(size)])  7.74 us
    ppermute x1, starting transfers between devices, per_device(): far = lax.ppermute(edges, 'cols', pairing(n_cols, 1))  4.71 us
    ppermute x2, starting transfers between devices, swap(): lax.ppermute(part, axis, pairing(lax.axis_size(axis), n))  3.01 us
    ppermute x2, starting transfers between devices, per_device(): ends[which] = lax.ppermute(end, 'rows', pairing(n_rows, which))  2.64 us
    ppermute x2, waiting for transfers between devices, swap(): lax.ppermute(part, axis, pairing(lax.axis_size(axis), n))  2.14 us
    ppermute x3, starting transfers between devices, per_device(): lax.ppermute(pairs[n], 'cols', [(i, i ^ 2 * n + 1) for i in range(n_cols)])  1.82 us
  transfers between devices with their start and end apart: 16, of which 3 were waited for; matrix products, arithmetic and copies ran while one was open for 0% of the time, Pallas kernels for 21%

profile of v7, /device:TPU:0, one launch (start us, length us, event | category | flops | bytes accessed | tf_op | source)
XLA Modules:
  0.0 38.9 jit_solution(17739386466801549936)
XLA Ops:
  0.9 1.9 %shard_map.216 = (bf16[64,32,128]{2,1,0:T(8,128)(2,1)S(1)}, bf16[4,208,128]{2,1,0:T(8,128)(2,1)S(1)}, bf16[960,128]{1,0:T(8,128)(2,1)S(1)}, bf16[176,128]{1,0:T(8,128)(2,1)S(1)}) custom-call(s32[8,128]{1,0:T(8,128)S(1)} %iota.37.at_ref, bf16[48,4,1024]{2,1,0:T(4,128)(2,1)} %x_hbm.1, bf16[64,32,128]{2,1,0:T(8,128)(2,1)} %cot_hbm.1), custom_call_target="tpu_custom_call" | custom-call | flops 2000000000 | bytes 6000000 | tf_op jit(solution)/shard_map/pallas_call | solution.py:488
  2.8 0.5 %collective-permute-start = (bf16[960,128]{1,0:T(8,128)(2,1)S(1)}, bf16[960,128]{1,0:T(8,128)(2,1)S(1)}, u32[]{:S(2)}, u32[]{:S(2)}) collective-permute-start(bf16[960,128]{1,0:T(8,128)(2,1)S(1)} %get-tuple-element.64), channel_id=1, source_target_pairs={{0,1},{1,0},{2,3},{3,2},{4,5},{5,4},{6,7},{7,6},{8,9},{9,8},{10,11... | collective-permute-start | bytes 737288 | tf_op jit(solution)/shard_map/ppermute | solution.py:558
  3.3 4.7 %collective-permute-start.1 = (bf16[176,128]{1,0:T(8,128)(2,1)S(1)}, bf16[176,128]{1,0:T(8,128)(2,1)S(1)}, u32[]{:S(2)}, u32[]{:S(2)}) collective-permute-start(bf16[176,128]{1,0:T(8,128)(2,1)S(1)} %get-tuple-element.67), channel_id=1, source_target_pairs={{0,7},{1,2},{2,1},{3,4},{4,3},{5,6},{6,5},{7,0},{8,15},{9,10},{10,... | collective-permute-start | bytes 135176 | tf_op jit(solution)/shard_map/ppermute | solution.py:559
  8.1 1.7 %collective-permute-start.5 = (bf16[2,208,128]{2,1,0:T(8,128)(2,1)S(1)}, bf16[2,208,128]{2,1,0:T(8,128)(2,1)S(1)}, u32[]{:S(2)}, u32[]{:S(2)}) collective-permute-start(bf16[2,208,128]{2,1,0:T(8,128)(2,1)S(1)} %get-tuple-element.79), channel_id=1, source_target_pairs={{0,5},{1,4},{2,7},{3,6},{4,1},{5,0},{6,3},{7,2},{8,13},{9,12},{10,... | collective-permute-start | bytes 319496 | tf_op jit(solution)/shard_map/ppermute | solution.py:562
  10.0 0.6 %shard_map.218 = (bf16[64,32,128]{2,1,0:T(8,128)(2,1)S(1)}, bf16[68,4,128]{2,1,0:T(4,128)(2,1)S(1)}, bf16[68,4,128]{2,1,0:T(4,128)(2,1)S(1)}) custom-call(s32[8,128]{1,0:T(8,128)S(1)} %iota.37.at_ref, bf16[64,32,128]{2,1,0:T(8,128)(2,1)S(1)} %get-tuple-element.63.cot_ref, bf16[960,128]{1,0:T(8,128)(2,1)S(1)} %collective-permute-done.got_ref.near_ref, ...), custom_call_target="tpu_custom_call" | custom-call | flops 10000000 | bytes 30000 | tf_op jit(solution)/shard_map/pallas_call | solution.py:488
  10.6 1.5 %collective-permute-start.2 = (bf16[68,4,128]{2,1,0:T(4,128)(2,1)S(1)}, bf16[68,4,128]{2,1,0:T(4,128)(2,1)S(1)}, u32[]{:S(2)}, u32[]{:S(2)}) collective-permute-start(bf16[68,4,128]{2,1,0:T(4,128)(2,1)S(1)} %get-tuple-element.69), channel_id=1, source_target_pairs={{0,8},{8,0},{16,24},{24,16},{1,9},{9,1},{17,25},{25,17},{2,10},{10... | collective-permute-start | bytes 208904 | tf_op jit(solution)/shard_map/ppermute | solution.py:506
  12.1 1.5 %collective-permute-start.3 = (bf16[68,4,128]{2,1,0:T(4,128)(2,1)S(1)}, bf16[68,4,128]{2,1,0:T(4,128)(2,1)S(1)}, u32[]{:S(2)}, u32[]{:S(2)}) collective-permute-start(bf16[68,4,128]{2,1,0:T(4,128)(2,1)S(1)} %get-tuple-element.70), channel_id=1, source_target_pairs={{0,24},{8,16},{16,8},{24,0},{1,25},{9,17},{17,9},{25,1},{2,26},{10... | collective-permute-start | bytes 208904 | tf_op jit(solution)/shard_map/ppermute | solution.py:506
  13.7 0.5 %shard_map.219 = (bf16[512,384]{1,0:T(8,128)(2,1)S(1)}, f32[64,512]{1,0:T(8,128)S(1)}, f32[64,512]{1,0:T(8,128)S(1)}, f32[4,64,128]{2,1,0:T(8,128)S(1)}) custom-call(bf16[48,64]{1,0:T(8,128)(2,1)S(1)} %bitcast.5, f32[49,64]{1,0:T(8,128)S(1)} %bitcast.4, f32[64]{0:T(128)S(1)} %copy-done.9, f32[64]{0:T(128)S(1)} %copy-done.10, f32[64]{0:T(128)S(1)} %copy-done.11, ...), custom_call_target="tpu_custom_call" | custom-call | flops 10000000 | bytes 30000 | tf_op jit(solution)/shard_map/pallas_call | solution.py:488
  14.2 1.7 %shard_map.220 = (bf16[64,256,128]{2,1,0:T(8,128)(2,1)S(1)}, f32[64,32,128]{2,1,0:T(8,128)S(1)}, f32[64,128]{1,0:T(8,128)S(1)}) custom-call(bf16[64,32,128]{2,1,0:T(8,128)(2,1)S(1)} %get-tuple-element.63.cot_ref, bf16[64,32,128]{2,1,0:T(8,128)(2,1)S(1)} %get-tuple-element.72.beside_ref, f32[64,512]{1,0:T(8,128)S(1)} %get-tuple-element.74.kb_ref, ...), custom_call_target="tpu_custom_call" | custom-call | flops 10000000 | bytes 30000 | tf_op jit(solution)/shard_map/pallas_call | solution.py:488
  15.9 2.1 %collective-permute-done.3.two_ref = bf16[68,4,128]{2,1,0:T(4,128)(2,1)S(1)} collective-permute-done((bf16[68,4,128]{2,1,0:T(4,128)(2,1)S(1)}, bf16[68,4,128]{2,1,0:T(4,128)(2,1)S(1)}, u32[]{:S(2)}, u32[]{:S(2)}) %collective-permute-start.3) | collective-permute-done | bytes 69664 | tf_op jit(solution)/shard_map/ppermute | solution.py:506
  18.1 1.0 %shard_map.221 = (bf16[64,128,128]{2,1,0:T(8,128)(2,1)S(1)}, f32[64,16,128]{2,1,0:T(8,128)S(1)}) custom-call(s32[8,128]{1,0:T(8,128)S(1)} %iota.37.at_ref, bf16[68,4,128]{2,1,0:T(4,128)(2,1)S(1)} %collective-permute-done.2.one_ref, bf16[68,4,128]{2,1,0:T(4,128)(2,1)S(1)} %collective-permute-done.3.two_ref, f32[64,32,128]{2,1,0:T(8,128)S(1)} %get-tuple-element.75.grad_ref, ...), custom_call_target="tpu_custom_call" | custom-call | flops 10000000 | bytes 30000 | tf_op jit(solution)/shard_map/pallas_call | solution.py:488
  19.2 3.9 %shard_map.223 = (bf16[64,32,128]{2,1,0:T(8,128)(2,1)S(1)}, f32[56,128]{1,0:T(8,128)S(1)}) custom-call(bf16[8,208,128]{2,1,0:T(8,128)(2,1)S(1)} %shard_map.222.x_ref, bf16[512,384]{1,0:T(8,128)(2,1)S(1)} %get-tuple-element.85.wk_ref, f32[4,64,128]{2,1,0:T(8,128)S(1)} %get-tuple-element.86.vec_ref, f32[64,32,128]{2,1,0:T(8,128)S(1)} %get-tuple-element.75.grad_ref, ...), custom_call_target="tpu_custom_call" | custom-call | flops 6000000000 | bytes 18000000 | tf_op jit(solution)/shard_map/pallas_call | solution.py:488
  23.1 0.9 %collective-permute-start.7 = (f32[56,128]{1,0:T(8,128)S(1)}, f32[56,128]{1,0:T(8,128)S(1)}, u32[]{:S(2)}, u32[]{:S(2)}) collective-permute-start(f32[56,128]{1,0:T(8,128)S(1)} %get-tuple-element.96), channel_id=1, source_target_pairs={{0,1},{1,0},{2,3},{3,2},{4,5},{5,4},{6,7},{7,6},{8,9},{9,8},{10,11... | collective-permute-start | bytes 86024 | tf_op jit(solution)/shard_map/ppermute | solution.py:624
  24.0 0.8 %shard_map.224 = (bf16[64,32,128]{2,1,0:T(8,128)(2,1)S(1)}, bf16[68,4,128]{2,1,0:T(4,128)(2,1)S(1)}, bf16[68,4,128]{2,1,0:T(4,128)(2,1)S(1)}) custom-call(s32[8,128]{1,0:T(8,128)S(1)} %iota.37.at_ref, bf16[8,208,128]{2,1,0:T(8,128)(2,1)S(1)} %shard_map.222.x_ref, bf16[64,32,128]{2,1,0:T(8,128)(2,1)S(1)} %get-tuple-element.102.norm_ref, ...), custom_call_target="tpu_custom_call" | custom-call | flops 1000000000 | bytes 3000000 | tf_op jit(solution)/shard_map/pallas_call | solution.py:488
  24.9 2.3 %collective-permute-start.10 = (f32[56,128]{1,0:T(8,128)S(1)}, f32[56,128]{1,0:T(8,128)S(1)}, u32[]{:S(2)}, u32[]{:S(2)}) collective-permute-start(f32[56,128]{1,0:T(8,128)S(1)} %add.51), channel_id=1, source_target_pairs={{0,7},{1,6},{2,5},{3,4},{4,3},{5,2},{6,1},{7,0},{8,15},{9,14},{10,... | collective-permute-start | bytes 86024 | tf_op jit(solution)/shard_map/ppermute | solution.py:624
  27.2 0.7 %collective-permute-start.9 = (f32[56,128]{1,0:T(8,128)S(1)}, f32[56,128]{1,0:T(8,128)S(1)}, u32[]{:S(2)}, u32[]{:S(2)}) collective-permute-start(f32[56,128]{1,0:T(8,128)S(1)} %add.51), channel_id=1, source_target_pairs={{0,5},{1,4},{2,7},{3,6},{4,1},{5,0},{6,3},{7,2},{8,13},{9,12},{10,... | collective-permute-start | bytes 86024 | tf_op jit(solution)/shard_map/ppermute | solution.py:624
  27.9 1.1 %collective-permute-start.8 = (f32[56,128]{1,0:T(8,128)S(1)}, f32[56,128]{1,0:T(8,128)S(1)}, u32[]{:S(2)}, u32[]{:S(2)}) collective-permute-start(f32[56,128]{1,0:T(8,128)S(1)} %add.51), channel_id=1, source_target_pairs={{0,3},{1,2},{2,1},{3,0},{4,7},{5,6},{6,5},{7,4},{8,11},{9,10},{10,... | collective-permute-start | bytes 86024 | tf_op jit(solution)/shard_map/ppermute | solution.py:624
  29.0 1.6 %collective-permute-start.12 = (bf16[68,4,128]{2,1,0:T(4,128)(2,1)S(1)}, bf16[68,4,128]{2,1,0:T(4,128)(2,1)S(1)}, u32[]{:S(2)}, u32[]{:S(2)}) collective-permute-start(bf16[68,4,128]{2,1,0:T(4,128)(2,1)S(1)} %get-tuple-element.109), channel_id=1, source_target_pairs={{0,24},{8,16},{16,8},{24,0},{1,25},{9,17},{17,9},{25,1},{2,26},{10... | collective-permute-start | bytes 208904 | tf_op jit(solution)/shard_map/ppermute | solution.py:629
  30.6 1.0 %collective-permute-start.11 = (bf16[68,4,128]{2,1,0:T(4,128)(2,1)S(1)}, bf16[68,4,128]{2,1,0:T(4,128)(2,1)S(1)}, u32[]{:S(2)}, u32[]{:S(2)}) collective-permute-start(bf16[68,4,128]{2,1,0:T(4,128)(2,1)S(1)} %get-tuple-element.108), channel_id=1, source_target_pairs={{0,8},{8,0},{16,24},{24,16},{1,9},{9,1},{17,25},{25,17},{2,10},{10... | collective-permute-start | bytes 208904 | tf_op jit(solution)/shard_map/ppermute | solution.py:629
  31.6 0.6 %shard_map.225.inner_ref = f32[16,32,128]{2,1,0:T(8,128)S(1)} custom-call(bf16[64,32,128]{2,1,0:T(8,128)(2,1)S(1)} %get-tuple-element.102.norm_ref, bf16[64,32,128]{2,1,0:T(8,128)(2,1)S(1)} %get-tuple-element.103.side_ref, f32[64,512]{1,0:T(8,128)S(1)} %get-tuple-element.104.kf_ref, f32[4,64,128]{2,1,0:T(8,128)S(1)} %get-tuple-element.86.vec_ref, ...), custom_call_target="tpu_custom_call" | custom-call | flops 2000000000 | bytes 6000000 | tf_op jit(solution)/shard_map/pallas_call | solution.py:488
  32.2 1.3 %collective-permute-start.15 = (f32[56,128]{1,0:T(8,128)S(1)}, f32[56,128]{1,0:T(8,128)S(1)}, u32[]{:S(2)}, u32[]{:S(2)}) collective-permute-start(f32[56,128]{1,0:T(8,128)S(1)} %add_add_fusion.refs_0_), channel_id=1, source_target_pairs={{0,25},{1,24},{2,27},{3,26},{4,29},{5,28},{6,31},{7,30},{8,17},{9,... | collective-permute-start | bytes 86024 | tf_op jit(solution)/shard_map/ppermute | solution.py:624
  33.5 1.3 %collective-permute-start.14 = (f32[56,128]{1,0:T(8,128)S(1)}, f32[56,128]{1,0:T(8,128)S(1)}, u32[]{:S(2)}, u32[]{:S(2)}) collective-permute-start(f32[56,128]{1,0:T(8,128)S(1)} %add_add_fusion.refs_0_), channel_id=1, source_target_pairs={{0,17},{1,16},{2,19},{3,18},{4,21},{5,20},{6,23},{7,22},{8,25},{9,... | collective-permute-start | bytes 86024 | tf_op jit(solution)/shard_map/ppermute | solution.py:624
  35.4 2.8 %shard_map.226 = bf16[64,32,128]{2,1,0:T(8,128)(2,1)} custom-call(s32[8,128]{1,0:T(8,128)S(1)} %iota.37.at_ref, bf16[68,4,128]{2,1,0:T(4,128)(2,1)S(1)} %collective-permute-done.11.one_ref, bf16[68,4,128]{2,1,0:T(4,128)(2,1)S(1)} %collective-permute-done.12.two_ref, bf16[64,32,128]{2,1,0:T(8,128)(2,1)S(1)} %get-tuple-element.102.norm_ref, ...), custom_call_target="tpu_custom_call" | custom-call | flops 3000000000 | bytes 9000000 | tf_op jit(solution)/shard_map/pallas_call | solution.py:488
  38.2 0.7 %shard_map.227 = (f32[48,64]{1,0:T(8,128)}, f32[64]{0:T(128)}, f32[64]{0:T(128)}, f32[64]{0:T(128)}, f32[64]{0:T(128)}, /*index=5*/f32[49,64]{1,0:T(8,128)}) custom-call(f32[56,128]{1,0:T(8,128)S(1)} %add_add_fusion.refs_0_, f32[56,128]{1,0:T(8,128)S(1)} %collective-permute-done.13.refs_1_, f32[56,128]{1,0:T(8,128)S(1)} %collective-permute-done.14.refs_2_, ...), custom_call_target="tpu_custom_call" | custom-call | flops 1000000000 | bytes 3000000 | tf_op jit(solution)/shard_map/pallas_call | solution.py:488
  (54 shorter events, 1.2 us)
Async XLA Ops:
  0.8 12.9 %copy-start.4 = (bf16[48,384]{1,0:T(8,128)(2,1)S(1)}, bf16[48,384]{1,0:T(8,128)(2,1)}, u32[]{:S(2)}) copy-start(bf16[48,384]{1,0:T(8,128)(2,1)} %constant.69.clone.spread_ref) | copy-start | bytes 110596
  0.8 12.9 %copy-start.6 = (f32[64,49]{0,1:T(8,128)S(1)}, f32[64,49]{0,1:T(8,128)}, u32[]{:S(2)}) copy-start(f32[64,49]{0,1:T(8,128)} %param.22) | copy-start | bytes 37636
  0.8 12.9 %copy-start.7 = (bf16[64,48]{0,1:T(8,128)(2,1)S(1)}, bf16[64,48]{0,1:T(8,128)(2,1)}, u32[]{:S(2)}) copy-start(bf16[64,48]{0,1:T(8,128)(2,1)} %param.18) | copy-start | bytes 18436
  0.8 12.9 %copy-start.9 = (f32[64]{0:T(128)S(1)}, f32[64]{0:T(128)}, u32[]{:S(2)}) copy-start(f32[64]{0:T(128)} %bias_ref.1) | copy-start | bytes 772
  0.8 13.3 %copy-start.5 = (f32[32,256]{1,0:T(8,128)S(1)}, f32[32,256]{1,0:T(8,128)}, u32[]{:S(2)}) copy-start(f32[32,256]{1,0:T(8,128)} %constant.75.clone.band_ref) | copy-start | bytes 98308
  0.9 17.2 %copy-start.8 = (f32[16,128]{1,0:T(8,128)S(1)}, f32[16,128]{1,0:T(8,128)}, u32[]{:S(2)}) copy-start(f32[16,128]{1,0:T(8,128)} %constant.76.clone.fringe_ref) | copy-start | bytes 24580
  2.8 16.4 %copy-start.13 = (bf16[56,384]{1,0:T(8,128)(2,1)S(1)}, bf16[56,384]{1,0:T(8,128)(2,1)}, u32[]{:S(2)}) copy-start(bf16[56,384]{1,0:T(8,128)(2,1)} %constant.77.clone.pick_ref) | copy-start | bytes 129028
  2.8 16.4 %copy-start.14 = (bf16[56,384]{1,0:T(8,128)(2,1)S(1)}, bf16[56,384]{1,0:T(8,128)(2,1)}, u32[]{:S(2)}) copy-start(bf16[56,384]{1,0:T(8,128)(2,1)} %constant.74.clone.taps_ref) | copy-start | bytes 129028
  2.8 5.2 %collective-permute-start = (bf16[960,128]{1,0:T(8,128)(2,1)S(1)}, bf16[960,128]{1,0:T(8,128)(2,1)S(1)}, u32[]{:S(2)}, u32[]{:S(2)}) collective-permute-start(bf16[960,128]{1,0:T(8,128)(2,1)S(1)} %get-tuple-element.64), channel_id=1, source_target_pairs={{0,1},{1,0},{2,3},{3,2},{4,5},{5,4},{6,7},{7,6},{8,9},{9,8},{10,11... | collective-permute-start | bytes 737288 | tf_op jit(solution)/shard_map/ppermute | solution.py:558
  3.3 6.6 %collective-permute-start.1 = (bf16[176,128]{1,0:T(8,128)(2,1)S(1)}, bf16[176,128]{1,0:T(8,128)(2,1)S(1)}, u32[]{:S(2)}, u32[]{:S(2)}) collective-permute-start(bf16[176,128]{1,0:T(8,128)(2,1)S(1)} %get-tuple-element.67), channel_id=1, source_target_pairs={{0,7},{1,2},{2,1},{3,4},{4,3},{5,6},{6,5},{7,0},{8,15},{9,10},{10,... | collective-permute-start | bytes 135176 | tf_op jit(solution)/shard_map/ppermute | solution.py:559
  8.1 11.0 %collective-permute-start.4 = (bf16[2,208,128]{2,1,0:T(8,128)(2,1)S(1)}, bf16[2,208,128]{2,1,0:T(8,128)(2,1)S(1)}, u32[]{:S(2)}, u32[]{:S(2)}) collective-permute-start(bf16[2,208,128]{2,1,0:T(8,128)(2,1)S(1)} %get-tuple-element.78), channel_id=1, source_target_pairs={{0,3},{1,2},{2,1},{3,0},{4,7},{5,6},{6,5},{7,4},{8,11},{9,10},{10,... | collective-permute-start | bytes 319496 | tf_op jit(solution)/shard_map/ppermute | solution.py:562
  8.1 11.0 %collective-permute-start.5 = (bf16[2,208,128]{2,1,0:T(8,128)(2,1)S(1)}, bf16[2,208,128]{2,1,0:T(8,128)(2,1)S(1)}, u32[]{:S(2)}, u32[]{:S(2)}) collective-permute-start(bf16[2,208,128]{2,1,0:T(8,128)(2,1)S(1)} %get-tuple-element.79), channel_id=1, source_target_pairs={{0,5},{1,4},{2,7},{3,6},{4,1},{5,0},{6,3},{7,2},{8,13},{9,12},{10,... | collective-permute-start | bytes 319496 | tf_op jit(solution)/shard_map/ppermute | solution.py:562
  9.8 9.3 %collective-permute-start.6 = (bf16[2,208,128]{2,1,0:T(8,128)(2,1)S(1)}, bf16[2,208,128]{2,1,0:T(8,128)(2,1)S(1)}, u32[]{:S(2)}, u32[]{:S(2)}) collective-permute-start(bf16[2,208,128]{2,1,0:T(8,128)(2,1)S(1)} %get-tuple-element.80), channel_id=1, source_target_pairs={{0,7},{1,6},{2,5},{3,4},{4,3},{5,2},{6,1},{7,0},{8,15},{9,14},{10,... | collective-permute-start | bytes 319496 | tf_op jit(solution)/shard_map/ppermute | solution.py:562
  10.6 5.3 %collective-permute-start.2 = (bf16[68,4,128]{2,1,0:T(4,128)(2,1)S(1)}, bf16[68,4,128]{2,1,0:T(4,128)(2,1)S(1)}, u32[]{:S(2)}, u32[]{:S(2)}) collective-permute-start(bf16[68,4,128]{2,1,0:T(4,128)(2,1)S(1)} %get-tuple-element.69), channel_id=1, source_target_pairs={{0,8},{8,0},{16,24},{24,16},{1,9},{9,1},{17,25},{25,17},{2,10},{10... | collective-permute-start | bytes 208904 | tf_op jit(solution)/shard_map/ppermute | solution.py:506
  12.1 6.0 %collective-permute-start.3 = (bf16[68,4,128]{2,1,0:T(4,128)(2,1)S(1)}, bf16[68,4,128]{2,1,0:T(4,128)(2,1)S(1)}, u32[]{:S(2)}, u32[]{:S(2)}) collective-permute-start(bf16[68,4,128]{2,1,0:T(4,128)(2,1)S(1)} %get-tuple-element.70), channel_id=1, source_target_pairs={{0,24},{8,16},{16,8},{24,0},{1,25},{9,17},{17,9},{25,1},{2,26},{10... | collective-permute-start | bytes 208904 | tf_op jit(solution)/shard_map/ppermute | solution.py:506
  23.1 1.8 %collective-permute-start.7 = (f32[56,128]{1,0:T(8,128)S(1)}, f32[56,128]{1,0:T(8,128)S(1)}, u32[]{:S(2)}, u32[]{:S(2)}) collective-permute-start(f32[56,128]{1,0:T(8,128)S(1)} %get-tuple-element.96), channel_id=1, source_target_pairs={{0,1},{1,0},{2,3},{3,2},{4,5},{5,4},{6,7},{7,6},{8,9},{9,8},{10,11... | collective-permute-start | bytes 86024 | tf_op jit(solution)/shard_map/ppermute | solution.py:624
  24.9 7.3 %collective-permute-start.10 = (f32[56,128]{1,0:T(8,128)S(1)}, f32[56,128]{1,0:T(8,128)S(1)}, u32[]{:S(2)}, u32[]{:S(2)}) collective-permute-start(f32[56,128]{1,0:T(8,128)S(1)} %add.51), channel_id=1, source_target_pairs={{0,7},{1,6},{2,5},{3,4},{4,3},{5,2},{6,1},{7,0},{8,15},{9,14},{10,... | collective-permute-start | bytes 86024 | tf_op jit(solution)/shard_map/ppermute | solution.py:624
  27.2 5.0 %collective-permute-start.9 = (f32[56,128]{1,0:T(8,128)S(1)}, f32[56,128]{1,0:T(8,128)S(1)}, u32[]{:S(2)}, u32[]{:S(2)}) collective-permute-start(f32[56,128]{1,0:T(8,128)S(1)} %add.51), channel_id=1, source_target_pairs={{0,5},{1,4},{2,7},{3,6},{4,1},{5,0},{6,3},{7,2},{8,13},{9,12},{10,... | collective-permute-start | bytes 86024 | tf_op jit(solution)/shard_map/ppermute | solution.py:624
  27.9 4.3 %collective-permute-start.8 = (f32[56,128]{1,0:T(8,128)S(1)}, f32[56,128]{1,0:T(8,128)S(1)}, u32[]{:S(2)}, u32[]{:S(2)}) collective-permute-start(f32[56,128]{1,0:T(8,128)S(1)} %add.51), channel_id=1, source_target_pairs={{0,3},{1,2},{2,1},{3,0},{4,7},{5,6},{6,5},{7,4},{8,11},{9,10},{10,... | collective-permute-start | bytes 86024 | tf_op jit(solution)/shard_map/ppermute | solution.py:624
  29.0 6.0 %collective-permute-start.12 = (bf16[68,4,128]{2,1,0:T(4,128)(2,1)S(1)}, bf16[68,4,128]{2,1,0:T(4,128)(2,1)S(1)}, u32[]{:S(2)}, u32[]{:S(2)}) collective-permute-start(bf16[68,4,128]{2,1,0:T(4,128)(2,1)S(1)} %get-tuple-element.109), channel_id=1, source_target_pairs={{0,24},{8,16},{16,8},{24,0},{1,25},{9,17},{17,9},{25,1},{2,26},{10... | collective-permute-start | bytes 208904 | tf_op jit(solution)/shard_map/ppermute | solution.py:629
  30.6 4.8 %collective-permute-start.11 = (bf16[68,4,128]{2,1,0:T(4,128)(2,1)S(1)}, bf16[68,4,128]{2,1,0:T(4,128)(2,1)S(1)}, u32[]{:S(2)}, u32[]{:S(2)}) collective-permute-start(bf16[68,4,128]{2,1,0:T(4,128)(2,1)S(1)} %get-tuple-element.108), channel_id=1, source_target_pairs={{0,8},{8,0},{16,24},{24,16},{1,9},{9,1},{17,25},{25,17},{2,10},{10... | collective-permute-start | bytes 208904 | tf_op jit(solution)/shard_map/ppermute | solution.py:629
  32.2 6.0 %collective-permute-start.15 = (f32[56,128]{1,0:T(8,128)S(1)}, f32[56,128]{1,0:T(8,128)S(1)}, u32[]{:S(2)}, u32[]{:S(2)}) collective-permute-start(f32[56,128]{1,0:T(8,128)S(1)} %add_add_fusion.refs_0_), channel_id=1, source_target_pairs={{0,25},{1,24},{2,27},{3,26},{4,29},{5,28},{6,31},{7,30},{8,17},{9,... | collective-permute-start | bytes 86024 | tf_op jit(solution)/shard_map/ppermute | solution.py:624
  33.5 4.7 %collective-permute-start.14 = (f32[56,128]{1,0:T(8,128)S(1)}, f32[56,128]{1,0:T(8,128)S(1)}, u32[]{:S(2)}, u32[]{:S(2)}) collective-permute-start(f32[56,128]{1,0:T(8,128)S(1)} %add_add_fusion.refs_0_), channel_id=1, source_target_pairs={{0,17},{1,16},{2,19},{3,18},{4,21},{5,20},{6,23},{7,22},{8,25},{9,... | collective-permute-start | bytes 86024 | tf_op jit(solution)/shard_map/ppermute | solution.py:624
  34.8 3.4 %collective-permute-start.13 = (f32[56,128]{1,0:T(8,128)S(1)}, f32[56,128]{1,0:T(8,128)S(1)}, u32[]{:S(2)}, u32[]{:S(2)}) collective-permute-start(f32[56,128]{1,0:T(8,128)S(1)} %add_add_fusion.refs_0_), channel_id=1, source_target_pairs={{0,9},{1,8},{2,11},{3,10},{4,13},{5,12},{6,15},{7,14},{8,1},{9,0},... | collective-permute-start | bytes 86024 | tf_op jit(solution)/shard_map/ppermute | solution.py:624
  (7 other events, 90.0 us)

commit v8 on v7

--- a/solution.py
+++ b/solution.py
@@ -383,9 +383,9 @@
         rim += pltpu.roll(diag_s[:, b, inner:], OUTER - b, 1)
     line = jnp.concatenate([line, rim], axis=1) * factor
     line = jnp.concatenate([jnp.zeros((LANES - channels, line.shape[1]), f32), line], axis=0)
-    out_ref[...] = sum(mm(taps_ref[...], part, NT) for part in split2(line))
+    out_ref[...] = mm(jnp.concatenate([taps_ref[...]] * 2, axis=1), jnp.concatenate(split2(line), axis=1), NT)
     parts = jnp.concatenate([jnp.sum(scale_part, axis=1), jnp.sum(shift_part, axis=1), total_ref[...]], axis=1)
-    first = sum(mm(pick_ref[...], part, NT) for part in split2(parts))
+    first = mm(jnp.concatenate([pick_ref[...]] * 2, axis=1), jnp.concatenate(split2(parts), axis=1), NT)
     out_ref[:, :channels] = first + by_color[:56]
 
 
@@ -542,7 +542,7 @@
             in_vmem(tile, bf16),
             in_vmem((chips, block_rows, LANES), bf16),
             in_vmem((chips * block_rows + edge_rows, LANES), bf16),
-            in_vmem((edge_rows + 48, LANES), bf16),
+            in_vmem((edge_rows + 32, LANES), bf16),
         ),
         2,
         at, *(pltpu.with_memory_space_constraint(arg, pltpu.HBM) for arg in (file_pixels, cotangent)),

time: 39.1 us -> 39.1 us (level)
  transfers between devices with their start and end apart: 16 -> 16, of which waited for: 3 -> 2; matrix products, arithmetic and copies ran while one was open for 0% -> 0% of each run, Pallas kernels for 21% -> 21%
where the time goes in v8:
time: 39.1 us; the launch traced here: 38.9 us
  starting transfers between devices  20.5 us (52%)
  Pallas kernels  14.7 us (38%)
  waiting for transfers between devices  2.62 us (7%)
  between operations  1 us (3%)
    pallas_call x12, Pallas kernels, kernel_call(): pl.pallas_call(body, out_shape=out_shape, compiler_params=pltpu.CompilerP...  14.7 us
    ppermute x7, starting transfers between devices, per_device(): lax.ppermute(result, ('rows', 'cols'), [(i, i ^ step) for i in range(size)])  7.73 us
    ppermute x1, starting transfers between devices, per_device(): far = lax.ppermute(edges, 'cols', pairing(n_cols, 1))  4.71 us
    ppermute x2, starting transfers between devices, swap(): lax.ppermute(part, axis, pairing(lax.axis_size(axis), n))  3.01 us
    ppermute x2, starting transfers between devices, per_device(): ends[which] = lax.ppermute(end, 'rows', pairing(n_rows, which))  2.67 us
    ppermute x2, waiting for transfers between devices, swap(): lax.ppermute(part, axis, pairing(lax.axis_size(axis), n))  2.11 us
    ppermute x3, starting transfers between devices, per_device(): lax.ppermute(pairs[n], 'cols', [(i, i ^ 2 * n + 1) for i in range(n_cols)])  1.82 us
  transfers between devices with their start and end apart: 16, of which 2 were waited for; matrix products, arithmetic and copies ran while one was open for 0% of the time, Pallas kernels for 21%

profile of v8, /device:TPU:0, one launch (start us, length us, event | category | flops | bytes accessed | tf_op | source)
XLA Modules:
  0.0 38.9 jit_solution(3869113196246589507)
XLA Ops:
  0.9 1.9 %shard_map.216 = (bf16[64,32,128]{2,1,0:T(8,128)(2,1)S(1)}, bf16[4,208,128]{2,1,0:T(8,128)(2,1)S(1)}, bf16[960,128]{1,0:T(8,128)(2,1)S(1)}, bf16[160,128]{1,0:T(8,128)(2,1)S(1)}) custom-call(s32[8,128]{1,0:T(8,128)S(1)} %iota.37.at_ref, bf16[48,4,1024]{2,1,0:T(4,128)(2,1)} %x_hbm.1, bf16[64,32,128]{2,1,0:T(8,128)(2,1)} %cot_hbm.1), custom_call_target="tpu_custom_call" | custom-call | flops 2000000000 | bytes 6000000 | tf_op jit(solution)/shard_map/pallas_call | solution.py:488
  2.8 0.5 %collective-permute-start = (bf16[960,128]{1,0:T(8,128)(2,1)S(1)}, bf16[960,128]{1,0:T(8,128)(2,1)S(1)}, u32[]{:S(2)}, u32[]{:S(2)}) collective-permute-start(bf16[960,128]{1,0:T(8,128)(2,1)S(1)} %get-tuple-element.64), channel_id=1, source_target_pairs={{0,1},{1,0},{2,3},{3,2},{4,5},{5,4},{6,7},{7,6},{8,9},{9,8},{10,11... | collective-permute-start | bytes 737288 | tf_op jit(solution)/shard_map/ppermute | solution.py:558
  3.3 4.7 %collective-permute-start.1 = (bf16[160,128]{1,0:T(8,128)(2,1)S(1)}, bf16[160,128]{1,0:T(8,128)(2,1)S(1)}, u32[]{:S(2)}, u32[]{:S(2)}) collective-permute-start(bf16[160,128]{1,0:T(8,128)(2,1)S(1)} %get-tuple-element.67), channel_id=1, source_target_pairs={{0,7},{1,2},{2,1},{3,4},{4,3},{5,6},{6,5},{7,0},{8,15},{9,10},{10,... | collective-permute-start | bytes 122888 | tf_op jit(solution)/shard_map/ppermute | solution.py:559
  8.1 1.7 %collective-permute-start.5 = (bf16[2,208,128]{2,1,0:T(8,128)(2,1)S(1)}, bf16[2,208,128]{2,1,0:T(8,128)(2,1)S(1)}, u32[]{:S(2)}, u32[]{:S(2)}) collective-permute-start(bf16[2,208,128]{2,1,0:T(8,128)(2,1)S(1)} %get-tuple-element.79), channel_id=1, source_target_pairs={{0,5},{1,4},{2,7},{3,6},{4,1},{5,0},{6,3},{7,2},{8,13},{9,12},{10,... | collective-permute-start | bytes 319496 | tf_op jit(solution)/shard_map/ppermute | solution.py:562
  9.9 0.6 %shard_map.218 = (bf16[64,32,128]{2,1,0:T(8,128)(2,1)S(1)}, bf16[68,4,128]{2,1,0:T(4,128)(2,1)S(1)}, bf16[68,4,128]{2,1,0:T(4,128)(2,1)S(1)}) custom-call(s32[8,128]{1,0:T(8,128)S(1)} %iota.37.at_ref, bf16[64,32,128]{2,1,0:T(8,128)(2,1)S(1)} %get-tuple-element.63.cot_ref, bf16[960,128]{1,0:T(8,128)(2,1)S(1)} %collective-permute-done.got_ref.near_ref, ...), custom_call_target="tpu_custom_call" | custom-call | flops 10000000 | bytes 30000 | tf_op jit(solution)/shard_map/pallas_call | solution.py:488
  10.5 1.5 %collective-permute-start.2 = (bf16[68,4,128]{2,1,0:T(4,128)(2,1)S(1)}, bf16[68,4,128]{2,1,0:T(4,128)(2,1)S(1)}, u32[]{:S(2)}, u32[]{:S(2)}) collective-permute-start(bf16[68,4,128]{2,1,0:T(4,128)(2,1)S(1)} %get-tuple-element.69), channel_id=1, source_target_pairs={{0,8},{8,0},{16,24},{24,16},{1,9},{9,1},{17,25},{25,17},{2,10},{10... | collective-permute-start | bytes 208904 | tf_op jit(solution)/shard_map/ppermute | solution.py:506
  12.1 1.5 %collective-permute-start.3 = (bf16[68,4,128]{2,1,0:T(4,128)(2,1)S(1)}, bf16[68,4,128]{2,1,0:T(4,128)(2,1)S(1)}, u32[]{:S(2)}, u32[]{:S(2)}) collective-permute-start(bf16[68,4,128]{2,1,0:T(4,128)(2,1)S(1)} %get-tuple-element.70), channel_id=1, source_target_pairs={{0,24},{8,16},{16,8},{24,0},{1,25},{9,17},{17,9},{25,1},{2,26},{10... | collective-permute-start | bytes 208904 | tf_op jit(solution)/shard_map/ppermute | solution.py:506
  13.6 0.5 %shard_map.219 = (bf16[512,384]{1,0:T(8,128)(2,1)S(1)}, f32[64,512]{1,0:T(8,128)S(1)}, f32[64,512]{1,0:T(8,128)S(1)}, f32[4,64,128]{2,1,0:T(8,128)S(1)}) custom-call(bf16[48,64]{1,0:T(8,128)(2,1)S(1)} %bitcast.5, f32[49,64]{1,0:T(8,128)S(1)} %bitcast.4, f32[64]{0:T(128)S(1)} %copy-done.9, f32[64]{0:T(128)S(1)} %copy-done.10, f32[64]{0:T(128)S(1)} %copy-done.11, ...), custom_call_target="tpu_custom_call" | custom-call | flops 10000000 | bytes 30000 | tf_op jit(solution)/shard_map/pallas_call | solution.py:488
  14.1 1.7 %shard_map.220 = (bf16[64,256,128]{2,1,0:T(8,128)(2,1)S(1)}, f32[64,32,128]{2,1,0:T(8,128)S(1)}, f32[64,128]{1,0:T(8,128)S(1)}) custom-call(bf16[64,32,128]{2,1,0:T(8,128)(2,1)S(1)} %get-tuple-element.63.cot_ref, bf16[64,32,128]{2,1,0:T(8,128)(2,1)S(1)} %get-tuple-element.72.beside_ref, f32[64,512]{1,0:T(8,128)S(1)} %get-tuple-element.74.kb_ref, ...), custom_call_target="tpu_custom_call" | custom-call | flops 10000000 | bytes 30000 | tf_op jit(solution)/shard_map/pallas_call | solution.py:488
  15.9 2.1 %collective-permute-done.3.two_ref = bf16[68,4,128]{2,1,0:T(4,128)(2,1)S(1)} collective-permute-done((bf16[68,4,128]{2,1,0:T(4,128)(2,1)S(1)}, bf16[68,4,128]{2,1,0:T(4,128)(2,1)S(1)}, u32[]{:S(2)}, u32[]{:S(2)}) %collective-permute-start.3) | collective-permute-done | bytes 69664 | tf_op jit(solution)/shard_map/ppermute | solution.py:506
  18.0 1.0 %shard_map.221 = (bf16[64,128,128]{2,1,0:T(8,128)(2,1)S(1)}, f32[64,16,128]{2,1,0:T(8,128)S(1)}) custom-call(s32[8,128]{1,0:T(8,128)S(1)} %iota.37.at_ref, bf16[68,4,128]{2,1,0:T(4,128)(2,1)S(1)} %collective-permute-done.2.one_ref, bf16[68,4,128]{2,1,0:T(4,128)(2,1)S(1)} %collective-permute-done.3.two_ref, f32[64,32,128]{2,1,0:T(8,128)S(1)} %get-tuple-element.75.grad_ref, ...), custom_call_target="tpu_custom_call" | custom-call | flops 10000000 | bytes 30000 | tf_op jit(solution)/shard_map/pallas_call | solution.py:488
  19.1 3.9 %shard_map.223 = (bf16[64,32,128]{2,1,0:T(8,128)(2,1)S(1)}, f32[56,128]{1,0:T(8,128)S(1)}) custom-call(bf16[8,208,128]{2,1,0:T(8,128)(2,1)S(1)} %shard_map.222.x_ref, bf16[512,384]{1,0:T(8,128)(2,1)S(1)} %get-tuple-element.85.wk_ref, f32[4,64,128]{2,1,0:T(8,128)S(1)} %get-tuple-element.86.vec_ref, f32[64,32,128]{2,1,0:T(8,128)S(1)} %get-tuple-element.75.grad_ref, ...), custom_call_target="tpu_custom_call" | custom-call | flops 6000000000 | bytes 18000000 | tf_op jit(solution)/shard_map/pallas_call | solution.py:488
  23.0 1.0 %collective-permute-start.7 = (f32[56,128]{1,0:T(8,128)S(1)}, f32[56,128]{1,0:T(8,128)S(1)}, u32[]{:S(2)}, u32[]{:S(2)}) collective-permute-start(f32[56,128]{1,0:T(8,128)S(1)} %get-tuple-element.96), channel_id=1, source_target_pairs={{0,1},{1,0},{2,3},{3,2},{4,5},{5,4},{6,7},{7,6},{8,9},{9,8},{10,11... | collective-permute-start | bytes 86024 | tf_op jit(solution)/shard_map/ppermute | solution.py:624
  24.0 0.8 %shard_map.224 = (bf16[64,32,128]{2,1,0:T(8,128)(2,1)S(1)}, bf16[68,4,128]{2,1,0:T(4,128)(2,1)S(1)}, bf16[68,4,128]{2,1,0:T(4,128)(2,1)S(1)}) custom-call(s32[8,128]{1,0:T(8,128)S(1)} %iota.37.at_ref, bf16[8,208,128]{2,1,0:T(8,128)(2,1)S(1)} %shard_map.222.x_ref, bf16[64,32,128]{2,1,0:T(8,128)(2,1)S(1)} %get-tuple-element.102.norm_ref, ...), custom_call_target="tpu_custom_call" | custom-call | flops 1000000000 | bytes 3000000 | tf_op jit(solution)/shard_map/pallas_call | solution.py:488
  24.9 2.3 %collective-permute-start.10 = (f32[56,128]{1,0:T(8,128)S(1)}, f32[56,128]{1,0:T(8,128)S(1)}, u32[]{:S(2)}, u32[]{:S(2)}) collective-permute-start(f32[56,128]{1,0:T(8,128)S(1)} %add.51), channel_id=1, source_target_pairs={{0,7},{1,6},{2,5},{3,4},{4,3},{5,2},{6,1},{7,0},{8,15},{9,14},{10,... | collective-permute-start | bytes 86024 | tf_op jit(solution)/shard_map/ppermute | solution.py:624
  27.2 0.7 %collective-permute-start.9 = (f32[56,128]{1,0:T(8,128)S(1)}, f32[56,128]{1,0:T(8,128)S(1)}, u32[]{:S(2)}, u32[]{:S(2)}) collective-permute-start(f32[56,128]{1,0:T(8,128)S(1)} %add.51), channel_id=1, source_target_pairs={{0,5},{1,4},{2,7},{3,6},{4,1},{5,0},{6,3},{7,2},{8,13},{9,12},{10,... | collective-permute-start | bytes 86024 | tf_op jit(solution)/shard_map/ppermute | solution.py:624
  27.9 1.1 %collective-permute-start.8 = (f32[56,128]{1,0:T(8,128)S(1)}, f32[56,128]{1,0:T(8,128)S(1)}, u32[]{:S(2)}, u32[]{:S(2)}) collective-permute-start(f32[56,128]{1,0:T(8,128)S(1)} %add.51), channel_id=1, source_target_pairs={{0,3},{1,2},{2,1},{3,0},{4,7},{5,6},{6,5},{7,4},{8,11},{9,10},{10,... | collective-permute-start | bytes 86024 | tf_op jit(solution)/shard_map/ppermute | solution.py:624
  28.9 1.6 %collective-permute-start.12 = (bf16[68,4,128]{2,1,0:T(4,128)(2,1)S(1)}, bf16[68,4,128]{2,1,0:T(4,128)(2,1)S(1)}, u32[]{:S(2)}, u32[]{:S(2)}) collective-permute-start(bf16[68,4,128]{2,1,0:T(4,128)(2,1)S(1)} %get-tuple-element.109), channel_id=1, source_target_pairs={{0,24},{8,16},{16,8},{24,0},{1,25},{9,17},{17,9},{25,1},{2,26},{10... | collective-permute-start | bytes 208904 | tf_op jit(solution)/shard_map/ppermute | solution.py:629
  30.6 1.0 %collective-permute-start.11 = (bf16[68,4,128]{2,1,0:T(4,128)(2,1)S(1)}, bf16[68,4,128]{2,1,0:T(4,128)(2,1)S(1)}, u32[]{:S(2)}, u32[]{:S(2)}) collective-permute-start(bf16[68,4,128]{2,1,0:T(4,128)(2,1)S(1)} %get-tuple-element.108), channel_id=1, source_target_pairs={{0,8},{8,0},{16,24},{24,16},{1,9},{9,1},{17,25},{25,17},{2,10},{10... | collective-permute-start | bytes 208904 | tf_op jit(solution)/shard_map/ppermute | solution.py:629
  31.6 0.6 %shard_map.225.inner_ref = f32[16,32,128]{2,1,0:T(8,128)S(1)} custom-call(bf16[64,32,128]{2,1,0:T(8,128)(2,1)S(1)} %get-tuple-element.102.norm_ref, bf16[64,32,128]{2,1,0:T(8,128)(2,1)S(1)} %get-tuple-element.103.side_ref, f32[64,512]{1,0:T(8,128)S(1)} %get-tuple-element.104.kf_ref, f32[4,64,128]{2,1,0:T(8,128)S(1)} %get-tuple-element.86.vec_ref, ...), custom_call_target="tpu_custom_call" | custom-call | flops 2000000000 | bytes 6000000 | tf_op jit(solution)/shard_map/pallas_call | solution.py:488
  32.2 1.3 %collective-permute-start.15 = (f32[56,128]{1,0:T(8,128)S(1)}, f32[56,128]{1,0:T(8,128)S(1)}, u32[]{:S(2)}, u32[]{:S(2)}) collective-permute-start(f32[56,128]{1,0:T(8,128)S(1)} %add_add_fusion.refs_0_), channel_id=1, source_target_pairs={{0,25},{1,24},{2,27},{3,26},{4,29},{5,28},{6,31},{7,30},{8,17},{9,... | collective-permute-start | bytes 86024 | tf_op jit(solution)/shard_map/ppermute | solution.py:624
  33.5 1.2 %collective-permute-start.14 = (f32[56,128]{1,0:T(8,128)S(1)}, f32[56,128]{1,0:T(8,128)S(1)}, u32[]{:S(2)}, u32[]{:S(2)}) collective-permute-start(f32[56,128]{1,0:T(8,128)S(1)} %add_add_fusion.refs_0_), channel_id=1, source_target_pairs={{0,17},{1,16},{2,19},{3,18},{4,21},{5,20},{6,23},{7,22},{8,25},{9,... | collective-permute-start | bytes 86024 | tf_op jit(solution)/shard_map/ppermute | solution.py:624
  35.4 2.8 %shard_map.226 = bf16[64,32,128]{2,1,0:T(8,128)(2,1)} custom-call(s32[8,128]{1,0:T(8,128)S(1)} %iota.37.at_ref, bf16[68,4,128]{2,1,0:T(4,128)(2,1)S(1)} %collective-permute-done.11.one_ref, bf16[68,4,128]{2,1,0:T(4,128)(2,1)S(1)} %collective-permute-done.12.two_ref, bf16[64,32,128]{2,1,0:T(8,128)(2,1)S(1)} %get-tuple-element.102.norm_ref, ...), custom_call_target="tpu_custom_call" | custom-call | flops 3000000000 | bytes 9000000 | tf_op jit(solution)/shard_map/pallas_call | solution.py:488
  38.2 0.7 %shard_map.227 = (f32[48,64]{1,0:T(8,128)}, f32[64]{0:T(128)}, f32[64]{0:T(128)}, f32[64]{0:T(128)}, f32[64]{0:T(128)}, /*index=5*/f32[49,64]{1,0:T(8,128)}) custom-call(f32[56,128]{1,0:T(8,128)S(1)} %add_add_fusion.refs_0_, f32[56,128]{1,0:T(8,128)S(1)} %collective-permute-done.13.refs_1_, f32[56,128]{1,0:T(8,128)S(1)} %collective-permute-done.14.refs_2_, ...), custom_call_target="tpu_custom_call" | custom-call | flops 1000000000 | bytes 3000000 | tf_op jit(solution)/shard_map/pallas_call | solution.py:488
  (54 shorter events, 1.2 us)
Async XLA Ops:
  0.8 12.8 %copy-start.4 = (bf16[48,384]{1,0:T(8,128)(2,1)S(1)}, bf16[48,384]{1,0:T(8,128)(2,1)}, u32[]{:S(2)}) copy-start(bf16[48,384]{1,0:T(8,128)(2,1)} %constant.69.clone.spread_ref) | copy-start | bytes 110596
  0.8 12.8 %copy-start.6 = (f32[64,49]{0,1:T(8,128)S(1)}, f32[64,49]{0,1:T(8,128)}, u32[]{:S(2)}) copy-start(f32[64,49]{0,1:T(8,128)} %param.22) | copy-start | bytes 37636
  0.8 12.8 %copy-start.7 = (bf16[64,48]{0,1:T(8,128)(2,1)S(1)}, bf16[64,48]{0,1:T(8,128)(2,1)}, u32[]{:S(2)}) copy-start(bf16[64,48]{0,1:T(8,128)(2,1)} %param.18) | copy-start | bytes 18436
  0.8 12.8 %copy-start.9 = (f32[64]{0:T(128)S(1)}, f32[64]{0:T(128)}, u32[]{:S(2)}) copy-start(f32[64]{0:T(128)} %bias_ref.1) | copy-start | bytes 772
  0.8 13.3 %copy-start.5 = (f32[32,256]{1,0:T(8,128)S(1)}, f32[32,256]{1,0:T(8,128)}, u32[]{:S(2)}) copy-start(f32[32,256]{1,0:T(8,128)} %constant.75.clone.band_ref) | copy-start | bytes 98308
  0.9 17.1 %copy-start.8 = (f32[16,128]{1,0:T(8,128)S(1)}, f32[16,128]{1,0:T(8,128)}, u32[]{:S(2)}) copy-start(f32[16,128]{1,0:T(8,128)} %constant.76.clone.fringe_ref) | copy-start | bytes 24580
  2.8 16.3 %copy-start.13 = (bf16[56,384]{1,0:T(8,128)(2,1)S(1)}, bf16[56,384]{1,0:T(8,128)(2,1)}, u32[]{:S(2)}) copy-start(bf16[56,384]{1,0:T(8,128)(2,1)} %constant.77.clone.pick_ref) | copy-start | bytes 129028
  2.8 16.3 %copy-start.14 = (bf16[56,384]{1,0:T(8,128)(2,1)S(1)}, bf16[56,384]{1,0:T(8,128)(2,1)}, u32[]{:S(2)}) copy-start(bf16[56,384]{1,0:T(8,128)(2,1)} %constant.74.clone.taps_ref) | copy-start | bytes 129028
  2.8 5.2 %collective-permute-start = (bf16[960,128]{1,0:T(8,128)(2,1)S(1)}, bf16[960,128]{1,0:T(8,128)(2,1)S(1)}, u32[]{:S(2)}, u32[]{:S(2)}) collective-permute-start(bf16[960,128]{1,0:T(8,128)(2,1)S(1)} %get-tuple-element.64), channel_id=1, source_target_pairs={{0,1},{1,0},{2,3},{3,2},{4,5},{5,4},{6,7},{7,6},{8,9},{9,8},{10,11... | collective-permute-start | bytes 737288 | tf_op jit(solution)/shard_map/ppermute | solution.py:558
  3.3 6.6 %collective-permute-start.1 = (bf16[160,128]{1,0:T(8,128)(2,1)S(1)}, bf16[160,128]{1,0:T(8,128)(2,1)S(1)}, u32[]{:S(2)}, u32[]{:S(2)}) collective-permute-start(bf16[160,128]{1,0:T(8,128)(2,1)S(1)} %get-tuple-element.67), channel_id=1, source_target_pairs={{0,7},{1,2},{2,1},{3,4},{4,3},{5,6},{6,5},{7,0},{8,15},{9,10},{10,... | collective-permute-start | bytes 122888 | tf_op jit(solution)/shard_map/ppermute | solution.py:559
  8.1 10.9 %collective-permute-start.4 = (bf16[2,208,128]{2,1,0:T(8,128)(2,1)S(1)}, bf16[2,208,128]{2,1,0:T(8,128)(2,1)S(1)}, u32[]{:S(2)}, u32[]{:S(2)}) collective-permute-start(bf16[2,208,128]{2,1,0:T(8,128)(2,1)S(1)} %get-tuple-element.78), channel_id=1, source_target_pairs={{0,3},{1,2},{2,1},{3,0},{4,7},{5,6},{6,5},{7,4},{8,11},{9,10},{10,... | collective-permute-start | bytes 319496 | tf_op jit(solution)/shard_map/ppermute | solution.py:562
  8.1 10.9 %collective-permute-start.5 = (bf16[2,208,128]{2,1,0:T(8,128)(2,1)S(1)}, bf16[2,208,128]{2,1,0:T(8,128)(2,1)S(1)}, u32[]{:S(2)}, u32[]{:S(2)}) collective-permute-start(bf16[2,208,128]{2,1,0:T(8,128)(2,1)S(1)} %get-tuple-element.79), channel_id=1, source_target_pairs={{0,5},{1,4},{2,7},{3,6},{4,1},{5,0},{6,3},{7,2},{8,13},{9,12},{10,... | collective-permute-start | bytes 319496 | tf_op jit(solution)/shard_map/ppermute | solution.py:562
  9.8 9.2 %collective-permute-start.6 = (bf16[2,208,128]{2,1,0:T(8,128)(2,1)S(1)}, bf16[2,208,128]{2,1,0:T(8,128)(2,1)S(1)}, u32[]{:S(2)}, u32[]{:S(2)}) collective-permute-start(bf16[2,208,128]{2,1,0:T(8,128)(2,1)S(1)} %get-tuple-element.80), channel_id=1, source_target_pairs={{0,7},{1,6},{2,5},{3,4},{4,3},{5,2},{6,1},{7,0},{8,15},{9,14},{10,... | collective-permute-start | bytes 319496 | tf_op jit(solution)/shard_map/ppermute | solution.py:562
  10.5 5.3 %collective-permute-start.2 = (bf16[68,4,128]{2,1,0:T(4,128)(2,1)S(1)}, bf16[68,4,128]{2,1,0:T(4,128)(2,1)S(1)}, u32[]{:S(2)}, u32[]{:S(2)}) collective-permute-start(bf16[68,4,128]{2,1,0:T(4,128)(2,1)S(1)} %get-tuple-element.69), channel_id=1, source_target_pairs={{0,8},{8,0},{16,24},{24,16},{1,9},{9,1},{17,25},{25,17},{2,10},{10... | collective-permute-start | bytes 208904 | tf_op jit(solution)/shard_map/ppermute | solution.py:506
  12.1 5.9 %collective-permute-start.3 = (bf16[68,4,128]{2,1,0:T(4,128)(2,1)S(1)}, bf16[68,4,128]{2,1,0:T(4,128)(2,1)S(1)}, u32[]{:S(2)}, u32[]{:S(2)}) collective-permute-start(bf16[68,4,128]{2,1,0:T(4,128)(2,1)S(1)} %get-tuple-element.70), channel_id=1, source_target_pairs={{0,24},{8,16},{16,8},{24,0},{1,25},{9,17},{17,9},{25,1},{2,26},{10... | collective-permute-start | bytes 208904 | tf_op jit(solution)/shard_map/ppermute | solution.py:506
  23.0 1.8 %collective-permute-start.7 = (f32[56,128]{1,0:T(8,128)S(1)}, f32[56,128]{1,0:T(8,128)S(1)}, u32[]{:S(2)}, u32[]{:S(2)}) collective-permute-start(f32[56,128]{1,0:T(8,128)S(1)} %get-tuple-element.96), channel_id=1, source_target_pairs={{0,1},{1,0},{2,3},{3,2},{4,5},{5,4},{6,7},{7,6},{8,9},{9,8},{10,11... | collective-permute-start | bytes 86024 | tf_op jit(solution)/shard_map/ppermute | solution.py:624
  24.9 7.3 %collective-permute-start.10 = (f32[56,128]{1,0:T(8,128)S(1)}, f32[56,128]{1,0:T(8,128)S(1)}, u32[]{:S(2)}, u32[]{:S(2)}) collective-permute-start(f32[56,128]{1,0:T(8,128)S(1)} %add.51), channel_id=1, source_target_pairs={{0,7},{1,6},{2,5},{3,4},{4,3},{5,2},{6,1},{7,0},{8,15},{9,14},{10,... | collective-permute-start | bytes 86024 | tf_op jit(solution)/shard_map/ppermute | solution.py:624
  27.2 5.0 %collective-permute-start.9 = (f32[56,128]{1,0:T(8,128)S(1)}, f32[56,128]{1,0:T(8,128)S(1)}, u32[]{:S(2)}, u32[]{:S(2)}) collective-permute-start(f32[56,128]{1,0:T(8,128)S(1)} %add.51), channel_id=1, source_target_pairs={{0,5},{1,4},{2,7},{3,6},{4,1},{5,0},{6,3},{7,2},{8,13},{9,12},{10,... | collective-permute-start | bytes 86024 | tf_op jit(solution)/shard_map/ppermute | solution.py:624
  27.9 4.3 %collective-permute-start.8 = (f32[56,128]{1,0:T(8,128)S(1)}, f32[56,128]{1,0:T(8,128)S(1)}, u32[]{:S(2)}, u32[]{:S(2)}) collective-permute-start(f32[56,128]{1,0:T(8,128)S(1)} %add.51), channel_id=1, source_target_pairs={{0,3},{1,2},{2,1},{3,0},{4,7},{5,6},{6,5},{7,4},{8,11},{9,10},{10,... | collective-permute-start | bytes 86024 | tf_op jit(solution)/shard_map/ppermute | solution.py:624
  28.9 6.0 %collective-permute-start.12 = (bf16[68,4,128]{2,1,0:T(4,128)(2,1)S(1)}, bf16[68,4,128]{2,1,0:T(4,128)(2,1)S(1)}, u32[]{:S(2)}, u32[]{:S(2)}) collective-permute-start(bf16[68,4,128]{2,1,0:T(4,128)(2,1)S(1)} %get-tuple-element.109), channel_id=1, source_target_pairs={{0,24},{8,16},{16,8},{24,0},{1,25},{9,17},{17,9},{25,1},{2,26},{10... | collective-permute-start | bytes 208904 | tf_op jit(solution)/shard_map/ppermute | solution.py:629
  30.6 4.8 %collective-permute-start.11 = (bf16[68,4,128]{2,1,0:T(4,128)(2,1)S(1)}, bf16[68,4,128]{2,1,0:T(4,128)(2,1)S(1)}, u32[]{:S(2)}, u32[]{:S(2)}) collective-permute-start(bf16[68,4,128]{2,1,0:T(4,128)(2,1)S(1)} %get-tuple-element.108), channel_id=1, source_target_pairs={{0,8},{8,0},{16,24},{24,16},{1,9},{9,1},{17,25},{25,17},{2,10},{10... | collective-permute-start | bytes 208904 | tf_op jit(solution)/shard_map/ppermute | solution.py:629
  32.2 6.0 %collective-permute-start.15 = (f32[56,128]{1,0:T(8,128)S(1)}, f32[56,128]{1,0:T(8,128)S(1)}, u32[]{:S(2)}, u32[]{:S(2)}) collective-permute-start(f32[56,128]{1,0:T(8,128)S(1)} %add_add_fusion.refs_0_), channel_id=1, source_target_pairs={{0,25},{1,24},{2,27},{3,26},{4,29},{5,28},{6,31},{7,30},{8,17},{9,... | collective-permute-start | bytes 86024 | tf_op jit(solution)/shard_map/ppermute | solution.py:624
  33.5 4.7 %collective-permute-start.14 = (f32[56,128]{1,0:T(8,128)S(1)}, f32[56,128]{1,0:T(8,128)S(1)}, u32[]{:S(2)}, u32[]{:S(2)}) collective-permute-start(f32[56,128]{1,0:T(8,128)S(1)} %add_add_fusion.refs_0_), channel_id=1, source_target_pairs={{0,17},{1,16},{2,19},{3,18},{4,21},{5,20},{6,23},{7,22},{8,25},{9,... | collective-permute-start | bytes 86024 | tf_op jit(solution)/shard_map/ppermute | solution.py:624
  34.7 3.5 %collective-permute-start.13 = (f32[56,128]{1,0:T(8,128)S(1)}, f32[56,128]{1,0:T(8,128)S(1)}, u32[]{:S(2)}, u32[]{:S(2)}) collective-permute-start(f32[56,128]{1,0:T(8,128)S(1)} %add_add_fusion.refs_0_), channel_id=1, source_target_pairs={{0,9},{1,8},{2,11},{3,10},{4,13},{5,12},{6,15},{7,14},{8,1},{9,0},... | collective-permute-start | bytes 86024 | tf_op jit(solution)/shard_map/ppermute | solution.py:624
  (7 other events, 89.7 us)
